TPU v7x, 32 devices: a whole 2x2x4 slice. The times are simulated.
32 devices in a mesh: dp: 8 (over y, x, core), seq: 4 (over z).
Axes of the slice: x: 2, y: 2, z: 4, core: 2. Of those that a mesh axis runs over, the one named last changes fastest.
Arguments:
- frames_in: bfloat16 [8, 2048, 1024], P('dp', 'seq'), may hold values from -6 to 6
- skip_in: bfloat16 [8, 2048, 1024], P('dp', 'seq'), may hold values from -6 to 6
- condition: bfloat16 [8, 2048, 1024], P('dp', 'seq'), may hold values from -6 to 6
- flow_time: float32 [8], replicated, may hold values from 0 to 1
- span_start: int32 [8], P('dp'), may hold values from 0 to 614, as said below
- span_length: int32 [8], P('dp'), may hold values from 1434 to 2048
- out_grad: bfloat16 [8, 2048, 1024], P('dp', 'seq'), may hold values from -0.0234375 to 0.0234375
- skip_proj_state: float32 [3, 2048, 1024], P(None, ('dp', 'seq')), as said below
- attn_qkv_state: float32 [3, 1024, 3072], P(None, ('dp', 'seq')), as said below
- attn_out_state: float32 [3, 1024, 1024], P(None, ('dp', 'seq')), as said below
- ffn_up_state: float32 [3, 1024, 4096], P(None, ('dp', 'seq')), as said below
- ffn_down_state: float32 [3, 4096, 1024], P(None, ('dp', 'seq')), as said below
- ada_mod_state: float32 [3, 1024, 6144], P(None, ('dp', 'seq')), as said below
Outputs:
- block_out: bfloat16 [8, 2048, 1024], P('dp', 'seq')
- frames_grad: bfloat16 [8, 2048, 1024], P('dp', 'seq')
- skip_grad: bfloat16 [8, 2048, 1024], P('dp', 'seq')
- skip_proj_new: float32 [2048, 1024], P(('dp', 'seq'))
- skip_proj_moments: float32 [2, 2048, 1024], P(None, ('dp', 'seq'))
- attn_qkv_new: float32 [1024, 3072], P(('dp', 'seq'))
- attn_qkv_moments: float32 [2, 1024, 3072], P(None, ('dp', 'seq'))
- attn_out_new: float32 [1024, 1024], P(('dp', 'seq'))
- attn_out_moments: float32 [2, 1024, 1024], P(None, ('dp', 'seq'))
- ffn_up_new: float32 [1024, 4096], P(('dp', 'seq'))
- ffn_up_moments: float32 [2, 1024, 4096], P(None, ('dp', 'seq'))
- ffn_down_new: float32 [4096, 1024], P(('dp', 'seq'))
- ffn_down_moments: float32 [2, 4096, 1024], P(None, ('dp', 'seq'))
- ada_mod_new: float32 [1024, 6144], P(('dp', 'seq'))
- ada_mod_moments: float32 [2, 1024, 6144], P(None, ('dp', 'seq'))
Inputs may be any that keep to these rules, and one draw needn't show every extreme that they name: span_start + span_length <= 2048 for every utterance. `skip_proj_state`: the second moment (index 2) is positive. `attn_qkv_state`: the second moment (index 2) is positive. `attn_out_state`: the second moment (index 2) is positive. `ffn_up_state`: the second moment (index 2) is positive. `ffn_down_state`: the second moment (index 2) is positive. `ada_mod_state`: the second moment (index 2) is positive.
All inputs are finite; a program needn't handle non-finite values.
Results may differ from a plain program's by a relative error of at most 0.025.
The roundings to bfloat16 on the way count: a program that leaves them out, or rounds other values in their place, can miss the bound.
Values may be sent and summed in bfloat16 or wider, within the bound.
No kernel may reach another device: no remote copies, remote signals or barrier semaphores. Data moves between devices by JAX's collectives and lax.ppermute only.
A program may use at most 384 MiB of HBM per device.

v0:
```python
import math

import jax
import jax.numpy as jnp
from jax import lax
from jax.sharding import PartitionSpec as P

D = 1024
HEADS = 16
DH = 64
FF = 4096
STEP = 3


highest = lax.Precision.HIGHEST


def layer_norm(values):
    centre = values - jnp.mean(values, axis=-1, keepdims=True)
    spread = jnp.mean(centre * centre, axis=-1, keepdims=True)
    return centre * lax.rsqrt(spread + 1e-06)


def modulate(values, scale_mod, shift_mod):
    return layer_norm(values) * (1.0 + scale_mod[:, None, :]) + shift_mod[:, None, :]


def time_features(flow_values, model_width):
    half_size = model_width // 2
    frequency = jnp.exp(-math.log(10000.0) * jnp.arange(half_size, dtype=jnp.float32) / half_size)
    angles = 1000.0 * flow_values[:, None] * frequency[None, :]
    return jax.nn.silu(jnp.concatenate([jnp.sin(angles), jnp.cos(angles)], axis=-1))


def rotary_tables(positions, head_size):
    half_size = head_size // 2
    frequency = jnp.exp(-math.log(10000.0) * jnp.arange(half_size, dtype=jnp.float32) / half_size)
    angles = positions.astype(jnp.float32)[:, None] * frequency[None, :]
    return (
        jnp.concatenate([jnp.cos(angles), jnp.cos(angles)], axis=-1),
        jnp.concatenate([jnp.sin(angles), jnp.sin(angles)], axis=-1),
    )


def rotate(values, cosine, sine_table):
    half_size = values.shape[-1] // 2
    turned = jnp.concatenate([-values[..., half_size:], values[..., :half_size]], axis=-1)
    return values * cosine[:, None, :] + turned * sine_table[:, None, :]


def gelu_tanh(values):
    return jax.nn.gelu(values, approximate=True)


def learning_rates():
    fans = (2 * D, D, D // 16, D, FF, D // 8)
    return tuple((2.0 * fan_value ** (-0.5) for fan_value in fans))


def adamw_step(state, gradient, rate):
    master, first_moment, second_moment = (state[0], state[1], state[2])
    first_moment = 0.5 * first_moment + 0.5 * gradient
    second_moment = 0.5 * second_moment + 0.5 * gradient * gradient
    correction = 1.0 - 0.5**STEP
    master = master - rate * (
        first_moment / correction / (jnp.sqrt(second_moment / correction) + 1e-08) + 0.01 * master
    )
    return (master, jnp.stack([first_moment, second_moment]))


def rows_product(left_rows, right_rows):
    return lax.dot_general(
        left_rows, right_rows, (((0,), (0,)), ((), ())), preferred_element_type=jnp.float32
    )


def column_product(left_rows, right_rows):
    return rows_product(left_rows, right_rows)


def back_product(left_rows, weight_full):
    return lax.dot_general(
        left_rows, weight_full, (((1,), (1,)), ((), ())), preferred_element_type=jnp.float32
    )


def block_scores(queries, key_part):
    return (
        jnp.einsum("uqhd,ukhd->uhqk", queries, key_part, preferred_element_type=jnp.float32) * 0.125
    )


def per_device(
    frames_in,
    skip_in,
    condition,
    flow_time,
    span_start,
    span_length,
    out_grad,
    skip_proj_state,
    attn_qkv_state,
    attn_out_state,
    ffn_up_state,
    ffn_down_state,
    ada_mod_state,
):
    utter_count, frame_count, model_width = frames_in.shape
    row_count = utter_count * frame_count
    hidden_width = ffn_up_state.shape[2]
    fold_ratio = hidden_width // model_width
    owned_rows = attn_qkv_state.shape[1]
    seq_index = lax.axis_index("seq")
    data_index = lax.axis_index("dp")
    length_all = frame_count * lax.axis_size("seq")
    positions = seq_index * frame_count + jnp.arange(frame_count, dtype=jnp.int32)
    span_stop = span_start + span_length
    inside = (
        (positions[None, :] >= span_start[:, None]) & (positions[None, :] < span_stop[:, None])
    ).astype(jnp.float32)
    skip_low = skip_proj_state[0].astype(jnp.bfloat16)
    qkv_low = attn_qkv_state[0].astype(jnp.bfloat16)
    out_low = attn_out_state[0].astype(jnp.bfloat16)
    up_low = ffn_up_state[0].astype(jnp.bfloat16)
    down_low = ffn_down_state[0].astype(jnp.bfloat16)
    mod_low = ada_mod_state[0].astype(jnp.bfloat16)
    mod_full = lax.all_gather(mod_low, ("dp", "seq"), axis=0, tiled=True)
    own_time = lax.dynamic_slice_in_dim(flow_time, data_index * utter_count, utter_count)
    time_own = time_features(own_time, model_width).astype(jnp.bfloat16)
    modulation = jnp.dot(time_own, mod_full, preferred_element_type=jnp.float32)
    shift_one, scale_one, gate_one, shift_two, scale_two, gate_two = jnp.split(
        modulation, 6, axis=1
    )
    skip_full, qkv_full, out_full = (
        lax.all_gather(skip_low, ("dp", "seq"), axis=0, tiled=True),
        lax.all_gather(qkv_low, ("dp", "seq"), axis=0, tiled=True),
        lax.all_gather(out_low, ("dp", "seq"), axis=0, tiled=True),
    )
    joined = jnp.concatenate([frames_in, skip_in], axis=-1).reshape(row_count, 2 * model_width)
    linear = jnp.dot(joined, skip_full, preferred_element_type=jnp.float32).reshape(
        utter_count, frame_count, model_width
    )
    hidden = linear + condition.astype(jnp.float32) * (1.0 - inside[..., None])
    normed_f, ln_one_back = jax.vjp(modulate, hidden, scale_one, shift_one)
    normed = normed_f.astype(jnp.bfloat16).reshape(row_count, model_width)
    packed = jnp.dot(normed, qkv_full, preferred_element_type=jnp.float32).reshape(
        utter_count, frame_count, 3, HEADS, DH
    )
    cosine, sine_table = rotary_tables(positions, DH)
    query_raw = packed[:, :, 0]
    key_raw = packed[:, :, 1]
    query_rot, rotate_back = jax.vjp(rotate, query_raw, cosine, sine_table)
    queries = query_rot.astype(jnp.bfloat16)
    key_low = (
        rotate(key_raw, cosine, sine_table)
        .astype(jnp.bfloat16)
        .reshape(utter_count, frame_count, model_width)
    )
    value_low = packed[:, :, 2].astype(jnp.bfloat16).reshape(utter_count, frame_count, model_width)
    key_all, value_all = (
        lax.all_gather(key_low, "seq", axis=1, tiled=True),
        lax.all_gather(value_low, "seq", axis=1, tiled=True),
    )
    key_heads = key_all.reshape(utter_count, length_all, HEADS, DH)
    value_heads = value_all.reshape(utter_count, length_all, HEADS, DH)
    block_size = min(512, length_all)
    block_total = length_all // block_size
    running_top = jnp.zeros((utter_count, HEADS, frame_count), jnp.float32)
    running_sum = jnp.zeros((utter_count, HEADS, frame_count), jnp.float32)
    for block_index in range(block_total):
        lower_edge = block_index * block_size
        scores = block_scores(queries, key_heads[:, lower_edge : lower_edge + block_size])
        block_top = jnp.max(scores, axis=-1)
        if block_index == 0:
            running_top = block_top
            running_sum = jnp.sum(jnp.exp(scores - block_top[..., None]), axis=-1)
        else:
            new_top = jnp.maximum(running_top, block_top)
            running_sum = running_sum * jnp.exp(running_top - new_top) + jnp.sum(
                jnp.exp(scores - new_top[..., None]), axis=-1
            )
            running_top = new_top
    log_total = running_top + jnp.log(running_sum)
    attended = jnp.zeros((utter_count, frame_count, HEADS, DH), jnp.float32)
    for block_index in range(block_total):
        lower_edge = block_index * block_size
        scores = block_scores(queries, key_heads[:, lower_edge : lower_edge + block_size])
        probs = jnp.exp(scores - log_total[..., None]).astype(jnp.bfloat16)
        attended = attended + jnp.einsum(
            "uhqk,ukhd->uqhd",
            probs,
            value_heads[:, lower_edge : lower_edge + block_size],
            preferred_element_type=jnp.float32,
        )
    attended_low = attended.reshape(row_count, model_width).astype(jnp.bfloat16)
    branch = jnp.dot(attended_low, out_full, preferred_element_type=jnp.float32).reshape(
        utter_count, frame_count, model_width
    )
    middle = hidden + gate_one[:, None, :] * branch
    normed_two_f, ln_two_back = jax.vjp(modulate, middle, scale_two, shift_two)
    normed_two = normed_two_f.astype(jnp.bfloat16).reshape(row_count, model_width)
    up_full, down_full = (
        lax.all_gather(up_low, ("dp", "seq"), axis=0, tiled=True),
        lax.all_gather(down_low, ("dp", "seq"), axis=0, tiled=True),
    )
    upward = jnp.dot(normed_two, up_full, preferred_element_type=jnp.float32)
    activated_f, gelu_back = jax.vjp(gelu_tanh, upward)
    activated = activated_f.astype(jnp.bfloat16)
    downward = jnp.dot(activated, down_full, preferred_element_type=jnp.float32).reshape(
        utter_count, frame_count, model_width
    )
    block_out = (middle + gate_two[:, None, :] * downward).astype(jnp.bfloat16)
    grad_rows = out_grad.astype(jnp.float32) * inside[..., None]
    up_back, down_back = (
        lax.all_gather(up_low, ("dp", "seq"), axis=0, tiled=True),
        lax.all_gather(down_low, ("dp", "seq"), axis=0, tiled=True),
    )
    down_cot = (
        (grad_rows * gate_two[:, None, :]).astype(jnp.bfloat16).reshape(row_count, model_width)
    )
    gate_two_grad = jnp.sum(grad_rows * downward, axis=1)
    act_grad = back_product(down_cot, down_back)
    up_cot = gelu_back(act_grad)[0].astype(jnp.bfloat16)
    normed_two_grad = back_product(up_cot, up_back).reshape(utter_count, frame_count, model_width)
    up_part = column_product(normed_two, up_cot)
    down_part = column_product(activated, down_cot)
    ffn_sum = lax.psum_scatter(
        jnp.concatenate(
            [up_part, down_part.reshape(owned_rows * lax.axis_size(("dp", "seq")), hidden_width)],
            axis=-1,
        ),
        ("dp", "seq"),
        scatter_dimension=0,
        tiled=True,
    )
    up_wgrad = ffn_sum[:, :hidden_width]
    down_wgrad = ffn_sum[:, hidden_width:].reshape(owned_rows * fold_ratio, model_width)
    middle_norm_grad, scale_two_grad, shift_two_grad = ln_two_back(normed_two_grad)
    middle_grad = grad_rows + middle_norm_grad
    skip_back, qkv_back, out_back = (
        lax.all_gather(skip_low, ("dp", "seq"), axis=0, tiled=True),
        lax.all_gather(qkv_low, ("dp", "seq"), axis=0, tiled=True),
        lax.all_gather(out_low, ("dp", "seq"), axis=0, tiled=True),
    )
    branch_cot = (
        (middle_grad * gate_one[:, None, :]).astype(jnp.bfloat16).reshape(row_count, model_width)
    )
    gate_one_grad = jnp.sum(middle_grad * branch, axis=1)
    attended_grad = (
        back_product(branch_cot, out_back)
        .astype(jnp.bfloat16)
        .reshape(utter_count, frame_count, HEADS, DH)
    )
    delta = jnp.zeros((utter_count, HEADS, frame_count), jnp.float32)
    for block_index in range(block_total):
        lower_edge = block_index * block_size
        scores = block_scores(queries, key_heads[:, lower_edge : lower_edge + block_size])
        probs = jnp.exp(scores - log_total[..., None])
        prob_grad = jnp.einsum(
            "uqhd,ukhd->uhqk",
            attended_grad,
            value_heads[:, lower_edge : lower_edge + block_size],
            preferred_element_type=jnp.float32,
        )
        delta = delta + jnp.sum(probs * prob_grad, axis=-1)
    query_grad = jnp.zeros((utter_count, frame_count, HEADS, DH), jnp.float32)
    for block_index in range(block_total):
        lower_edge = block_index * block_size
        key_part = key_heads[:, lower_edge : lower_edge + block_size]
        scores = block_scores(queries, key_part)
        probs = jnp.exp(scores - log_total[..., None])
        prob_grad = jnp.einsum(
            "uqhd,ukhd->uhqk",
            attended_grad,
            value_heads[:, lower_edge : lower_edge + block_size],
            preferred_element_type=jnp.float32,
        )
        score_grad = (probs * (prob_grad - delta[..., None])).astype(jnp.bfloat16)
        query_grad = (
            query_grad
            + jnp.einsum(
                "uhqk,ukhd->uqhd", score_grad, key_part, preferred_element_type=jnp.float32
            )
            * 0.125
        )
    count = lax.axis_size("seq") * frame_count
    sub_block = math.gcd(count, 512)

    def piece_terms(piece_start):
        key_part = lax.dynamic_slice_in_dim(key_heads, piece_start, sub_block, 1)
        value_part = lax.dynamic_slice_in_dim(value_heads, piece_start, sub_block, 1)
        scores = block_scores(queries, key_part)
        probs = jnp.exp(scores - log_total[..., None])
        prob_grad = jnp.einsum(
            "uqhd,ukhd->uhqk", attended_grad, value_part, preferred_element_type=jnp.float32
        )
        score_grad = (probs * (prob_grad - delta[..., None])).astype(jnp.bfloat16)
        key_grad = (
            jnp.einsum("uhqk,uqhd->kuhd", score_grad, queries, preferred_element_type=jnp.float32)
            * 0.125
        )
        value_grad = jnp.einsum(
            "uhqk,uqhd->kuhd",
            probs.astype(jnp.bfloat16),
            attended_grad,
            preferred_element_type=jnp.float32,
        )
        return jnp.concatenate(
            [
                key_grad.reshape(sub_block, utter_count, model_width),
                value_grad.reshape(sub_block, utter_count, model_width),
            ],
            axis=-1,
        )

    piece_starts = sub_block * jnp.arange(count // sub_block, dtype=jnp.int32)
    kv_grad = lax.psum_scatter(
        lax.map(piece_terms, piece_starts)
        .reshape(count, utter_count, 2 * model_width)
        .astype(jnp.bfloat16),
        "seq",
        scatter_dimension=0,
        tiled=True,
    ).astype(jnp.float32)
    kv_grad = jnp.moveaxis(kv_grad, 0, 1)
    key_grad_local = kv_grad[..., :model_width].reshape(utter_count, frame_count, HEADS, DH)
    value_grad_local = kv_grad[..., model_width:]
    query_raw_grad = rotate_back(query_grad)[0].reshape(utter_count, frame_count, model_width)
    key_raw_grad = rotate_back(key_grad_local)[0].reshape(utter_count, frame_count, model_width)
    packed_cot = (
        jnp.concatenate([query_raw_grad, key_raw_grad, value_grad_local], axis=-1)
        .astype(jnp.bfloat16)
        .reshape(row_count, 3 * model_width)
    )
    normed_grad = back_product(packed_cot, qkv_back).reshape(utter_count, frame_count, model_width)
    hidden_norm_grad, scale_one_grad, shift_one_grad = ln_one_back(normed_grad)
    hidden_grad = (
        (middle_grad + hidden_norm_grad).astype(jnp.bfloat16).reshape(row_count, model_width)
    )
    joined_grad = back_product(hidden_grad, skip_back).astype(jnp.bfloat16)
    frames_grad = joined_grad[:, :model_width].reshape(utter_count, frame_count, model_width)
    skip_grad = joined_grad[:, model_width:].reshape(utter_count, frame_count, model_width)
    skip_part = column_product(joined, hidden_grad).reshape(
        owned_rows * lax.axis_size(("dp", "seq")), 2 * model_width
    )
    qkv_part = column_product(normed, packed_cot)
    out_part = column_product(attended_low, branch_cot)
    attention_sum = lax.psum_scatter(
        jnp.concatenate([skip_part, qkv_part, out_part], axis=-1),
        ("dp", "seq"),
        scatter_dimension=0,
        tiled=True,
    )
    skip_wgrad = attention_sum[:, : 2 * model_width].reshape(2 * owned_rows, model_width)
    qkv_wgrad = attention_sum[:, 2 * model_width : 5 * model_width]
    out_wgrad = attention_sum[:, 5 * model_width :]
    mod_cot = jnp.concatenate(
        [
            shift_one_grad,
            scale_one_grad,
            gate_one_grad,
            shift_two_grad,
            scale_two_grad,
            gate_two_grad,
        ],
        axis=-1,
    )
    time_own_f = time_own.astype(jnp.float32)
    mod_wgrad = lax.psum_scatter(
        lax.dot_general(
            time_own_f,
            mod_cot,
            (((0,), (0,)), ((), ())),
            precision=highest,
            preferred_element_type=jnp.float32,
        ),
        ("dp", "seq"),
        scatter_dimension=0,
        tiled=True,
    )
    rates = learning_rates()
    skip_new, skip_moments = adamw_step(skip_proj_state, skip_wgrad, rates[0])
    qkv_new, qkv_moments = adamw_step(attn_qkv_state, qkv_wgrad, rates[1])
    out_new, out_moments = adamw_step(attn_out_state, out_wgrad, rates[2])
    up_new, up_moments = adamw_step(ffn_up_state, up_wgrad, rates[3])
    down_new, down_moments = adamw_step(ffn_down_state, down_wgrad, rates[4])
    mod_new, mod_moments = adamw_step(ada_mod_state, mod_wgrad, rates[5])
    return (
        block_out,
        frames_grad,
        skip_grad,
        skip_new,
        skip_moments,
        qkv_new,
        qkv_moments,
        out_new,
        out_moments,
        up_new,
        up_moments,
        down_new,
        down_moments,
        mod_new,
        mod_moments,
    )


def solution(mesh):
    placed = (
        P("dp", "seq", None),
        P("dp", "seq", None),
        P("dp", "seq", None),
        P(),
        P("dp"),
        P("dp"),
        P("dp", "seq", None),
        P(None, ("dp", "seq"), None),
        P(None, ("dp", "seq"), None),
        P(None, ("dp", "seq"), None),
        P(None, ("dp", "seq"), None),
        P(None, ("dp", "seq"), None),
        P(None, ("dp", "seq"), None),
    )
    return jax.shard_map(
        per_device,
        mesh=mesh,
        in_specs=placed,
        out_specs=(
            P("dp", "seq", None),
            P("dp", "seq", None),
            P("dp", "seq", None),
            P(("dp", "seq"), None),
            P(None, ("dp", "seq"), None),
            P(("dp", "seq"), None),
            P(None, ("dp", "seq"), None),
            P(("dp", "seq"), None),
            P(None, ("dp", "seq"), None),
            P(("dp", "seq"), None),
            P(None, ("dp", "seq"), None),
            P(("dp", "seq"), None),
            P(None, ("dp", "seq"), None),
            P(("dp", "seq"), None),
            P(None, ("dp", "seq"), None),
        ),
        check_vma=False,
    )
```

profile of v0, /device:TPU:0, one launch (start us, length us, event | category | flops | bytes accessed | tf_op | source)
XLA Modules:
  0.0 2343.9 jit_solution(15299802108987196406)
XLA Ops:
  18.3 58.1 %all-gather.9.cloned.1.call-done = bf16[2048,1024]{1,0:T(8,128)(2,1)} async-done(((bf16[64,1024]{1,0:T(8,128)(2,1)}), bf16[2048,1024]{1,0:T(8,128)(2,1)}) %all-gather.9.cloned.1.call-update) | async-done | bytes 4194320 | tf_op jit(solution)/shard_map/all_gather | solution.py:135
  76.4 5.5 fusion.182
  82.3 65.7 %all-gather.13.cloned.1.call-done = bf16[1024,3072]{1,0:T(8,128)(2,1)} async-done(((bf16[32,3072]{1,0:T(8,128)(2,1)}), bf16[1024,3072]{1,0:T(8,128)(2,1)}) %all-gather.13.cloned.1.call-update) | async-done | bytes 6291472 | tf_op jit(solution)/shard_map/all_gather | solution.py:136
  148.0 8.6 copy.44
  156.6 89.4 %all-gather.11.cloned.1.call-done = bf16[1024,6144]{1,0:T(8,128)(2,1)} async-done(((bf16[32,6144]{1,0:T(8,128)(2,1)}), bf16[1024,6144]{1,0:T(8,128)(2,1)}) %all-gather.11.cloned.1.call-update) | async-done | bytes 12582928 | tf_op jit(solution)/shard_map/all_gather | solution.py:127
  246.0 6.5 fusion.183
  278.1 62.7 %all-gather.17.cloned.1.call-done = bf16[1,2048,1024]{1,2,0:T(8,128)(2,1)} async-done(((bf16[1,512,1024]{1,2,0:T(8,128)(2,1)}), bf16[1,2048,1024]{1,2,0:T(8,128)(2,1)}) %all-gather.17.cloned.1.call-update) | async-done | bytes 4194320 | tf_op jit(solution)/shard_map/all_gather | solution.py:161
  340.8 10.3 multiply_reduce_fusion.7
  351.1 8.2 multiply_reduce_fusion.6
  359.2 8.2 multiply_reduce_fusion.5
  367.4 8.2 multiply_reduce_fusion.4
  375.6 9.1 exponential_reduce_fusion.3
  384.7 8.6 exponential_reduce_fusion.2
  393.3 8.7 exponential_reduce_fusion.1
  402.0 8.6 exponential_reduce_fusion
  410.6 11.5 all-gather.15.cloned.1.call-done
  422.1 10.7 fusion.32
  432.8 10.1 fusion.30
  446.8 10.6 add_convert_fusion.3
  457.5 23.0 all-gather.19.cloned.1.call-done
  480.5 4.2 fusion.176
  486.4 73.9 %all-gather.21.cloned.1.call-done = bf16[1024,4096]{1,0:T(8,128)(2,1)} async-done(((bf16[32,4096]{1,0:T(8,128)(2,1)}), bf16[1024,4096]{1,0:T(8,128)(2,1)}) %all-gather.21.cloned.1.call-update) | async-done | bytes 8388624 | tf_op jit(solution)/shard_map/all_gather | solution.py:203
  560.3 12.0 fusion.170
  572.3 67.5 %all-gather.23.cloned.1.call-done = bf16[4096,1024]{1,0:T(8,128)(2,1)} async-done(((bf16[128,1024]{1,0:T(8,128)(2,1)}), bf16[4096,1024]{1,0:T(8,128)(2,1)}) %all-gather.23.cloned.1.call-update) | async-done | bytes 8388624 | tf_op jit(solution)/shard_map/all_gather | solution.py:204
  639.8 12.9 fusion.42
  652.7 5.4 fusion.60
  663.6 9.6 fusion.88
  673.2 8.2 fusion.89
  681.4 8.1 fusion.82
  689.7 39.9 %multiply_reduce_fusion.2 = (f32[16,512]{1,0:T(8,128)S(1)}, f32[16,512]{1,0:T(8,128)S(1)}, f32[16,512]{1,0:T(8,128)S(1)}, f32[16,512]{1,0:T(8,128)S(1)}, f32[16,512,512]{1,2,0:T(8,128)}) fusion(f32[16,512,512]{1,2,0:T(8,128)} %get-tuple-element.177, f32[16,512]{1,0:T(8,128)S(1)} %log_add_fusion, f32[16,512,512]{1,2,0:T(8,128)} %fusion.82, ...), kind=kOutput, calls=%fused_computation.31 | convolution fusion | flops 603947008 | bytes 136478720 | tf_op jit(solution)/shard_map/uqhd,ukhd->uhqk/dot_general | solution.py:259
  729.6 166.0 %while.10 = (s32[]{:T(128)}, bf16[4,512,1,2048]{3,1,0,2:T(8,128)(2,1)}, s32[4]{0:T(128)S(1)}, bf16[1,2048,16,64]{1,3,2,0:T(8,128)(2,1)}, bf16[1,512,16,64]{1,3,2...) while((s32[]{:T(128)}, ...), condition=%wide.region_19.20_spmd, body=%wide.region_18.19_spmd.sunk | while | flops 2186280960 | bytes 75596488 | solution.py:318
  732.3 11.9 fusion.228
  744.2 11.2 fusion.230
  755.4 8.5 fusion.229
  773.8 11.9 fusion.228
  785.7 11.2 fusion.230
  796.9 8.5 fusion.229
  815.3 11.9 fusion.228
  827.2 11.2 fusion.230
  838.4 8.5 fusion.229
  856.8 11.8 fusion.228
  868.6 11.2 fusion.230
  879.8 8.5 fusion.229
  895.7 15.5 fusion.51
  911.2 14.1 fusion.53
  925.4 14.1 fusion.52
  939.5 17.1 bitcast_multiply_fusion.5
  962.7 4.6 fusion.106
  967.3 71.6 %reduce-scatter.5.cloned.1.call-done = bf16[512,1,2048]{2,0,1:T(8,128)(2,1)} async-done(((bf16[2048,1,2048]{2,0,1:T(8,128)(2,1)}), bf16[512,1,2048]{2,0,1:T(8,128)(2,1)}) %reduce-scatter.5.cloned.1.call-update) | async-done | bytes 2097168 | tf_op jit(solution)/shard_map/reduce_scatter | solution.py:317
  1051.6 9.9 fusion.74
  1061.6 6.7 fusion.62
  1071.9 11.9 fusion.59
  1083.9 5.7 fusion.73
  1089.6 9.9 reshape.1064
  1099.5 17.8 pad_maximum_fusion.1
  1120.8 14.5 broadcast_multiply_fusion
  1136.6 17.9 fusion.112
  1154.6 21.5 reshape.1067
  1176.1 12.2 fusion.168
  1188.3 18.5 pad_maximum_fusion
  1206.9 4.6 convolution_convert_fusion
  1213.1 150.5 %reduce-scatter.7.cloned.1.call-done = f32[32,6144]{1,0:T(8,128)} async-done(((f32[1024,6144]{1,0:T(8,128)}), f32[32,6144]{1,0:T(8,128)}) %reduce-scatter.7.cloned.1.call-update) | async-done | bytes 786448 | tf_op jit(solution)/shard_map/reduce_scatter | solution.py:348
  1373.8 242.4 %reduce-scatter.11.cloned.1.call-done = f32[32,6144]{1,0:T(8,128)} async-done(((f32[1024,6144]{1,0:T(8,128)}), f32[32,6144]{1,0:T(8,128)}) %reduce-scatter.11.cloned.1.call-update) | async-done | bytes 786448 | tf_op jit(solution)/shard_map/reduce_scatter | solution.py:369
  1620.1 709.9 %reduce-scatter.9.cloned.1.call-done = f32[32,8192]{1,0:T(8,128)} async-done(((f32[1024,8192]{1,0:T(8,128)}), f32[32,8192]{1,0:T(8,128)}) %reduce-scatter.9.cloned.1.call-update) | async-done | bytes 1048592 | tf_op jit(solution)/shard_map/reduce_scatter | solution.py:227
  (305 shorter events, 127.4 us)
Async XLA Ops:
  7.2 69.2 %all-gather.9.cloned.1.call-start = ((), (), s32[]{:S(2)}) async-start(), calls=%async_computation.4 | async-start | bytes 4325376 | tf_op jit(solution)/shard_map/all_gather | solution.py:135
  8.9 139.1 %all-gather.13.cloned.1.call-start = ((), (), s32[]{:S(2)}) async-start(), calls=%async_computation.6 | async-start | bytes 6488064 | tf_op jit(solution)/shard_map/all_gather | solution.py:136
  10.6 235.4 %all-gather.11.cloned.1.call-start = ((), (), s32[]{:S(2)}) async-start(), calls=%async_computation.5 | async-start | bytes 12976128 | tf_op jit(solution)/shard_map/all_gather | solution.py:127
  12.6 328.1 %all-gather.17.cloned.1.call-start = ((), (), s32[]{:S(2)}) async-start(), calls=%async_computation.8 | async-start | bytes 5242880 | tf_op jit(solution)/shard_map/all_gather | solution.py:161
  17.6 257.3 %copy-start.31 = (f32[512,64]{0,1:T(8,128)}, f32[512,64]{0,1:T(8,128)S(1)}, u32[]{:S(2)}) copy-start(f32[512,64]{0,1:T(8,128)S(1)} %get-tuple-element.157) | copy-start | bytes 393220
  18.3 256.6 %copy-start.29 = (f32[512,64]{0,1:T(8,128)}, f32[512,64]{0,1:T(8,128)S(1)}, u32[]{:S(2)}) copy-start(f32[512,64]{0,1:T(8,128)S(1)} %get-tuple-element.159) | copy-start | bytes 393220
  81.9 398.6 %copy-start.3 = (f32[1,512,1024]{2,1,0:T(8,128)}, f32[1,512,1024]{2,1,0:T(8,128)S(1)}, u32[]{:S(2)}) copy-start(f32[1,512,1024]{2,1,0:T(8,128)S(1)} %get-tuple-element.169) | copy-start | bytes 6291460
  81.9 170.7 %copy-start.49 = (f32[512]{0:T(512)}, f32[512]{0:T(512)S(1)}, u32[]{:S(2)}) copy-start(f32[512]{0:T(512)S(1)} %broadcast_multiply_fusion.5) | copy-start | bytes 6148
  82.3 74.4 %copy-start.57 = (f32[512]{0:T(512)}, f32[512]{0:T(512)S(1)}, u32[]{:S(2)}) copy-start(f32[512]{0:T(512)S(1)} %multiply_reduce_fusion.9) | copy-start | bytes 6148
  82.3 170.3 %copy-start.51 = (f32[512]{0:T(512)}, f32[512]{0:T(512)S(1)}, u32[]{:S(2)}) copy-start(f32[512]{0:T(512)S(1)} %fusion.153) | copy-start | bytes 6148
  246.0 6.6 copy-start.24
  252.5 307.7 %copy-start.68 = (f32[1,1024]{1,0:T(1,128)}, f32[1,1024]{1,0:T(1,128)S(1)}, u32[]{:S(2)}) copy-start(f32[1,1024]{1,0:T(1,128)S(1)} %get-tuple-element.165) | copy-start | bytes 12292
  252.6 387.2 %copy-start.70 = (f32[1,1024]{1,0:T(1,128)}, f32[1,1024]{1,0:T(1,128)S(1)}, u32[]{:S(2)}) copy-start(f32[1,1024]{1,0:T(1,128)S(1)} %get-tuple-element.160) | copy-start | bytes 12292
  252.6 405.6 %copy-start.59 = (f32[1,1024]{1,0:T(1,128)}, f32[1,1024]{1,0:T(1,128)S(1)}, u32[]{:S(2)}) copy-start(f32[1,1024]{1,0:T(1,128)S(1)} %get-tuple-element.161) | copy-start | bytes 12292
  252.6 406.3 %copy-start.53 = (f32[1,1024]{1,0:T(1,128)}, f32[1,1024]{1,0:T(1,128)S(1)}, u32[]{:S(2)}) copy-start(f32[1,1024]{1,0:T(1,128)S(1)} %get-tuple-element.164) | copy-start | bytes 12292
  261.6 160.5 %all-gather.15.cloned.1.call-start = ((), (), s32[]{:S(2)}) async-start(), calls=%async_computation.7 | async-start | bytes 5242880 | tf_op jit(solution)/shard_map/all_gather | solution.py:162
  264.4 216.1 %all-gather.19.cloned.1.call-start = ((), (), s32[]{:S(2)}) async-start(), calls=%async_computation.9 | async-start | bytes 2162688 | tf_op jit(solution)/shard_map/all_gather | solution.py:137
  266.0 294.3 %all-gather.21.cloned.1.call-start = ((), (), s32[]{:S(2)}) async-start(), calls=%async_computation.10 | async-start | bytes 8650752 | tf_op jit(solution)/shard_map/all_gather | solution.py:203
  267.9 371.9 %all-gather.23.cloned.1.call-start = ((), (), s32[]{:S(2)}) async-start(), calls=%async_computation.11 | async-start | bytes 8650752 | tf_op jit(solution)/shard_map/all_gather | solution.py:204
  269.8 769.1 %reduce-scatter.5.cloned.1.call-start = ((), (), s32[]{:S(2)}) async-start(), calls=%async_computation.12 | async-start | bytes 10485760 | tf_op jit(solution)/shard_map/reduce_scatter | solution.py:317
  270.6 388.4 %copy-start.62 = (f32[512]{0:T(512)}, f32[512]{0:T(512)S(1)}, u32[]{:S(2)}) copy-start(f32[512]{0:T(512)S(1)} %fusion.152) | copy-start | bytes 6148
  340.8 10.3 copy-start.1
  422.1 10.7 copy-start.11
  422.1 20.7 slice-start
  422.1 20.7 slice-start.1
  432.8 10.1 slice-start.2
  432.8 10.1 slice-start.3
  457.5 27.2 %copy-start.14 = (bf16[16,64,512]{2,1,0:T(8,128)(2,1)}, bf16[16,64,512]{2,1,0:T(8,128)(2,1)S(1)}, u32[]{:S(2)}) copy-start(bf16[16,64,512]{2,1,0:T(8,128)(2,1)S(1)} %add_convert_fusion.3) | copy-start | bytes 3145732
  484.7 173.5 %copy-start.55 = (f32[512]{0:T(512)}, f32[512]{0:T(512)S(1)}, u32[]{:S(2)}) copy-start(f32[512]{0:T(512)S(1)} %broadcast_multiply_fusion.4) | copy-start | bytes 6148
  486.4 171.8 %copy-start.64 = (f32[512]{0:T(512)}, f32[512]{0:T(512)S(1)}, u32[]{:S(2)}) copy-start(f32[512]{0:T(512)S(1)} %fusion.154) | copy-start | bytes 6148
  560.3 79.5 %copy-start.38 = (bf16[1,512,1024]{2,1,0:T(8,128)(2,1)S(1)}, bf16[1,512,1024]{2,1,0:T(8,128)(2,1)}, u32[]{:S(2)}) copy-start(bf16[1,512,1024]{2,1,0:T(8,128)(2,1)} %param.21) | copy-start | bytes 3145732
  639.8 12.9 copy-start.8
  639.8 12.9 copy-start.73
  663.6 9.6 copy-start.12
  673.2 16.4 slice-start.4
  673.2 16.4 slice-start.5
  681.4 8.2 slice-start.6
  681.4 8.2 slice-start.7
  689.6 39.9 %copy-start.5 = (bf16[1,512,16,64]{1,3,2,0:T(8,128)(2,1)S(1)}, bf16[1,512,16,64]{1,3,2,0:T(8,128)(2,1)}, u32[]{:S(2)}) copy-start(bf16[1,512,16,64]{1,3,2,0:T(8,128)(2,1)} %fusion.58) | copy-start | bytes 3145732
  689.6 39.9 %copy-start.76 = (s32[4]{0:T(128)S(1)}, s32[4]{0:T(128)}, u32[]{:S(2)}) copy-start(s32[4]{0:T(128)} %iota_multiply_fusion) | copy-start | bytes 52
  895.7 467.9 %reduce-scatter.7.cloned.1.call-start = ((), (), s32[]{:S(2)}) async-start(), calls=%async_computation.13 | async-start | bytes 25952256 | tf_op jit(solution)/shard_map/reduce_scatter | solution.py:348
  895.7 15.5 copy-start.2
  925.4 14.1 copy-start.43
  1046.0 5.6 copy-start.4
  1046.0 5.6 copy-start.46
  1051.6 9.9 copy-start.27
  1051.6 9.9 copy-start.28
  1061.5 6.8 copy-start.58
  1061.5 7.5 copy-start.39
  1068.3 15.6 copy-start.19
  1071.9 12.0 copy-start.74
  1071.9 12.0 copy-start.75
  1117.3 498.9 %reduce-scatter.11.cloned.1.call-start = ((), (), s32[]{:S(2)}) async-start(), calls=%async_computation.15 | async-start | bytes 25952256 | tf_op jit(solution)/shard_map/reduce_scatter | solution.py:369
  1135.4 1194.6 %reduce-scatter.9.cloned.1.call-start = ((), (), s32[]{:S(2)}) async-start(), calls=%async_computation.14 | async-start | bytes 34603008 | tf_op jit(solution)/shard_map/reduce_scatter | solution.py:227
  1154.6 21.5 copy-start.10
  1154.6 21.5 copy-start.56
  1154.6 21.5 copy-start.60
  1154.6 21.5 copy-start.65
  1154.6 21.5 copy-start.69
  1176.1 12.3 copy-start
  1211.6 153.8 %copy-start.42 = (f32[3,32,1024]{2,1,0:T(8,128)S(1)}, f32[3,32,1024]{2,1,0:T(8,128)}, u32[]{:S(2)}) copy-start(f32[3,32,1024]{2,1,0:T(8,128)} %param.24) | copy-start | bytes 1179652
  1211.6 156.2 %copy-start.34 = (f32[3,64,1024]{2,1,0:T(8,128)S(1)}, f32[3,64,1024]{2,1,0:T(8,128)}, u32[]{:S(2)}) copy-start(f32[3,64,1024]{2,1,0:T(8,128)} %param.22) | copy-start | bytes 2359300
  1367.1 249.1 %copy-start.33 = (f32[3,32,6144]{2,1,0:T(8,128)S(1)}, f32[3,32,6144]{2,1,0:T(8,128)}, u32[]{:S(2)}) copy-start(f32[3,32,6144]{2,1,0:T(8,128)} %param.27) | copy-start | bytes 7077892
  1620.1 713.2 %copy-start.25 = (f32[3,128,1024]{2,1,0:T(8,128)S(1)}, f32[3,128,1024]{2,1,0:T(8,128)}, u32[]{:S(2)}) copy-start(f32[3,128,1024]{2,1,0:T(8,128)} %param.26) | copy-start | bytes 4718596
  (37 other events, 122.9 us)
Sparse Core Ops, SparseCore 0:
  11.6 64.7 all-gather.8
  79.9 68.0 all-gather.12
  151.5 94.5 all-gather.10
  261.7 78.9 all-gather.16
  342.8 79.2 all-gather.14
  425.4 54.9 all-gather.18
  484.0 76.2 all-gather.20
  563.8 75.9 all-gather.22
  895.8 143.0 reduce-scatter.4
  1117.4 246.0 reduce-scatter.6
  1371.1 245.0 reduce-scatter.10
  1618.4 711.5 reduce-scatter.8
where the time goes:
time: 2350 us; the launch traced here: 2340 us
  waiting for transfers between devices  1630 us (69%)
  matrix products  448 us (19%)
  other arithmetic  138 us (6%)
  local copies, waits for them, and re-layouts  105 us (4%)
    reduce_scatter x1, waiting for transfers between devices, per_device(): lax.psum_scatter(jnp.concatenate([up_part, down_part.reshape(owned_rows *...  710 us
    reduce_scatter x1, waiting for transfers between devices, per_device(): lax.psum_scatter(lax.dot_general(time_own_f, mod_cot, (((0,), (0,)), ((),...  242 us
    reduce_scatter x1, waiting for transfers between devices, per_device(): lax.psum_scatter(jnp.concatenate([skip_part, qkv_part, out_part], axis=-1...  150 us
    all_gather x1, waiting for transfers between devices, per_device(): mod_full = lax.all_gather(mod_low, ('dp', 'seq'), axis=0, tiled=True)  89.4 us
    dot_general x8, matrix products, block_scores(): jnp.einsum('uqhd,ukhd->uhqk', queries, key_part, preferred_element_type=j...  82.3 us
    all_gather x1, waiting for transfers between devices, per_device(): lax.all_gather(up_low, ('dp', 'seq'), axis=0, tiled=True)  73.9 us
    reduce_scatter x1, waiting for transfers between devices, per_device(): lax.psum_scatter(lax.map(piece_terms, piece_starts).reshape(count, utter_...  71.6 us
    all_gather x1, waiting for transfers between devices, per_device(): lax.all_gather(down_low, ('dp', 'seq'), axis=0, tiled=True)  67.5 us
  transfers between devices with their start and end apart: 12, of which 12 were waited for; matrix products, arithmetic and copies ran while one was open for 14% of the time, Pallas kernels for 0%

commit v1 on v0

v1 whole, which is shorter than its diff:
```python
import functools
import math

import jax
import jax.numpy as jnp
from jax import lax
from jax.experimental import pallas as pl
from jax.experimental.pallas import tpu as pltpu
from jax.sharding import PartitionSpec as P

D = 1024
HEADS = 16
DH = 64
FF = 4096
STEP = 3
LOG2E = 1.4426950408889634
BF = jnp.bfloat16
F32 = jnp.float32
MIB = 2**20
highest = lax.Precision.HIGHEST


def dot_nn(a, b):
    return lax.dot_general(a, b, (((1,), (0,)), ((), ())), preferred_element_type=F32)


def dot_nt(a, b):
    return lax.dot_general(a, b, (((1,), (1,)), ((), ())), preferred_element_type=F32)


def dot_tn(a, b):
    return lax.dot_general(a, b, (((0,), (0,)), ((), ())), preferred_element_type=F32)


def params(mib):
    return pltpu.CompilerParams(vmem_limit_bytes=mib * MIB)


def cost(flops, moved):
    return pl.CostEstimate(flops=int(flops), bytes_accessed=int(moved), transcendentals=0)


def whole(shape):
    return pl.BlockSpec(shape, lambda i: (0,) * len(shape))


def time_features(flow_values, model_width):
    half_size = model_width // 2
    frequency = jnp.exp(-math.log(10000.0) * jnp.arange(half_size, dtype=F32) / half_size)
    angles = 1000.0 * flow_values[:, None] * frequency[None, :]
    return jax.nn.silu(jnp.concatenate([jnp.sin(angles), jnp.cos(angles)], axis=-1))


def rotary_tables(positions, heads):
    half = DH // 2
    frequency = jnp.exp(-math.log(10000.0) * jnp.arange(half, dtype=F32) / half)
    angles = positions.astype(F32)[:, None] * frequency[None, :]
    cosine, sine = jnp.cos(angles), jnp.sin(angles)
    return (
        jnp.concatenate([cosine, cosine] * heads, axis=-1),
        jnp.concatenate([-sine, sine] * heads, axis=-1),
    )


def swap_halves(values):
    width = values.shape[1]
    half = DH // 2
    if width == DH:
        return jnp.concatenate([values[:, half:], values[:, :half]], axis=1)
    lane = lax.broadcasted_iota(jnp.int32, (1, width), 1)
    first = (lane % DH) < half
    return jnp.where(
        first, pltpu.roll(values, width - half, 1), pltpu.roll(values, half, 1)
    )


def normalise(values):
    centre = values - jnp.mean(values, axis=-1, keepdims=True)
    spread = jnp.mean(centre * centre, axis=-1, keepdims=True)
    inverse = lax.rsqrt(spread + 1e-06)
    return centre * inverse, inverse


def norm_back(normal, inverse, scaled):
    return inverse * (
        scaled
        - jnp.mean(scaled, axis=-1, keepdims=True)
        - normal * jnp.mean(scaled * normal, axis=-1, keepdims=True)
    )


def gelu_and_slope(u):
    root = math.sqrt(2.0 / math.pi)
    square = u * u
    t = jnp.tanh(root * u * (1.0 + 0.044715 * square))
    half = 0.5 * (1.0 + t)
    slope = half + 0.5 * u * (1.0 - t * t) * (root * (1.0 + 3.0 * 0.044715 * square))
    return u * half, slope


def learning_rates():
    fans = (2 * D, D, D // 16, D, FF, D // 8)
    return tuple((2.0 * fan_value ** (-0.5) for fan_value in fans))


def adamw_step(state, gradient, rate):
    master, first_moment, second_moment = (state[0], state[1], state[2])
    first_moment = 0.5 * first_moment + 0.5 * gradient
    second_moment = 0.5 * second_moment + 0.5 * gradient * gradient
    correction = 1.0 - 0.5**STEP
    master = master - rate * (
        first_moment / correction / (jnp.sqrt(second_moment / correction) + 1e-08) + 0.01 * master
    )
    return (master, jnp.stack([first_moment, second_moment]))


def skip_kernel(fr_ref, sk_ref, cond_ref, w_ref, mod_ref, hidden_ref, normed_ref):
    width = fr_ref.shape[1]
    hidden = (
        dot_nn(fr_ref[...], w_ref[:width])
        + dot_nn(sk_ref[...], w_ref[width:])
        + cond_ref[...].astype(F32)
    )
    hidden_ref[...] = hidden
    normal, _ = normalise(hidden)
    normed_ref[...] = (normal * (1.0 + mod_ref[1:2]) + mod_ref[0:1]).astype(BF)


def skip_forward(frames, skips, cond, weight, mod):
    rows, width = frames.shape
    block = min(256, rows)
    row_spec = pl.BlockSpec((block, width), lambda i: (i, 0))
    return pl.pallas_call(
        skip_kernel,
        grid=(rows // block,),
        in_specs=[row_spec, row_spec, row_spec, whole(weight.shape), whole(mod.shape)],
        out_specs=[row_spec, row_spec],
        out_shape=[
            jax.ShapeDtypeStruct((rows, width), F32),
            jax.ShapeDtypeStruct((rows, width), BF),
        ],
        compiler_params=params(40),
        cost_estimate=cost(4 * rows * width * width, 12 * rows * width + 4 * width * width),
    )(frames, skips, cond, weight, mod)


def qkv_kernel(x_ref, wq_ref, wk_ref, wv_ref, cos_ref, sin_ref, out_ref):
    x = x_ref[...]
    cosine, sine = cos_ref[...], sin_ref[...]
    pairs = out_ref.shape[0]
    q, k, v = dot_nn(x, wq_ref[...]), dot_nn(x, wk_ref[...]), dot_nn(x, wv_ref[...])
    for j in range(pairs):
        part = slice(j * 128, (j + 1) * 128)
        out_ref[j, :, 0:128] = (q[:, part] * cosine + swap_halves(q[:, part]) * sine).astype(BF)
        out_ref[j, :, 128:256] = (k[:, part] * cosine + swap_halves(k[:, part]) * sine).astype(BF)
        out_ref[j, :, 256:384] = v[:, part].astype(BF)


def qkv_forward(normed, weight, cosine, sine):
    rows, width = normed.shape
    pairs = width // 128
    per_step = 2
    cols = 128 * per_step
    steps = pairs // per_step

    def columns(part):
        return pl.BlockSpec((width, cols), lambda i: (0, part * steps + i))

    return pl.pallas_call(
        qkv_kernel,
        grid=(steps,),
        in_specs=[
            whole(normed.shape),
            columns(0),
            columns(1),
            columns(2),
            whole(cosine.shape),
            whole(sine.shape),
        ],
        out_specs=pl.BlockSpec((per_step, rows, 384), lambda i: (i, 0, 0)),
        out_shape=jax.ShapeDtypeStruct((pairs, rows, 384), BF),
        compiler_params=params(40),
        cost_estimate=cost(6 * rows * width * width, 8 * rows * width + 6 * width * width),
    )(normed, weight, weight, weight, cosine, sine)


def attend_kernel(heads, block, qkv_ref, out_ref, log_ref):
    width = heads * DH
    i = pl.program_id(0)
    q = qkv_ref[pl.ds(pl.multiple_of(i * block, block), block), 0:width]
    k = qkv_ref[:, width : 2 * width]
    v = qkv_ref[:, 2 * width : 3 * width]
    lane = lax.broadcasted_iota(jnp.int32, (1, width), 1) // DH
    outs = []
    for h in range(heads):
        own = jnp.where(lane == h, q, jnp.zeros_like(q)) if heads > 1 else q
        scores = dot_nt(k, own) * (0.125 * LOG2E)
        top = jnp.max(scores, axis=0, keepdims=True)
        probs = jnp.exp2(scores - top)
        total = jnp.sum(probs, axis=0, keepdims=True)
        outs.append(dot_tn(v[:, h * DH : (h + 1) * DH], probs.astype(BF)) * (1.0 / total))
        log_ref[h : h + 1, :] = top + jnp.log2(total)
    out_ref[...] = (jnp.concatenate(outs, axis=0) if heads > 1 else outs[0]).T.astype(BF)


def attend(qkv, heads):
    length = qkv.shape[0]
    width = heads * DH
    block = min(512, length)
    return pl.pallas_call(
        functools.partial(attend_kernel, heads, block),
        grid=(length // block,),
        in_specs=[whole(qkv.shape)],
        out_specs=[
            pl.BlockSpec((block, width), lambda i: (i, 0)),
            pl.BlockSpec((heads, block), lambda i: (0, i)),
        ],
        out_shape=[
            jax.ShapeDtypeStruct((length, width), BF),
            jax.ShapeDtypeStruct((heads, length), F32),
        ],
        compiler_params=params(50),
        cost_estimate=cost(16 * length * length * DH * heads, 8 * length * width),
    )(qkv)


def attend_back_kernel(
    heads, block, qkv_ref, do_ref, o_ref, log_ref, cos_ref, sin_ref, out_ref, dq_sum, delta
):
    width = heads * DH
    i = pl.program_id(0)
    lane = lax.broadcasted_iota(jnp.int32, (1, width), 1) // DH

    @pl.when(i == 0)
    def _():
        dq_sum[...] = jnp.zeros_like(dq_sum)
        product = (do_ref[...].astype(F32) * o_ref[...].astype(F32)).T
        for h in range(heads):
            delta[h : h + 1, :] = jnp.sum(product[h * DH : (h + 1) * DH], axis=0, keepdims=True)

    here = pl.ds(pl.multiple_of(i * block, block), block)
    q = qkv_ref[:, 0:width]
    k = qkv_ref[here, width : 2 * width]
    v = qkv_ref[here, 2 * width : 3 * width]
    do = do_ref[...]
    k_turned = k.T
    dk = dv = None
    for h in range(heads):
        own = lane == h
        k_own = jnp.where(own, k, jnp.zeros_like(k)) if heads > 1 else k
        v_own = jnp.where(own, v, jnp.zeros_like(v)) if heads > 1 else v
        scores = dot_nt(k_own, q) * (0.125 * LOG2E)
        probs = jnp.exp2(scores - log_ref[h : h + 1, :])
        prob_grad = dot_nt(v_own, do)
        score_grad = (probs * (prob_grad - delta[h : h + 1, :])).astype(BF)
        part = slice(h * DH, (h + 1) * DH)
        dq_sum[part, :] += dot_nn(k_turned[part], score_grad)
        dv_own = dot_nn(probs.astype(BF), do)
        dk_own = dot_nn(score_grad, q)
        dv = dv_own if dv is None else jnp.where(own, dv_own, dv)
        dk = dk_own if dk is None else jnp.where(own, dk_own, dk)
    dk = dk * 0.125
    out_ref[here, width : 2 * width] = (
        dk * cos_ref[here, :] - swap_halves(dk) * sin_ref[here, :]
    ).astype(BF)
    out_ref[here, 2 * width : 3 * width] = dv.astype(BF)

    @pl.when(i == pl.num_programs(0) - 1)
    def _():
        dq = (dq_sum[...] * 0.125).T
        out_ref[:, 0:width] = (dq * cos_ref[...] - swap_halves(dq) * sin_ref[...]).astype(BF)


def attend_back(qkv, do, o, log_total, cosine, sine, heads):
    length = qkv.shape[0]
    width = heads * DH
    block = min(512, length)
    return pl.pallas_call(
        functools.partial(attend_back_kernel, heads, block),
        grid=(length // block,),
        in_specs=[whole(a.shape) for a in (qkv, do, o, log_total, cosine, sine)],
        out_specs=whole(qkv.shape),
        out_shape=jax.ShapeDtypeStruct(qkv.shape, BF),
        scratch_shapes=[pltpu.VMEM((width, length), F32), pltpu.VMEM((heads, length), F32)],
        compiler_params=params(58),
        cost_estimate=cost(24 * length * length * DH * heads, 20 * length * width),
    )(qkv, do, o, log_total, cosine, sine)


def gather_columns(refs, out_ref, heads):
    count = len(refs)
    groups = refs[0].shape[0]
    width = heads * DH
    for j in range(groups):
        for c in range(count):
            at = (j * count + c) * width
            out_ref[:, at : at + width] = refs[c][j]


def out_kernel(count, heads, *refs):
    o_refs = refs[:count]
    w_ref, hidden_ref, mod_ref, attended_ref, branch_ref, middle_ref, normed_ref = refs[count:]
    gather_columns(o_refs, attended_ref, heads)
    branch = dot_nn(attended_ref[...], w_ref[...])
    branch_ref[...] = branch
    middle = hidden_ref[...] + mod_ref[2:3] * branch
    middle_ref[...] = middle
    normal, _ = normalise(middle)
    normed_ref[...] = (normal * (1.0 + mod_ref[4:5]) + mod_ref[3:4]).astype(BF)


def out_forward(o_chunks, heads, weight, hidden, mod):
    rows, width = hidden.shape
    block = min(256, rows)
    row_spec = pl.BlockSpec((block, width), lambda i: (i, 0))
    groups = o_chunks[0].shape[0]
    o_spec = pl.BlockSpec((groups, block, heads * DH), lambda i: (0, i, 0))
    return pl.pallas_call(
        functools.partial(out_kernel, len(o_chunks), heads),
        grid=(rows // block,),
        in_specs=[o_spec] * len(o_chunks) + [whole(weight.shape), row_spec, whole(mod.shape)],
        out_specs=[row_spec] * 4,
        out_shape=[
            jax.ShapeDtypeStruct((rows, width), BF),
            jax.ShapeDtypeStruct((rows, width), F32),
            jax.ShapeDtypeStruct((rows, width), F32),
            jax.ShapeDtypeStruct((rows, width), BF),
        ],
        compiler_params=params(40),
        cost_estimate=cost(2 * rows * width * width, 18 * rows * width + 2 * width * width),
    )(*o_chunks, weight, hidden, mod)


def ffn_kernel(x_ref, dc_ref, up_ref, dn_ref, y_ref, dx_ref, gu_ref, gd_ref, x_turned):
    @pl.when(pl.program_id(0) == 0)
    def _():
        x_turned[...] = x_ref[...].T
        y_ref[...] = jnp.zeros_like(y_ref)
        dx_ref[...] = jnp.zeros_like(dx_ref)

    dc = dc_ref[...]
    up, dn = up_ref[...], dn_ref[...]
    value, slope = gelu_and_slope(dot_nn(x_ref[...], up))
    activated = value.astype(BF)
    up_cot = (dot_nt(dc, dn) * slope).astype(BF)
    y_ref[...] += dot_nn(activated, dn)
    dx_ref[...] += dot_nt(up_cot, up)
    gu_ref[...] = dot_nn(x_turned[...], up_cot).astype(BF)
    gd_ref[...] = dot_tn(activated, dc).astype(BF)


def ffn(x, dc, up, dn):
    rows, width = x.shape
    hidden_width = up.shape[1]
    block = min(512, hidden_width)
    up_spec = pl.BlockSpec((width, block), lambda i: (0, i))
    dn_spec = pl.BlockSpec((block, width), lambda i: (i, 0))
    return pl.pallas_call(
        ffn_kernel,
        grid=(hidden_width // block,),
        in_specs=[whole(x.shape), whole(x.shape), up_spec, dn_spec],
        out_specs=[whole(x.shape), whole(x.shape), up_spec, dn_spec],
        out_shape=[
            jax.ShapeDtypeStruct((rows, width), F32),
            jax.ShapeDtypeStruct((rows, width), F32),
            jax.ShapeDtypeStruct(up.shape, BF),
            jax.ShapeDtypeStruct(dn.shape, BF),
        ],
        scratch_shapes=[pltpu.VMEM((width, rows), BF)],
        compiler_params=params(60),
        cost_estimate=cost(12 * rows * width * hidden_width, 8 * width * hidden_width),
    )(x, dc, up, dn)


def mid_kernel(count, heads, *refs):
    y_ref, dx_ref, middle_ref, branch_ref, grad_ref, w_ref, mod_ref = refs[:7]
    block_ref, mgrad_ref, bcot_ref, sums_ref = refs[7:11]
    chunk_refs = refs[11:]

    @pl.when(pl.program_id(0) == 0)
    def _():
        sums_ref[...] = jnp.zeros_like(sums_ref)

    y, middle, w = y_ref[...], middle_ref[...], dx_ref[...]
    grad = grad_ref[...].astype(F32)
    block_ref[...] = (middle + mod_ref[5:6] * y).astype(BF)
    normal, inverse = normalise(middle)
    middle_grad = grad + norm_back(normal, inverse, w * (1.0 + mod_ref[4:5]))
    mgrad_ref[...] = middle_grad
    branch_cot = (middle_grad * mod_ref[2:3]).astype(BF)
    bcot_ref[...] = branch_cot
    sums_ref[0:1] += jnp.sum(middle_grad * branch_ref[...], axis=0, keepdims=True)
    sums_ref[1:2] += jnp.sum(w, axis=0, keepdims=True)
    sums_ref[2:3] += jnp.sum(w * normal, axis=0, keepdims=True)
    sums_ref[3:4] += jnp.sum(grad * y, axis=0, keepdims=True)
    attended_grad = dot_nt(branch_cot, w_ref[...]).astype(BF)
    width = heads * DH
    for j in range(chunk_refs[0].shape[0]):
        for c in range(count):
            at = (j * count + c) * width
            chunk_refs[c][j] = attended_grad[:, at : at + width]


def mid_back(y, dx, middle, branch, grad, weight, mod, groups, count, heads):
    rows, width = y.shape
    block = min(256, rows)
    row_spec = pl.BlockSpec((block, width), lambda i: (i, 0))
    chunk_spec = pl.BlockSpec((groups, block, heads * DH), lambda i: (0, i, 0))
    return pl.pallas_call(
        functools.partial(mid_kernel, count, heads),
        grid=(rows // block,),
        in_specs=[row_spec] * 5 + [whole(weight.shape), whole(mod.shape)],
        out_specs=[row_spec] * 3 + [whole((8, width))] + [chunk_spec] * count,
        out_shape=[
            jax.ShapeDtypeStruct((rows, width), BF),
            jax.ShapeDtypeStruct((rows, width), F32),
            jax.ShapeDtypeStruct((rows, width), BF),
            jax.ShapeDtypeStruct((8, width), F32),
        ]
        + [jax.ShapeDtypeStruct((groups, rows, heads * DH), BF)] * count,
        compiler_params=params(50),
        cost_estimate=cost(2 * rows * width * width, 28 * rows * width + 2 * width * width),
    )(y, dx, middle, branch, grad, weight, mod)


def last_kernel(count, heads, *refs):
    chunk_refs = refs[:count]
    hidden_ref, mgrad_ref, wqkv_ref, wskip_ref, mod_ref = refs[count : count + 5]
    cot_ref, hgrad_ref, frames_ref, skips_ref, sums_ref = refs[count + 5 :]

    @pl.when(pl.program_id(0) == 0)
    def _():
        sums_ref[...] = jnp.zeros_like(sums_ref)

    width = heads * DH
    model = hidden_ref.shape[1]
    for j in range(chunk_refs[0].shape[0]):
        for c in range(count):
            at = (j * count + c) * width
            for part in range(3):
                cot_ref[:, part * model + at : part * model + at + width] = chunk_refs[c][
                    j, :, part * width : (part + 1) * width
                ]
    w = dot_nt(cot_ref[...], wqkv_ref[...])
    normal, inverse = normalise(hidden_ref[...])
    sums_ref[0:1] += jnp.sum(w, axis=0, keepdims=True)
    sums_ref[1:2] += jnp.sum(w * normal, axis=0, keepdims=True)
    hidden_grad = (
        mgrad_ref[...] + norm_back(normal, inverse, w * (1.0 + mod_ref[1:2]))
    ).astype(BF)
    hgrad_ref[...] = hidden_grad
    frames_ref[...] = dot_nt(hidden_grad, wskip_ref[:model]).astype(BF)
    skips_ref[...] = dot_nt(hidden_grad, wskip_ref[model:]).astype(BF)


def last_back(chunks, heads, hidden, middle_grad, w_qkv, w_skip, mod):
    rows, width = hidden.shape
    block = min(256, rows)
    row_spec = pl.BlockSpec((block, width), lambda i: (i, 0))
    groups = chunks[0].shape[0]
    chunk_spec = pl.BlockSpec((groups, block, 3 * heads * DH), lambda i: (0, i, 0))
    return pl.pallas_call(
        functools.partial(last_kernel, len(chunks), heads),
        grid=(rows // block,),
        in_specs=[chunk_spec] * len(chunks)
        + [row_spec, row_spec, whole(w_qkv.shape), whole(w_skip.shape), whole(mod.shape)],
        out_specs=[
            pl.BlockSpec((block, 3 * width), lambda i: (i, 0)),
            row_spec,
            row_spec,
            row_spec,
            whole((8, width)),
        ],
        out_shape=[
            jax.ShapeDtypeStruct((rows, 3 * width), BF),
            jax.ShapeDtypeStruct((rows, width), BF),
            jax.ShapeDtypeStruct((rows, width), BF),
            jax.ShapeDtypeStruct((rows, width), BF),
            jax.ShapeDtypeStruct((8, width), F32),
        ],
        compiler_params=params(58),
        cost_estimate=cost(10 * rows * width * width, 26 * rows * width + 10 * width * width),
    )(*chunks, hidden, middle_grad, w_qkv, w_skip, mod)


def bits_of(axis):
    size = lax.axis_size(axis)
    return [(axis, b) for b in reversed(range(size.bit_length() - 1))]


def my_bit(level):
    axis, bit = level
    return (lax.axis_index(axis) >> bit) & 1


def swap(values, level):
    axis, bit = level
    return lax.ppermute(values, axis, [(i, i ^ (1 << bit)) for i in range(lax.axis_size(axis))])


def scatter_sum(grad, order):
    dims = bits_of("dp") + bits_of("seq")
    rows, cols = grad.shape
    terms = [grad.reshape([2] * len(dims) + [rows // 2 ** len(dims), cols])]
    for level in order:
        at, mine = dims.index(level), my_bit(level)
        dims.pop(at)

        def halves(side):
            return [lax.dynamic_index_in_dim(t, side, at, keepdims=False) for t in terms]

        leaving = halves(1 - mine)
        total = leaving[0]
        if len(leaving) > 1:
            total = sum(t.astype(F32) for t in leaving).astype(grad.dtype)
        arrived = swap(total, level)
        terms = halves(mine) + [arrived]
    return sum(t.astype(F32) for t in terms)


def exchange(values, axis):
    return lax.all_to_all(values, axis, 0, 0, tiled=True)


def modulation_rows(partial, order):
    dims = bits_of("dp")
    count, cols = partial.shape
    held = partial.reshape([2] * len(dims) + [count // 2 ** len(dims), cols])
    for level in order:
        at, mine = dims.index(level), my_bit(level)
        dims.pop(at)
        leaving = lax.dynamic_index_in_dim(held, 1 - mine, at, keepdims=False)
        held = lax.dynamic_index_in_dim(held, mine, at, keepdims=False) + swap(leaving, level)
    for level in bits_of("seq"):
        held = held + swap(held, level)
    return held


def modulation_cots(own, total_count):
    for level in bits_of("seq"):
        own = own + swap(own, level)
    for level in reversed(bits_of("dp")):
        other = swap(own, level)
        mine = my_bit(level)
        own = jnp.where(
            mine == 0,
            jnp.concatenate([own, other], axis=0),
            jnp.concatenate([other, own], axis=0),
        )
    return own


def per_device(
    frames_in,
    skip_in,
    condition,
    flow_time,
    span_start,
    span_length,
    out_grad,
    skip_proj_state,
    attn_qkv_state,
    attn_out_state,
    ffn_up_state,
    ffn_down_state,
    ada_mod_state,
):
    utter_count, rows, width = frames_in.shape
    seq = lax.axis_size("seq")
    everyone = ("dp", "seq")
    owned = attn_qkv_state.shape[1]
    length = rows * seq
    me = lax.axis_index(everyone)
    positions = lax.axis_index("seq") * rows + jnp.arange(rows, dtype=jnp.int32)

    group_heads = HEADS // seq
    heads = min(2, group_heads)
    count = group_heads // heads

    skip_full = lax.all_gather(skip_proj_state[0].astype(BF), everyone, axis=0, tiled=True)
    qkv_full = lax.all_gather(attn_qkv_state[0].astype(BF), everyone, axis=0, tiled=True)
    out_full = lax.all_gather(attn_out_state[0].astype(BF), everyone, axis=0, tiled=True)
    up_full = lax.all_gather(ffn_up_state[0].astype(BF), everyone, axis=0, tiled=True)
    down_full = lax.all_gather(ffn_down_state[0].astype(BF), everyone, axis=0, tiled=True)

    dp_bits, seq_bits = bits_of("dp"), bits_of("seq")
    core, planes = dp_bits[-1], dp_bits[:-1]

    time_code = time_features(flow_time, width).astype(BF)
    time_own = lax.dynamic_slice_in_dim(time_code, me * owned, owned, 1)
    mod_part = jnp.dot(time_own, ada_mod_state[0].astype(BF), preferred_element_type=F32)
    modulation = modulation_rows(mod_part, [core] + planes)

    cos_all, sin_all = rotary_tables(jnp.arange(length, dtype=jnp.int32), heads)
    cos_own, sin_own = rotary_tables(positions, 2)
    span_stop = span_start + span_length

    outs = []
    assert utter_count == 1
    mod = modulation.reshape(6, width)
    inside = (positions >= span_start[0]) & (positions < span_stop[0])
    frames, skips = frames_in[0], skip_in[0]
    cond = jnp.where(inside[:, None], jnp.zeros_like(condition[0]), condition[0])
    grad = jnp.where(inside[:, None], out_grad[0], jnp.zeros_like(out_grad[0]))
    down_cot = (grad.astype(F32) * mod[5:6]).astype(BF)

    hidden, normed = skip_forward(frames, skips, cond, skip_full, mod)
    packed = qkv_forward(normed, qkv_full, cos_own, sin_own)
    if heads == 2:
        packed = packed.reshape(seq, count, rows, 3 * heads * DH)
    else:
        packed = packed.reshape(HEADS // 2, rows, 3, 2, DH).transpose(0, 3, 1, 2, 4)
        packed = packed.reshape(seq, count, rows, 3 * heads * DH)
    qkv_chunks = [exchange(packed[:, c], "seq").reshape(length, -1) for c in range(count)]
    attended = [attend(chunk, heads) for chunk in qkv_chunks]
    o_chunks = [exchange(o.reshape(seq, rows, heads * DH), "seq") for o, _ in attended]

    attended_low, branch, middle, normed_two = out_forward(
        o_chunks, heads, out_full, hidden, mod
    )
    downward, normed_two_grad, up_part, down_part = ffn(normed_two, down_cot, up_full, down_full)
    mid = mid_back(
        downward, normed_two_grad, middle, branch, grad, out_full, mod, seq, count, heads
    )
    block_out, middle_grad, branch_cot, mid_sums = mid[:4]
    up_wgrad = scatter_sum(up_part, [core] + planes + seq_bits)
    down_wgrad = scatter_sum(down_part, [core] + planes[::-1] + seq_bits)

    cot_chunks = []
    for c in range(count):
        do = exchange(mid[4 + c], "seq").reshape(length, heads * DH)
        o, log_total = attended[c]
        back = attend_back(qkv_chunks[c], do, o, log_total, cos_all, sin_all, heads)
        cot_chunks.append(exchange(back.reshape(seq, rows, 3 * heads * DH), "seq"))
    out_part = dot_tn(attended_low, branch_cot).astype(BF)
    out_wgrad = scatter_sum(out_part, [core] + planes[::-1] + seq_bits)

    packed_cot, hidden_grad, frames_grad, skip_grad, last_sums = last_back(
        cot_chunks, heads, hidden, middle_grad, qkv_full, skip_full, mod
    )
    skip_part = jnp.concatenate(
        [dot_tn(frames, hidden_grad).astype(BF), dot_tn(skips, hidden_grad).astype(BF)], axis=0
    )
    skip_wgrad = scatter_sum(skip_part, [core] + planes[::-1] + seq_bits)
    qkv_part = dot_tn(normed, packed_cot).astype(BF)
    qkv_wgrad = scatter_sum(qkv_part, [core] + planes + seq_bits)

    mod_cot = jnp.concatenate(
        [last_sums[0], last_sums[1], mid_sums[0], mid_sums[1], mid_sums[2], mid_sums[3]]
    ).reshape(1, 6 * width)
    mod_cots = modulation_cots(mod_cot, flow_time.shape[0])
    mod_wgrad = lax.dot_general(
        time_own.astype(F32),
        mod_cots,
        (((0,), (0,)), ((), ())),
        precision=highest,
        preferred_element_type=F32,
    )

    states = (
        skip_proj_state,
        attn_qkv_state,
        attn_out_state,
        ffn_up_state,
        ffn_down_state,
        ada_mod_state,
    )
    grads = (skip_wgrad, qkv_wgrad, out_wgrad, up_wgrad, down_wgrad, mod_wgrad)
    outs = [block_out[None], frames_grad[None], skip_grad[None]]
    for state, gradient, rate in zip(states, grads, learning_rates()):
        outs.extend(adamw_step(state, gradient, rate))
    return tuple(outs)


def solution(mesh):
    tokens = P("dp", "seq", None)
    state = P(None, ("dp", "seq"), None)
    master = P(("dp", "seq"), None)
    return jax.shard_map(
        per_device,
        mesh=mesh,
        in_specs=(tokens, tokens, tokens, P(), P("dp"), P("dp"), tokens) + (state,) * 6,
        out_specs=(tokens,) * 3 + (master, state) * 6,
        check_vma=False,
    )
```

time: 2350 us -> 841 us (0.36)
  waiting for transfers between devices: 1630 us -> 439 us
  matrix products: 448 us -> 14.1 us
  Pallas kernels: 0 us -> 149 us
  other arithmetic: 138 us -> 57.3 us
  starting transfers between devices: 0.68 us -> 65 us
  local copies, waits for them, and re-layouts: 105 us -> 41.5 us
  blocking collectives: 0 us -> 49.5 us
    reduce_scatter x4 -> x0, waiting for transfers between devices: 1170 us -> none  [the longest x1 710 us: per_device(): lax.psum_scatter(jnp.concatenate([up_part, down_part.reshape(owned_rows *...]
    dot_general x44 -> x6, matrix products: 448 us -> 14.1 us  [the longest x4 9.26 us: dot_tn(): lax.dot_general(a, b, (((0,), (0,)), ((), ())), preferred_element_type=F32)]
    all_gather x8 -> x5, waiting for transfers between devices: 452 us -> 180 us  [the longest x1 79.8 us: per_device(): lax.all_gather(ffn_down_state[0].astype(BF), everyone, axis=0, tiled=True)]
    ppermute x0 -> x35, waiting for transfers between devices: none -> 190 us  [swap(): lax.ppermute(values, axis, [(i, i ^ 1 << bit) for i in range(lax.axis_siz...]
    pallas_call x0 -> x10, Pallas kernels: none -> 149 us  [the longest x2 54.5 us: attend_back(): pl.pallas_call(functools.partial(attend_back_kernel, heads, block), grid=...]
    all_to_all x0 -> x7, waiting for transfers between devices: none -> 69.2 us  [exchange(): return lax.all_to_all(values, axis, 0, 0, tiled=True)]
    all_to_all x0 -> x1, blocking collectives: none -> 49.5 us  [exchange(): return lax.all_to_all(values, axis, 0, 0, tiled=True)]
    reduce_sum x10 -> x0, other arithmetic: 39 us -> none  [the longest x3 25.9 us: per_device(): jnp.sum(jnp.exp(scores - new_top[..., None]), axis=-1)]
  transfers between devices with their start and end apart: 12 -> 47, of which waited for: 12 -> 29; matrix products, arithmetic and copies ran while one was open for 14% -> 11% of each run, Pallas kernels for 0% -> 13%
where the time goes in v1:
time: 841 us; the launch traced here: 832 us
  waiting for transfers between devices  439 us (52%)
  Pallas kernels  149 us (18%)
  starting transfers between devices  65 us (8%)
  other arithmetic  57.3 us (7%)
  blocking collectives  49.5 us (6%)
  local copies, waits for them, and re-layouts  41.5 us (5%)
  between operations  16.4 us (2%)
  matrix products  14.1 us (2%)
    ppermute x35, waiting for transfers between devices, swap(): lax.ppermute(values, axis, [(i, i ^ 1 << bit) for i in range(lax.axis_siz...  190 us
    all_gather x1, waiting for transfers between devices, per_device(): lax.all_gather(ffn_down_state[0].astype(BF), everyone, axis=0, tiled=True)  79.8 us
    all_to_all x7, waiting for transfers between devices, exchange(): return lax.all_to_all(values, axis, 0, 0, tiled=True)  69.2 us
    all_gather x1, waiting for transfers between devices, per_device(): lax.all_gather(attn_qkv_state[0].astype(BF), everyone, axis=0, tiled=True)  62.6 us
    pallas_call x2, Pallas kernels, attend_back(): pl.pallas_call(functools.partial(attend_back_kernel, heads, block), grid=...  54.5 us
    all_to_all x1, blocking collectives, exchange(): return lax.all_to_all(values, axis, 0, 0, tiled=True)  49.5 us
    all_gather x1, waiting for transfers between devices, per_device(): lax.all_gather(skip_proj_state[0].astype(BF), everyone, axis=0, tiled=True)  37.3 us
    ppermute x35, starting transfers between devices, swap(): lax.ppermute(values, axis, [(i, i ^ 1 << bit) for i in range(lax.axis_siz...  35.6 us
  transfers between devices with their start and end apart: 47, of which 29 were waited for; matrix products, arithmetic and copies ran while one was open for 11% of the time, Pallas kernels for 13%

profile of v1, /device:TPU:0, one launch (start us, length us, event | category | flops | bytes accessed | tf_op | source)
XLA Modules:
  0.0 832.2 jit_solution(8126127335695252783)
XLA Ops:
  14.3 1.8 bitcast_convert_fusion
  20.0 2.6 collective-permute-start.1
  22.5 2.6 collective-permute-done.1
  26.8 2.3 collective-permute-done.2
  29.2 2.6 collective-permute-start.3
  39.3 37.3 %all-gather.6.cloned.1.call-done.w_ref.refs_5_ = bf16[2048,1024]{1,0:T(8,128)(2,1)} async-done(((bf16[64,1024]{1,0:T(8,128)(2,1)}), bf16[2048,1024]{1,0:T(8,128)(2,1)}) %all-gather.6.cloned.1.call-update) | async-done | bytes 4194320 | tf_op jit(solution)/shard_map/all_gather | solution.py:580
  76.6 2.2 copy-done.12
  81.3 3.1 shard_map.244
  85.7 62.6 %all-gather.8.cloned.1.call-done.wq_ref.wk_ref.wv_ref.refs_4_ = bf16[1024,3072]{1,0:T(8,128)(2,1)} async-done(((bf16[32,3072]{1,0:T(8,128)(2,1)}), bf16[1024,3072]{1,0:T(8,128)(2,1)}) %all-gather.8.cloned.1.call-update) | async-done | bytes 6291472 | tf_op jit(solution)/shard_map/all_gather | solution.py:581
  148.2 2.8 copy-done
  151.0 5.7 shard_map.245
  158.1 49.5 %all_to_all.40 = bf16[4,512,384]{2,1,0:T(8,128)(2,1)S(1)} all-to-all(bf16[4,512,384]{2,1,0:T(8,128)(2,1)S(1)} %get-tuple-element.83), channel_id=1, replica_groups=mesh['dp'=8,'seq'=4] {'seq'}, dimensions={0} | all-to-all | bytes 3145728 | tf_op jit(solution)/shard_map/all_to_all | solution.py:522
  207.7 3.6 all-to-all-start.2
  211.2 14.7 %shard_map.246 = (bf16[2048,128]{1,0:T(8,128)(2,1)S(1)}, f32[2,2048]{1,0:T(2,128)S(1)}) custom-call(bf16[2048,384]{1,0:T(8,128)(2,1)S(1)} %bitcast.559), custom_call_target="tpu_custom_call" | custom-call | flops 8589934592 | bytes 2097152 | tf_op jit(solution)/shard_map/pallas_call | solution.py:210
  227.4 24.5 %all-to-all-done.2 = bf16[4,512,384]{2,1,0:T(8,128)(2,1)S(1)} async-done(((bf16[4,512,384]{2,1,0:T(8,128)(2,1)}), bf16[4,512,384]{2,1,0:T(8,128)(2,1)S(1)}, u32[]{:S(2)}, u32[]{:S(2)}) %all-to-all-start.2) | async-done | bytes 1572896 | tf_op jit(solution)/shard_map/all_to_all | solution.py:522
  251.9 3.7 all-to-all-start.1
  255.6 15.4 %shard_map.247 = (bf16[2048,128]{1,0:T(8,128)(2,1)}, f32[2,2048]{1,0:T(2,128)S(1)}) custom-call(bf16[2048,384]{1,0:T(8,128)(2,1)S(1)} %bitcast.561), custom_call_target="tpu_custom_call" | custom-call | flops 8589934592 | bytes 2097152 | tf_op jit(solution)/shard_map/pallas_call | solution.py:210
  271.5 5.3 all-to-all-done.1.refs_0_
  276.8 3.5 all-to-all-start.3
  280.3 2.5 multiply_convert_fusion
  282.8 26.2 %all-to-all-done.3.refs_1_ = bf16[4,512,128]{2,1,0:T(8,128)(2,1)S(1)} async-done(((bf16[4,512,128]{2,1,0:T(8,128)(2,1)}), bf16[4,512,128]{2,1,0:T(8,128)(2,1)S(1)}, u32[]{:S(2)}, u32[]{:S(2)}) %all-to-all-start.3) | async-done | bytes 524320 | tf_op jit(solution)/shard_map/all_to_all | solution.py:522
  312.3 2.1 shard_map.248
  318.8 79.8 %all-gather.14.cloned.1.call-done.dn_ref = bf16[4096,1024]{1,0:T(8,128)(2,1)} async-done(((bf16[128,1024]{1,0:T(8,128)(2,1)}), bf16[4096,1024]{1,0:T(8,128)(2,1)}) %all-gather.14.cloned.1.call-update) | async-done | bytes 8388624 | tf_op jit(solution)/shard_map/all_gather | solution.py:584
  398.5 33.3 %shard_map.249 = (f32[512,1024]{1,0:T(8,128)}, f32[512,1024]{1,0:T(8,128)}, bf16[1024,4096]{1,0:T(8,128)(2,1)}, bf16[4096,1024]{1,0:T(8,128)(2,1)}) custom-call(bf16[512,1024]{1,0:T(8,128)(2,1)} %copy-done.19, bf16[512,1024]{1,0:T(8,128)(2,1)} %get-tuple-element.75.dc_ref, bf16[1024,4096]{1,0:T(8,128)(2,1)} %all-gather.12.cloned.1.call-done.up_ref, ...), custom_call_target="tpu_custom_call" | custom-call | flops 25769803776 | bytes 33554432 | tf_op jit(solution)/shard_map/pallas_call | solution.py:358
  431.8 7.2 shard_map.250
  440.0 4.5 all-to-all-start.6
  444.6 3.7 fusion.35
  448.3 3.0 pad_maximum_fusion.2
  453.1 6.8 all-to-all-done.6
  459.8 4.3 all-to-all-start.4
  464.1 27.3 %shard_map.252 = bf16[2048,384]{1,0:T(8,128)(2,1)} custom-call(bf16[2048,384]{1,0:T(8,128)(2,1)} %bitcast.562, bf16[2048,128]{1,0:T(8,128)(2,1)} %bitcast.30.do_ref, bf16[2048,128]{1,0:T(8,128)(2,1)} %get-tuple-element.42.o_ref, f32[2,2048]{1,0:T(2,128)} %copy-done.21, f32[2048,128]{1,0:T(8,128)} %get-tuple-element.110.cos_ref, ...), custom_call_target="tpu_custom_call" | custom-call | flops 12884901888 | bytes 5242880 | tf_op jit(solution)/shard_map/pallas_call | solution.py:278
  491.4 5.1 all-to-all-start.7
  499.2 27.2 %shard_map.251 = bf16[2048,384]{1,0:T(8,128)(2,1)} custom-call(bf16[2048,384]{1,0:T(8,128)(2,1)} %bitcast.560, bf16[2048,128]{1,0:T(8,128)(2,1)} %bitcast.28.do_ref, bf16[2048,128]{1,0:T(8,128)(2,1)} %copy-done.10, f32[2,2048]{1,0:T(2,128)} %copy-done.20, f32[2048,128]{1,0:T(8,128)} %get-tuple-element.110.cos_ref, f32[2048,128]{1,0:T(8,128)} %get-tuple-element.111.sin_ref), custom_call_target="tpu_custom_call" | custom-call | flops 12884901888 | bytes 5242880 | tf_op jit(solution)/shard_map/pallas_call | solution.py:278
  526.4 6.4 all-to-all-done.7.refs_1_
  532.9 4.6 all-to-all-start.5
  540.1 4.7 dynamic-slice_bitcast_fusion
  547.0 2.7 collective-permute-start.18
  549.7 4.8 dynamic-slice_bitcast_fusion.1
  554.4 25.1 %collective-permute-done.18 = bf16[2,32,1024]{2,1,0:T(8,128)(2,1)S(1)} collective-permute-done((bf16[2,32,1024]{2,1,0:T(8,128)(2,1)S(1)}, bf16[2,32,1024]{2,1,0:T(8,128)(2,1)S(1)}, u32[]{:S(2)}, u32[]{:S(2)}) %collective-permute-start.18) | collective-permute-done | bytes 131104 | tf_op jit(solution)/shard_map/ppermute | solution.py:498
  580.5 4.2 collective-permute-done.19
  586.4 12.9 %shard_map.253 = (bf16[512,3072]{1,0:T(8,128)(2,1)}, bf16[512,1024]{1,0:T(8,128)(2,1)}, bf16[512,1024]{1,0:T(8,128)(2,1)}, bf16[512,1024]{1,0:T(8,128)(2,1)}, f32[8,1024]{1,0:T(8,128)}) custom-call(bf16[4,512,384]{2,1,0:T(8,128)(2,1)} %all-to-all-done.5.refs_0_, bf16[4,512,384]{2,1,0:T(8,128)(2,1)} %all-to-all-done.7.refs_1_, f32[512,1024]{1,0:T(8,128)} %copy-done.2, ...), custom_call_target="tpu_custom_call" | custom-call | flops 5368709120 | bytes 24117248 | tf_op jit(solution)/shard_map/pallas_call | solution.py:462
  600.3 2.7 convert_bitcast_fusion
  606.4 2.0 collective-permute-start.31
  608.4 4.0 convolution_convert_fusion
  612.8 4.0 fusion
  618.2 3.7 fusion.1
  626.7 39.8 %collective-permute-done.33 = f32[2,6144]{1,0:T(2,128)S(1)} collective-permute-done((f32[2,6144]{1,0:T(2,128)S(1)}, f32[2,6144]{1,0:T(2,128)S(1)}, u32[]{:S(2)}, u32[]{:S(2)}) %collective-permute-start.33) | collective-permute-done | bytes 49184 | tf_op jit(solution)/shard_map/ppermute | solution.py:498
  668.8 2.9 collective-permute-done.34
  671.7 3.6 fusion.42
  675.3 2.8 fusion.3
  679.1 2.7 fusion.4
  682.9 6.1 collective-permute-done.6
  693.1 20.7 %collective-permute-done.7 = bf16[2,2,64,1024]{3,2,1,0:T(8,128)(2,1)S(1)} collective-permute-done((bf16[2,2,64,1024]{3,2,1,0:T(8,128)(2,1)S(1)}, bf16[2,2,64,1024]{3,2,1,0:T(8,128)(2,1)S(1)}, u32[]{:S(2)}, u32[]{:S(2)}) %collective-permute-start.7) | collective-permute-done | bytes 524320 | tf_op jit(solution)/shard_map/ppermute | solution.py:498
  714.9 2.0 collective-permute-start.8
  717.9 10.0 %collective-permute-done.8 = bf16[2,64,1024]{2,1,0:T(8,128)(2,1)S(1)} collective-permute-done((bf16[2,64,1024]{2,1,0:T(8,128)(2,1)S(1)}, bf16[2,64,1024]{2,1,0:T(8,128)(2,1)S(1)}, u32[]{:S(2)}, u32[]{:S(2)}) %collective-permute-start.8) | collective-permute-done | bytes 262176 | tf_op jit(solution)/shard_map/ppermute | solution.py:498
  730.5 2.9 collective-permute-start.28
  737.9 30.3 %collective-permute-done.28 = bf16[2,128,1024]{2,1,0:T(8,128)(2,1)S(1)} collective-permute-done((bf16[2,128,1024]{2,1,0:T(8,128)(2,1)S(1)}, bf16[2,128,1024]{2,1,0:T(8,128)(2,1)S(1)}, u32[]{:S(2)}, u32[]{:S(2)}) %collective-permute-start.28) | collective-permute-done | bytes 524320 | tf_op jit(solution)/shard_map/ppermute | solution.py:498
  769.6 8.9 %collective-permute-done.23 = bf16[2,32,4096]{2,1,0:T(8,128)(2,1)S(1)} collective-permute-done((bf16[2,32,4096]{2,1,0:T(8,128)(2,1)S(1)}, bf16[2,32,4096]{2,1,0:T(8,128)(2,1)S(1)}, u32[]{:S(2)}, u32[]{:S(2)}) %collective-permute-start.23) | collective-permute-done | bytes 524320 | tf_op jit(solution)/shard_map/ppermute | solution.py:498
  780.4 3.6 collective-permute-done.29
  785.3 4.3 collective-permute-done.24
  791.9 6.4 collective-permute-done.12
  798.6 2.7 collective-permute-start.13
  802.4 14.5 %collective-permute-done.13 = bf16[2,32,3072]{2,1,0:T(8,128)(2,1)S(1)} collective-permute-done((bf16[2,32,3072]{2,1,0:T(8,128)(2,1)S(1)}, bf16[2,32,3072]{2,1,0:T(8,128)(2,1)S(1)}, u32[]{:S(2)}, u32[]{:S(2)}) %collective-permute-start.13) | collective-permute-done | bytes 393248 | tf_op jit(solution)/shard_map/ppermute | solution.py:498
  819.4 3.6 collective-permute-done.14
  (211 shorter events, 87.4 us)
Async XLA Ops:
  7.2 8.9 %copy-start.29 = (f32[8]{0:T(128)S(1)}, f32[8]{0:T(128)}, u32[]{:S(2)}) copy-start(f32[8]{0:T(128)} %param.16) | copy-start | bytes 100
  7.2 12.4 %copy-start.26 = (bf16[1,512,1024]{2,1,0:T(8,128)(2,1)S(1)}, bf16[1,512,1024]{2,1,0:T(8,128)(2,1)}, u32[]{:S(2)}) copy-start(bf16[1,512,1024]{2,1,0:T(8,128)(2,1)} %param.15) | copy-start | bytes 3145732
  7.2 69.4 %all-gather.6.cloned.1.call-start = ((), (), s32[]{:S(2)}) async-start(), calls=%async_computation.8 | async-start | bytes 4325376 | tf_op jit(solution)/shard_map/all_gather | solution.py:580
  9.0 139.2 %all-gather.8.cloned.1.call-start = ((), (), s32[]{:S(2)}) async-start(), calls=%async_computation.9 | async-start | bytes 6488064 | tf_op jit(solution)/shard_map/all_gather | solution.py:581
  10.7 272.1 %all-gather.10.cloned.1.call-start = ((), (), s32[]{:S(2)}) async-start(), calls=%async_computation.10 | async-start | bytes 2162688 | tf_op jit(solution)/shard_map/all_gather | solution.py:582
  12.4 306.4 %all-gather.12.cloned.1.call-start = ((), (), s32[]{:S(2)}) async-start(), calls=%async_computation.11 | async-start | bytes 8650752 | tf_op jit(solution)/shard_map/all_gather | solution.py:583
  14.2 384.3 %all-gather.14.cloned.1.call-start = ((), (), s32[]{:S(2)}) async-start(), calls=%async_computation.12 | async-start | bytes 8650752 | tf_op jit(solution)/shard_map/all_gather | solution.py:584
  17.8 2.0 collective-permute-start
  20.0 5.2 collective-permute-start.1
  25.3 3.9 collective-permute-start.2
  29.2 4.9 collective-permute-start.3
  34.1 3.9 collective-permute-start.4
  39.3 392.5 %copy-start.11 = (f32[6,1024]{1,0:T(8,128)}, f32[6,1024]{1,0:T(8,128)S(1)}, u32[]{:S(2)}) copy-start(f32[6,1024]{1,0:T(8,128)S(1)} %reshape.530.mod_ref.refs_4_.refs_6_) | copy-start | bytes 73732
  85.7 71.0 %copy-start.8 = (bf16[512,1024]{1,0:T(8,128)(2,1)}, bf16[512,1024]{1,0:T(8,128)(2,1)S(1)}, u32[]{:S(2)}) copy-start(bf16[512,1024]{1,0:T(8,128)(2,1)S(1)} %get-tuple-element.40.x_ref) | copy-start | bytes 3145732
  207.7 18.3 %copy-start.6 = (bf16[4,512,384]{2,1,0:T(8,128)(2,1)}, bf16[4,512,384]{2,1,0:T(8,128)(2,1)S(1)}, u32[]{:S(2)}) copy-start(bf16[4,512,384]{2,1,0:T(8,128)(2,1)S(1)} %all_to_all.40) | copy-start | bytes 4718596
  207.7 44.2 %all-to-all-start.2 = ((bf16[4,512,384]{2,1,0:T(8,128)(2,1)}), bf16[4,512,384]{2,1,0:T(8,128)(2,1)S(1)}, u32[]{:S(2)}, u32[]{:S(2)}) async-start(bf16[4,512,384]{2,1,0:T(8,128)(2,1)} %get-tuple-element.82), calls=%async_computation.2 | async-start | bytes 3145728 | tf_op jit(solution)/shard_map/all_to_all | solution.py:522
  251.9 19.1 %copy-start.7 = (bf16[4,512,384]{2,1,0:T(8,128)(2,1)}, bf16[4,512,384]{2,1,0:T(8,128)(2,1)S(1)}, u32[]{:S(2)}) copy-start(bf16[4,512,384]{2,1,0:T(8,128)(2,1)S(1)} %all-to-all-done.2) | copy-start | bytes 4718596
  251.9 24.9 %all-to-all-start.1 = ((bf16[4,512,128]{2,1,0:T(8,128)(2,1)}), bf16[4,512,128]{2,1,0:T(8,128)(2,1)S(1)}, u32[]{:S(2)}, u32[]{:S(2)}) async-start(bf16[4,512,128]{2,1,0:T(8,128)(2,1)} %bitcast.563), calls=%async_computation.1 | async-start | bytes 1048576 | tf_op jit(solution)/shard_map/all_to_all | solution.py:522
  276.8 32.3 %all-to-all-start.3 = ((bf16[4,512,128]{2,1,0:T(8,128)(2,1)}), bf16[4,512,128]{2,1,0:T(8,128)(2,1)S(1)}, u32[]{:S(2)}, u32[]{:S(2)}) async-start(bf16[4,512,128]{2,1,0:T(8,128)(2,1)} %bitcast.21), calls=%async_computation.3 | async-start | bytes 1048576 | tf_op jit(solution)/shard_map/all_to_all | solution.py:522
  440.0 19.8 %all-to-all-start.6 = ((bf16[4,512,128]{2,1,0:T(8,128)(2,1)}), bf16[4,512,128]{2,1,0:T(8,128)(2,1)}, u32[]{:S(2)}, u32[]{:S(2)}) async-start(bf16[4,512,128]{2,1,0:T(8,128)(2,1)} %get-tuple-element.52), calls=%async_computation.6 | async-start | bytes 1048576 | tf_op jit(solution)/shard_map/all_to_all | solution.py:522
  452.7 43.7 %collective-permute-start.15 = (bf16[2,2,2,2,32,1024]{5,4,3,2,1,0:T(8,128)(2,1)S(1)}, bf16[2,2,2,2,32,1024]{5,4,3,2,1,0:T(8,128)(2,1)}, u32[]{:S(2)}, u32[]{:S(2)}) collective-permute-start(bf16[2,2,2,2,32,1024]{5,4,3,2,1,0:T(8,128)(2,1)S(1)} %dynamic-slice_bitcast_fusion.4), channel_id=1, source_target_pairs={{0,4},{4,0},{8,12},{12,8},{16,20},{20,16},{24,28},{28,24},{1,5},{5... | collective-permute-start | bytes 3145736 | tf_op jit(solution)/shard_map/ppermute | solution.py:498
  459.8 31.6 %all-to-all-start.4 = ((bf16[4,512,128]{2,1,0:T(8,128)(2,1)}), bf16[4,512,128]{2,1,0:T(8,128)(2,1)}, u32[]{:S(2)}, u32[]{:S(2)}) async-start(bf16[4,512,128]{2,1,0:T(8,128)(2,1)} %get-tuple-element.50), calls=%async_computation.4 | async-start | bytes 1048576 | tf_op jit(solution)/shard_map/all_to_all | solution.py:522
  491.4 41.5 %all-to-all-start.7 = ((bf16[4,512,384]{2,1,0:T(8,128)(2,1)}), bf16[4,512,384]{2,1,0:T(8,128)(2,1)}, u32[]{:S(2)}, u32[]{:S(2)}) async-start(bf16[4,512,384]{2,1,0:T(8,128)(2,1)} %bitcast.601), calls=%async_computation.7 | async-start | bytes 3145728 | tf_op jit(solution)/shard_map/all_to_all | solution.py:522
  497.7 39.8 %collective-permute-start.16 = (bf16[2,2,2,32,1024]{4,3,2,1,0:T(8,128)(2,1)S(1)}, bf16[2,2,2,32,1024]{4,3,2,1,0:T(8,128)(2,1)S(1)}, u32[]{:S(2)}, u32[]{:S(2)}) collective-permute-start(bf16[2,2,2,32,1024]{4,3,2,1,0:T(8,128)(2,1)S(1)} %fusion.9), channel_id=1, source_target_pairs={{0,8},{4,12},{8,0},{12,4},{16,24},{20,28},{24,16},{28,20},{1,9},{5... | collective-permute-start | bytes 1572872 | tf_op jit(solution)/shard_map/ppermute | solution.py:498
  532.9 53.6 %all-to-all-start.5 = ((bf16[4,512,384]{2,1,0:T(8,128)(2,1)}), bf16[4,512,384]{2,1,0:T(8,128)(2,1)}, u32[]{:S(2)}, u32[]{:S(2)}) async-start(bf16[4,512,384]{2,1,0:T(8,128)(2,1)} %bitcast.600), calls=%async_computation.5 | async-start | bytes 3145728 | tf_op jit(solution)/shard_map/all_to_all | solution.py:522
  538.6 7.3 collective-permute-start.17
  544.8 67.9 %collective-permute-start.25 = (bf16[2,2,2,2,128,1024]{5,4,3,2,1,0:T(8,128)(2,1)}, bf16[2,2,2,2,128,1024]{5,4,3,2,1,0:T(8,128)(2,1)}, u32[]{:S(2)}, u32[]{:S(2)}) collective-permute-start(bf16[2,2,2,2,128,1024]{5,4,3,2,1,0:T(8,128)(2,1)} %dynamic-slice_bitcast_fusion), channel_id=1, source_target_pairs={{0,4},{4,0},{8,12},{12,8},{16,20},{20,16},{24,28},{28,24},{1,5},{5... | collective-permute-start | bytes 12582920 | tf_op jit(solution)/shard_map/ppermute | solution.py:498
  545.9 33.6 %copy-start.28 = (bf16[2,2,32,1024]{3,2,1,0:T(8,128)(2,1)}, bf16[2,2,32,1024]{3,2,1,0:T(8,128)(2,1)S(1)}, u32[]{:S(2)}) copy-start(bf16[2,2,32,1024]{3,2,1,0:T(8,128)(2,1)S(1)} %collective-permute-done.17) | copy-start | bytes 786436
  547.0 32.5 %collective-permute-start.18 = (bf16[2,32,1024]{2,1,0:T(8,128)(2,1)S(1)}, bf16[2,32,1024]{2,1,0:T(8,128)(2,1)S(1)}, u32[]{:S(2)}, u32[]{:S(2)}) collective-permute-start(bf16[2,32,1024]{2,1,0:T(8,128)(2,1)S(1)} %fusion.37), channel_id=1, source_target_pairs={{0,2},{1,3},{2,0},{3,1},{4,6},{5,7},{6,4},{7,5},{8,10},{9,11},{10,... | collective-permute-start | bytes 393224 | tf_op jit(solution)/shard_map/ppermute | solution.py:498
  549.6 35.1 %copy-start.27 = (f32[3,32,1024]{2,1,0:T(8,128)S(1)}, f32[3,32,1024]{2,1,0:T(8,128)}, u32[]{:S(2)}) copy-start(f32[3,32,1024]{2,1,0:T(8,128)} %param.22) | copy-start | bytes 1179652
  554.4 63.8 %collective-permute-start.20 = (bf16[2,2,2,2,32,4096]{5,4,3,2,1,0:T(8,128)(2,1)}, bf16[2,2,2,2,32,4096]{5,4,3,2,1,0:T(8,128)(2,1)}, u32[]{:S(2)}, u32[]{:S(2)}) collective-permute-start(bf16[2,2,2,2,32,4096]{5,4,3,2,1,0:T(8,128)(2,1)} %dynamic-slice_bitcast_fusion.1), channel_id=1, source_target_pairs={{0,4},{4,0},{8,12},{12,8},{16,20},{20,16},{24,28},{28,24},{1,5},{5... | collective-permute-start | bytes 12582920 | tf_op jit(solution)/shard_map/ppermute | solution.py:498
  580.4 4.3 collective-permute-start.19
  586.4 13.8 %copy-start.14 = (bf16[1,512,1024]{2,1,0:T(8,128)(2,1)S(1)}, bf16[1,512,1024]{2,1,0:T(8,128)(2,1)}, u32[]{:S(2)}) copy-start(bf16[1,512,1024]{2,1,0:T(8,128)(2,1)} %param.14) | copy-start | bytes 3145732
  600.2 6.1 collective-permute-start.30
  604.3 8.4 %slice-start.2 = ((s8[8388608]{0:T(1024)(128)(4,1)}), s8[4194304]{0:T(1024)(128)(4,1)S(1)}, s32[]{:S(2)}) async-start(s8[8388608]{0:T(1024)(128)(4,1)} %bitcast.581), calls=%async_computation.15 | async-start | bytes 8388608
  604.8 13.4 %slice-start = ((s8[8388608]{0:T(1024)(128)(4,1)}), s8[4194304]{0:T(1024)(128)(4,1)S(1)}, s32[]{:S(2)}) async-start(s8[8388608]{0:T(1024)(128)(4,1)} %bitcast.573), calls=%async_computation.13 | async-start | bytes 8388608
  606.3 18.1 %collective-permute-start.5 = (bf16[2,2,2,2,64,1024]{5,4,3,2,1,0:T(8,128)(2,1)}, bf16[2,2,2,2,64,1024]{5,4,3,2,1,0:T(8,128)(2,1)}, u32[]{:S(2)}, u32[]{:S(2)}) collective-permute-start(bf16[2,2,2,2,64,1024]{5,4,3,2,1,0:T(8,128)(2,1)} %dynamic-slice_bitcast_fusion.3), channel_id=1, source_target_pairs={{0,4},{4,0},{8,12},{12,8},{16,20},{20,16},{24,28},{28,24},{1,5},{5... | collective-permute-start | bytes 6291464 | tf_op jit(solution)/shard_map/ppermute | solution.py:498
  606.4 6.0 collective-permute-start.31
  608.4 4.3 slice-start.3
  608.4 9.8 %slice-start.1 = ((s8[8388608]{0:T(1024)(128)(4,1)}), s8[4194304]{0:T(1024)(128)(4,1)S(1)}, s32[]{:S(2)}) async-start(s8[8388608]{0:T(1024)(128)(4,1)} %bitcast.573), calls=%async_computation.14 | async-start | bytes 8388608
  612.4 10.3 %collective-permute-start.32 = (f32[1,6144]{1,0:T(1,128)S(1)}, f32[1,6144]{1,0:T(1,128)S(1)}, u32[]{:S(2)}, u32[]{:S(2)}) collective-permute-start(f32[1,6144]{1,0:T(1,128)S(1)} %add.1293), channel_id=1, source_target_pairs={{0,4},{4,0},{8,12},{12,8},{16,20},{20,16},{24,28},{28,24},{1,5},{5... | collective-permute-start | bytes 73736 | tf_op jit(solution)/shard_map/ppermute | solution.py:498
  616.8 58.5 %collective-permute-start.26 = (bf16[2,2,2,128,1024]{4,3,2,1,0:T(8,128)(2,1)}, bf16[2,2,2,128,1024]{4,3,2,1,0:T(8,128)(2,1)S(1)}, u32[]{:S(2)}, u32[]{:S(2)}) collective-permute-start(bf16[2,2,2,128,1024]{4,3,2,1,0:T(8,128)(2,1)} %fusion), channel_id=1, source_target_pairs={{0,8},{4,12},{8,0},{12,4},{16,24},{20,28},{24,16},{28,20},{1,9},{5... | collective-permute-start | bytes 6291464 | tf_op jit(solution)/shard_map/ppermute | solution.py:498
  621.9 57.2 %collective-permute-start.21 = (bf16[2,2,2,32,4096]{4,3,2,1,0:T(8,128)(2,1)}, bf16[2,2,2,32,4096]{4,3,2,1,0:T(8,128)(2,1)S(1)}, u32[]{:S(2)}, u32[]{:S(2)}) collective-permute-start(bf16[2,2,2,32,4096]{4,3,2,1,0:T(8,128)(2,1)} %fusion.1), channel_id=1, source_target_pairs={{0,16},{4,20},{8,24},{12,28},{16,0},{20,4},{24,8},{28,12},{1,17},{... | collective-permute-start | bytes 6291464 | tf_op jit(solution)/shard_map/ppermute | solution.py:498
  622.7 94.2 %collective-permute-start.10 = (bf16[2,2,2,2,32,3072]{5,4,3,2,1,0:T(8,128)(2,1)S(1)}, bf16[2,2,2,2,32,3072]{5,4,3,2,1,0:T(8,128)(2,1)S(1)}, u32[]{:S(2)}, u32[]{:S(2)}) collective-permute-start(bf16[2,2,2,2,32,3072]{5,4,3,2,1,0:T(8,128)(2,1)S(1)} %dynamic-slice_bitcast_fusion.2), channel_id=1, source_target_pairs={{0,4},{4,0},{8,12},{12,8},{16,20},{20,16},{24,28},{28,24},{1,5},{5... | collective-permute-start | bytes 9437192 | tf_op jit(solution)/shard_map/ppermute | solution.py:498
  622.9 43.6 %collective-permute-start.33 = (f32[2,6144]{1,0:T(2,128)S(1)}, f32[2,6144]{1,0:T(2,128)S(1)}, u32[]{:S(2)}, u32[]{:S(2)}) collective-permute-start(f32[2,6144]{1,0:T(2,128)S(1)} %maximum_select_fusion.3), channel_id=1, source_target_pairs={{0,8},{4,12},{8,0},{12,4},{16,24},{20,28},{24,16},{28,20},{1,9},{5... | collective-permute-start | bytes 147464 | tf_op jit(solution)/shard_map/ppermute | solution.py:498
  626.0 62.9 %collective-permute-start.6 = (bf16[2,2,2,64,1024]{4,3,2,1,0:T(8,128)(2,1)S(1)}, bf16[2,2,2,64,1024]{4,3,2,1,0:T(8,128)(2,1)S(1)}, u32[]{:S(2)}, u32[]{:S(2)}) collective-permute-start(bf16[2,2,2,64,1024]{4,3,2,1,0:T(8,128)(2,1)S(1)} %fusion.5), channel_id=1, source_target_pairs={{0,8},{4,12},{8,0},{12,4},{16,24},{20,28},{24,16},{28,20},{1,9},{5... | collective-permute-start | bytes 3145736 | tf_op jit(solution)/shard_map/ppermute | solution.py:498
  666.6 5.2 collective-permute-start.34
  678.1 50.9 %collective-permute-start.27 = (bf16[2,2,128,1024]{3,2,1,0:T(8,128)(2,1)}, bf16[2,2,128,1024]{3,2,1,0:T(8,128)(2,1)S(1)}, u32[]{:S(2)}, u32[]{:S(2)}) collective-permute-start(bf16[2,2,128,1024]{3,2,1,0:T(8,128)(2,1)} %fusion.3), channel_id=1, source_target_pairs={{0,16},{4,20},{8,24},{12,28},{16,0},{20,4},{24,8},{28,12},{1,17},{... | collective-permute-start | bytes 3145736 | tf_op jit(solution)/shard_map/ppermute | solution.py:498
  681.8 51.7 %collective-permute-start.22 = (bf16[2,2,32,4096]{3,2,1,0:T(8,128)(2,1)}, bf16[2,2,32,4096]{3,2,1,0:T(8,128)(2,1)S(1)}, u32[]{:S(2)}, u32[]{:S(2)}) collective-permute-start(bf16[2,2,32,4096]{3,2,1,0:T(8,128)(2,1)} %fusion.4), channel_id=1, source_target_pairs={{0,8},{4,12},{8,0},{12,4},{16,24},{20,28},{24,16},{28,20},{1,9},{5... | collective-permute-start | bytes 3145736 | tf_op jit(solution)/shard_map/ppermute | solution.py:498
  690.3 23.5 %collective-permute-start.7 = (bf16[2,2,64,1024]{3,2,1,0:T(8,128)(2,1)S(1)}, bf16[2,2,64,1024]{3,2,1,0:T(8,128)(2,1)S(1)}, u32[]{:S(2)}, u32[]{:S(2)}) collective-permute-start(bf16[2,2,64,1024]{3,2,1,0:T(8,128)(2,1)S(1)} %fusion.10), channel_id=1, source_target_pairs={{0,16},{4,20},{8,24},{12,28},{16,0},{20,4},{24,8},{28,12},{1,17},{... | collective-permute-start | bytes 1572872 | tf_op jit(solution)/shard_map/ppermute | solution.py:498
  714.9 13.0 %collective-permute-start.8 = (bf16[2,64,1024]{2,1,0:T(8,128)(2,1)S(1)}, bf16[2,64,1024]{2,1,0:T(8,128)(2,1)S(1)}, u32[]{:S(2)}, u32[]{:S(2)}) collective-permute-start(bf16[2,64,1024]{2,1,0:T(8,128)(2,1)S(1)} %fusion.22), channel_id=1, source_target_pairs={{0,2},{1,3},{2,0},{3,1},{4,6},{5,7},{6,4},{7,5},{8,10},{9,11},{10,... | collective-permute-start | bytes 786440 | tf_op jit(solution)/shard_map/ppermute | solution.py:498
  717.5 62.1 %collective-permute-start.11 = (bf16[2,2,2,32,3072]{4,3,2,1,0:T(8,128)(2,1)S(1)}, bf16[2,2,2,32,3072]{4,3,2,1,0:T(8,128)(2,1)S(1)}, u32[]{:S(2)}, u32[]{:S(2)}) collective-permute-start(bf16[2,2,2,32,3072]{4,3,2,1,0:T(8,128)(2,1)S(1)} %fusion.2), channel_id=1, source_target_pairs={{0,16},{4,20},{8,24},{12,28},{16,0},{20,4},{24,8},{28,12},{1,17},{... | collective-permute-start | bytes 4718600 | tf_op jit(solution)/shard_map/ppermute | solution.py:498
  728.9 6.2 copy-start.25
  728.9 6.2 collective-permute-start.9
  730.5 37.8 %collective-permute-start.28 = (bf16[2,128,1024]{2,1,0:T(8,128)(2,1)S(1)}, bf16[2,128,1024]{2,1,0:T(8,128)(2,1)S(1)}, u32[]{:S(2)}, u32[]{:S(2)}) collective-permute-start(bf16[2,128,1024]{2,1,0:T(8,128)(2,1)S(1)} %fusion.7), channel_id=1, source_target_pairs={{0,2},{1,3},{2,0},{3,1},{4,6},{5,7},{6,4},{7,5},{8,10},{9,11},{10,... | collective-permute-start | bytes 1572872 | tf_op jit(solution)/shard_map/ppermute | solution.py:498
  734.8 43.7 %collective-permute-start.23 = (bf16[2,32,4096]{2,1,0:T(8,128)(2,1)S(1)}, bf16[2,32,4096]{2,1,0:T(8,128)(2,1)S(1)}, u32[]{:S(2)}, u32[]{:S(2)}) collective-permute-start(bf16[2,32,4096]{2,1,0:T(8,128)(2,1)S(1)} %fusion.8), channel_id=1, source_target_pairs={{0,2},{1,3},{2,0},{3,1},{4,6},{5,7},{6,4},{7,5},{8,10},{9,11},{10,... | collective-permute-start | bytes 1572872 | tf_op jit(solution)/shard_map/ppermute | solution.py:498
  769.5 14.6 %copy-start.23 = (f32[3,128,1024]{2,1,0:T(8,128)S(1)}, f32[3,128,1024]{2,1,0:T(8,128)}, u32[]{:S(2)}) copy-start(f32[3,128,1024]{2,1,0:T(8,128)} %param.24) | copy-start | bytes 4718596
  769.5 14.5 %collective-permute-start.29 = (bf16[128,1024]{1,0:T(8,128)(2,1)S(1)}, bf16[128,1024]{1,0:T(8,128)(2,1)S(1)}, u32[]{:S(2)}, u32[]{:S(2)}) collective-permute-start(bf16[128,1024]{1,0:T(8,128)(2,1)S(1)} %fusion.17), channel_id=1, source_target_pairs={{0,1},{1,0},{2,3},{3,2},{4,5},{5,4},{6,7},{7,6},{8,9},{9,8},{10,11... | collective-permute-start | bytes 786440 | tf_op jit(solution)/shard_map/ppermute | solution.py:498
  779.5 10.0 %collective-permute-start.24 = (bf16[32,4096]{1,0:T(8,128)(2,1)S(1)}, bf16[32,4096]{1,0:T(8,128)(2,1)S(1)}, u32[]{:S(2)}, u32[]{:S(2)}) collective-permute-start(bf16[32,4096]{1,0:T(8,128)(2,1)S(1)} %fusion.19), channel_id=1, source_target_pairs={{0,1},{1,0},{2,3},{3,2},{4,5},{5,4},{6,7},{7,6},{8,9},{9,8},{10,11... | collective-permute-start | bytes 786440 | tf_op jit(solution)/shard_map/ppermute | solution.py:498
  780.0 9.5 %copy-start.22 = (f32[3,32,4096]{2,1,0:T(8,128)S(1)}, f32[3,32,4096]{2,1,0:T(8,128)}, u32[]{:S(2)}) copy-start(f32[3,32,4096]{2,1,0:T(8,128)} %param.23) | copy-start | bytes 4718596
  780.0 18.4 %collective-permute-start.12 = (bf16[2,2,32,3072]{3,2,1,0:T(8,128)(2,1)S(1)}, bf16[2,2,32,3072]{3,2,1,0:T(8,128)(2,1)S(1)}, u32[]{:S(2)}, u32[]{:S(2)}) collective-permute-start(bf16[2,2,32,3072]{3,2,1,0:T(8,128)(2,1)S(1)} %fusion.6), channel_id=1, source_target_pairs={{0,8},{4,12},{8,0},{12,4},{16,24},{20,28},{24,16},{28,20},{1,9},{5... | collective-permute-start | bytes 2359304 | tf_op jit(solution)/shard_map/ppermute | solution.py:498
  798.6 18.3 %collective-permute-start.13 = (bf16[2,32,3072]{2,1,0:T(8,128)(2,1)S(1)}, bf16[2,32,3072]{2,1,0:T(8,128)(2,1)S(1)}, u32[]{:S(2)}, u32[]{:S(2)}) collective-permute-start(bf16[2,32,3072]{2,1,0:T(8,128)(2,1)S(1)} %fusion.12), channel_id=1, source_target_pairs={{0,2},{1,3},{2,0},{3,1},{4,6},{5,7},{6,4},{7,5},{8,10},{9,11},{10,... | collective-permute-start | bytes 1179656 | tf_op jit(solution)/shard_map/ppermute | solution.py:498
  817.1 6.0 collective-permute-start.14
  817.1 5.9 copy-start.24
  (19 other events, 34.8 us)
Sparse Core Ops, SparseCore 0:
  11.6 64.9 all-gather.5
  80.1 68.0 all-gather.7
  151.7 58.1 all-gather.9
  213.3 105.4 all-gather.11
  322.1 76.3 all-gather.13

commit v2 on v1

--- a/solution.py
+++ b/solution.py
@@ -114,7 +114,24 @@
     return (master, jnp.stack([first_moment, second_moment]))
 
 
-def skip_kernel(fr_ref, sk_ref, cond_ref, w_ref, mod_ref, hidden_ref, normed_ref):
+def stack_rows(packed_ref, out_ref, owned):
+    cols = out_ref.shape[1]
+    pieces = packed_ref.shape[1] // cols
+    for r in range(packed_ref.shape[0] // owned):
+        for q in range(pieces):
+            at = (r * pieces + q) * owned
+            out_ref[at : at + owned] = packed_ref[
+                r * owned : (r + 1) * owned, q * cols : (q + 1) * cols
+            ]
+
+
+def skip_kernel(
+    owned, fr_ref, sk_ref, cond_ref, packed_ref, mod_ref, hidden_ref, normed_ref, w_ref
+):
+    @pl.when(pl.program_id(0) == 0)
+    def _():
+        stack_rows(packed_ref, w_ref, owned)
+
     width = fr_ref.shape[1]
     hidden = (
         dot_nn(fr_ref[...], w_ref[:width])
@@ -126,45 +143,53 @@
     normed_ref[...] = (normal * (1.0 + mod_ref[1:2]) + mod_ref[0:1]).astype(BF)
 
 
-def skip_forward(frames, skips, cond, weight, mod):
+def skip_weight(weight, owned, width):
+    if owned % 16 == 0:
+        return weight, pl.BlockSpec((width, 2 * width), lambda i: (0, 0)), owned
+    full = stacked(weight[:, : 2 * width], owned, width)
+    return full, whole(full.shape), 2 * width
+
+
+def skip_forward(frames, skips, cond, weight, mod, owned):
     rows, width = frames.shape
     block = min(256, rows)
     row_spec = pl.BlockSpec((block, width), lambda i: (i, 0))
+    weight, weight_spec, piece = skip_weight(weight, owned, width)
     return pl.pallas_call(
-        skip_kernel,
+        functools.partial(skip_kernel, piece),
         grid=(rows // block,),
-        in_specs=[row_spec, row_spec, row_spec, whole(weight.shape), whole(mod.shape)],
+        in_specs=[row_spec, row_spec, row_spec, weight_spec, whole(mod.shape)],
         out_specs=[row_spec, row_spec],
         out_shape=[
             jax.ShapeDtypeStruct((rows, width), F32),
             jax.ShapeDtypeStruct((rows, width), BF),
         ],
+        scratch_shapes=[pltpu.VMEM((2 * width, width), BF)],
         compiler_params=params(40),
         cost_estimate=cost(4 * rows * width * width, 12 * rows * width + 4 * width * width),
     )(frames, skips, cond, weight, mod)
 
 
-def qkv_kernel(x_ref, wq_ref, wk_ref, wv_ref, cos_ref, sin_ref, out_ref):
-    x = x_ref[...]
+def qkv_kernel(x_ref, wq_ref, wk_ref, wv_ref, cos_ref, sin_ref, out_ref, w_ref):
+    for part, ref in enumerate((wq_ref, wk_ref, wv_ref)):
+        w_ref[:, part * 128 : (part + 1) * 128] = ref[...]
+    packed = dot_nn(x_ref[...], w_ref[...])
     cosine, sine = cos_ref[...], sin_ref[...]
-    pairs = out_ref.shape[0]
-    q, k, v = dot_nn(x, wq_ref[...]), dot_nn(x, wk_ref[...]), dot_nn(x, wv_ref[...])
-    for j in range(pairs):
-        part = slice(j * 128, (j + 1) * 128)
-        out_ref[j, :, 0:128] = (q[:, part] * cosine + swap_halves(q[:, part]) * sine).astype(BF)
-        out_ref[j, :, 128:256] = (k[:, part] * cosine + swap_halves(k[:, part]) * sine).astype(BF)
-        out_ref[j, :, 256:384] = v[:, part].astype(BF)
-
-
-def qkv_forward(normed, weight, cosine, sine):
+    for part in range(2):
+        raw = packed[:, part * 128 : (part + 1) * 128]
+        out_ref[0, :, part * 128 : (part + 1) * 128] = (
+            raw * cosine + swap_halves(raw) * sine
+        ).astype(BF)
+    out_ref[0, :, 256:384] = packed[:, 256:384].astype(BF)
+
+
+def qkv_forward(normed, weight, cosine, sine, first, stride):
     rows, width = normed.shape
     pairs = width // 128
-    per_step = 2
-    cols = 128 * per_step
-    steps = pairs // per_step
+    steps = pairs // stride
 
     def columns(part):
-        return pl.BlockSpec((width, cols), lambda i: (0, part * steps + i))
+        return pl.BlockSpec((width, 128), lambda i: (0, (2 + part) * pairs + i * stride + first))
 
     return pl.pallas_call(
         qkv_kernel,
@@ -177,10 +202,13 @@
             whole(cosine.shape),
             whole(sine.shape),
         ],
-        out_specs=pl.BlockSpec((per_step, rows, 384), lambda i: (i, 0, 0)),
-        out_shape=jax.ShapeDtypeStruct((pairs, rows, 384), BF),
+        out_specs=pl.BlockSpec((1, rows, 384), lambda i: (i, 0, 0)),
+        out_shape=jax.ShapeDtypeStruct((steps, rows, 384), BF),
+        scratch_shapes=[pltpu.VMEM((width, 384), BF)],
         compiler_params=params(40),
-        cost_estimate=cost(6 * rows * width * width, 8 * rows * width + 6 * width * width),
+        cost_estimate=cost(
+            6 * rows * width * 128 * steps, 8 * rows * 128 * steps + 6 * width * 128 * steps
+        ),
     )(normed, weight, weight, weight, cosine, sine)
 
 
@@ -309,7 +337,7 @@
     normed_ref[...] = (normal * (1.0 + mod_ref[4:5]) + mod_ref[3:4]).astype(BF)
 
 
-def out_forward(o_chunks, heads, weight, hidden, mod):
+def out_forward(o_chunks, heads, weight, hidden, mod, at):
     rows, width = hidden.shape
     block = min(256, rows)
     row_spec = pl.BlockSpec((block, width), lambda i: (i, 0))
@@ -318,7 +346,8 @@
     return pl.pallas_call(
         functools.partial(out_kernel, len(o_chunks), heads),
         grid=(rows // block,),
-        in_specs=[o_spec] * len(o_chunks) + [whole(weight.shape), row_spec, whole(mod.shape)],
+        in_specs=[o_spec] * len(o_chunks)
+        + [pl.BlockSpec((width, width), lambda i: (0, at)), row_spec, whole(mod.shape)],
         out_specs=[row_spec] * 4,
         out_shape=[
             jax.ShapeDtypeStruct((rows, width), BF),
@@ -331,13 +360,31 @@
     )(*o_chunks, weight, hidden, mod)
 
 
-def ffn_kernel(x_ref, dc_ref, up_ref, dn_ref, y_ref, dx_ref, gu_ref, gd_ref, x_turned):
-    @pl.when(pl.program_id(0) == 0)
+def ffn_kernel(
+    owned, x_ref, dc_ref, up_ref, packed_ref, y_ref, dx_ref, grads_ref, x_turned, dn_ref, gu, gd, sems
+):
+    i, last = pl.program_id(0), pl.num_programs(0) - 1
+    slot = lax.rem(i, 2)
+    block = up_ref.shape[1]
+    part = packed_ref.shape[0]
+    pieces = block // part
+
+    def sends(step, at):
+        across = pl.ds(pl.multiple_of(step * block, block), block)
+        down = pl.ds(pl.multiple_of(step * part, part), part)
+        half = grads_ref.shape[1] // 2
+        return (
+            pltpu.make_async_copy(gu.at[at], grads_ref.at[:, across], sems.at[0, at]),
+            pltpu.make_async_copy(gd.at[at], grads_ref.at[down, pl.ds(half, half)], sems.at[1, at]),
+        )
+
+    @pl.when(i == 0)
     def _():
         x_turned[...] = x_ref[...].T
         y_ref[...] = jnp.zeros_like(y_ref)
         dx_ref[...] = jnp.zeros_like(dx_ref)
 
+    stack_rows(packed_ref, dn_ref, owned)
     dc = dc_ref[...]
     up, dn = up_ref[...], dn_ref[...]
     value, slope = gelu_and_slope(dot_nn(x_ref[...], up))
@@ -345,31 +392,73 @@
     up_cot = (dot_nt(dc, dn) * slope).astype(BF)
     y_ref[...] += dot_nn(activated, dn)
     dx_ref[...] += dot_nt(up_cot, up)
-    gu_ref[...] = dot_nn(x_turned[...], up_cot).astype(BF)
-    gd_ref[...] = dot_tn(activated, dc).astype(BF)
-
-
-def ffn(x, dc, up, dn):
+
+    @pl.when(i >= 2)
+    def _():
+        for copy in sends(i - 2, slot):
+            copy.wait()
+
+    gu[slot] = dot_nn(x_turned[...], up_cot).astype(BF)
+    down_grad = dot_tn(activated, dc).astype(BF)
+    width = dc.shape[1]
+    for r in range(part // owned):
+        for q in range(pieces):
+            at = (r * pieces + q) * owned
+            gd[slot, r * owned : (r + 1) * owned, q * width : (q + 1) * width] = down_grad[
+                at : at + owned
+            ]
+    for copy in sends(i, slot):
+        copy.start()
+
+    @pl.when(i == last)
+    def _():
+        for copy in sends(last - 1, 1 - slot) + sends(last, slot):
+            copy.wait()
+
+
+def ffn(x, dc, weights, owned):
     rows, width = x.shape
-    hidden_width = up.shape[1]
-    block = min(512, hidden_width)
-    up_spec = pl.BlockSpec((width, block), lambda i: (0, i))
-    dn_spec = pl.BlockSpec((block, width), lambda i: (i, 0))
-    return pl.pallas_call(
-        ffn_kernel,
-        grid=(hidden_width // block,),
-        in_specs=[whole(x.shape), whole(x.shape), up_spec, dn_spec],
-        out_specs=[whole(x.shape), whole(x.shape), up_spec, dn_spec],
+    hidden_width = FF
+    pieces = hidden_width // width
+    steps = hidden_width // 512
+    block = 512
+    part = block // pieces
+    packed = weights
+    if owned % 16:
+        full = stacked(weights[:, :hidden_width], owned, width)
+        packed = side_by_side_blocks(full, part, pieces)
+    piece = owned if owned % 16 == 0 else part
+    y, dx, grads = pl.pallas_call(
+        functools.partial(ffn_kernel, piece),
+        grid=(steps,),
+        in_specs=[
+            whole(x.shape),
+            whole(x.shape),
+            pl.BlockSpec((width, block), lambda i: (0, steps + i)),
+            pl.BlockSpec((part, hidden_width), lambda i: (i, 0)),
+        ],
+        out_specs=[whole(x.shape), whole(x.shape), pl.BlockSpec(memory_space=pl.ANY)],
         out_shape=[
             jax.ShapeDtypeStruct((rows, width), F32),
             jax.ShapeDtypeStruct((rows, width), F32),
-            jax.ShapeDtypeStruct(up.shape, BF),
-            jax.ShapeDtypeStruct(dn.shape, BF),
-        ],
-        scratch_shapes=[pltpu.VMEM((width, rows), BF)],
+            jax.ShapeDtypeStruct((width, 2 * hidden_width), BF),
+        ],
+        scratch_shapes=[
+            pltpu.VMEM((width, rows), BF),
+            pltpu.VMEM((block, width), BF),
+            pltpu.VMEM((2, width, block), BF),
+            pltpu.VMEM((2, part, hidden_width), BF),
+            pltpu.SemaphoreType.DMA((2, 2)),
+        ],
         compiler_params=params(60),
         cost_estimate=cost(12 * rows * width * hidden_width, 8 * width * hidden_width),
-    )(x, dc, up, dn)
+    )(x, dc, weights, packed)
+    if owned % 16:
+        full = stacked(grads[:, hidden_width:], part, width)
+        grads = jnp.concatenate(
+            [grads[:, :hidden_width], side_by_side_blocks(full, owned, pieces)], axis=1
+        )
+    return y, dx, grads
 
 
 def mid_kernel(count, heads, *refs):
@@ -401,7 +490,7 @@
             chunk_refs[c][j] = attended_grad[:, at : at + width]
 
 
-def mid_back(y, dx, middle, branch, grad, weight, mod, groups, count, heads):
+def mid_back(y, dx, middle, branch, grad, weight, mod, groups, count, heads, at):
     rows, width = y.shape
     block = min(256, rows)
     row_spec = pl.BlockSpec((block, width), lambda i: (i, 0))
@@ -409,7 +498,8 @@
     return pl.pallas_call(
         functools.partial(mid_kernel, count, heads),
         grid=(rows // block,),
-        in_specs=[row_spec] * 5 + [whole(weight.shape), whole(mod.shape)],
+        in_specs=[row_spec] * 5
+        + [pl.BlockSpec((width, width), lambda i: (0, at)), whole(mod.shape)],
         out_specs=[row_spec] * 3 + [whole((8, width))] + [chunk_spec] * count,
         out_shape=[
             jax.ShapeDtypeStruct((rows, width), BF),
@@ -423,14 +513,15 @@
     )(y, dx, middle, branch, grad, weight, mod)
 
 
-def last_kernel(count, heads, *refs):
+def last_kernel(count, heads, owned, *refs):
     chunk_refs = refs[:count]
-    hidden_ref, mgrad_ref, wqkv_ref, wskip_ref, mod_ref = refs[count : count + 5]
-    cot_ref, hgrad_ref, frames_ref, skips_ref, sums_ref = refs[count + 5 :]
+    hidden_ref, mgrad_ref, wq_ref, wk_ref, wv_ref, packed_ref, mod_ref = refs[count : count + 7]
+    hgrad_ref, frames_ref, skips_ref, sums_ref, wskip_ref, cot_ref = refs[count + 7 :]
 
     @pl.when(pl.program_id(0) == 0)
     def _():
         sums_ref[...] = jnp.zeros_like(sums_ref)
+        stack_rows(packed_ref, wskip_ref, owned)
 
     width = heads * DH
     model = hidden_ref.shape[1]
@@ -441,7 +532,11 @@
                 cot_ref[:, part * model + at : part * model + at + width] = chunk_refs[c][
                     j, :, part * width : (part + 1) * width
                 ]
-    w = dot_nt(cot_ref[...], wqkv_ref[...])
+    w = (
+        dot_nt(cot_ref[:, :model], wq_ref[...])
+        + dot_nt(cot_ref[:, model : 2 * model], wk_ref[...])
+        + dot_nt(cot_ref[:, 2 * model :], wv_ref[...])
+    )
     normal, inverse = normalise(hidden_ref[...])
     sums_ref[0:1] += jnp.sum(w, axis=0, keepdims=True)
     sums_ref[1:2] += jnp.sum(w * normal, axis=0, keepdims=True)
@@ -453,34 +548,81 @@
     skips_ref[...] = dot_nt(hidden_grad, wskip_ref[model:]).astype(BF)
 
 
-def last_back(chunks, heads, hidden, middle_grad, w_qkv, w_skip, mod):
+def last_back(chunks, heads, hidden, middle_grad, weights, mod, owned):
     rows, width = hidden.shape
     block = min(256, rows)
     row_spec = pl.BlockSpec((block, width), lambda i: (i, 0))
     groups = chunks[0].shape[0]
     chunk_spec = pl.BlockSpec((groups, block, 3 * heads * DH), lambda i: (0, i, 0))
+    w_skip, skip_spec, piece = skip_weight(weights, owned, width)
+
+    def part_spec(part):
+        return pl.BlockSpec((width, width), lambda i: (0, 2 + part))
+
     return pl.pallas_call(
-        functools.partial(last_kernel, len(chunks), heads),
+        functools.partial(last_kernel, len(chunks), heads, piece),
         grid=(rows // block,),
         in_specs=[chunk_spec] * len(chunks)
-        + [row_spec, row_spec, whole(w_qkv.shape), whole(w_skip.shape), whole(mod.shape)],
+        + [row_spec, row_spec, part_spec(0), part_spec(1), part_spec(2)]
+        + [skip_spec, whole(mod.shape)],
         out_specs=[
-            pl.BlockSpec((block, 3 * width), lambda i: (i, 0)),
             row_spec,
             row_spec,
             row_spec,
             whole((8, width)),
         ],
         out_shape=[
-            jax.ShapeDtypeStruct((rows, 3 * width), BF),
             jax.ShapeDtypeStruct((rows, width), BF),
             jax.ShapeDtypeStruct((rows, width), BF),
             jax.ShapeDtypeStruct((rows, width), BF),
             jax.ShapeDtypeStruct((8, width), F32),
         ],
+        scratch_shapes=[pltpu.VMEM((2 * width, width), BF), pltpu.VMEM((block, 3 * width), BF)],
         compiler_params=params(58),
         cost_estimate=cost(10 * rows * width * width, 26 * rows * width + 10 * width * width),
-    )(*chunks, hidden, middle_grad, w_qkv, w_skip, mod)
+    )(*chunks, hidden, middle_grad, weights, weights, weights, w_skip, mod)
+
+
+def qkv_grad_kernel(extra, *refs):
+    x_ref, chunk_ref = refs[:2]
+    out_ref, x_turned = refs[2 + extra], refs[3 + extra]
+
+    @pl.when(pl.program_id(0) == 0)
+    def _():
+        x_turned[...] = x_ref[...].T
+        if extra:
+            refs[4 + extra][...] = refs[2][...].T
+
+    cols = chunk_ref.shape[2]
+    out_ref[:, :cols] = dot_nn(x_turned[...], chunk_ref[0]).astype(BF)
+    if extra:
+        out_ref[:, cols:] = dot_nn(refs[4 + extra][...], refs[3][...]).astype(BF)
+
+
+def qkv_grad(normed, chunk, *extra):
+    groups, rows, cols = chunk.shape
+    width = normed.shape[1]
+    more = width // groups if extra else 0
+    if cols % 128:
+        parts = [dot_tn(normed, chunk.transpose(1, 0, 2).reshape(rows, groups * cols))]
+        parts += [dot_tn(*extra)] if extra else []
+        parts = [p.reshape(width, groups, -1) for p in parts]
+        return jnp.concatenate(parts, axis=2).reshape(width, -1).astype(BF)
+    extra_specs = [whole((rows, width)), pl.BlockSpec((rows, more), lambda i: (0, i))]
+    turned = pltpu.VMEM((width, rows), BF)
+    return pl.pallas_call(
+        functools.partial(qkv_grad_kernel, len(extra)),
+        grid=(groups,),
+        in_specs=[whole(normed.shape), pl.BlockSpec((1, rows, cols), lambda i: (i, 0, 0))]
+        + extra_specs[: len(extra)],
+        out_specs=pl.BlockSpec((width, cols + more), lambda i: (0, i)),
+        out_shape=jax.ShapeDtypeStruct((width, groups * (cols + more)), BF),
+        scratch_shapes=[turned] * (2 if extra else 1),
+        compiler_params=params(30),
+        cost_estimate=cost(
+            2 * rows * width * groups * (cols + more), 5 * width * groups * (cols + more)
+        ),
+    )(normed, chunk, *extra)
 
 
 def bits_of(axis):
@@ -498,24 +640,43 @@
     return lax.ppermute(values, axis, [(i, i ^ (1 << bit)) for i in range(lax.axis_size(axis))])
 
 
-def scatter_sum(grad, order):
-    dims = bits_of("dp") + bits_of("seq")
-    rows, cols = grad.shape
-    terms = [grad.reshape([2] * len(dims) + [rows // 2 ** len(dims), cols])]
-    for level in order:
-        at, mine = dims.index(level), my_bit(level)
-        dims.pop(at)
+def after(values, *others):
+    return lax.optimization_barrier((values, *others))[0]
+
+
+class ScatterSum:
+    def __init__(self, grad, order, dims):
+        self.dims, self.order = list(dims), list(order)
+        rows, cols = grad.shape
+        split = [2] * len(self.dims)
+        self.terms = [grad.reshape(split + [rows // 2 ** len(split), cols])]
+
+    def hold(self, *waits):
+        if waits:
+            self.terms[-1] = after(self.terms[-1], *waits)
+
+    def step(self, *waits):
+        self.hold(*waits)
+        level = self.order.pop(0)
+        at, mine = self.dims.index(level), my_bit(level)
+        self.dims.pop(at)
 
         def halves(side):
-            return [lax.dynamic_index_in_dim(t, side, at, keepdims=False) for t in terms]
+            return [lax.dynamic_index_in_dim(t, side, at, keepdims=False) for t in self.terms]
 
         leaving = halves(1 - mine)
         total = leaving[0]
         if len(leaving) > 1:
-            total = sum(t.astype(F32) for t in leaving).astype(grad.dtype)
+            total = sum(t.astype(F32) for t in leaving).astype(total.dtype)
+        self.sent = total
         arrived = swap(total, level)
-        terms = halves(mine) + [arrived]
-    return sum(t.astype(F32) for t in terms)
+        self.terms = halves(mine) + [arrived]
+        return arrived
+
+    def total(self):
+        while self.order:
+            self.step()
+        return sum(t.astype(F32) for t in self.terms)
 
 
 def exchange(values, axis):
@@ -536,18 +697,55 @@
     return held
 
 
-def modulation_cots(own, total_count):
-    for level in bits_of("seq"):
-        own = own + swap(own, level)
-    for level in reversed(bits_of("dp")):
-        other = swap(own, level)
-        mine = my_bit(level)
-        own = jnp.where(
-            mine == 0,
-            jnp.concatenate([own, other], axis=0),
-            jnp.concatenate([other, own], axis=0),
-        )
-    return own
+class ModulationCots:
+    def __init__(self, own):
+        self.own, self.order = own, bits_of("seq") + bits_of("dp")[::-1]
+
+    def step(self, *waits):
+        level = self.order.pop(0)
+        own = after(self.own, *waits)
+        if level[0] == "seq":
+            self.own = own + swap(own, level)
+        else:
+            self.own = gather_pairwise(own, [level])
+
+
+def side_by_side(own, rows):
+    return jnp.concatenate(jnp.split(own, own.shape[0] // rows, axis=0), axis=1)
+
+
+def stacked(full, rows, cols):
+    pieces = full.shape[1] // cols
+    blocks = full.reshape(full.shape[0] // rows, rows, pieces, cols)
+    return blocks.transpose(0, 2, 1, 3).reshape(full.shape[0] * pieces, cols)
+
+
+def side_by_side_blocks(full, rows, pieces):
+    cols = full.shape[1]
+    blocks = full.reshape(full.shape[0] // (rows * pieces), pieces, rows, cols)
+    return blocks.transpose(0, 2, 1, 3).reshape(full.shape[0] // pieces, pieces * cols)
+
+
+def gather_pairwise(own, order, last_wait=None, last_use=None):
+    rows, cols = own.shape
+    held, bits = own.reshape(1, rows, cols), []
+    for level in order:
+        if last_wait is not None and len(bits) == len(order) - 1:
+            held = after(held, last_wait)
+        other = swap(held, level)
+        if last_use is not None and len(bits) == len(order) - 1:
+            other = after(other, last_use)
+        at = sum(1 for bit in bits if bit > level[1])
+        bits.append(level[1])
+        shape = [2] * (len(bits) - 1)
+        own_part = held.reshape(shape + [rows, cols])
+        other_part = other.reshape(shape + [rows, cols])
+        held = jnp.where(
+            my_bit(level) == 0,
+            jnp.stack([own_part, other_part], axis=at),
+            jnp.stack([other_part, own_part], axis=at),
+        ).reshape(2 ** len(bits), rows, cols)
+    return held.reshape(-1, cols)
 
 
 def per_device(
@@ -569,6 +767,7 @@
     seq = lax.axis_size("seq")
     everyone = ("dp", "seq")
     owned = attn_qkv_state.shape[1]
+    hidden_width = ffn_up_state.shape[2]
     length = rows * seq
     me = lax.axis_index(everyone)
     positions = lax.axis_index("seq") * rows + jnp.arange(rows, dtype=jnp.int32)
@@ -577,11 +776,16 @@
     heads = min(2, group_heads)
     count = group_heads // heads
 
-    skip_full = lax.all_gather(skip_proj_state[0].astype(BF), everyone, axis=0, tiled=True)
-    qkv_full = lax.all_gather(attn_qkv_state[0].astype(BF), everyone, axis=0, tiled=True)
-    out_full = lax.all_gather(attn_out_state[0].astype(BF), everyone, axis=0, tiled=True)
-    up_full = lax.all_gather(ffn_up_state[0].astype(BF), everyone, axis=0, tiled=True)
-    down_full = lax.all_gather(ffn_down_state[0].astype(BF), everyone, axis=0, tiled=True)
+    first_full = lax.all_gather(
+        jnp.concatenate(
+            [side_by_side(skip_proj_state[0].astype(BF), owned), attn_qkv_state[0].astype(BF)],
+            axis=1,
+        ),
+        everyone,
+        axis=0,
+        tiled=True,
+    )
+    out_at = 2 * hidden_width // width
 
     dp_bits, seq_bits = bits_of("dp"), bits_of("seq")
     core, planes = dp_bits[-1], dp_bits[:-1]
@@ -604,51 +808,129 @@
     grad = jnp.where(inside[:, None], out_grad[0], jnp.zeros_like(out_grad[0]))
     down_cot = (grad.astype(F32) * mod[5:6]).astype(BF)
 
-    hidden, normed = skip_forward(frames, skips, cond, skip_full, mod)
-    packed = qkv_forward(normed, qkv_full, cos_own, sin_own)
+    hidden, normed = skip_forward(frames, skips, cond, first_full, mod, owned)
     if heads == 2:
-        packed = packed.reshape(seq, count, rows, 3 * heads * DH)
+        packed = []
+        for c in range(count):
+            x = after(normed, packed[-1]) if packed else normed
+            packed.append(qkv_forward(x, first_full, cos_own, sin_own, c, count))
     else:
+        packed = qkv_forward(normed, first_full, cos_own, sin_own, 0, 1)
         packed = packed.reshape(HEADS // 2, rows, 3, 2, DH).transpose(0, 3, 1, 2, 4)
-        packed = packed.reshape(seq, count, rows, 3 * heads * DH)
-    qkv_chunks = [exchange(packed[:, c], "seq").reshape(length, -1) for c in range(count)]
+        packed = [packed.reshape(seq, rows, 3 * DH)]
+    second_own = jnp.concatenate(
+        [
+            side_by_side(ffn_down_state[0].astype(BF), owned),
+            ffn_up_state[0].astype(BF),
+            attn_out_state[0].astype(BF),
+        ],
+        axis=1,
+    )
+    second_own = gather_pairwise(after(second_own, modulation), seq_bits, first_full, packed[-1])
+    second_full = lax.all_gather(second_own, "dp", axis=0, tiled=True)
+    qkv_chunks = [exchange(part, "seq").reshape(length, -1) for part in packed]
     attended = [attend(chunk, heads) for chunk in qkv_chunks]
     o_chunks = [exchange(o.reshape(seq, rows, heads * DH), "seq") for o, _ in attended]
 
     attended_low, branch, middle, normed_two = out_forward(
-        o_chunks, heads, out_full, hidden, mod
-    )
-    downward, normed_two_grad, up_part, down_part = ffn(normed_two, down_cot, up_full, down_full)
+        o_chunks, heads, second_full, hidden, mod, out_at
+    )
+    downward, normed_two_grad, ffn_part = ffn(normed_two, down_cot, second_full, owned)
     mid = mid_back(
-        downward, normed_two_grad, middle, branch, grad, out_full, mod, seq, count, heads
+        downward,
+        normed_two_grad,
+        middle,
+        branch,
+        grad,
+        second_full,
+        mod,
+        seq,
+        count,
+        heads,
+        out_at,
     )
     block_out, middle_grad, branch_cot, mid_sums = mid[:4]
-    up_wgrad = scatter_sum(up_part, [core] + planes + seq_bits)
-    down_wgrad = scatter_sum(down_part, [core] + planes[::-1] + seq_bits)
-
-    cot_chunks = []
+    every_bit = dp_bits + seq_bits
+    rising = seq_bits[::-1]
+    ffn_part = lax.psum_scatter(ffn_part, "dp", scatter_dimension=0, tiled=True)
+    backs = []
     for c in range(count):
         do = exchange(mid[4 + c], "seq").reshape(length, heads * DH)
         o, log_total = attended[c]
-        back = attend_back(qkv_chunks[c], do, o, log_total, cos_all, sin_all, heads)
-        cot_chunks.append(exchange(back.reshape(seq, rows, 3 * heads * DH), "seq"))
-    out_part = dot_tn(attended_low, branch_cot).astype(BF)
-    out_wgrad = scatter_sum(out_part, [core] + planes[::-1] + seq_bits)
-
-    packed_cot, hidden_grad, frames_grad, skip_grad, last_sums = last_back(
-        cot_chunks, heads, hidden, middle_grad, qkv_full, skip_full, mod
+        backs.append(attend_back(qkv_chunks[c], do, o, log_total, cos_all, sin_all, heads))
+    cot_chunks = [exchange(b.reshape(seq, rows, 3 * heads * DH), "seq") for b in backs]
+
+    sent = [backs[-1]]
+
+    def leave(part):
+        part.step(sent[-1])
+        sent.append(part.sent)
+
+    ffn_sum = None
+    qkv_sums = []
+    for c in range(count):
+        if c == count - 1:
+            ffn_sum = ScatterSum(after(ffn_part, cot_chunks[-1]), rising, seq_bits)
+            leave(ffn_sum)
+        extra = () if c else (attended_low, branch_cot)
+        grad_part = qkv_grad(normed, after(cot_chunks[c], sent[-1]), *extra)
+        order = planes if c % 2 else planes[::-1]
+        qkv_sums.append(ScatterSum(grad_part, [core] + order + rising, every_bit))
+        leave(qkv_sums[-1])
+        if c < count - 1:
+            leave(qkv_sums[-1])
+    for part in qkv_sums:
+        leave(part)
+    cot_chunks[-1] = after(cot_chunks[-1], sent[-1])
+    hidden_grad, frames_grad, skip_grad, last_sums = last_back(
+        cot_chunks, heads, hidden, middle_grad, first_full, mod, owned
     )
     skip_part = jnp.concatenate(
         [dot_tn(frames, hidden_grad).astype(BF), dot_tn(skips, hidden_grad).astype(BF)], axis=0
     )
-    skip_wgrad = scatter_sum(skip_part, [core] + planes[::-1] + seq_bits)
-    qkv_part = dot_tn(normed, packed_cot).astype(BF)
-    qkv_wgrad = scatter_sum(qkv_part, [core] + planes + seq_bits)
-
+    half = width // 2
+    skip_sums = [
+        ScatterSum(skip_part[:, :half], [core] + planes[::-1] + rising, every_bit),
+        ScatterSum(skip_part[:, half:], [core] + planes + rising, every_bit),
+    ]
     mod_cot = jnp.concatenate(
         [last_sums[0], last_sums[1], mid_sums[0], mid_sums[1], mid_sums[2], mid_sums[3]]
     ).reshape(1, 6 * width)
-    mod_cots = modulation_cots(mod_cot, flow_time.shape[0])
+    mod_cots = ModulationCots(mod_cot)
+    others = [ffn_sum] + qkv_sums
+    marks, finished = [], {}
+    for part in others:
+        part.hold(hidden_grad)
+    while skip_sums[0].order:
+        for part in skip_sums:
+            leave(part)
+        marks.append(sent[-1])
+        for part in others:
+            if part.order:
+                leave(part)
+            else:
+                finished.setdefault(part, len(marks) - 1)
+        if mod_cots.order:
+            mod_cots.step(sent[-1])
+    for part in others:
+        while part.order:
+            leave(part)
+        part.hold(marks[min(finished.get(part, len(marks)) + 1, len(marks) - 1)])
+    while mod_cots.order:
+        mod_cots.step()
+    mod_cots = mod_cots.own
+    ffn_total = ffn_sum.total()
+    up_wgrad = ffn_total[:, :hidden_width]
+    down_wgrad = stacked(ffn_total[:, hidden_width:], owned, width)
+    skip_wgrad = jnp.concatenate([part.total() for part in skip_sums], axis=1)
+    qkv_totals = [part.total().reshape(owned, seq, -1) for part in qkv_sums]
+    chunk_cols = 3 * heads * DH
+    out_wgrad = qkv_totals[0][:, :, chunk_cols:].reshape(owned, width)
+    qkv_wgrad = jnp.stack(
+        [t[:, :, :chunk_cols].reshape(owned, seq, 3, heads * DH) for t in qkv_totals], axis=3
+    )
+    qkv_wgrad = qkv_wgrad.transpose(0, 2, 1, 3, 4).reshape(owned, 3 * width)
+
     mod_wgrad = lax.dot_general(
         time_own.astype(F32),
         mod_cots,

time: 841 us -> 612 us (0.73)
  waiting for transfers between devices: 439 us -> 185 us
  Pallas kernels: 149 us -> 171 us
  other arithmetic: 57.3 us -> 74.1 us
  blocking collectives: 49.5 us -> 40 us
    all_gather x5 -> x2, waiting for transfers between devices: 180 us -> 39.7 us  [the longest x1 39.7 us: per_device(): lax.all_gather(jnp.concatenate([side_by_side(skip_proj_state[0].astype(BF...]
    ppermute x35 -> x34, waiting for transfers between devices: 190 us -> 65.9 us  [swap(): lax.ppermute(values, axis, [(i, i ^ 1 << bit) for i in range(lax.axis_siz...]
    pallas_call x3 -> x5, Pallas kernels: 49.2 us -> 63 us  [the longest x1 35.6 us: ffn(): pl.pallas_call(functools.partial(ffn_kernel, piece), grid=(steps,), in_sp...]
    add x2 -> x11, other arithmetic: 0.06 us -> 10.9 us  [the longest x5 6.08 us: total(): return sum((t.astype(F32) for t in self.terms))]
    all_to_all x7, waiting for transfers between devices: 69.2 us -> 78.9 us  [exchange(): return lax.all_to_all(values, axis, 0, 0, tiled=True)]
    all_to_all x1, blocking collectives: 49.5 us -> 40 us  [exchange(): return lax.all_to_all(values, axis, 0, 0, tiled=True)]
    ppermute x35 -> x34, starting transfers between devices: 35.6 us -> 39.6 us  [swap(): lax.ppermute(values, axis, [(i, i ^ 1 << bit) for i in range(lax.axis_siz...]
    unnamed x77 -> x97, local copies, waits for them, and re-layouts: 18.7 us -> 19.9 us
  transfers between devices with their start and end apart: 47 -> 44, of which waited for: 29 -> 17; matrix products, arithmetic and copies ran while one was open for 11% -> 14% of each run, Pallas kernels for 13% -> 22%
where the time goes in v2:
time: 612 us; the launch traced here: 602 us
  waiting for transfers between devices  185 us (30%)
  Pallas kernels  171 us (28%)
  other arithmetic  74.1 us (12%)
  starting transfers between devices  69.5 us (11%)
  blocking collectives  40 us (7%)
  local copies, waits for them, and re-layouts  37.2 us (6%)
  between operations  16.4 us (3%)
  matrix products  8.84 us (1%)
    all_to_all x7, waiting for transfers between devices, exchange(): return lax.all_to_all(values, axis, 0, 0, tiled=True)  78.9 us
    ppermute x34, waiting for transfers between devices, swap(): lax.ppermute(values, axis, [(i, i ^ 1 << bit) for i in range(lax.axis_siz...  65.9 us
    pallas_call x2, Pallas kernels, attend_back(): pl.pallas_call(functools.partial(attend_back_kernel, heads, block), grid=...  54.8 us
    all_to_all x1, blocking collectives, exchange(): return lax.all_to_all(values, axis, 0, 0, tiled=True)  40 us
    all_gather x1, waiting for transfers between devices, per_device(): lax.all_gather(jnp.concatenate([side_by_side(skip_proj_state[0].astype(BF...  39.7 us
    ppermute x34, starting transfers between devices, swap(): lax.ppermute(values, axis, [(i, i ^ 1 << bit) for i in range(lax.axis_siz...  39.6 us
    pallas_call x1, Pallas kernels, ffn(): pl.pallas_call(functools.partial(ffn_kernel, piece), grid=(steps,), in_sp...  35.6 us
    pallas_call x2, Pallas kernels, attend(): pl.pallas_call(functools.partial(attend_kernel, heads, block), grid=(leng...  32.1 us
  transfers between devices with their start and end apart: 44, of which 17 were waited for; matrix products, arithmetic and copies ran while one was open for 14% of the time, Pallas kernels for 22%

profile of v2, /device:TPU:0, one launch (start us, length us, event | category | flops | bytes accessed | tf_op | source)
XLA Modules:
  0.0 602.1 jit_solution(12242077615924255968)
XLA Ops:
  14.2 2.8 collective-permute-start.1
  17.0 2.2 collective-permute-done.1
  19.3 1.9 collective-permute-start.2
  21.2 2.0 collective-permute-done.2
  23.2 3.0 collective-permute-start.3
  31.3 1.8 collective-permute-done.4
  34.4 2.7 collective-permute-start.5
  38.4 37.0 %collective-permute-done.5 = bf16[1,32,9216]{2,1,0:T(8,128)(2,1)S(1)} collective-permute-done((bf16[1,32,9216]{2,1,0:T(8,128)(2,1)S(1)}, bf16[1,32,9216]{2,1,0:T(8,128)(2,1)S(1)}, u32[]{:S(2)}, u32[]{:S(2)}) %collective-permute-start.5) | collective-permute-done | bytes 589856 | tf_op jit(solution)/shard_map/ppermute | solution.py:640
  76.6 39.7 %all-gather.3.cloned.1.call-done.packed_ref.wq_ref.wk_ref.wv_ref.refs_4_.refs_5_.refs_6_.refs_7_ = bf16[1024,5120]{1,0:T(8,128)(2,1)} async-done(((bf16[32,5120]{1,0:T(8,128)(2,1)}), bf16[1024,5120]{1,0:T(8,128)(2,1)}) %all-gather.3.cloned.1.call-update) | async-done | bytes 10485776 | tf_op jit(solution)/shard_map/all_gather | solution.py:779
  121.8 5.7 shard_map.244
  128.8 5.7 shard_map.245
  134.4 4.9 shard_map.247
  139.3 5.4 collective-permute-done.6
  144.7 2.8 maximum_select_fusion
  149.1 40.0 %all_to_all.40 = bf16[4,512,384]{2,1,0:T(8,128)(2,1)} all-to-all(bf16[4,512,384]{2,1,0:T(8,128)(2,1)S(1)} %shard_map.247), channel_id=1, replica_groups=mesh['dp'=8,'seq'=4] {'seq'}, dimensions={0} | all-to-all | bytes 3145728 | tf_op jit(solution)/shard_map/all_to_all | solution.py:683
  189.1 4.6 all-to-all-start
  193.8 15.4 %shard_map.248 = (bf16[2048,128]{1,0:T(8,128)(2,1)}, f32[2,2048]{1,0:T(2,128)S(1)}) custom-call(bf16[2048,384]{1,0:T(8,128)(2,1)S(1)} %bitcast.445), custom_call_target="tpu_custom_call" | custom-call | flops 8589934592 | bytes 2097152 | tf_op jit(solution)/shard_map/pallas_call | solution.py:238
  209.1 20.5 %all-to-all-done = bf16[4,512,384]{2,1,0:T(8,128)(2,1)} async-done(((bf16[4,512,384]{2,1,0:T(8,128)(2,1)}), bf16[4,512,384]{2,1,0:T(8,128)(2,1)}, u32[]{:S(2)}, u32[]{:S(2)}) %all-to-all-start) | async-done | bytes 1572896 | tf_op jit(solution)/shard_map/all_to_all | solution.py:683
  229.7 3.7 all-to-all-start.3
  233.4 16.8 %shard_map.246 = (bf16[2048,128]{1,0:T(8,128)(2,1)}, f32[2,2048]{1,0:T(2,128)S(1)}) custom-call(bf16[2048,384]{1,0:T(8,128)(2,1)} %bitcast.15.qkv_ref), custom_call_target="tpu_custom_call" | custom-call | flops 8589934592 | bytes 2097152 | tf_op jit(solution)/shard_map/pallas_call | solution.py:238
  250.7 5.1 all-to-all-start.1
  255.8 2.5 multiply_convert_fusion
  258.3 10.9 %all-to-all-done.1.refs_0_ = bf16[4,512,128]{2,1,0:T(8,128)(2,1)S(1)} async-done(((bf16[4,512,128]{2,1,0:T(8,128)(2,1)}), bf16[4,512,128]{2,1,0:T(8,128)(2,1)S(1)}, u32[]{:S(2)}, u32[]{:S(2)}) %all-to-all-start.1) | async-done | bytes 524320 | tf_op jit(solution)/shard_map/all_to_all | solution.py:683
  270.8 3.7 shard_map.249
  279.1 35.6 %shard_map.250 = (f32[512,1024]{1,0:T(8,128)}, f32[512,1024]{1,0:T(8,128)}, bf16[1024,8192]{1,0:T(8,128)(2,1)}) custom-call(bf16[512,1024]{1,0:T(8,128)(2,1)} %copy-done.19, bf16[512,1024]{1,0:T(8,128)(2,1)} %get-tuple-element.143.dc_ref, bf16[1024,9216]{1,0:T(8,128)(2,1)} %all-gather.5.cloned.1.call-done.refs_2_.up_ref.packed_ref.refs_5_, ...), custom_call_target="tpu_custom_call" | custom-call | flops 25769803776 | bytes 33554432 | tf_op jit(solution)/shard_map/pallas_call | solution.py:431
  314.7 7.2 %shard_map.251 = (bf16[512,1024]{1,0:T(8,128)(2,1)}, f32[512,1024]{1,0:T(8,128)}, bf16[512,1024]{1,0:T(8,128)(2,1)S(1)}, f32[8,1024]{1,0:T(8,128)S(1)}, bf16[4,5...) custom-call(f32[512,1024]{1,0:T(8,128)} %get-tuple-element.88.refs_0_, f32[512,1024]{1,0:T(8,128)} %get-tuple-element.89.refs_1_, ...), custom_call_target="tpu_custom_call" | custom-call | flops 1073741824 | bytes 16777216 | tf_op jit(solution)/shard_map/pallas_call | solution.py:498
  322.9 3.9 all-to-all-start.4
  326.9 3.7 fusion.42
  330.6 3.0 pad_maximum_fusion.2
  333.6 7.1 %all-to-all-done.4 = bf16[4,512,128]{2,1,0:T(8,128)(2,1)S(1)} async-done(((bf16[4,512,128]{2,1,0:T(8,128)(2,1)}), bf16[4,512,128]{2,1,0:T(8,128)(2,1)S(1)}, u32[]{:S(2)}, u32[]{:S(2)}) %all-to-all-start.4) | async-done | bytes 524320 | tf_op jit(solution)/shard_map/all_to_all | solution.py:683
  340.7 3.5 all-to-all-start.6
  344.2 27.3 %shard_map.252 = bf16[2048,384]{1,0:T(8,128)(2,1)} custom-call(bf16[2048,384]{1,0:T(8,128)(2,1)} %bitcast.15.qkv_ref, bf16[2048,128]{1,0:T(8,128)(2,1)} %bitcast.472, bf16[2048,128]{1,0:T(8,128)(2,1)} %get-tuple-element.80.o_ref, f32[2,2048]{1,0:T(2,128)} %copy-done.21, f32[2048,128]{1,0:T(8,128)} %get-tuple-element.182.cos_ref, ...), custom_call_target="tpu_custom_call" | custom-call | flops 12884901888 | bytes 5242880 | tf_op jit(solution)/shard_map/pallas_call | solution.py:306
  371.5 5.2 all-to-all-start.5
  376.7 27.6 %shard_map.253 = bf16[2048,384]{1,0:T(8,128)(2,1)} custom-call(bf16[2048,384]{1,0:T(8,128)(2,1)} %bitcast.444, bf16[2048,128]{1,0:T(8,128)(2,1)} %bitcast.473, bf16[2048,128]{1,0:T(8,128)(2,1)} %get-tuple-element.82.o_ref, f32[2,2048]{1,0:T(2,128)} %copy-done.20, f32[2048,128]{1,0:T(8,128)} %get-tuple-element.182.cos_ref, f32[2048,128]{1,0:T(8,128)} %get-tuple-element.183.sin_ref), custom_call_target="tpu_custom_call" | custom-call | flops 12884901888 | bytes 5242880 | tf_op jit(solution)/shard_map/pallas_call | solution.py:306
  404.2 8.3 %all-to-all-done.5.refs_1_.refs_0_ = bf16[4,512,384]{2,1,0:T(8,128)(2,1)S(1)} async-done(((bf16[4,512,384]{2,1,0:T(8,128)(2,1)}), bf16[4,512,384]{2,1,0:T(8,128)(2,1)S(1)}, u32[]{:S(2)}, u32[]{:S(2)}) %all-to-all-start.5) | async-done | bytes 1572896 | tf_op jit(solution)/shard_map/all_to_all | solution.py:683
  412.6 1.8 copy-done.11
  415.7 5.1 shard_map.254
  420.9 1.9 dynamic-slice_bitcast_fusion
  424.1 3.8 all-to-all-start.7
  429.4 3.1 fusion
  433.7 32.1 %all-to-all-done.7.refs_1_ = bf16[4,512,384]{2,1,0:T(8,128)(2,1)S(1)} async-done(((bf16[4,512,384]{2,1,0:T(8,128)(2,1)}), bf16[4,512,384]{2,1,0:T(8,128)(2,1)S(1)}, u32[]{:S(2)}, u32[]{:S(2)}) %all-to-all-start.7) | async-done | bytes 1572896 | tf_op jit(solution)/shard_map/all_to_all | solution.py:683
  465.8 2.8 dynamic-slice_bitcast_fusion.4
  468.6 3.4 shard_map.255
  475.2 2.6 fusion.3
  479.4 2.8 fusion.2
  483.1 13.1 %shard_map.256 = (bf16[512,1024]{1,0:T(8,128)(2,1)}, bf16[512,1024]{1,0:T(8,128)(2,1)}, bf16[512,1024]{1,0:T(8,128)(2,1)}, f32[8,1024]{1,0:T(8,128)}) custom-call(bf16[4,512,384]{2,1,0:T(8,128)(2,1)} %copy-done.2, bf16[4,512,384]{2,1,0:T(8,128)(2,1)} %copy-done.5, f32[512,1024]{1,0:T(8,128)} %copy-done.3, f32[512,1024]{1,0:T(8,128)} %get-tuple-element.110.refs_3_, ...), custom_call_target="tpu_custom_call" | custom-call | flops 5368709120 | bytes 24117248 | tf_op jit(solution)/shard_map/pallas_call | solution.py:562
  496.3 2.7 convert_bitcast_fusion
  502.4 2.0 fusion.7
  506.3 5.7 collective-permute-done.11
  513.5 1.8 collective-permute-start.29
  515.5 2.6 collective-permute-start.28
  524.9 6.0 %collective-permute-done.16 = bf16[2,32,2560]{2,1,0:T(8,128)(2,1)S(1)} collective-permute-done((bf16[2,32,2560]{2,1,0:T(8,128)(2,1)S(1)}, bf16[2,32,2560]{2,1,0:T(8,128)(2,1)S(1)}, u32[]{:S(2)}, u32[]{:S(2)}) %collective-permute-start.16) | collective-permute-done | bytes 327712 | tf_op jit(solution)/shard_map/ppermute | solution.py:640
  531.0 2.1 fusion.44
  533.0 1.9 fusion.41
  534.9 2.0 collective-permute-start.26
  536.9 2.5 collective-permute-done.30
  540.8 1.9 fusion.25
  544.3 1.9 fusion.24
  554.2 1.7 fusion.60
  560.5 1.8 fusion.57
  563.3 1.8 fusion.56
  578.4 1.7 collective-permute-start.25
  582.0 2.3 fusion.32
  590.3 3.5 fusion.58
  (243 shorter events, 94.1 us)
Async XLA Ops:
  7.2 109.1 %all-gather.3.cloned.1.call-start = ((), (), s32[]{:S(2)}) async-start(), calls=%async_computation.9 | async-start | bytes 10813440 | tf_op jit(solution)/shard_map/all_gather | solution.py:779
  10.0 259.2 %all-gather.5.cloned.1.call-start = ((), (), s32[]{:S(2)}) async-start(), calls=%async_computation.10 | async-start | bytes 21233664 | tf_op jit(solution)/shard_map/all_gather | solution.py:830
  12.4 1.6 collective-permute-start
  14.2 5.0 collective-permute-start.1
  19.3 3.9 collective-permute-start.2
  23.2 5.5 collective-permute-start.3
  28.8 4.4 collective-permute-start.4
  34.4 41.0 %collective-permute-start.5 = (bf16[1,32,9216]{2,1,0:T(8,128)(2,1)S(1)}, bf16[1,32,9216]{2,1,0:T(8,128)(2,1)S(1)}, u32[]{:S(2)}, u32[]{:S(2)}) collective-permute-start(bf16[1,32,9216]{2,1,0:T(8,128)(2,1)S(1)} %bitcast.469), channel_id=1, source_target_pairs={{0,2},{1,3},{2,0},{3,1},{4,6},{5,7},{6,4},{7,5},{8,10},{9,11},{10,... | collective-permute-start | bytes 1769480 | tf_op jit(solution)/shard_map/ppermute | solution.py:640
  38.4 80.7 %copy-start.30 = (bf16[1,512,1024]{2,1,0:T(8,128)(2,1)S(1)}, bf16[1,512,1024]{2,1,0:T(8,128)(2,1)}, u32[]{:S(2)}) copy-start(bf16[1,512,1024]{2,1,0:T(8,128)(2,1)} %param.15) | copy-start | bytes 3145732
  116.3 28.4 %collective-permute-start.6 = (bf16[2,32,9216]{2,1,0:T(8,128)(2,1)}, bf16[2,32,9216]{2,1,0:T(8,128)(2,1)}, u32[]{:S(2)}, u32[]{:S(2)}) collective-permute-start(bf16[2,32,9216]{2,1,0:T(8,128)(2,1)} %maximum_select_fusion.1), channel_id=1, source_target_pairs={{0,1},{1,0},{2,3},{3,2},{4,5},{5,4},{6,7},{7,6},{8,9},{9,8},{10,11... | collective-permute-start | bytes 3538952 | tf_op jit(solution)/shard_map/ppermute | solution.py:640
  119.3 195.4 %copy-start.18 = (f32[6,1024]{1,0:T(8,128)}, f32[6,1024]{1,0:T(8,128)S(1)}, u32[]{:S(2)}) copy-start(f32[6,1024]{1,0:T(8,128)S(1)} %reshape.657.mod_ref.refs_4_.refs_6_.refs_8_) | copy-start | bytes 73732
  121.8 7.0 %copy-start = (bf16[1024,5120]{1,0:T(8,128)(2,1)S(1)}, bf16[1024,5120]{1,0:T(8,128)(2,1)}, u32[]{:S(2)}) copy-start(bf16[1024,5120]{1,0:T(8,128)(2,1)} %all-gather.3.cloned.1.call-done.packed_ref.wq_ref.wk_ref.wv_ref.refs_4_.refs_5_.refs_6_.refs_7_) | copy-start | bytes 31457284
  189.1 4.6 copy-start.9
  189.1 40.5 %all-to-all-start = ((bf16[4,512,384]{2,1,0:T(8,128)(2,1)}), bf16[4,512,384]{2,1,0:T(8,128)(2,1)}, u32[]{:S(2)}, u32[]{:S(2)}) async-start(bf16[4,512,384]{2,1,0:T(8,128)(2,1)} %shard_map.245), calls=%async_computation | async-start | bytes 3145728 | tf_op jit(solution)/shard_map/all_to_all | solution.py:683
  209.1 41.0 %copy-start.20 = (f32[2,2048]{1,0:T(2,128)}, f32[2,2048]{1,0:T(2,128)S(1)}, u32[]{:S(2)}) copy-start(f32[2,2048]{1,0:T(2,128)S(1)} %get-tuple-element.96.log_ref) | copy-start | bytes 49156
  229.7 21.1 %all-to-all-start.3 = ((bf16[4,512,128]{2,1,0:T(8,128)(2,1)}), bf16[4,512,128]{2,1,0:T(8,128)(2,1)S(1)}, u32[]{:S(2)}, u32[]{:S(2)}) async-start(bf16[4,512,128]{2,1,0:T(8,128)(2,1)} %bitcast.18), calls=%async_computation.3 | async-start | bytes 1048576 | tf_op jit(solution)/shard_map/all_to_all | solution.py:683
  250.7 18.5 %all-to-all-start.1 = ((bf16[4,512,128]{2,1,0:T(8,128)(2,1)}), bf16[4,512,128]{2,1,0:T(8,128)(2,1)S(1)}, u32[]{:S(2)}, u32[]{:S(2)}) async-start(bf16[4,512,128]{2,1,0:T(8,128)(2,1)} %bitcast.16), calls=%async_computation.1 | async-start | bytes 1048576 | tf_op jit(solution)/shard_map/all_to_all | solution.py:683
  255.8 210.0 %reduce-scatter.2.cloned.1.call-start = ((), (), s32[]{:S(2)}) async-start(), calls=%async_computation.11 | async-start | bytes 18874368 | tf_op jit(solution)/shard_map/reduce_scatter | solution.py:855
  322.9 17.8 %all-to-all-start.4 = ((bf16[4,512,128]{2,1,0:T(8,128)(2,1)}), bf16[4,512,128]{2,1,0:T(8,128)(2,1)S(1)}, u32[]{:S(2)}, u32[]{:S(2)}) async-start(bf16[4,512,128]{2,1,0:T(8,128)(2,1)} %get-tuple-element.93), calls=%async_computation.4 | async-start | bytes 1048576 | tf_op jit(solution)/shard_map/all_to_all | solution.py:683
  340.7 3.5 copy-start.34
  340.7 30.7 %all-to-all-start.6 = ((bf16[4,512,128]{2,1,0:T(8,128)(2,1)}), bf16[4,512,128]{2,1,0:T(8,128)(2,1)S(1)}, u32[]{:S(2)}, u32[]{:S(2)}) async-start(bf16[4,512,128]{2,1,0:T(8,128)(2,1)} %get-tuple-element.95), calls=%async_computation.6 | async-start | bytes 1048576 | tf_op jit(solution)/shard_map/all_to_all | solution.py:683
  371.5 5.2 copy-start.35
  371.5 41.1 %all-to-all-start.5 = ((bf16[4,512,384]{2,1,0:T(8,128)(2,1)}), bf16[4,512,384]{2,1,0:T(8,128)(2,1)S(1)}, u32[]{:S(2)}, u32[]{:S(2)}) async-start(bf16[4,512,384]{2,1,0:T(8,128)(2,1)} %bitcast.465), calls=%async_computation.5 | async-start | bytes 3145728 | tf_op jit(solution)/shard_map/all_to_all | solution.py:683
  412.6 8.3 %copy-start.2 = (bf16[4,512,384]{2,1,0:T(8,128)(2,1)}, bf16[4,512,384]{2,1,0:T(8,128)(2,1)S(1)}, u32[]{:S(2)}) copy-start(bf16[4,512,384]{2,1,0:T(8,128)(2,1)S(1)} %all-to-all-done.5.refs_1_.refs_0_) | copy-start | bytes 4718596
  424.1 5.3 collective-permute-start.7
  424.1 41.6 %all-to-all-start.7 = ((bf16[4,512,384]{2,1,0:T(8,128)(2,1)}), bf16[4,512,384]{2,1,0:T(8,128)(2,1)S(1)}, u32[]{:S(2)}, u32[]{:S(2)}) async-start(bf16[4,512,384]{2,1,0:T(8,128)(2,1)} %bitcast.464), calls=%async_computation.7 | async-start | bytes 3145728 | tf_op jit(solution)/shard_map/all_to_all | solution.py:683
  432.5 42.7 %collective-permute-start.9 = (bf16[2,2,2,32,2560]{4,3,2,1,0:T(8,128)(2,1)}, bf16[2,2,2,32,2560]{4,3,2,1,0:T(8,128)(2,1)}, u32[]{:S(2)}, u32[]{:S(2)}) collective-permute-start(bf16[2,2,2,32,2560]{4,3,2,1,0:T(8,128)(2,1)} %fusion), channel_id=1, source_target_pairs={{0,8},{4,12},{8,0},{12,4},{16,24},{20,28},{24,16},{28,20},{1,9},{5... | collective-permute-start | bytes 3932168 | tf_op jit(solution)/shard_map/ppermute | solution.py:640
  465.8 6.3 %copy-start.5 = (bf16[4,512,384]{2,1,0:T(8,128)(2,1)}, bf16[4,512,384]{2,1,0:T(8,128)(2,1)S(1)}, u32[]{:S(2)}) copy-start(bf16[4,512,384]{2,1,0:T(8,128)(2,1)S(1)} %all-to-all-done.7.refs_1_) | copy-start | bytes 4718596
  475.1 4.3 collective-permute-start.8
  475.1 26.0 %collective-permute-start.13 = (bf16[2,32,8192]{2,1,0:T(8,128)(2,1)}, bf16[2,32,8192]{2,1,0:T(8,128)(2,1)S(1)}, u32[]{:S(2)}, u32[]{:S(2)}) collective-permute-start(bf16[2,32,8192]{2,1,0:T(8,128)(2,1)} %dynamic-slice_bitcast_fusion.4), channel_id=1, source_target_pairs={{0,1},{1,0},{2,3},{3,2},{4,5},{5,4},{6,7},{7,6},{8,9},{9,8},{10,11... | collective-permute-start | bytes 3145736 | tf_op jit(solution)/shard_map/ppermute | solution.py:640
  477.8 24.6 %collective-permute-start.12 = (bf16[2,2,32,2560]{3,2,1,0:T(8,128)(2,1)}, bf16[2,2,32,2560]{3,2,1,0:T(8,128)(2,1)}, u32[]{:S(2)}, u32[]{:S(2)}) collective-permute-start(bf16[2,2,32,2560]{3,2,1,0:T(8,128)(2,1)} %fusion.3), channel_id=1, source_target_pairs={{0,16},{4,20},{8,24},{12,28},{16,0},{20,4},{24,8},{28,12},{1,17},{... | collective-permute-start | bytes 1966088 | tf_op jit(solution)/shard_map/ppermute | solution.py:640
  479.4 16.8 %copy-start.28 = (bf16[2,2,2,2,32,1536]{5,4,3,2,1,0:T(8,128)(2,1)}, bf16[2,2,2,2,32,1536]{5,4,3,2,1,0:T(8,128)(2,1)S(1)}, u32[]{:S(2)}) copy-start(bf16[2,2,2,2,32,1536]{5,4,3,2,1,0:T(8,128)(2,1)S(1)} %collective-permute-done.8) | copy-start | bytes 4718596
  482.1 29.9 %collective-permute-start.11 = (bf16[2,2,2,32,1536]{4,3,2,1,0:T(8,128)(2,1)}, bf16[2,2,2,32,1536]{4,3,2,1,0:T(8,128)(2,1)}, u32[]{:S(2)}, u32[]{:S(2)}) collective-permute-start(bf16[2,2,2,32,1536]{4,3,2,1,0:T(8,128)(2,1)} %fusion.2), channel_id=1, source_target_pairs={{0,16},{4,20},{8,24},{12,28},{16,0},{20,4},{24,8},{28,12},{1,17},{... | collective-permute-start | bytes 2359304 | tf_op jit(solution)/shard_map/ppermute | solution.py:640
  483.1 13.2 %copy-start.15 = (bf16[1,512,1024]{2,1,0:T(8,128)(2,1)S(1)}, bf16[1,512,1024]{2,1,0:T(8,128)(2,1)}, u32[]{:S(2)}) copy-start(bf16[1,512,1024]{2,1,0:T(8,128)(2,1)} %param.14) | copy-start | bytes 3145732
  501.1 20.2 %copy-start.22 = (bf16[2048,512]{1,0:T(8,128)(2,1)}, bf16[2048,512]{1,0:T(8,128)(2,1)S(1)}, u32[]{:S(2)}) copy-start(bf16[2048,512]{1,0:T(8,128)(2,1)S(1)} %get-tuple-element.147) | copy-start | bytes 6291460
  501.5 20.7 %collective-permute-start.17 = (bf16[2,2,2,2,64,512]{5,4,3,2,1,0:T(8,128)(2,1)S(1)}, bf16[2,2,2,2,64,512]{5,4,3,2,1,0:T(8,128)(2,1)S(1)}, u32[]{:S(2)}, u32[]{:S(2)}) collective-permute-start(bf16[2,2,2,2,64,512]{5,4,3,2,1,0:T(8,128)(2,1)S(1)} %dynamic-slice_bitcast_fusion.2), channel_id=1, source_target_pairs={{0,4},{4,0},{8,12},{12,8},{16,20},{20,16},{24,28},{28,24},{1,5},{5... | collective-permute-start | bytes 3145736 | tf_op jit(solution)/shard_map/ppermute | solution.py:640
  504.4 15.8 %collective-permute-start.10 = (bf16[2,2,2,2,64,512]{5,4,2,3,1,0:T(8,128)(2,1)S(1)}, bf16[2,2,2,2,64,512]{5,4,2,3,1,0:T(8,128)(2,1)S(1)}, u32[]{:S(2)}, u32[]{:S(2)}) collective-permute-start(bf16[2,2,2,2,64,512]{5,4,2,3,1,0:T(8,128)(2,1)S(1)} %copy.119), channel_id=1, source_target_pairs={{0,4},{4,0},{8,12},{12,8},{16,20},{20,16},{24,28},{28,24},{1,5},{5... | collective-permute-start | bytes 3145736 | tf_op jit(solution)/shard_map/ppermute | solution.py:640
  513.5 4.9 collective-permute-start.29
  515.2 15.7 %collective-permute-start.16 = (bf16[2,32,2560]{2,1,0:T(8,128)(2,1)S(1)}, bf16[2,32,2560]{2,1,0:T(8,128)(2,1)S(1)}, u32[]{:S(2)}, u32[]{:S(2)}) collective-permute-start(bf16[2,32,2560]{2,1,0:T(8,128)(2,1)S(1)} %fusion.12), channel_id=1, source_target_pairs={{0,1},{1,0},{2,3},{3,2},{4,5},{5,4},{6,7},{7,6},{8,9},{9,8},{10,11... | collective-permute-start | bytes 983048 | tf_op jit(solution)/shard_map/ppermute | solution.py:640
  515.5 31.1 %collective-permute-start.28 = (bf16[32,8192]{1,0:T(8,128)(2,1)}, bf16[32,8192]{1,0:T(8,128)(2,1)}, u32[]{:S(2)}, u32[]{:S(2)}) collective-permute-start(bf16[32,8192]{1,0:T(8,128)(2,1)} %fusion.7), channel_id=1, source_target_pairs={{0,2},{1,3},{2,0},{3,1},{4,6},{5,7},{6,4},{7,5},{8,10},{9,11},{10,... | collective-permute-start | bytes 1572872 | tf_op jit(solution)/shard_map/ppermute | solution.py:640
  518.4 14.7 %collective-permute-start.15 = (bf16[2,2,32,1536]{3,2,1,0:T(8,128)(2,1)S(1)}, bf16[2,2,32,1536]{3,2,1,0:T(8,128)(2,1)S(1)}, u32[]{:S(2)}, u32[]{:S(2)}) collective-permute-start(bf16[2,2,32,1536]{3,2,1,0:T(8,128)(2,1)S(1)} %fusion.9), channel_id=1, source_target_pairs={{0,8},{4,12},{8,0},{12,4},{16,24},{20,28},{24,16},{28,20},{1,9},{5... | collective-permute-start | bytes 1179656 | tf_op jit(solution)/shard_map/ppermute | solution.py:640
  520.2 14.7 %copy-start.33 = (bf16[2,2,2,2,64,512]{5,4,2,3,1,0:T(8,128)(2,1)}, bf16[2,2,2,2,64,512]{5,4,2,3,1,0:T(8,128)(2,1)S(1)}, u32[]{:S(2)}) copy-start(bf16[2,2,2,2,64,512]{5,4,2,3,1,0:T(8,128)(2,1)S(1)} %collective-permute-done.10) | copy-start | bytes 3145732
  521.3 19.5 %collective-permute-start.14 = (bf16[2,2,2,64,512]{4,3,2,1,0:T(8,128)(2,1)}, bf16[2,2,2,64,512]{4,3,2,1,0:T(8,128)(2,1)}, u32[]{:S(2)}, u32[]{:S(2)}) collective-permute-start(bf16[2,2,2,64,512]{4,3,2,1,0:T(8,128)(2,1)} %fusion.6), channel_id=1, source_target_pairs={{0,8},{4,12},{8,0},{12,4},{16,24},{20,28},{24,16},{28,20},{1,9},{5... | collective-permute-start | bytes 1572872 | tf_op jit(solution)/shard_map/ppermute | solution.py:640
  523.2 21.1 %collective-permute-start.20 = (bf16[2,2,2,64,512]{4,3,2,1,0:T(8,128)(2,1)S(1)}, bf16[2,2,2,64,512]{4,3,2,1,0:T(8,128)(2,1)S(1)}, u32[]{:S(2)}, u32[]{:S(2)}) collective-permute-start(bf16[2,2,2,64,512]{4,3,2,1,0:T(8,128)(2,1)S(1)} %fusion.5), channel_id=1, source_target_pairs={{0,16},{4,20},{8,24},{12,28},{16,0},{20,4},{24,8},{28,12},{1,17},{... | collective-permute-start | bytes 1572872 | tf_op jit(solution)/shard_map/ppermute | solution.py:640
  534.9 4.5 collective-permute-start.30
  534.9 32.8 %collective-permute-start.26 = (bf16[32,2560]{1,0:T(8,128)(2,1)}, bf16[32,2560]{1,0:T(8,128)(2,1)}, u32[]{:S(2)}, u32[]{:S(2)}) collective-permute-start(bf16[32,2560]{1,0:T(8,128)(2,1)} %fusion.44), channel_id=1, source_target_pairs={{0,2},{1,3},{2,0},{3,1},{4,6},{5,7},{6,4},{7,5},{8,10},{9,11},{10,... | collective-permute-start | bytes 491528 | tf_op jit(solution)/shard_map/ppermute | solution.py:640
  539.4 14.8 %collective-permute-start.19 = (bf16[2,32,1536]{2,1,0:T(8,128)(2,1)}, bf16[2,32,1536]{2,1,0:T(8,128)(2,1)}, u32[]{:S(2)}, u32[]{:S(2)}) collective-permute-start(bf16[2,32,1536]{2,1,0:T(8,128)(2,1)} %fusion.41), channel_id=1, source_target_pairs={{0,1},{1,0},{2,3},{3,2},{4,5},{5,4},{6,7},{7,6},{8,9},{9,8},{10,11... | collective-permute-start | bytes 589832 | tf_op jit(solution)/shard_map/ppermute | solution.py:640
  542.7 5.5 copy-start.25
  542.7 17.7 %collective-permute-start.18 = (bf16[2,2,64,512]{3,2,1,0:T(8,128)(2,1)}, bf16[2,2,64,512]{3,2,1,0:T(8,128)(2,1)}, u32[]{:S(2)}, u32[]{:S(2)}) collective-permute-start(bf16[2,2,64,512]{3,2,1,0:T(8,128)(2,1)} %fusion.25), channel_id=1, source_target_pairs={{0,16},{4,20},{8,24},{12,28},{16,0},{20,4},{24,8},{28,12},{1,17},{... | collective-permute-start | bytes 786440 | tf_op jit(solution)/shard_map/ppermute | solution.py:640
  546.2 17.1 %collective-permute-start.22 = (bf16[2,2,64,512]{3,2,1,0:T(8,128)(2,1)}, bf16[2,2,64,512]{3,2,1,0:T(8,128)(2,1)}, u32[]{:S(2)}, u32[]{:S(2)}) collective-permute-start(bf16[2,2,64,512]{3,2,1,0:T(8,128)(2,1)} %fusion.24), channel_id=1, source_target_pairs={{0,8},{4,12},{8,0},{12,4},{16,24},{20,28},{24,16},{28,20},{1,9},{5... | collective-permute-start | bytes 786440 | tf_op jit(solution)/shard_map/ppermute | solution.py:640
  553.0 4.7 copy-start.39
  553.0 4.7 copy-start.26
  553.0 4.7 copy-start.27
  556.0 18.8 %collective-permute-start.27 = (bf16[32,1536]{1,0:T(8,128)(2,1)}, bf16[32,1536]{1,0:T(8,128)(2,1)}, u32[]{:S(2)}, u32[]{:S(2)}) collective-permute-start(bf16[32,1536]{1,0:T(8,128)(2,1)} %fusion.60), channel_id=1, source_target_pairs={{0,2},{1,3},{2,0},{3,1},{4,6},{5,7},{6,4},{7,5},{8,10},{9,11},{10,... | collective-permute-start | bytes 294920 | tf_op jit(solution)/shard_map/ppermute | solution.py:640
  557.7 2.1 collective-permute-start.31
  558.7 9.0 %copy-start.38 = (bf16[2,32,2560]{2,1,0:T(8,128)(2,1)S(1)}, bf16[2,32,2560]{2,1,0:T(8,128)(2,1)}, u32[]{:S(2)}) copy-start(bf16[2,32,2560]{2,1,0:T(8,128)(2,1)} %copy-done.37) | copy-start | bytes 983044
  559.8 9.5 %copy-start.29 = (f32[3,32,1024]{2,1,0:T(8,128)S(1)}, f32[3,32,1024]{2,1,0:T(8,128)}, u32[]{:S(2)}) copy-start(f32[3,32,1024]{2,1,0:T(8,128)} %param.22) | copy-start | bytes 1179652
  562.3 10.4 %collective-permute-start.21 = (bf16[2,64,512]{2,1,0:T(8,128)(2,1)}, bf16[2,64,512]{2,1,0:T(8,128)(2,1)}, u32[]{:S(2)}, u32[]{:S(2)}) collective-permute-start(bf16[2,64,512]{2,1,0:T(8,128)(2,1)} %fusion.57), channel_id=1, source_target_pairs={{0,1},{1,0},{2,3},{3,2},{4,5},{5,4},{6,7},{7,6},{8,9},{9,8},{10,11... | collective-permute-start | bytes 393224 | tf_op jit(solution)/shard_map/ppermute | solution.py:640
  565.1 8.6 %collective-permute-start.24 = (bf16[2,64,512]{2,1,0:T(8,128)(2,1)}, bf16[2,64,512]{2,1,0:T(8,128)(2,1)}, u32[]{:S(2)}, u32[]{:S(2)}) collective-permute-start(bf16[2,64,512]{2,1,0:T(8,128)(2,1)} %fusion.56), channel_id=1, source_target_pairs={{0,1},{1,0},{2,3},{3,2},{4,5},{5,4},{6,7},{7,6},{8,9},{9,8},{10,11... | collective-permute-start | bytes 393224 | tf_op jit(solution)/shard_map/ppermute | solution.py:640
  566.1 4.9 collective-permute-start.32
  577.1 8.2 %collective-permute-start.23 = (bf16[64,512]{1,0:T(8,128)(2,1)S(1)}, bf16[64,512]{1,0:T(8,128)(2,1)S(1)}, u32[]{:S(2)}, u32[]{:S(2)}) collective-permute-start(bf16[64,512]{1,0:T(8,128)(2,1)S(1)} %fusion.74), channel_id=1, source_target_pairs={{0,2},{1,3},{2,0},{3,1},{4,6},{5,7},{6,4},{7,5},{8,10},{9,11},{10,... | collective-permute-start | bytes 196616 | tf_op jit(solution)/shard_map/ppermute | solution.py:640
  578.4 7.9 %collective-permute-start.25 = (bf16[64,512]{1,0:T(8,128)(2,1)S(1)}, bf16[64,512]{1,0:T(8,128)(2,1)S(1)}, u32[]{:S(2)}, u32[]{:S(2)}) collective-permute-start(bf16[64,512]{1,0:T(8,128)(2,1)S(1)} %fusion.72), channel_id=1, source_target_pairs={{0,2},{1,3},{2,0},{3,1},{4,6},{5,7},{6,4},{7,5},{8,10},{9,11},{10,... | collective-permute-start | bytes 196616 | tf_op jit(solution)/shard_map/ppermute | solution.py:640
  580.1 9.1 %collective-permute-start.33 = (f32[1,4,6144]{2,1,0:T(4,128)}, f32[1,4,6144]{2,1,0:T(4,128)S(1)}, u32[]{:S(2)}, u32[]{:S(2)}) collective-permute-start(f32[1,4,6144]{2,1,0:T(4,128)} %bitcast.159), channel_id=1, source_target_pairs={{0,16},{4,20},{8,24},{12,28},{16,0},{20,4},{24,8},{28,12},{1,17},{... | collective-permute-start | bytes 294920 | tf_op jit(solution)/shard_map/ppermute | solution.py:640
  582.0 5.3 copy-start.24
  (23 other events, 37.9 us)
Sparse Core Ops, SparseCore 0:
  11.4 104.8 all-gather.2
  149.2 97.2 all-gather.4
  314.8 114.1 reduce-scatter.1

commit v3 on v2

v3 whole, which is shorter than its diff:
```python
import functools
import math

import jax
import jax.numpy as jnp
from jax import lax
from jax.experimental import pallas as pl
from jax.experimental.pallas import tpu as pltpu
from jax.sharding import PartitionSpec as P

D = 1024
HEADS = 16
DH = 64
FF = 4096
STEP = 3
LOG2E = 1.4426950408889634
BF = jnp.bfloat16
F32 = jnp.float32
MIB = 2**20
highest = lax.Precision.HIGHEST


def dot_nn(a, b):
    return lax.dot_general(a, b, (((1,), (0,)), ((), ())), preferred_element_type=F32)


def dot_nt(a, b):
    return lax.dot_general(a, b, (((1,), (1,)), ((), ())), preferred_element_type=F32)


def dot_tn(a, b):
    return lax.dot_general(a, b, (((0,), (0,)), ((), ())), preferred_element_type=F32)


def params(mib):
    return pltpu.CompilerParams(vmem_limit_bytes=mib * MIB)


def cost(flops, moved):
    return pl.CostEstimate(flops=int(flops), bytes_accessed=int(moved), transcendentals=0)


def whole(shape):
    return pl.BlockSpec(shape, lambda *_: (0,) * len(shape))


def with_place(grid, in_specs, out_specs, scratch_shapes=()):
    return pltpu.PrefetchScalarGridSpec(
        num_scalar_prefetch=1,
        grid=grid,
        in_specs=in_specs,
        out_specs=out_specs,
        scratch_shapes=scratch_shapes,
    )


def time_features(flow_values, model_width):
    half_size = model_width // 2
    frequency = jnp.exp(-math.log(10000.0) * jnp.arange(half_size, dtype=F32) / half_size)
    angles = 1000.0 * flow_values[:, None] * frequency[None, :]
    return jax.nn.silu(jnp.concatenate([jnp.sin(angles), jnp.cos(angles)], axis=-1))


def rotary_tables(positions, heads):
    half = DH // 2
    frequency = jnp.exp(-math.log(10000.0) * jnp.arange(half, dtype=F32) / half)
    angles = positions.astype(F32)[:, None] * frequency[None, :]
    cosine, sine = jnp.cos(angles), jnp.sin(angles)
    return (
        jnp.concatenate([cosine, cosine] * heads, axis=-1),
        jnp.concatenate([-sine, sine] * heads, axis=-1),
    )


def swap_halves(values):
    width = values.shape[1]
    half = DH // 2
    if width == DH:
        return jnp.concatenate([values[:, half:], values[:, :half]], axis=1)
    lane = lax.broadcasted_iota(jnp.int32, (1, width), 1)
    first = (lane % DH) < half
    return jnp.where(
        first, pltpu.roll(values, width - half, 1), pltpu.roll(values, half, 1)
    )


def normalise(values):
    centre = values - jnp.mean(values, axis=-1, keepdims=True)
    spread = jnp.mean(centre * centre, axis=-1, keepdims=True)
    inverse = lax.rsqrt(spread + 1e-06)
    return centre * inverse, inverse


def norm_back(normal, inverse, scaled):
    return inverse * (
        scaled
        - jnp.mean(scaled, axis=-1, keepdims=True)
        - normal * jnp.mean(scaled * normal, axis=-1, keepdims=True)
    )


def gelu_and_slope(u):
    root = math.sqrt(2.0 / math.pi)
    square = u * u
    t = jnp.tanh(root * u * (1.0 + 0.044715 * square))
    half = 0.5 * (1.0 + t)
    slope = half + 0.5 * u * (1.0 - t * t) * (root * (1.0 + 3.0 * 0.044715 * square))
    return u * half, slope


def learning_rates():
    fans = (2 * D, D, D // 16, D, FF, D // 8)
    return tuple((2.0 * fan_value ** (-0.5) for fan_value in fans))


def adamw_step(state, gradient, rate):
    master, first_moment, second_moment = (state[0], state[1], state[2])
    first_moment = 0.5 * first_moment + 0.5 * gradient
    second_moment = 0.5 * second_moment + 0.5 * gradient * gradient
    correction = 1.0 - 0.5**STEP
    master = master - rate * (
        first_moment / correction / (jnp.sqrt(second_moment / correction) + 1e-08) + 0.01 * master
    )
    return (master, jnp.stack([first_moment, second_moment]))


def stack_rows(packed_ref, out_ref, owned):
    cols = out_ref.shape[1]
    pieces = packed_ref.shape[1] // cols
    for r in range(packed_ref.shape[0] // owned):
        for q in range(pieces):
            at = (r * pieces + q) * owned
            out_ref[at : at + owned] = packed_ref[
                r * owned : (r + 1) * owned, q * cols : (q + 1) * cols
            ]


def skip_kernel(
    owned, fr_ref, sk_ref, cond_ref, packed_ref, mod_ref, hidden_ref, normed_ref, w_ref
):
    @pl.when(pl.program_id(0) == 0)
    def _():
        stack_rows(packed_ref, w_ref, owned)

    width = fr_ref.shape[1]
    hidden = (
        dot_nn(fr_ref[...], w_ref[:width])
        + dot_nn(sk_ref[...], w_ref[width:])
        + cond_ref[...].astype(F32)
    )
    hidden_ref[...] = hidden
    normal, _ = normalise(hidden)
    normed_ref[...] = (normal * (1.0 + mod_ref[1:2]) + mod_ref[0:1]).astype(BF)


def skip_weight(weight, owned, width):
    if owned % 16 == 0:
        return weight, pl.BlockSpec((width, 2 * width), lambda *_: (0, 0)), owned
    full = stacked(weight[:, : 2 * width], owned, width)
    return full, whole(full.shape), 2 * width


def skip_forward(frames, skips, cond, weight, mod, owned):
    rows, width = frames.shape
    block = min(256, rows)
    row_spec = pl.BlockSpec((block, width), lambda i: (i, 0))
    weight, weight_spec, piece = skip_weight(weight, owned, width)
    return pl.pallas_call(
        functools.partial(skip_kernel, piece),
        grid=(rows // block,),
        in_specs=[row_spec, row_spec, row_spec, weight_spec, whole(mod.shape)],
        out_specs=[row_spec, row_spec],
        out_shape=[
            jax.ShapeDtypeStruct((rows, width), F32),
            jax.ShapeDtypeStruct((rows, width), BF),
        ],
        scratch_shapes=[pltpu.VMEM((2 * width, width), BF)],
        compiler_params=params(60),
        cost_estimate=cost(4 * rows * width * width, 12 * rows * width + 4 * width * width),
    )(frames, skips, cond, weight, mod)


def qkv_kernel(stride, me_ref, x_ref, wq_ref, wk_ref, wv_ref, cos_ref, sin_ref, *refs):
    out_refs, w_ref = refs[:-1], refs[-1]
    size = 128 * stride
    for part, ref in enumerate((wq_ref, wk_ref, wv_ref)):
        w_ref[:, part * size : (part + 1) * size] = ref[...]
    packed = dot_nn(x_ref[...], w_ref[...])
    cosine, sine = cos_ref[...], sin_ref[...]
    turned = []
    for at in range(0, 2 * size, 128):
        raw = packed[:, at : at + 128]
        turned.append((raw * cosine + swap_halves(raw) * sine).astype(BF))
    value = packed[:, 2 * size :].astype(BF)
    groups = len(out_refs) // stride
    for d in range(groups):

        @pl.when(pl.program_id(0) == d)
        def _(d=d):
            for c in range(stride):
                out_ref = out_refs[c * groups + d]
                out_ref[:, 0:128] = turned[c]
                out_ref[:, 128:256] = turned[stride + c]
                out_ref[:, 256:384] = value[:, c * 128 : (c + 1) * 128]


def qkv_forward(normed, weight, cosine, sine, stride, me):
    rows, width = normed.shape
    size = 128 * stride
    groups = width // size

    def columns(part):
        return pl.BlockSpec(
            (width, size),
            lambda i, me: (0, (2 + part) * groups + lax.bitwise_xor(i, me[0])),
        )

    outs = pl.pallas_call(
        functools.partial(qkv_kernel, stride),
        grid_spec=with_place(
            (groups,),
            [
                whole(normed.shape),
                columns(0),
                columns(1),
                columns(2),
                whole(cosine.shape),
                whole(sine.shape),
            ],
            [whole((rows, 384))] * (groups * stride),
            [pltpu.VMEM((width, 3 * size), BF)],
        ),
        out_shape=[jax.ShapeDtypeStruct((rows, 384), BF)] * (groups * stride),
        compiler_params=params(60),
        cost_estimate=cost(6 * rows * width * width, 8 * rows * width + 6 * width * width),
    )(me, normed, weight, weight, weight, cosine, sine)
    return [outs[c * groups : (c + 1) * groups] for c in range(stride)]


def attend_kernel(heads, block, count, *refs):
    piece_refs, out_refs = refs[:count], refs[count : 2 * count]
    log_ref, qkv_ref = refs[2 * count :]
    width = heads * DH
    rows = piece_refs[0].shape[0]
    i = pl.program_id(0)

    @pl.when(i == 0)
    def _():
        for d, ref in enumerate(piece_refs):
            qkv_ref[d * rows : (d + 1) * rows] = ref[...]

    q = qkv_ref[pl.ds(pl.multiple_of(i * block, block), block), 0:width]
    k = qkv_ref[:, width : 2 * width]
    v = qkv_ref[:, 2 * width : 3 * width]
    lane = lax.broadcasted_iota(jnp.int32, (1, width), 1) // DH
    outs = []
    for h in range(heads):
        own = jnp.where(lane == h, q, jnp.zeros_like(q)) if heads > 1 else q
        scores = dot_nt(k, own) * (0.125 * LOG2E)
        top = jnp.max(scores, axis=0, keepdims=True)
        probs = jnp.exp2(scores - top)
        total = jnp.sum(probs, axis=0, keepdims=True)
        outs.append(dot_tn(v[:, h * DH : (h + 1) * DH], probs.astype(BF)) * (1.0 / total))
        log_ref[h : h + 1, :] = top + jnp.log2(total)
    out = (jnp.concatenate(outs, axis=0) if heads > 1 else outs[0]).T.astype(BF)
    per = block // rows
    for d, out_ref in enumerate(out_refs):

        @pl.when(i == d // per)
        def _(d=d, out_ref=out_ref):
            out_ref[...] = out[(d % per) * rows : (d % per + 1) * rows]


def attend(pieces, heads):
    count, rows = len(pieces), pieces[0].shape[0]
    length = count * rows
    width = heads * DH
    block = min(512, length)
    outs = pl.pallas_call(
        functools.partial(attend_kernel, heads, block, count),
        grid=(length // block,),
        in_specs=[whole(p.shape) for p in pieces],
        out_specs=[whole((rows, width))] * count
        + [pl.BlockSpec((heads, block), lambda i: (0, i))],
        out_shape=[jax.ShapeDtypeStruct((rows, width), BF)] * count
        + [jax.ShapeDtypeStruct((heads, length), F32)],
        scratch_shapes=[pltpu.VMEM((length, 3 * width), BF)],
        compiler_params=params(60),
        cost_estimate=cost(16 * length * length * DH * heads, 8 * length * width),
    )(*pieces)
    return outs[:count], outs[count]


def attend_back_kernel(heads, block, count, *refs):
    piece_refs, do_refs, o_refs = refs[:count], refs[count : 2 * count], refs[2 * count : 3 * count]
    log_ref, cos_ref, sin_ref = refs[3 * count : 3 * count + 3]
    out_refs = refs[3 * count + 3 : 4 * count + 3]
    qkv_ref, do_ref, dq_sum, delta = refs[4 * count + 3 :]
    width = heads * DH
    rows = piece_refs[0].shape[0]
    i = pl.program_id(0)
    lane = lax.broadcasted_iota(jnp.int32, (1, width), 1) // DH

    @pl.when(i == 0)
    def _():
        dq_sum[...] = jnp.zeros_like(dq_sum)
        for d in range(count):
            at = slice(d * rows, (d + 1) * rows)
            qkv_ref[at] = piece_refs[d][...]
            do_own = do_refs[d][...]
            do_ref[at] = do_own
            product = (do_own.astype(F32) * o_refs[d][...].astype(F32)).T
            for h in range(heads):
                delta[h : h + 1, at] = jnp.sum(
                    product[h * DH : (h + 1) * DH], axis=0, keepdims=True
                )

    here = pl.ds(pl.multiple_of(i * block, block), block)
    q = qkv_ref[:, 0:width]
    k = qkv_ref[here, width : 2 * width]
    v = qkv_ref[here, 2 * width : 3 * width]
    do = do_ref[...]
    k_turned = k.T
    dk = dv = None
    for h in range(heads):
        own = lane == h
        k_own = jnp.where(own, k, jnp.zeros_like(k)) if heads > 1 else k
        v_own = jnp.where(own, v, jnp.zeros_like(v)) if heads > 1 else v
        scores = dot_nt(k_own, q) * (0.125 * LOG2E)
        probs = jnp.exp2(scores - log_ref[h : h + 1, :])
        prob_grad = dot_nt(v_own, do)
        score_grad = (probs * (prob_grad - delta[h : h + 1, :])).astype(BF)
        part = slice(h * DH, (h + 1) * DH)
        dq_sum[part, :] += dot_nn(k_turned[part], score_grad)
        dv_own = dot_nn(probs.astype(BF), do)
        dk_own = dot_nn(score_grad, q)
        dv = dv_own if dv is None else jnp.where(own, dv_own, dv)
        dk = dk_own if dk is None else jnp.where(own, dk_own, dk)
    dk = dk * 0.125
    dk = (dk * cos_ref[here, :] - swap_halves(dk) * sin_ref[here, :]).astype(BF)
    dv = dv.astype(BF)
    per = block // rows
    for d, out_ref in enumerate(out_refs):

        @pl.when(i == d // per)
        def _(d=d, out_ref=out_ref):
            at = slice((d % per) * rows, (d % per + 1) * rows)
            out_ref[:, width : 2 * width] = dk[at]
            out_ref[:, 2 * width : 3 * width] = dv[at]

    @pl.when(i == pl.num_programs(0) - 1)
    def _():
        dq = (dq_sum[...] * 0.125).T
        dq = (dq * cos_ref[...] - swap_halves(dq) * sin_ref[...]).astype(BF)
        for d, out_ref in enumerate(out_refs):
            out_ref[:, 0:width] = dq[d * rows : (d + 1) * rows]


def attend_back(pieces, do, chunk, o, log_total, cosine, sine, heads):
    count, rows = len(pieces), pieces[0].shape[0]
    length = count * rows
    width = heads * DH
    block = min(512, length)
    operands = (*pieces, *do, *o, log_total, cosine, sine)
    return pl.pallas_call(
        functools.partial(attend_back_kernel, heads, block, count),
        grid=(length // block,),
        in_specs=[whole(p.shape) for p in pieces]
        + [pl.BlockSpec((rows, width), lambda i: (0, chunk))] * count
        + [whole(a.shape) for a in operands[2 * count :]],
        out_specs=[whole((rows, 3 * width))] * count,
        out_shape=[jax.ShapeDtypeStruct((rows, 3 * width), BF)] * count,
        scratch_shapes=[
            pltpu.VMEM((length, 3 * width), BF),
            pltpu.VMEM((length, width), BF),
            pltpu.VMEM((width, length), F32),
            pltpu.VMEM((heads, length), F32),
        ],
        compiler_params=params(60),
        cost_estimate=cost(24 * length * length * DH * heads, 20 * length * width),
    )(*operands)


def pieces_at(me_ref, count, groups, width, part=0, parts_width=0):
    for c in range(count):
        for d in range(groups):
            at = (lax.bitwise_xor(me_ref[0], d) * count + c) * width + part * parts_width
            yield c, d, pl.ds(pl.multiple_of(at, 128), width)


def out_kernel(count, groups, me_ref, *refs):
    o_refs = refs[: count * groups]
    w_ref, hidden_ref, mod_ref, attended_ref, branch_ref, middle_ref, normed_ref = refs[
        count * groups :
    ]
    for c, d, columns in pieces_at(me_ref, count, groups, o_refs[0].shape[1]):
        attended_ref[:, columns] = o_refs[c * groups + d][...]
    branch = dot_nn(attended_ref[...], w_ref[...])
    branch_ref[...] = branch
    middle = hidden_ref[...] + mod_ref[2:3] * branch
    middle_ref[...] = middle
    normal, _ = normalise(middle)
    normed_ref[...] = (normal * (1.0 + mod_ref[4:5]) + mod_ref[3:4]).astype(BF)


def out_forward(chunks, weight, hidden, mod, at, me):
    rows, width = hidden.shape
    block = min(256, rows)
    row_spec = pl.BlockSpec((block, width), lambda i, *_: (i, 0))
    count, groups = len(chunks), len(chunks[0])
    o_spec = pl.BlockSpec((block, chunks[0][0].shape[1]), lambda i, *_: (i, 0))
    return pl.pallas_call(
        functools.partial(out_kernel, count, groups),
        grid_spec=with_place(
            (rows // block,),
            [o_spec] * (count * groups)
            + [pl.BlockSpec((width, width), lambda *_: (0, at)), row_spec, whole(mod.shape)],
            [row_spec] * 4,
        ),
        out_shape=[
            jax.ShapeDtypeStruct((rows, width), BF),
            jax.ShapeDtypeStruct((rows, width), F32),
            jax.ShapeDtypeStruct((rows, width), F32),
            jax.ShapeDtypeStruct((rows, width), BF),
        ],
        compiler_params=params(60),
        cost_estimate=cost(2 * rows * width * width, 18 * rows * width + 2 * width * width),
    )(me, *[piece for chunk in chunks for piece in chunk], weight, hidden, mod)


def ffn_kernel(
    owned, x_ref, dc_ref, up_ref, packed_ref, y_ref, dx_ref, activated_ref, up_cot_ref, dn_ref
):
    @pl.when(pl.program_id(0) == 0)
    def _():
        y_ref[...] = jnp.zeros_like(y_ref)
        dx_ref[...] = jnp.zeros_like(dx_ref)

    stack_rows(packed_ref, dn_ref, owned)
    up, dn = up_ref[...], dn_ref[...]
    value, slope = gelu_and_slope(dot_nn(x_ref[...], up))
    activated = value.astype(BF)
    up_cot = (dot_nt(dc_ref[...], dn) * slope).astype(BF)
    activated_ref[...] = activated
    up_cot_ref[...] = up_cot
    y_ref[...] += dot_nn(activated, dn)
    dx_ref[...] += dot_nt(up_cot, up)


def ffn_grad_kernel(
    owned, x_ref, dc_ref, activated_ref, up_cot_ref, grads_ref, x_turned, gu, gd, sems
):
    i, last = pl.program_id(0), pl.num_programs(0) - 1
    slot = lax.rem(i, 2)
    block = up_cot_ref.shape[1]
    part = gd.shape[1]
    pieces = block // part

    def sends(step, at):
        across = pl.ds(pl.multiple_of(step * block, block), block)
        down = pl.ds(pl.multiple_of(step * part, part), part)
        half = grads_ref.shape[1] // 2
        return (
            pltpu.make_async_copy(gu.at[at], grads_ref.at[:, across], sems.at[0, at]),
            pltpu.make_async_copy(gd.at[at], grads_ref.at[down, pl.ds(half, half)], sems.at[1, at]),
        )

    @pl.when(i == 0)
    def _():
        x_turned[...] = x_ref[...].T

    @pl.when(i >= 2)
    def _():
        for copy in sends(i - 2, slot):
            copy.wait()

    dc = dc_ref[...]
    gu[slot] = dot_nn(x_turned[...], up_cot_ref[...]).astype(BF)
    down_grad = dot_tn(activated_ref[...], dc).astype(BF)
    width = dc.shape[1]
    for r in range(part // owned):
        for q in range(pieces):
            at = (r * pieces + q) * owned
            gd[slot, r * owned : (r + 1) * owned, q * width : (q + 1) * width] = down_grad[
                at : at + owned
            ]
    for copy in sends(i, slot):
        copy.start()

    @pl.when(i == last)
    def _():
        for copy in sends(last - 1, 1 - slot) + sends(last, slot):
            copy.wait()


FFN_BLOCK = 512


def ffn(x, dc, weights, owned):
    rows, width = x.shape
    hidden_width = FF
    pieces = hidden_width // width
    block = FFN_BLOCK
    steps = hidden_width // block
    part = block // pieces
    packed, piece = weights, owned
    if owned % 16:
        full = stacked(weights[:, :hidden_width], owned, width)
        packed, piece = side_by_side_blocks(full, part, pieces), part
    across = pl.BlockSpec((rows, block), lambda i: (0, i))
    return pl.pallas_call(
        functools.partial(ffn_kernel, piece),
        grid=(steps,),
        in_specs=[
            whole(x.shape),
            whole(x.shape),
            pl.BlockSpec((width, block), lambda i: (0, steps + i)),
            pl.BlockSpec((part, hidden_width), lambda i: (i, 0)),
        ],
        out_specs=[whole(x.shape), whole(x.shape), across, across],
        out_shape=[
            jax.ShapeDtypeStruct((rows, width), F32),
            jax.ShapeDtypeStruct((rows, width), F32),
            jax.ShapeDtypeStruct((rows, hidden_width), BF),
            jax.ShapeDtypeStruct((rows, hidden_width), BF),
        ],
        scratch_shapes=[pltpu.VMEM((block, width), BF)],
        compiler_params=params(60),
        cost_estimate=cost(8 * rows * width * hidden_width, 8 * width * hidden_width),
    )(x, dc, weights, packed)


def ffn_grad(x, dc, activated, up_cot, owned):
    rows, width = x.shape
    hidden_width = activated.shape[1]
    pieces = hidden_width // width
    block = FFN_BLOCK
    part = block // pieces
    across = pl.BlockSpec((rows, block), lambda i: (0, i))
    grads = pl.pallas_call(
        functools.partial(ffn_grad_kernel, owned if owned % 16 == 0 else part),
        grid=(hidden_width // block,),
        in_specs=[whole(x.shape), whole(x.shape), across, across],
        out_specs=pl.BlockSpec(memory_space=pl.ANY),
        out_shape=jax.ShapeDtypeStruct((width, 2 * hidden_width), BF),
        scratch_shapes=[
            pltpu.VMEM((width, rows), BF),
            pltpu.VMEM((2, width, block), BF),
            pltpu.VMEM((2, part, hidden_width), BF),
            pltpu.SemaphoreType.DMA((2, 2)),
        ],
        compiler_params=params(60),
        cost_estimate=cost(4 * rows * width * hidden_width, 8 * width * hidden_width),
    )(x, dc, activated, up_cot)
    if owned % 16:
        full = stacked(grads[:, hidden_width:], part, width)
        grads = jnp.concatenate(
            [grads[:, :hidden_width], side_by_side_blocks(full, owned, pieces)], axis=1
        )
    return grads


def mid_kernel(groups, me_ref, *refs):
    y_ref, dx_ref, middle_ref, branch_ref, grad_ref, w_ref, mod_ref = refs[:7]
    block_ref, mgrad_ref, bcot_ref, sums_ref = refs[7:11]
    piece_refs, attended_grad = refs[11:-1], refs[-1]

    @pl.when(pl.program_id(0) == 0)
    def _():
        sums_ref[...] = jnp.zeros_like(sums_ref)

    y, middle, w = y_ref[...], middle_ref[...], dx_ref[...]
    grad = grad_ref[...].astype(F32)
    block_ref[...] = (middle + mod_ref[5:6] * y).astype(BF)
    normal, inverse = normalise(middle)
    middle_grad = grad + norm_back(normal, inverse, w * (1.0 + mod_ref[4:5]))
    mgrad_ref[...] = middle_grad
    branch_cot = (middle_grad * mod_ref[2:3]).astype(BF)
    bcot_ref[...] = branch_cot
    sums_ref[0:1] += jnp.sum(middle_grad * branch_ref[...], axis=0, keepdims=True)
    sums_ref[1:2] += jnp.sum(w, axis=0, keepdims=True)
    sums_ref[2:3] += jnp.sum(w * normal, axis=0, keepdims=True)
    sums_ref[3:4] += jnp.sum(grad * y, axis=0, keepdims=True)
    attended_grad[...] = dot_nt(branch_cot, w_ref[...]).astype(BF)
    for _, d, columns in pieces_at(me_ref, 1, groups, piece_refs[0].shape[1]):
        piece_refs[d][...] = attended_grad[:, columns]


def mid_back(y, dx, middle, branch, grad, weight, mod, at, me, groups):
    rows, width = y.shape
    block = min(256, rows)
    cols = width // groups
    row_spec = pl.BlockSpec((block, width), lambda i, *_: (i, 0))
    piece_spec = pl.BlockSpec((block, cols), lambda i, *_: (i, 0))
    return pl.pallas_call(
        functools.partial(mid_kernel, groups),
        grid_spec=with_place(
            (rows // block,),
            [row_spec] * 5 + [pl.BlockSpec((width, width), lambda *_: (0, at)), whole(mod.shape)],
            [row_spec] * 3 + [whole((8, width))] + [piece_spec] * groups,
            [pltpu.VMEM((block, width), BF)],
        ),
        out_shape=[
            jax.ShapeDtypeStruct((rows, width), BF),
            jax.ShapeDtypeStruct((rows, width), F32),
            jax.ShapeDtypeStruct((rows, width), BF),
            jax.ShapeDtypeStruct((8, width), F32),
        ]
        + [jax.ShapeDtypeStruct((rows, cols), BF)] * groups,
        compiler_params=params(60),
        cost_estimate=cost(2 * rows * width * width, 28 * rows * width + 2 * width * width),
    )(me, y, dx, middle, branch, grad, weight, mod)


def last_kernel(count, groups, owned, me_ref, *refs):
    piece_refs = refs[: count * groups]
    rest = refs[count * groups :]
    hidden_ref, mgrad_ref, wq_ref, wk_ref, wv_ref, packed_ref, mod_ref = rest[:7]
    hgrad_ref, frames_ref, skips_ref, sums_ref, wskip_ref, cot_ref = rest[7:]

    @pl.when(pl.program_id(0) == 0)
    def _():
        sums_ref[...] = jnp.zeros_like(sums_ref)
        stack_rows(packed_ref, wskip_ref, owned)

    width = piece_refs[0].shape[1] // 3
    model = hidden_ref.shape[1]
    for part in range(3):
        for c, d, columns in pieces_at(me_ref, count, groups, width, part, model):
            cot_ref[:, columns] = piece_refs[c * groups + d][
                :, part * width : (part + 1) * width
            ]
    w = (
        dot_nt(cot_ref[:, :model], wq_ref[...])
        + dot_nt(cot_ref[:, model : 2 * model], wk_ref[...])
        + dot_nt(cot_ref[:, 2 * model :], wv_ref[...])
    )
    normal, inverse = normalise(hidden_ref[...])
    sums_ref[0:1] += jnp.sum(w, axis=0, keepdims=True)
    sums_ref[1:2] += jnp.sum(w * normal, axis=0, keepdims=True)
    hidden_grad = (
        mgrad_ref[...] + norm_back(normal, inverse, w * (1.0 + mod_ref[1:2]))
    ).astype(BF)
    hgrad_ref[...] = hidden_grad
    frames_ref[...] = dot_nt(hidden_grad, wskip_ref[:model]).astype(BF)
    skips_ref[...] = dot_nt(hidden_grad, wskip_ref[model:]).astype(BF)


def last_back(chunks, hidden, middle_grad, weights, mod, owned, me):
    rows, width = hidden.shape
    block = min(256, rows)
    row_spec = pl.BlockSpec((block, width), lambda i, *_: (i, 0))
    count, groups = len(chunks), len(chunks[0])
    piece_spec = pl.BlockSpec((block, chunks[0][0].shape[1]), lambda i, *_: (i, 0))
    w_skip, skip_spec, piece = skip_weight(weights, owned, width)

    def part_spec(part):
        return pl.BlockSpec((width, width), lambda *_: (0, 2 + part))

    return pl.pallas_call(
        functools.partial(last_kernel, count, groups, piece),
        grid_spec=with_place(
            (rows // block,),
            [piece_spec] * (count * groups)
            + [row_spec, row_spec, part_spec(0), part_spec(1), part_spec(2)]
            + [skip_spec, whole(mod.shape)],
            [row_spec, row_spec, row_spec, whole((8, width))],
            [pltpu.VMEM((2 * width, width), BF), pltpu.VMEM((block, 3 * width), BF)],
        ),
        out_shape=[
            jax.ShapeDtypeStruct((rows, width), BF),
            jax.ShapeDtypeStruct((rows, width), BF),
            jax.ShapeDtypeStruct((rows, width), BF),
            jax.ShapeDtypeStruct((8, width), F32),
        ],
        compiler_params=params(60),
        cost_estimate=cost(2 * rows * width * width, 4 * rows * width),
    )(
        me,
        *[piece for chunk in chunks for piece in chunk],
        hidden,
        middle_grad,
        weights,
        weights,
        weights,
        w_skip,
        mod,
    )


def out_wgrad_kernel(left_ref, right_ref, out_ref):
    out_ref[...] = dot_tn(left_ref[...], right_ref[...]).astype(BF)


def out_wgrad_part(left, right, columns):
    rows, width = left.shape
    block = 512
    first = columns // block - width // block
    return pl.pallas_call(
        out_wgrad_kernel,
        grid=(width // block,),
        in_specs=[whole(left.shape), pl.BlockSpec((rows, block), lambda i: (0, i))],
        out_specs=pl.BlockSpec((width, block), lambda i: (0, first + i)),
        out_shape=jax.ShapeDtypeStruct((width, columns), BF),
        compiler_params=params(60),
        cost_estimate=cost(2 * rows * width * width, 6 * width * width),
    )(left, right)


def qkv_grad_kernel(groups, me_ref, *refs):
    x_ref, piece_refs = refs[0], refs[1 : 1 + groups]
    out_ref, piece, x_turned = refs[-3:]
    i = pl.program_id(0)

    @pl.when(i == 0)
    def _():
        x_turned[...] = x_ref[...].T

    for d, ref in enumerate(piece_refs):

        @pl.when(i == d)
        def _(ref=ref):
            piece[...] = ref[...]

    out_ref[...] = dot_nn(x_turned[...], piece[...]).astype(BF)


def qkv_grad(normed, pieces, me, held=None):
    groups = len(pieces)
    rows, cols = pieces[0].shape
    width = normed.shape[1]
    given = [] if held is None else [held]
    return pl.pallas_call(
        functools.partial(qkv_grad_kernel, groups),
        grid_spec=with_place(
            (groups,),
            [whole(normed.shape)]
            + [whole((rows, cols))] * groups
            + [pl.BlockSpec(memory_space=pl.ANY)] * len(given),
            pl.BlockSpec((width, cols), lambda i, me: (0, lax.bitwise_xor(i, me[0]))),
            [pltpu.VMEM((rows, cols), BF), pltpu.VMEM((width, rows), BF)],
        ),
        out_shape=jax.ShapeDtypeStruct((width, groups * cols) if held is None else held.shape, BF),
        input_output_aliases={2 + groups: 0} if given else {},
        compiler_params=params(60),
        cost_estimate=cost(rows * width, 1024),
    )(me, normed, *pieces, *given)


def update_kernel(grads_of, rates, *refs):
    count = len(rates)
    outs, states, given = refs[-2 * count :], refs[-3 * count : -2 * count], refs[: -3 * count]
    correction = 1.0 - 0.5**STEP
    for at, rows, cols, gradient in grads_of(*given):
        state, new_ref, moments_ref = states[at], outs[2 * at], outs[2 * at + 1]
        master = state[0, rows, cols]
        first = 0.5 * state[1, rows, cols] + 0.5 * gradient
        second = 0.5 * state[2, rows, cols] + 0.5 * gradient * gradient
        moments_ref[0, rows, cols] = first
        moments_ref[1, rows, cols] = second
        new_ref[rows, cols] = master - rates[at] * (
            first / correction / (jnp.sqrt(second / correction) + 1e-08) + 0.01 * master
        )


def update(grads_of, given, states, rates):
    shapes = []
    for state in states:
        _, rows, cols = state.shape
        shapes += [(rows, cols), (2, rows, cols)]
    moved = 6 * sum(state.size for state in states) * 4 // 3
    return pl.pallas_call(
        functools.partial(update_kernel, grads_of, rates),
        grid=(1,),
        in_specs=[whole(a.shape) for a in (*given, *states)],
        out_specs=[whole(shape) for shape in shapes],
        out_shape=[jax.ShapeDtypeStruct(shape, F32) for shape in shapes],
        compiler_params=params(60),
        cost_estimate=cost(moved, moved),
    )(*given, *states)


def skip_grads(*refs):
    half = refs[0].shape[1]
    for side in range(2):
        rest, arrived = refs[2 * side][...], refs[2 * side + 1][...]
        yield 0, slice(None), slice(side * half, (side + 1) * half), rest + arrived.astype(F32)


def ffn_grads(rest_ref, arrived_ref):
    owned, cols = rest_ref.shape
    hidden_width, width = cols // 2, D
    for q in range(cols // width):
        at = slice(q * width, (q + 1) * width)
        gradient = rest_ref[:, at] + arrived_ref[:, at].astype(F32)
        if q * width < hidden_width:
            yield 0, slice(None), at, gradient
        else:
            r = q - hidden_width // width
            yield 1, slice(r * owned, (r + 1) * owned), slice(None), gradient


def attention_columns(count, groups):
    cols = D // (count * groups)
    for c in range(count):
        for j in range(groups):
            for part in range(3):
                yield 0, part * D + (j * count + c) * cols, cols
        if c == 0:
            yield 1, 0, D


def attention_grads(count, groups, rest_ref, arrived_ref):
    at = 0
    for weight, to, cols in attention_columns(count, groups):
        here = slice(at, at + cols)
        gradient = rest_ref[:, here] + arrived_ref[:, here].astype(F32)
        yield weight, slice(None), slice(to, to + cols), gradient
        at += cols


def modulation_grads(time_ref, cots_ref):
    for at in range(0, cots_ref.shape[1], D):
        gradient = lax.dot_general(
            time_ref[...],
            cots_ref[:, at : at + D],
            (((0,), (0,)), ((), ())),
            precision=highest,
            preferred_element_type=F32,
        )
        yield 0, slice(None), slice(at, at + D), gradient


def bits_of(axis):
    size = lax.axis_size(axis)
    return [(axis, b) for b in reversed(range(size.bit_length() - 1))]


def my_bit(level):
    axis, bit = level
    return (lax.axis_index(axis) >> bit) & 1


def swap(values, level):
    axis, bit = level
    return lax.ppermute(values, axis, [(i, i ^ (1 << bit)) for i in range(lax.axis_size(axis))])


def after(values, *others):
    return lax.optimization_barrier((values, *others))[0]


class ModulationCots:
    def __init__(self, own):
        self.own, self.order = own, bits_of("seq")[::-1] + bits_of("dp")[::-1]
        self.arrived = None

    def settle(self, *waits):
        if self.arrived is None:
            return
        level, other = self.arrived
        other = after(other, *waits) if waits else other
        if level[0] == "seq":
            self.own = self.own + other
        else:
            self.own = jnp.where(
                my_bit(level) == 0,
                jnp.concatenate([self.own, other], axis=0),
                jnp.concatenate([other, self.own], axis=0),
            )
        self.arrived = None

    def step(self, *waits):
        self.settle(*waits)
        level = self.order.pop(0)
        self.arrived = (level, swap(self.own, level))


class ScatterSum:
    def __init__(self, grad, order, dims):
        self.dims, self.order = list(dims), list(order)
        rows, cols = grad.shape
        split = [2] * len(self.dims)
        self.terms = [grad.reshape(split + [rows // 2 ** len(split), cols])]

    def hold(self, *waits):
        if waits:
            self.terms[-1] = after(self.terms[-1], *waits)

    def step(self, *waits, late=()):
        self.hold(*waits)
        level = self.order.pop(0)
        at, mine = self.dims.index(level), my_bit(level)
        self.dims.pop(at)

        def halves(side):
            return [lax.dynamic_index_in_dim(t, side, at, keepdims=False) for t in self.terms]

        leaving = halves(1 - mine)
        total = leaving[0]
        if len(leaving) > 1:
            total = sum(t.astype(F32) for t in leaving).astype(total.dtype)
        total = after(total, *late) if late else total
        self.sent = total
        arrived = swap(total, level)
        self.terms = halves(mine) + [arrived]
        return arrived

    def ends(self):
        return [sum(t.astype(F32) for t in self.terms[:-1]), self.terms[-1]]


def exchange(pieces):
    places = range(len(pieces))
    return [pieces[0]] + [
        lax.ppermute(pieces[d], "seq", [(i, i ^ d) for i in places]) for d in places[1:]
    ]


def dot_tn_exact(left, right):
    return lax.dot_general(
        left,
        right,
        (((0,), (0,)), ((), ())),
        precision=highest,
        preferred_element_type=F32,
    )


def attention_total(total, count, groups):
    runs, at = ([], []), 0
    for weight, to, cols in attention_columns(count, groups):
        runs[weight].append((to, total[:, at : at + cols]))
        at += cols
    return [jnp.concatenate([v for _, v in sorted(r, key=lambda v: v[0])], axis=1) for r in runs]


def in_order(pieces, me, parts):
    groups, rows = len(pieces), pieces[0].shape[0]
    stack = jnp.take(jnp.stack(pieces), jnp.arange(groups) ^ me[0], axis=0)
    return stack.reshape(groups, rows, parts, -1).transpose(1, 2, 0, 3).reshape(rows, -1)


def by_place(values, me, groups):
    parts = jnp.split(values, groups, axis=1)
    stack = jnp.take(jnp.stack(parts), jnp.arange(groups) ^ me[0], axis=0)
    return [stack[d] for d in range(groups)]


def modulation_rows(partial, order, wait):
    dims = bits_of("dp")
    count, cols = partial.shape
    held = partial.reshape([2] * len(dims) + [count // 2 ** len(dims), cols])
    for level in order:
        at, mine = dims.index(level), my_bit(level)
        dims.pop(at)
        leaving = lax.dynamic_index_in_dim(held, 1 - mine, at, keepdims=False)
        held = lax.dynamic_index_in_dim(held, mine, at, keepdims=False) + swap(leaving, level)
    held = after(held, wait)
    for level in bits_of("seq"):
        held = held + swap(held, level)
    return held


def side_by_side(own, rows):
    return jnp.concatenate(jnp.split(own, own.shape[0] // rows, axis=0), axis=1)


def stacked(full, rows, cols):
    pieces = full.shape[1] // cols
    blocks = full.reshape(full.shape[0] // rows, rows, pieces, cols)
    return blocks.transpose(0, 2, 1, 3).reshape(full.shape[0] * pieces, cols)


def side_by_side_blocks(full, rows, pieces):
    cols = full.shape[1]
    blocks = full.reshape(full.shape[0] // (rows * pieces), pieces, rows, cols)
    return blocks.transpose(0, 2, 1, 3).reshape(full.shape[0] // pieces, pieces * cols)


def gather_pairwise(own, order, last_waits=(), last_use=()):
    rows, cols = own.shape
    held, bits = own.reshape(1, rows, cols), []
    for level in order:
        last = len(bits) == len(order) - 1
        if last and last_waits:
            held = after(held, *last_waits)
        other = swap(held, level)
        if last and last_use:
            other = after(other, *last_use)
        at = sum(1 for bit in bits if bit > level[1])
        bits.append(level[1])
        shape = [2] * (len(bits) - 1)
        own_part = held.reshape(shape + [rows, cols])
        other_part = other.reshape(shape + [rows, cols])
        held = jnp.where(
            my_bit(level) == 0,
            jnp.stack([own_part, other_part], axis=at),
            jnp.stack([other_part, own_part], axis=at),
        ).reshape(2 ** len(bits), rows, cols)
    return held.reshape(-1, cols)


def per_device(
    frames_in,
    skip_in,
    condition,
    flow_time,
    span_start,
    span_length,
    out_grad,
    skip_proj_state,
    attn_qkv_state,
    attn_out_state,
    ffn_up_state,
    ffn_down_state,
    ada_mod_state,
):
    utter_count, rows, width = frames_in.shape
    seq = lax.axis_size("seq")
    everyone = ("dp", "seq")
    owned = attn_qkv_state.shape[1]
    hidden_width = ffn_up_state.shape[2]
    length = rows * seq
    me = lax.axis_index(everyone)
    positions = lax.axis_index("seq") * rows + jnp.arange(rows, dtype=jnp.int32)

    group_heads = HEADS // seq
    heads = min(2, group_heads)
    count = group_heads // heads

    first_own = jnp.concatenate(
        [side_by_side(skip_proj_state[0].astype(BF), owned), attn_qkv_state[0].astype(BF)],
        axis=1,
    )
    first_part = gather_pairwise(first_own, bits_of("seq"))
    first_full = lax.all_gather(first_part, "dp", axis=0, tiled=True)
    out_at = 2 * hidden_width // width

    dp_bits, seq_bits = bits_of("dp"), bits_of("seq")
    core, planes = dp_bits[-1], dp_bits[:-1]

    time_code = time_features(flow_time, width).astype(BF)
    time_own = lax.dynamic_slice_in_dim(time_code, me * owned, owned, 1)
    mod_part = jnp.dot(time_own, ada_mod_state[0].astype(BF), preferred_element_type=F32)
    modulation = modulation_rows(mod_part, [core] + planes, first_part)

    place = lax.axis_index("seq").astype(jnp.int32).reshape(1)
    frame = jnp.arange(length, dtype=jnp.int32)
    frame = ((frame // rows) ^ place) * rows + frame % rows
    cos_all, sin_all = rotary_tables(frame, heads)
    wide = heads == 2
    cos_own, sin_own = rotary_tables(positions, 2)
    span_stop = span_start + span_length

    outs = []
    assert utter_count == 1
    mod = modulation.reshape(6, width)
    inside = (positions >= span_start[0]) & (positions < span_stop[0])
    frames, skips = frames_in[0], skip_in[0]
    cond = jnp.where(inside[:, None], jnp.zeros_like(condition[0]), condition[0])
    grad = jnp.where(inside[:, None], out_grad[0], jnp.zeros_like(out_grad[0]))
    down_cot = (grad.astype(F32) * mod[5:6]).astype(BF)

    hidden, normed = skip_forward(frames, skips, cond, first_full, mod, owned)
    if wide:
        packed = qkv_forward(normed, first_full, cos_own, sin_own, count, place)
    else:
        (pairs,) = qkv_forward(normed, first_full, cos_own, sin_own, 1, 0 * place)
        split = jnp.concatenate(
            [p.reshape(rows, 3, 2, DH).transpose(0, 2, 1, 3).reshape(rows, -1) for p in pairs],
            axis=1,
        )
        packed = [by_place(split, place, seq)]
    arrived = [exchange(part) for part in packed]
    second_own = jnp.concatenate(
        [
            side_by_side(ffn_down_state[0].astype(BF), owned),
            ffn_up_state[0].astype(BF),
            attn_out_state[0].astype(BF),
        ],
        axis=1,
    )
    early = (cos_all, sin_all, cos_own, sin_own, cond, grad, down_cot)
    second_own = gather_pairwise(after(second_own, modulation), seq_bits, early, (normed,))
    second_full = lax.all_gather(second_own, "dp", axis=0, tiled=True)
    qkv_chunks, attended = [], []
    for pieces in arrived:
        waits = attended[-1][0][:1] if attended else [second_own]
        pieces[1:] = [after(piece, *waits) for piece in pieces[1:]]
        qkv_chunks.append(pieces)
        attended.append(attend(pieces, heads))
    o_chunks = []
    for c, (o, _) in enumerate(attended):
        pieces = exchange(o)
        if c < count - 1:
            pieces[1:] = [after(piece, attended[c + 1][0][0]) for piece in pieces[1:]]
        o_chunks.append(pieces)
    here = place
    if not wide:
        o_chunks, here = [[in_order(o_chunks[0], place, 1)]], 0 * place

    attended_low, branch, middle, normed_two = out_forward(
        o_chunks, second_full, hidden, mod, out_at, here
    )
    downward, normed_two_grad, *ffn_kept = ffn(normed_two, down_cot, second_full, owned)
    mid = mid_back(
        downward,
        normed_two_grad,
        middle,
        branch,
        grad,
        second_full,
        mod,
        out_at,
        here,
        seq if wide else 1,
    )
    do_pieces = exchange(mid[4:] if wide else by_place(mid[4], place, seq))
    block_out, middle_grad, branch_cot, mid_sums = mid[:4]
    every_bit = dp_bits + seq_bits
    rising = seq_bits[::-1]
    columns = 3 * width // count + width
    qkv_part = out_wgrad_part(attended_low, branch_cot, columns) if wide else mid[4]
    ffn_whole = ffn_grad(after(normed_two, qkv_part), down_cot, *ffn_kept, owned)
    ffn_whole = after(ffn_whole, *do_pieces[1:])
    ffn_part = lax.psum_scatter(ffn_whole, "dp", scatter_dimension=0, tiled=True)
    do_pieces[1:] = [after(piece, ffn_whole) for piece in do_pieces[1:]]
    backs = []
    for c in range(count):
        o, log_total = attended[c]
        backs.append(
            attend_back(qkv_chunks[c], do_pieces, c, o, log_total, cos_all, sin_all, heads)
        )
    cot_chunks = [exchange(b) for b in backs]

    sent = [backs[-1][0]]

    def leave(part):
        part.step(sent[-1])
        sent.append(part.sent)

    def wait_in_turn(pieces):
        return pieces[:1] + [after(piece, sent[-1]) for piece in pieces[1:]]

    def full_sum(grad_part, planes_first):
        return ScatterSum(grad_part, [core] + planes_first, every_bit)

    qkv_sums = []
    for c in range(count):
        pieces = cot_chunks[c] = wait_in_turn(cot_chunks[c])
        if not wide:
            cot_chunks = [[in_order(pieces, place, 3)]]
            qkv_part = jnp.concatenate(
                [dot_tn(normed, cot_chunks[0][0]), dot_tn(attended_low, branch_cot)], axis=1
            ).astype(BF)
        else:
            qkv_part = qkv_grad(normed, pieces, place, None if c else qkv_part)
        qkv_sums.append(full_sum(qkv_part, planes[::-1]))
        leave(qkv_sums[-1])
        if c < count - 1:
            leave(qkv_sums[-1])
    ffn_sum = ScatterSum(ffn_part, rising, seq_bits)
    ffn_sum.step(late=(cot_chunks[-1][-1],))
    sent.append(ffn_sum.sent)
    for part in qkv_sums:
        leave(part)
    cot_chunks[-1] = [after(piece, sent[-1]) for piece in cot_chunks[-1]]
    hidden_grad, frames_grad, skip_grad, last_sums = last_back(
        cot_chunks, hidden, middle_grad, first_full, mod, owned, here
    )
    skip_cot = after(hidden_grad, *[part.terms[-1] for part in qkv_sums])
    skip_part = jnp.concatenate(
        [dot_tn(frames, skip_cot).astype(BF), dot_tn(skips, skip_cot).astype(BF)], axis=0
    )
    skip_part = after(skip_part, ffn_sum.terms[-1])
    half = width // 2
    skip_sums = [
        ScatterSum(skip_part[:, :half], [core] + planes[::-1] + rising, every_bit),
        ScatterSum(skip_part[:, half:], [core] + planes + rising, every_bit),
    ]
    mod_cot = jnp.concatenate(
        [last_sums[0], last_sums[1], mid_sums[0], mid_sums[1], mid_sums[2], mid_sums[3]]
    ).reshape(1, 6 * width)
    mod_cots = ModulationCots(mod_cot)
    time_rows = time_own.astype(F32)
    qkv_sum, marks = None, []
    rows_held = owned * seq
    for part in [ffn_sum] + qkv_sums:
        part.hold(hidden_grad)
    mod_cots.step()
    while skip_sums[0].order or qkv_sum is None or qkv_sum.order:
        for part in skip_sums:
            if part.order:
                leave(part)
        marks.append(sent[-1])
        if mod_cots.order:
            mod_cots.step(sent[-1])
        later = [part for part in qkv_sums if part.order]
        for part in later + ([ffn_sum] if ffn_sum.order else []):
            leave(part)
        if qkv_sum is not None and qkv_sum.order and len(marks) > 3:
            leave(qkv_sum)
        if not later and qkv_sum is None:
            for part in qkv_sums:
                part.hold(sent[-1])
            qkv_done = [sum(p.ends()).astype(BF).reshape(rows_held, -1) for p in qkv_sums]
            qkv_sum = ScatterSum(jnp.concatenate(qkv_done, axis=1), rising, seq_bits)
            leave(qkv_sum)
    while ffn_sum.order:
        leave(ffn_sum)
    while mod_cots.order:
        mod_cots.step()
    mod_cots.settle(marks[-1])
    mod_cots = mod_cots.own
    ffn_sum.hold(marks[-3])

    rates = learning_rates()
    outs = [block_out[None], frames_grad[None], skip_grad[None]]
    if owned % 16:
        ffn_total, qkv_total = sum(ffn_sum.ends()), sum(qkv_sum.ends())
        skip_total = jnp.concatenate([sum(part.ends()) for part in skip_sums], axis=1)
        mod_total = dot_tn_exact(time_rows, mod_cots)
        qkv_total, out_total = attention_total(
            qkv_total, count if wide else 1, seq if wide else 1
        )
        grads = (
            skip_total.reshape(2 * owned, width),
            qkv_total,
            out_total,
            ffn_total[:, :hidden_width],
            stacked(ffn_total[:, hidden_width:], owned, width),
            mod_total,
        )
        states = (
            skip_proj_state,
            attn_qkv_state,
            attn_out_state,
            ffn_up_state,
            ffn_down_state,
            ada_mod_state,
        )
        for state, gradient, rate in zip(states, grads, rates):
            outs.extend(adamw_step(state, gradient, rate))
        return tuple(outs)
    ffn_new = update(ffn_grads, ffn_sum.ends(), [ffn_up_state, ffn_down_state], rates[3:5])
    qkv_new = update(
        functools.partial(attention_grads, count if wide else 1, seq if wide else 1),
        qkv_sum.ends(),
        [attn_qkv_state, attn_out_state],
        rates[1:3],
    )
    mod_new = update(
        modulation_grads, [time_rows, after(mod_cots, marks[-1])], [ada_mod_state], rates[5:6]
    )
    skip_new = update(
        skip_grads,
        skip_sums[0].ends() + skip_sums[1].ends(),
        [skip_proj_state],
        rates[:1],
    )
    outs += [*skip_new, *qkv_new, *ffn_new, *mod_new]
    return tuple(outs)


def solution(mesh):
    tokens = P("dp", "seq", None)
    state = P(None, ("dp", "seq"), None)
    master = P(("dp", "seq"), None)
    return jax.shard_map(
        per_device,
        mesh=mesh,
        in_specs=(tokens, tokens, tokens, P(), P("dp"), P("dp"), tokens) + (state,) * 6,
        out_specs=(tokens,) * 3 + (master, state) * 6,
        check_vma=False,
    )
```

time: 612 us -> 569 us (0.930)
  blocking collectives: 40 us -> 0 us
  Pallas kernels: 171 us -> 205 us
  other arithmetic: 74.1 us -> 41.1 us
  starting transfers between devices: 69.5 us -> 88 us
  local copies, waits for them, and re-layouts: 37.2 us -> 23.1 us
    all_to_all x7 -> x0, waiting for transfers between devices: 78.9 us -> none  [exchange(): return lax.all_to_all(values, axis, 0, 0, tiled=True)]
    ppermute x0 -> x21, waiting for transfers between devices: none -> 63.6 us  [exchange(): lax.ppermute(pieces[d], 'seq', [(i, i ^ d) for i in places])]
    ppermute x0 -> x21, starting transfers between devices: none -> 45.9 us  [exchange(): lax.ppermute(pieces[d], 'seq', [(i, i ^ d) for i in places])]
    pallas_call x11 -> x16, Pallas kernels: 130 us -> 173 us  [the longest x2 55.4 us: attend_back(): pl.pallas_call(functools.partial(attend_back_kernel, heads, block, count)...]
    all_to_all x1 -> x0, blocking collectives: 40 us -> none  [exchange(): return lax.all_to_all(values, axis, 0, 0, tiled=True)]
    all_gather x1, waiting for transfers between devices: 39.7 us -> 6.94 us  [per_device(): first_full = lax.all_gather(first_part, 'dp', axis=0, tiled=True)]
    all_to_all x7 -> x0, starting transfers between devices: 29.7 us -> none  [exchange(): return lax.all_to_all(values, axis, 0, 0, tiled=True)]
    ppermute x34, waiting for transfers between devices: 65.9 us -> 92.7 us  [swap(): lax.ppermute(values, axis, [(i, i ^ 1 << bit) for i in range(lax.axis_siz...]
  transfers between devices with their start and end apart: 44 -> 58, of which waited for: 17 -> 25; matrix products, arithmetic and copies ran while one was open for 14% -> 10% of each run, Pallas kernels for 22% -> 28%
where the time goes in v3:
time: 569 us; the launch traced here: 559 us
  Pallas kernels  205 us (36%)
  waiting for transfers between devices  181 us (32%)
  starting transfers between devices  88 us (15%)
  other arithmetic  41.1 us (7%)
  local copies, waits for them, and re-layouts  23.1 us (4%)
  between operations  16.3 us (3%)
    ppermute x34, waiting for transfers between devices, swap(): lax.ppermute(values, axis, [(i, i ^ 1 << bit) for i in range(lax.axis_siz...  92.7 us
    ppermute x21, waiting for transfers between devices, exchange(): lax.ppermute(pieces[d], 'seq', [(i, i ^ d) for i in places])  63.6 us
    pallas_call x2, Pallas kernels, attend_back(): pl.pallas_call(functools.partial(attend_back_kernel, heads, block, count)...  55.4 us
    ppermute x21, starting transfers between devices, exchange(): lax.ppermute(pieces[d], 'seq', [(i, i ^ d) for i in places])  45.9 us
    ppermute x34, starting transfers between devices, swap(): lax.ppermute(values, axis, [(i, i ^ 1 << bit) for i in range(lax.axis_siz...  41.7 us
    pallas_call x2, Pallas kernels, attend(): pl.pallas_call(functools.partial(attend_kernel, heads, block, count), gri...  34.6 us
    pallas_call x1, Pallas kernels, ffn(): pl.pallas_call(functools.partial(ffn_kernel, piece), grid=(steps,), in_sp...  24.9 us
    reduce_scatter x1, waiting for transfers between devices, per_device(): lax.psum_scatter(ffn_whole, 'dp', scatter_dimension=0, tiled=True)  17.7 us
  transfers between devices with their start and end apart: 58, of which 25 were waited for; matrix products, arithmetic and copies ran while one was open for 10% of the time, Pallas kernels for 28%

profile of v3, /device:TPU:0, one launch (start us, length us, event | category | flops | bytes accessed | tf_op | source)
XLA Modules:
  0.0 559.5 jit_solution(6126443287205262282)
XLA Ops:
  9.5 4.1 collective-permute-start
  13.6 14.7 %collective-permute-done = bf16[1,32,5120]{2,1,0:T(8,128)(2,1)S(1)} collective-permute-done((bf16[1,32,5120]{2,1,0:T(8,128)(2,1)S(1)}, bf16[1,32,5120]{2,1,0:T(8,128)(2,1)S(1)}, u32[]{:S(2)}, u32[]{:S(2)}) %collective-permute-start) | collective-permute-done | bytes 327712 | tf_op jit(solution)/shard_map/ppermute | solution.py:846
  29.3 15.1 %collective-permute-done.1 = bf16[2,32,5120]{2,1,0:T(8,128)(2,1)S(1)} collective-permute-done((bf16[2,32,5120]{2,1,0:T(8,128)(2,1)S(1)}, bf16[2,32,5120]{2,1,0:T(8,128)(2,1)S(1)}, u32[]{:S(2)}, u32[]{:S(2)}) %collective-permute-start.1) | collective-permute-done | bytes 655392 | tf_op jit(solution)/shard_map/ppermute | solution.py:846
  48.5 3.7 fusion.17
  53.3 3.0 pad_maximum_fusion.1
  57.8 3.8 collective-permute-done.3
  64.0 2.2 collective-permute-done.4
  67.0 3.3 collective-permute-start.5
  72.1 1.9 collective-permute-start.6
  77.9 3.0 collective-permute-start.8
  83.6 20.7 %collective-permute-done.8 = bf16[1,32,9216]{2,1,0:T(8,128)(2,1)S(1)} collective-permute-done((bf16[1,32,9216]{2,1,0:T(8,128)(2,1)S(1)}, bf16[1,32,9216]{2,1,0:T(8,128)(2,1)S(1)}, u32[]{:S(2)}, u32[]{:S(2)}) %collective-permute-start.8) | collective-permute-done | bytes 589856 | tf_op jit(solution)/shard_map/ppermute | solution.py:846
  105.3 6.9 %all-gather.3.cloned.1.call-done.packed_ref.wq_ref.wk_ref.wv_ref.refs_10_.refs_11_.refs_12_.refs_13_ = bf16[1024,5120]{1,0:T(8,128)(2,1)} async-done(((bf16[128,5120]{1,0:T(8,128)(2,1)}), bf16[1024,5120]{1,0:T(8,128)(2,1)}) %all-gather.3.cloned.1.call-update) | async-done | bytes 10485776 | tf_op jit(solution)/shard_map/all_gather | solution.py:1037
  112.2 7.1 %shard_map.244 = (f32[512,1024]{1,0:T(8,128)}, bf16[512,1024]{1,0:T(8,128)(2,1)}) custom-call(bf16[512,1024]{1,0:T(8,128)(2,1)} %bitcast.319, bf16[512,1024]{1,0:T(8,128)(2,1)} %bitcast.318, bf16[512,1024]{1,0:T(8,128)(2,1)} %bitcast_select_fusion.1.cond_ref, ...), custom_call_target="tpu_custom_call" | custom-call | flops 2147483648 | bytes 10485760 | tf_op jit(solution)/shard_map/pallas_call | solution.py:168
  119.3 13.0 %collective-permute-done.9 = bf16[2,32,9216]{2,1,0:T(8,128)(2,1)S(1)} collective-permute-done((bf16[2,32,9216]{2,1,0:T(8,128)(2,1)S(1)}, bf16[2,32,9216]{2,1,0:T(8,128)(2,1)S(1)}, u32[]{:S(2)}, u32[]{:S(2)}) %collective-permute-start.9) | collective-permute-done | bytes 1179680 | tf_op jit(solution)/shard_map/ppermute | solution.py:846
  134.6 9.4 %shard_map.245 = (bf16[512,384]{1,0:T(8,128)(2,1)}, bf16[512,384]{1,0:T(8,128)(2,1)}, bf16[512,384]{1,0:T(8,128)(2,1)}, bf16[512,384]{1,0:T(8,128)(2,1)}, bf16[5...) custom-call(s32[1]{0:T(128)} %bitcast.me_ref, ...), custom_call_target="tpu_custom_call" | custom-call | flops 3221225472 | bytes 10485760 | tf_op jit(solution)/shard_map/pallas_call | solution.py:218
  143.9 2.2 collective-permute-start.11
  146.1 2.2 collective-permute-start.7
  148.3 2.2 collective-permute-start.15
  150.5 7.6 %collective-permute-done.11.refs_3_ = bf16[512,384]{1,0:T(8,128)(2,1)S(1)} collective-permute-done((bf16[512,384]{1,0:T(8,128)(2,1)}, bf16[512,384]{1,0:T(8,128)(2,1)S(1)}, u32[]{:S(2)}, u32[]{:S(2)}) %collective-permute-start.11) | collective-permute-done | bytes 393248 | tf_op jit(solution)/shard_map/ppermute | solution.py:916
  158.1 17.2 %collective-permute-start.13 = (bf16[512,384]{1,0:T(8,128)(2,1)}, bf16[512,384]{1,0:T(8,128)(2,1)S(1)}, u32[]{:S(2)}, u32[]{:S(2)}) collective-permute-start(bf16[512,384]{1,0:T(8,128)(2,1)} %get-tuple-element.152), channel_id=1, source_target_pairs={{0,1},{1,0},{2,3},{3,2},{4,5},{5,4},{6,7},{7,6},{8,9},{9,8},{10,11... | collective-permute-start | bytes 1179656 | tf_op jit(solution)/shard_map/ppermute | solution.py:916
  175.3 22.5 %collective-permute-done.10.refs_2_ = bf16[512,384]{1,0:T(8,128)(2,1)S(1)} collective-permute-done((bf16[512,384]{1,0:T(8,128)(2,1)}, bf16[512,384]{1,0:T(8,128)(2,1)S(1)}, u32[]{:S(2)}, u32[]{:S(2)}) %collective-permute-start.10) | collective-permute-done | bytes 393248 | tf_op jit(solution)/shard_map/ppermute | solution.py:916
  198.7 17.1 %shard_map.246 = (bf16[512,128]{1,0:T(8,128)(2,1)}, bf16[512,128]{1,0:T(8,128)(2,1)}, bf16[512,128]{1,0:T(8,128)(2,1)}, bf16[512,128]{1,0:T(8,128)(2,1)}, f32[2,2048]{1,0:T(2,128)}) custom-call(bf16[512,384]{1,0:T(8,128)(2,1)} %get-tuple-element.139.refs_0_, bf16[512,384]{1,0:T(8,128)(2,1)} %copy-done.37, bf16[512,384]{1,0:T(8,128)(2,1)} %copy-done.36, ...), custom_call_target="tpu_custom_call" | custom-call | flops 8589934592 | bytes 2097152 | tf_op jit(solution)/shard_map/pallas_call | solution.py:279
  217.7 17.4 %shard_map.247 = (bf16[512,128]{1,0:T(8,128)(2,1)}, bf16[512,128]{1,0:T(8,128)(2,1)}, bf16[512,128]{1,0:T(8,128)(2,1)}, bf16[512,128]{1,0:T(8,128)(2,1)}, f32[2,2048]{1,0:T(2,128)}) custom-call(bf16[512,384]{1,0:T(8,128)(2,1)} %get-tuple-element.151.refs_0_, bf16[512,384]{1,0:T(8,128)(2,1)} %copy-done.34, bf16[512,384]{1,0:T(8,128)(2,1)} %copy-done.33, ...), custom_call_target="tpu_custom_call" | custom-call | flops 8589934592 | bytes 2097152 | tf_op jit(solution)/shard_map/pallas_call | solution.py:279
  235.1 2.4 collective-permute-start.18
  237.6 2.2 collective-permute-start.19
  239.9 2.1 collective-permute-start.20
  241.9 3.0 collective-permute-done.12.refs_1_
  244.9 2.1 collective-permute-done.20.refs_7_
  247.7 6.0 %shard_map.248 = (bf16[512,1024]{1,0:T(8,128)(2,1)}, f32[512,1024]{1,0:T(8,128)}, f32[512,1024]{1,0:T(8,128)}, bf16[512,1024]{1,0:T(8,128)(2,1)}) custom-call(s32[1]{0:T(128)} %bitcast.me_ref, bf16[512,128]{1,0:T(8,128)(2,1)} %get-tuple-element.149.refs_0_.refs_8_, bf16[512,128]{1,0:T(8,128)(2,1)} %copy-done.25, bf16[512,128]{1,0:T(8,128)(2,1)} %copy-done.23, ...), custom_call_target="tpu_custom_call" | custom-call | flops 1073741824 | bytes 11534336 | tf_op jit(solution)/shard_map/pallas_call | solution.py:412
  253.6 24.9 %shard_map.249 = (f32[512,1024]{1,0:T(8,128)}, f32[512,1024]{1,0:T(8,128)}, bf16[512,4096]{1,0:T(8,128)(2,1)}, bf16[512,4096]{1,0:T(8,128)(2,1)}) custom-call(bf16[512,1024]{1,0:T(8,128)(2,1)} %get-tuple-element.178.x_ref, bf16[512,1024]{1,0:T(8,128)(2,1)} %get-tuple-element.261.dc_ref, ...), custom_call_target="tpu_custom_call" | custom-call | flops 17179869184 | bytes 33554432 | tf_op jit(solution)/shard_map/pallas_call | solution.py:511
  278.5 8.0 %shard_map.250 = (bf16[512,1024]{1,0:T(8,128)(2,1)}, f32[512,1024]{1,0:T(8,128)}, bf16[512,1024]{1,0:T(8,128)(2,1)}, f32[8,1024]{1,0:T(8,128)}, bf16[512,256]{1,...) custom-call(s32[1]{0:T(128)} %bitcast.me_ref, ...), custom_call_target="tpu_custom_call" | custom-call | flops 1073741824 | bytes 16777216 | tf_op jit(solution)/shard_map/pallas_call | solution.py:595
  286.6 4.1 shard_map.251.refs_5_
  295.0 14.5 %shard_map.252 = bf16[1024,8192]{1,0:T(8,128)(2,1)} custom-call(bf16[512,1024]{1,0:T(8,128)(2,1)} %get-tuple-element.178.x_ref, bf16[512,1024]{1,0:T(8,128)(2,1)} %get-tuple-element.261.dc_ref, bf16[512,4096]{1,0:T(8,128)(2,1)} %get-tuple-element.179.activated_ref, bf16[512,4096]{1,0:T(8,128)(2,1)} %get-tuple-element.180.up_cot_ref), custom_call_target="tpu_custom_call" | custom-call | flops 8589934592 | bytes 33554432 | tf_op jit(solution)/shard_map/pallas_call | solution.py:540
  310.4 27.7 %shard_map.253 = (bf16[512,384]{1,0:T(8,128)(2,1)}, bf16[512,384]{1,0:T(8,128)(2,1)}, bf16[512,384]{1,0:T(8,128)(2,1)}, bf16[512,384]{1,0:T(8,128)(2,1)}) custom-call(bf16[512,384]{1,0:T(8,128)(2,1)} %get-tuple-element.139.refs_0_, bf16[512,384]{1,0:T(8,128)(2,1)} %copy-done.37, bf16[512,384]{1,0:T(8,128)(2,1)} %copy-done.36, bf16[512,384]{1,0:T(8,128)(2,1)} %copy-done.35, ...), custom_call_target="tpu_custom_call" | custom-call | flops 12884901888 | bytes 5242880 | tf_op jit(solution)/shard_map/pallas_call | solution.py:365
  338.2 2.2 collective-permute-start.26
  340.4 2.6 collective-permute-start.25
  343.0 27.6 %shard_map.254 = (bf16[512,384]{1,0:T(8,128)(2,1)}, bf16[512,384]{1,0:T(8,128)(2,1)}, bf16[512,384]{1,0:T(8,128)(2,1)}, bf16[512,384]{1,0:T(8,128)(2,1)}) custom-call(bf16[512,384]{1,0:T(8,128)(2,1)} %get-tuple-element.151.refs_0_, bf16[512,384]{1,0:T(8,128)(2,1)} %copy-done.34, bf16[512,384]{1,0:T(8,128)(2,1)} %copy-done.33, bf16[512,384]{1,0:T(8,128)(2,1)} %copy-done.32, ...), custom_call_target="tpu_custom_call" | custom-call | flops 12884901888 | bytes 5242880 | tf_op jit(solution)/shard_map/pallas_call | solution.py:365
  371.8 6.2 %shard_map.255 = bf16[1024,2560]{1,0:T(8,128)(2,1)} custom-call(s32[1]{0:T(128)} %bitcast.me_ref, bf16[512,1024]{1,0:T(8,128)(2,1)} %get-tuple-element.138.x_ref.refs_0_, bf16[512,384]{1,0:T(8,128)(2,1)} %get-tuple-element.188.refs_1_.refs_0_, bf16[512,384]{1,0:T(8,128)(2,1)} %copy-done.8, ...), custom_call_target="tpu_custom_call", output_to_operand_aliasing={{}: (6, {})} | custom-call | flops 524288 | bytes 1024 | tf_op jit(solution)/shard_map/pallas_call | solution.py:733
  378.1 3.4 dynamic-slice_bitcast_fusion
  386.6 3.6 fusion
  391.7 3.9 collective-permute-done.30.refs_4_.refs_7_
  395.6 24.1 %collective-permute-done.29.refs_3_.refs_6_ = bf16[512,384]{1,0:T(8,128)(2,1)S(1)} collective-permute-done((bf16[512,384]{1,0:T(8,128)(2,1)}, bf16[512,384]{1,0:T(8,128)(2,1)S(1)}, u32[]{:S(2)}, u32[]{:S(2)}) %collective-permute-start.29) | collective-permute-done | bytes 393248 | tf_op jit(solution)/shard_map/ppermute | solution.py:916
  421.2 6.1 %shard_map.256 = bf16[1024,1536]{1,0:T(8,128)(2,1)} custom-call(s32[1]{0:T(128)} %bitcast.me_ref, bf16[512,1024]{1,0:T(8,128)(2,1)} %get-tuple-element.138.x_ref.refs_0_, bf16[512,384]{1,0:T(8,128)(2,1)} %get-tuple-element.209.refs_1_.refs_4_, bf16[512,384]{1,0:T(8,128)(2,1)} %copy-done.11, bf16[512,384]{1,0:T(8,128)(2,1)} %copy-done.10, ...), custom_call_target="tpu_custom_call" | custom-call | flops 524288 | bytes 1024 | tf_op jit(solution)/shard_map/pallas_call | solution.py:733
  427.3 2.7 dynamic-slice_bitcast_fusion.1
  430.0 17.7 %reduce-scatter.2.cloned.1.call-done = bf16[128,8192]{1,0:T(8,128)(2,1)} async-done(((bf16[1024,8192]{1,0:T(8,128)(2,1)}), bf16[128,8192]{1,0:T(8,128)(2,1)}) %reduce-scatter.2.cloned.1.call-update) | async-done | bytes 2097168 | tf_op jit(solution)/shard_map/reduce_scatter | solution.py:1127
  447.7 2.4 dynamic-slice_bitcast_fusion.4
  450.1 2.6 fusion.4
  452.7 2.2 fusion.1
  455.2 2.4 collective-permute-start.33
  459.0 14.4 %shard_map.257 = (bf16[512,1024]{1,0:T(8,128)(2,1)}, bf16[512,1024]{1,0:T(8,128)(2,1)}, bf16[512,1024]{1,0:T(8,128)(2,1)}, f32[8,1024]{1,0:T(8,128)}) custom-call(s32[1]{0:T(128)} %bitcast.me_ref, bf16[512,384]{1,0:T(8,128)(2,1)} %get-tuple-element.188.refs_1_.refs_0_, bf16[512,384]{1,0:T(8,128)(2,1)} %copy-done.8, bf16[512,384]{1,0:T(8,128)(2,1)} %copy-done.7, ...), custom_call_target="tpu_custom_call" | custom-call | flops 1073741824 | bytes 2097152 | tf_op jit(solution)/shard_map/pallas_call | solution.py:660
  475.1 3.0 convert_bitcast_fusion
  479.8 2.9 collective-permute-done.35
  487.2 2.4 convert_add_fusion.6
  494.6 4.0 collective-permute-done.39
  498.6 2.0 fusion.3
  506.3 3.5 collective-permute-done.41
  512.9 3.0 collective-permute-done.49.refs_1_
  515.8 4.6 shard_map.260
  522.6 2.0 collective-permute-start.46
  533.8 2.2 collective-permute-start.47
  536.7 4.1 shard_map.261
  540.9 5.0 collective-permute-done.47.refs_3_
  546.5 2.4 shard_map.258
  549.6 2.9 shard_map.259
  (250 shorter events, 77.4 us)
Async XLA Ops:
  7.2 105.1 %all-gather.3.cloned.1.call-start = ((), (), s32[]{:S(2)}) async-start(), calls=%async_computation.1 | async-start | bytes 11796480 | tf_op jit(solution)/shard_map/all_gather | solution.py:1037
  9.5 18.8 %collective-permute-start = (bf16[1,32,5120]{2,1,0:T(8,128)(2,1)S(1)}, bf16[1,32,5120]{2,1,0:T(8,128)(2,1)S(1)}, u32[]{:S(2)}, u32[]{:S(2)}) collective-permute-start(bf16[1,32,5120]{2,1,0:T(8,128)(2,1)S(1)} %get-tuple-element.278), channel_id=1, source_target_pairs={{0,2},{1,3},{2,0},{3,1},{4,6},{5,7},{6,4},{7,5},{8,10},{9,11},{10,... | collective-permute-start | bytes 983048 | tf_op jit(solution)/shard_map/ppermute | solution.py:846
  28.5 16.0 %collective-permute-start.1 = (bf16[2,32,5120]{2,1,0:T(8,128)(2,1)S(1)}, bf16[2,32,5120]{2,1,0:T(8,128)(2,1)S(1)}, u32[]{:S(2)}, u32[]{:S(2)}) collective-permute-start(bf16[2,32,5120]{2,1,0:T(8,128)(2,1)S(1)} %maximum_select_fusion.4), channel_id=1, source_target_pairs={{0,1},{1,0},{2,3},{3,2},{4,5},{5,4},{6,7},{7,6},{8,9},{9,8},{10,11... | collective-permute-start | bytes 1966088 | tf_op jit(solution)/shard_map/ppermute | solution.py:846
  45.8 201.2 %all-gather.5.cloned.1.call-start = ((), (), s32[]{:S(2)}) async-start(), calls=%async_computation.2 | async-start | bytes 21233664 | tf_op jit(solution)/shard_map/all_gather | solution.py:1086
  48.2 8.1 %collective-permute-start.2 = (f32[2,2,1,6144]{3,2,1,0:T(1,128)S(1)}, f32[2,2,1,6144]{3,2,1,0:T(1,128)S(1)}, u32[]{:S(2)}, u32[]{:S(2)}) collective-permute-start(f32[2,2,1,6144]{3,2,1,0:T(1,128)S(1)} %constant_dynamic-slice_fusion), channel_id=1, source_target_pairs={{0,4},{4,0},{8,12},{12,8},{16,20},{20,16},{24,28},{28,24},{1,5},{5... | collective-permute-start | bytes 294920 | tf_op jit(solution)/shard_map/ppermute | solution.py:846
  56.3 24.5 %copy-start.12 = (bf16[1,512,1024]{2,1,0:T(8,128)(2,1)S(1)}, bf16[1,512,1024]{2,1,0:T(8,128)(2,1)}, u32[]{:S(2)}) copy-start(bf16[1,512,1024]{2,1,0:T(8,128)(2,1)} %param.15) | copy-start | bytes 3145732
  56.5 5.2 collective-permute-start.3
  61.7 4.5 collective-permute-start.4
  67.0 5.1 collective-permute-start.5
  72.1 4.5 collective-permute-start.6
  77.9 26.5 %collective-permute-start.8 = (bf16[1,32,9216]{2,1,0:T(8,128)(2,1)S(1)}, bf16[1,32,9216]{2,1,0:T(8,128)(2,1)S(1)}, u32[]{:S(2)}, u32[]{:S(2)}) collective-permute-start(bf16[1,32,9216]{2,1,0:T(8,128)(2,1)S(1)} %bitcast.320), channel_id=1, source_target_pairs={{0,2},{1,3},{2,0},{3,1},{4,6},{5,7},{6,4},{7,5},{8,10},{9,11},{10,... | collective-permute-start | bytes 1769480 | tf_op jit(solution)/shard_map/ppermute | solution.py:846
  104.6 27.7 %collective-permute-start.9 = (bf16[2,32,9216]{2,1,0:T(8,128)(2,1)S(1)}, bf16[2,32,9216]{2,1,0:T(8,128)(2,1)S(1)}, u32[]{:S(2)}, u32[]{:S(2)}) collective-permute-start(bf16[2,32,9216]{2,1,0:T(8,128)(2,1)S(1)} %maximum_select_fusion.2), channel_id=1, source_target_pairs={{0,1},{1,0},{2,3},{3,2},{4,5},{5,4},{6,7},{7,6},{8,9},{9,8},{10,11... | collective-permute-start | bytes 3538952 | tf_op jit(solution)/shard_map/ppermute | solution.py:846
  134.3 313.4 %reduce-scatter.2.cloned.1.call-start = ((), (), s32[]{:S(2)}) async-start(), calls=%async_computation.3 | async-start | bytes 18874368 | tf_op jit(solution)/shard_map/reduce_scatter | solution.py:1127
  143.9 14.2 %collective-permute-start.11 = (bf16[512,384]{1,0:T(8,128)(2,1)}, bf16[512,384]{1,0:T(8,128)(2,1)S(1)}, u32[]{:S(2)}, u32[]{:S(2)}) collective-permute-start(bf16[512,384]{1,0:T(8,128)(2,1)} %get-tuple-element.147), channel_id=1, source_target_pairs={{0,3},{1,2},{2,1},{3,0},{4,7},{5,6},{6,5},{7,4},{8,11},{9,10},{10,... | collective-permute-start | bytes 1179656 | tf_op jit(solution)/shard_map/ppermute | solution.py:916
  146.1 51.8 %collective-permute-start.10 = (bf16[512,384]{1,0:T(8,128)(2,1)}, bf16[512,384]{1,0:T(8,128)(2,1)S(1)}, u32[]{:S(2)}, u32[]{:S(2)}) collective-permute-start(bf16[512,384]{1,0:T(8,128)(2,1)} %get-tuple-element.145), channel_id=1, source_target_pairs={{0,2},{1,3},{2,0},{3,1},{4,6},{5,7},{6,4},{7,5},{8,10},{9,11},{10,... | collective-permute-start | bytes 1179656 | tf_op jit(solution)/shard_map/ppermute | solution.py:916
  146.1 51.8 %collective-permute-start.7 = (bf16[512,384]{1,0:T(8,128)(2,1)}, bf16[512,384]{1,0:T(8,128)(2,1)S(1)}, u32[]{:S(2)}, u32[]{:S(2)}) collective-permute-start(bf16[512,384]{1,0:T(8,128)(2,1)} %get-tuple-element.140), channel_id=1, source_target_pairs={{0,1},{1,0},{2,3},{3,2},{4,5},{5,4},{6,7},{7,6},{8,9},{9,8},{10,11... | collective-permute-start | bytes 1179656 | tf_op jit(solution)/shard_map/ppermute | solution.py:916
  148.3 67.6 %collective-permute-start.15 = (bf16[512,384]{1,0:T(8,128)(2,1)}, bf16[512,384]{1,0:T(8,128)(2,1)S(1)}, u32[]{:S(2)}, u32[]{:S(2)}) collective-permute-start(bf16[512,384]{1,0:T(8,128)(2,1)} %get-tuple-element.156), channel_id=1, source_target_pairs={{0,3},{1,2},{2,1},{3,0},{4,7},{5,6},{6,5},{7,4},{8,11},{9,10},{10,... | collective-permute-start | bytes 1179656 | tf_op jit(solution)/shard_map/ppermute | solution.py:916
  150.5 65.4 %collective-permute-start.14 = (bf16[512,384]{1,0:T(8,128)(2,1)}, bf16[512,384]{1,0:T(8,128)(2,1)S(1)}, u32[]{:S(2)}, u32[]{:S(2)}) collective-permute-start(bf16[512,384]{1,0:T(8,128)(2,1)} %get-tuple-element.154), channel_id=1, source_target_pairs={{0,2},{1,3},{2,0},{3,1},{4,6},{5,7},{6,4},{7,5},{8,10},{9,11},{10,... | collective-permute-start | bytes 1179656 | tf_op jit(solution)/shard_map/ppermute | solution.py:916
  158.1 39.8 %copy-start.35 = (bf16[512,384]{1,0:T(8,128)(2,1)}, bf16[512,384]{1,0:T(8,128)(2,1)S(1)}, u32[]{:S(2)}) copy-start(bf16[512,384]{1,0:T(8,128)(2,1)S(1)} %collective-permute-done.11.refs_3_) | copy-start | bytes 1179652
  158.1 57.8 %collective-permute-start.13 = (bf16[512,384]{1,0:T(8,128)(2,1)}, bf16[512,384]{1,0:T(8,128)(2,1)S(1)}, u32[]{:S(2)}, u32[]{:S(2)}) collective-permute-start(bf16[512,384]{1,0:T(8,128)(2,1)} %get-tuple-element.152), channel_id=1, source_target_pairs={{0,1},{1,0},{2,3},{3,2},{4,5},{5,4},{6,7},{7,6},{8,9},{9,8},{10,11... | collective-permute-start | bytes 1179656 | tf_op jit(solution)/shard_map/ppermute | solution.py:916
  215.9 23.9 %collective-permute-start.17 = (bf16[512,128]{1,0:T(8,128)(2,1)}, bf16[512,128]{1,0:T(8,128)(2,1)S(1)}, u32[]{:S(2)}, u32[]{:S(2)}) collective-permute-start(bf16[512,128]{1,0:T(8,128)(2,1)} %get-tuple-element.162.refs_11_), channel_id=1, source_target_pairs={{0,3},{1,2},{2,1},{3,0},{4,7},{5,6},{6,5},{7,4},{8,11},{9,10},{10,... | collective-permute-start | bytes 393224 | tf_op jit(solution)/shard_map/ppermute | solution.py:916
  217.7 24.3 %collective-permute-start.16 = (bf16[512,128]{1,0:T(8,128)(2,1)}, bf16[512,128]{1,0:T(8,128)(2,1)S(1)}, u32[]{:S(2)}, u32[]{:S(2)}) collective-permute-start(bf16[512,128]{1,0:T(8,128)(2,1)} %get-tuple-element.160.refs_10_), channel_id=1, source_target_pairs={{0,2},{1,3},{2,0},{3,1},{4,6},{5,7},{6,4},{7,5},{8,10},{9,11},{10,... | collective-permute-start | bytes 393224 | tf_op jit(solution)/shard_map/ppermute | solution.py:916
  235.1 9.8 %collective-permute-start.18 = (bf16[512,128]{1,0:T(8,128)(2,1)}, bf16[512,128]{1,0:T(8,128)(2,1)S(1)}, u32[]{:S(2)}, u32[]{:S(2)}) collective-permute-start(bf16[512,128]{1,0:T(8,128)(2,1)} %get-tuple-element.164.refs_9_), channel_id=1, source_target_pairs={{0,1},{1,0},{2,3},{3,2},{4,5},{5,4},{6,7},{7,6},{8,9},{9,8},{10,11... | collective-permute-start | bytes 393224 | tf_op jit(solution)/shard_map/ppermute | solution.py:916
  237.5 7.4 %collective-permute-start.12 = (bf16[512,128]{1,0:T(8,128)(2,1)S(1)}, bf16[512,128]{1,0:T(8,128)(2,1)S(1)}, u32[]{:S(2)}, u32[]{:S(2)}) collective-permute-start(bf16[512,128]{1,0:T(8,128)(2,1)S(1)} %copy-done.44), channel_id=1, source_target_pairs={{0,1},{1,0},{2,3},{3,2},{4,5},{5,4},{6,7},{7,6},{8,9},{9,8},{10,11... | collective-permute-start | bytes 393224 | tf_op jit(solution)/shard_map/ppermute | solution.py:916
  237.6 7.3 %collective-permute-start.19 = (bf16[512,128]{1,0:T(8,128)(2,1)}, bf16[512,128]{1,0:T(8,128)(2,1)S(1)}, u32[]{:S(2)}, u32[]{:S(2)}) collective-permute-start(bf16[512,128]{1,0:T(8,128)(2,1)} %get-tuple-element.165.refs_10_), channel_id=1, source_target_pairs={{0,2},{1,3},{2,0},{3,1},{4,6},{5,7},{6,4},{7,5},{8,10},{9,11},{10,... | collective-permute-start | bytes 393224 | tf_op jit(solution)/shard_map/ppermute | solution.py:916
  239.9 7.2 %collective-permute-start.20 = (bf16[512,128]{1,0:T(8,128)(2,1)}, bf16[512,128]{1,0:T(8,128)(2,1)S(1)}, u32[]{:S(2)}, u32[]{:S(2)}) collective-permute-start(bf16[512,128]{1,0:T(8,128)(2,1)} %get-tuple-element.166.refs_11_), channel_id=1, source_target_pairs={{0,3},{1,2},{2,1},{3,0},{4,7},{5,6},{6,5},{7,4},{8,11},{9,10},{10,... | collective-permute-start | bytes 393224 | tf_op jit(solution)/shard_map/ppermute | solution.py:916
  290.6 18.9 %collective-permute-start.21 = (bf16[512,256]{1,0:T(8,128)(2,1)S(1)}, bf16[512,256]{1,0:T(8,128)(2,1)S(1)}, u32[]{:S(2)}, u32[]{:S(2)}) collective-permute-start(bf16[512,256]{1,0:T(8,128)(2,1)S(1)} %copy-done.43), channel_id=1, source_target_pairs={{0,1},{1,0},{2,3},{3,2},{4,5},{5,4},{6,7},{7,6},{8,9},{9,8},{10,11... | collective-permute-start | bytes 786440 | tf_op jit(solution)/shard_map/ppermute | solution.py:916
  292.2 17.3 %collective-permute-start.22 = (bf16[512,256]{1,0:T(8,128)(2,1)S(1)}, bf16[512,256]{1,0:T(8,128)(2,1)S(1)}, u32[]{:S(2)}, u32[]{:S(2)}) collective-permute-start(bf16[512,256]{1,0:T(8,128)(2,1)S(1)} %copy-done.42), channel_id=1, source_target_pairs={{0,2},{1,3},{2,0},{3,1},{4,6},{5,7},{6,4},{7,5},{8,10},{9,11},{10,... | collective-permute-start | bytes 786440 | tf_op jit(solution)/shard_map/ppermute | solution.py:916
  293.4 16.2 %collective-permute-start.23 = (bf16[512,256]{1,0:T(8,128)(2,1)S(1)}, bf16[512,256]{1,0:T(8,128)(2,1)S(1)}, u32[]{:S(2)}, u32[]{:S(2)}) collective-permute-start(bf16[512,256]{1,0:T(8,128)(2,1)S(1)} %copy-done.41), channel_id=1, source_target_pairs={{0,3},{1,2},{2,1},{3,0},{4,7},{5,6},{6,5},{7,4},{8,11},{9,10},{10,... | collective-permute-start | bytes 786440 | tf_op jit(solution)/shard_map/ppermute | solution.py:916
  338.2 32.5 %collective-permute-start.26 = (bf16[512,384]{1,0:T(8,128)(2,1)}, bf16[512,384]{1,0:T(8,128)(2,1)S(1)}, u32[]{:S(2)}, u32[]{:S(2)}) collective-permute-start(bf16[512,384]{1,0:T(8,128)(2,1)} %get-tuple-element.195), channel_id=1, source_target_pairs={{0,3},{1,2},{2,1},{3,0},{4,7},{5,6},{6,5},{7,4},{8,11},{9,10},{10,... | collective-permute-start | bytes 1179656 | tf_op jit(solution)/shard_map/ppermute | solution.py:916
  340.4 30.5 %collective-permute-start.25 = (bf16[512,384]{1,0:T(8,128)(2,1)}, bf16[512,384]{1,0:T(8,128)(2,1)S(1)}, u32[]{:S(2)}, u32[]{:S(2)}) collective-permute-start(bf16[512,384]{1,0:T(8,128)(2,1)} %get-tuple-element.193), channel_id=1, source_target_pairs={{0,2},{1,3},{2,0},{3,1},{4,6},{5,7},{6,4},{7,5},{8,10},{9,11},{10,... | collective-permute-start | bytes 1179656 | tf_op jit(solution)/shard_map/ppermute | solution.py:916
  343.0 27.9 %collective-permute-start.24 = (bf16[512,384]{1,0:T(8,128)(2,1)}, bf16[512,384]{1,0:T(8,128)(2,1)S(1)}, u32[]{:S(2)}, u32[]{:S(2)}) collective-permute-start(bf16[512,384]{1,0:T(8,128)(2,1)} %get-tuple-element.189), channel_id=1, source_target_pairs={{0,1},{1,0},{2,3},{3,2},{4,5},{5,4},{6,7},{7,6},{8,9},{9,8},{10,11... | collective-permute-start | bytes 1179656 | tf_op jit(solution)/shard_map/ppermute | solution.py:916
  381.5 5.1 collective-permute-start.28
  381.5 14.1 %collective-permute-start.30 = (bf16[512,384]{1,0:T(8,128)(2,1)}, bf16[512,384]{1,0:T(8,128)(2,1)S(1)}, u32[]{:S(2)}, u32[]{:S(2)}) collective-permute-start(bf16[512,384]{1,0:T(8,128)(2,1)} %get-tuple-element.203), channel_id=1, source_target_pairs={{0,3},{1,2},{2,1},{3,0},{4,7},{5,6},{6,5},{7,4},{8,11},{9,10},{10,... | collective-permute-start | bytes 1179656 | tf_op jit(solution)/shard_map/ppermute | solution.py:916
  382.9 36.7 %collective-permute-start.29 = (bf16[512,384]{1,0:T(8,128)(2,1)}, bf16[512,384]{1,0:T(8,128)(2,1)S(1)}, u32[]{:S(2)}, u32[]{:S(2)}) collective-permute-start(bf16[512,384]{1,0:T(8,128)(2,1)} %get-tuple-element.201), channel_id=1, source_target_pairs={{0,2},{1,3},{2,0},{3,1},{4,6},{5,7},{6,4},{7,5},{8,10},{9,11},{10,... | collective-permute-start | bytes 1179656 | tf_op jit(solution)/shard_map/ppermute | solution.py:916
  384.7 35.0 %collective-permute-start.27 = (bf16[512,384]{1,0:T(8,128)(2,1)}, bf16[512,384]{1,0:T(8,128)(2,1)S(1)}, u32[]{:S(2)}, u32[]{:S(2)}) collective-permute-start(bf16[512,384]{1,0:T(8,128)(2,1)} %get-tuple-element.197), channel_id=1, source_target_pairs={{0,1},{1,0},{2,3},{3,2},{4,5},{5,4},{6,7},{7,6},{8,9},{9,8},{10,11... | collective-permute-start | bytes 1179656 | tf_op jit(solution)/shard_map/ppermute | solution.py:916
  386.6 40.7 %copy-start.4 = (bf16[2,2,2,2,32,2560]{5,4,3,2,1,0:T(8,128)(2,1)}, bf16[2,2,2,2,32,2560]{5,4,3,2,1,0:T(8,128)(2,1)S(1)}, u32[]{:S(2)}) copy-start(bf16[2,2,2,2,32,2560]{5,4,3,2,1,0:T(8,128)(2,1)S(1)} %collective-permute-done.28) | copy-start | bytes 7864324
  390.3 59.9 %collective-permute-start.32 = (bf16[2,2,2,32,2560]{4,3,2,1,0:T(8,128)(2,1)}, bf16[2,2,2,32,2560]{4,3,2,1,0:T(8,128)(2,1)}, u32[]{:S(2)}, u32[]{:S(2)}) collective-permute-start(bf16[2,2,2,32,2560]{4,3,2,1,0:T(8,128)(2,1)} %fusion), channel_id=1, source_target_pairs={{0,8},{4,12},{8,0},{12,4},{16,24},{20,28},{24,16},{28,20},{1,9},{5... | collective-permute-start | bytes 3932168 | tf_op jit(solution)/shard_map/ppermute | solution.py:846
  395.6 24.1 %copy-start.9 = (bf16[512,384]{1,0:T(8,128)(2,1)}, bf16[512,384]{1,0:T(8,128)(2,1)S(1)}, u32[]{:S(2)}) copy-start(bf16[512,384]{1,0:T(8,128)(2,1)S(1)} %collective-permute-done.30.refs_4_.refs_7_) | copy-start | bytes 1179652
  430.0 22.7 %collective-permute-start.31 = (bf16[2,2,2,2,32,1536]{5,4,3,2,1,0:T(8,128)(2,1)}, bf16[2,2,2,2,32,1536]{5,4,3,2,1,0:T(8,128)(2,1)}, u32[]{:S(2)}, u32[]{:S(2)}) collective-permute-start(bf16[2,2,2,2,32,1536]{5,4,3,2,1,0:T(8,128)(2,1)} %dynamic-slice_bitcast_fusion.1), channel_id=1, source_target_pairs={{0,4},{4,0},{8,12},{12,8},{16,20},{20,16},{24,28},{28,24},{1,5},{5... | collective-permute-start | bytes 4718600 | tf_op jit(solution)/shard_map/ppermute | solution.py:846
  454.9 20.2 %collective-permute-start.34 = (bf16[2,2,2,32,1536]{4,3,2,1,0:T(8,128)(2,1)}, bf16[2,2,2,32,1536]{4,3,2,1,0:T(8,128)(2,1)S(1)}, u32[]{:S(2)}, u32[]{:S(2)}) collective-permute-start(bf16[2,2,2,32,1536]{4,3,2,1,0:T(8,128)(2,1)} %fusion.1), channel_id=1, source_target_pairs={{0,8},{4,12},{8,0},{12,4},{16,24},{20,28},{24,16},{28,20},{1,9},{5... | collective-permute-start | bytes 2359304 | tf_op jit(solution)/shard_map/ppermute | solution.py:846
  455.2 19.8 %collective-permute-start.33 = (bf16[2,2,32,2560]{3,2,1,0:T(8,128)(2,1)}, bf16[2,2,32,2560]{3,2,1,0:T(8,128)(2,1)}, u32[]{:S(2)}, u32[]{:S(2)}) collective-permute-start(bf16[2,2,32,2560]{3,2,1,0:T(8,128)(2,1)} %fusion.4), channel_id=1, source_target_pairs={{0,16},{4,20},{8,24},{12,28},{16,0},{20,4},{24,8},{28,12},{1,17},{... | collective-permute-start | bytes 1966088 | tf_op jit(solution)/shard_map/ppermute | solution.py:846
  457.6 25.1 %collective-permute-start.35 = (bf16[2,32,8192]{2,1,0:T(8,128)(2,1)}, bf16[2,32,8192]{2,1,0:T(8,128)(2,1)}, u32[]{:S(2)}, u32[]{:S(2)}) collective-permute-start(bf16[2,32,8192]{2,1,0:T(8,128)(2,1)} %dynamic-slice_bitcast_fusion.4), channel_id=1, source_target_pairs={{0,1},{1,0},{2,3},{3,2},{4,5},{5,4},{6,7},{7,6},{8,9},{9,8},{10,11... | collective-permute-start | bytes 3145736 | tf_op jit(solution)/shard_map/ppermute | solution.py:846
  474.3 9.1 %collective-permute-start.50 = (f32[1,6144]{1,0:T(1,128)S(1)}, f32[1,6144]{1,0:T(1,128)S(1)}, u32[]{:S(2)}, u32[]{:S(2)}) collective-permute-start(f32[1,6144]{1,0:T(1,128)S(1)} %bitcast.323), channel_id=1, source_target_pairs={{0,1},{1,0},{2,3},{3,2},{4,5},{5,4},{6,7},{7,6},{8,9},{9,8},{10,11... | collective-permute-start | bytes 73736 | tf_op jit(solution)/shard_map/ppermute | solution.py:846
  483.0 21.4 %copy-start.2 = (bf16[2048,512]{1,0:T(8,128)(2,1)}, bf16[2048,512]{1,0:T(8,128)(2,1)S(1)}, u32[]{:S(2)}) copy-start(bf16[2048,512]{1,0:T(8,128)(2,1)S(1)} %get-tuple-element.266) | copy-start | bytes 6291460
  483.1 26.8 %copy-start.1 = (bf16[2048,512]{1,0:T(8,128)(2,1)}, bf16[2048,512]{1,0:T(8,128)(2,1)S(1)}, u32[]{:S(2)}) copy-start(bf16[2048,512]{1,0:T(8,128)(2,1)S(1)} %get-tuple-element.265) | copy-start | bytes 6291460
  483.3 9.4 %collective-permute-start.38 = (bf16[2,2,2,2,64,512]{5,4,3,2,1,0:T(8,128)(2,1)S(1)}, bf16[2,2,2,2,64,512]{5,4,3,2,1,0:T(8,128)(2,1)S(1)}, u32[]{:S(2)}, u32[]{:S(2)}) collective-permute-start(bf16[2,2,2,2,64,512]{5,4,3,2,1,0:T(8,128)(2,1)S(1)} %dynamic-slice_bitcast_fusion.2), channel_id=1, source_target_pairs={{0,4},{4,0},{8,12},{12,8},{16,20},{20,16},{24,28},{28,24},{1,5},{5... | collective-permute-start | bytes 3145736 | tf_op jit(solution)/shard_map/ppermute | solution.py:846
  483.5 11.0 %collective-permute-start.51 = (f32[1,6144]{1,0:T(1,128)S(1)}, f32[1,6144]{1,0:T(1,128)S(1)}, u32[]{:S(2)}, u32[]{:S(2)}) collective-permute-start(f32[1,6144]{1,0:T(1,128)S(1)} %add.752), channel_id=1, source_target_pairs={{0,2},{1,3},{2,0},{3,1},{4,6},{5,7},{6,4},{7,5},{8,10},{9,11},{10,... | collective-permute-start | bytes 73736 | tf_op jit(solution)/shard_map/ppermute | solution.py:846
  485.2 5.9 %collective-permute-start.36 = (bf16[2,2,2,2,64,512]{5,4,2,3,1,0:T(8,128)(2,1)S(1)}, bf16[2,2,2,2,64,512]{5,4,2,3,1,0:T(8,128)(2,1)S(1)}, u32[]{:S(2)}, u32[]{:S(2)}) collective-permute-start(bf16[2,2,2,2,64,512]{5,4,2,3,1,0:T(8,128)(2,1)S(1)} %copy.58), channel_id=1, source_target_pairs={{0,4},{4,0},{8,12},{12,8},{16,20},{20,16},{24,28},{28,24},{1,5},{5... | collective-permute-start | bytes 3145736 | tf_op jit(solution)/shard_map/ppermute | solution.py:846
  486.6 12.0 %collective-permute-start.39 = (bf16[2,2,32,1536]{3,2,1,0:T(8,128)(2,1)S(1)}, bf16[2,2,32,1536]{3,2,1,0:T(8,128)(2,1)S(1)}, u32[]{:S(2)}, u32[]{:S(2)}) collective-permute-start(bf16[2,2,32,1536]{3,2,1,0:T(8,128)(2,1)S(1)} %fusion.10), channel_id=1, source_target_pairs={{0,16},{4,20},{8,24},{12,28},{16,0},{20,4},{24,8},{28,12},{1,17},{... | collective-permute-start | bytes 1179656 | tf_op jit(solution)/shard_map/ppermute | solution.py:846
  489.6 26.2 %collective-permute-start.49 = (bf16[32,8192]{1,0:T(8,128)(2,1)S(1)}, bf16[32,8192]{1,0:T(8,128)(2,1)}, u32[]{:S(2)}, u32[]{:S(2)}) collective-permute-start(bf16[32,8192]{1,0:T(8,128)(2,1)S(1)} %get-tuple-element.270), channel_id=1, source_target_pairs={{0,2},{1,3},{2,0},{3,1},{4,6},{5,7},{6,4},{7,5},{8,10},{9,11},{10,... | collective-permute-start | bytes 1572872 | tf_op jit(solution)/shard_map/ppermute | solution.py:846
  491.2 13.2 %collective-permute-start.37 = (bf16[2,2,2,64,512]{4,3,2,1,0:T(8,128)(2,1)S(1)}, bf16[2,2,2,64,512]{4,3,2,1,0:T(8,128)(2,1)S(1)}, u32[]{:S(2)}, u32[]{:S(2)}) collective-permute-start(bf16[2,2,2,64,512]{4,3,2,1,0:T(8,128)(2,1)S(1)} %fusion.6), channel_id=1, source_target_pairs={{0,8},{4,12},{8,0},{12,4},{16,24},{20,28},{24,16},{28,20},{1,9},{5... | collective-permute-start | bytes 1572872 | tf_op jit(solution)/shard_map/ppermute | solution.py:846
  492.9 16.9 %collective-permute-start.41 = (bf16[2,2,2,64,512]{4,3,2,1,0:T(8,128)(2,1)S(1)}, bf16[2,2,2,64,512]{4,3,2,1,0:T(8,128)(2,1)S(1)}, u32[]{:S(2)}, u32[]{:S(2)}) collective-permute-start(bf16[2,2,2,64,512]{4,3,2,1,0:T(8,128)(2,1)S(1)} %fusion.5), channel_id=1, source_target_pairs={{0,16},{4,20},{8,24},{12,28},{16,0},{20,4},{24,8},{28,12},{1,17},{... | collective-permute-start | bytes 1572872 | tf_op jit(solution)/shard_map/ppermute | solution.py:846
  494.5 17.7 %collective-permute-start.52 = (f32[1,6144]{1,0:T(1,128)S(1)}, f32[1,6144]{1,0:T(1,128)S(1)}, u32[]{:S(2)}, u32[]{:S(2)}) collective-permute-start(f32[1,6144]{1,0:T(1,128)S(1)} %add.753), channel_id=1, source_target_pairs={{0,4},{4,0},{8,12},{12,8},{16,20},{20,16},{24,28},{28,24},{1,5},{5... | collective-permute-start | bytes 73736 | tf_op jit(solution)/shard_map/ppermute | solution.py:846
  502.0 24.6 %collective-permute-start.43 = (bf16[2,32,4096]{2,1,0:T(8,128)(2,1)S(1)}, bf16[2,32,4096]{2,1,0:T(8,128)(2,1)S(1)}, u32[]{:S(2)}, u32[]{:S(2)}) collective-permute-start(bf16[2,32,4096]{2,1,0:T(8,128)(2,1)S(1)} %dynamic-slice_bitcast_fusion.5), channel_id=1, source_target_pairs={{0,1},{1,0},{2,3},{3,2},{4,5},{5,4},{6,7},{7,6},{8,9},{9,8},{10,11... | collective-permute-start | bytes 1572872 | tf_op jit(solution)/shard_map/ppermute | solution.py:846
  504.5 15.9 %collective-permute-start.40 = (bf16[2,2,64,512]{3,2,1,0:T(8,128)(2,1)S(1)}, bf16[2,2,64,512]{3,2,1,0:T(8,128)(2,1)S(1)}, u32[]{:S(2)}, u32[]{:S(2)}) collective-permute-start(bf16[2,2,64,512]{3,2,1,0:T(8,128)(2,1)S(1)} %fusion.13), channel_id=1, source_target_pairs={{0,16},{4,20},{8,24},{12,28},{16,0},{20,4},{24,8},{28,12},{1,17},{... | collective-permute-start | bytes 786440 | tf_op jit(solution)/shard_map/ppermute | solution.py:846
  510.7 10.9 %collective-permute-start.44 = (bf16[2,2,64,512]{3,2,1,0:T(8,128)(2,1)}, bf16[2,2,64,512]{3,2,1,0:T(8,128)(2,1)S(1)}, u32[]{:S(2)}, u32[]{:S(2)}) collective-permute-start(bf16[2,2,64,512]{3,2,1,0:T(8,128)(2,1)} %fusion.12), channel_id=1, source_target_pairs={{0,8},{4,12},{8,0},{12,4},{16,24},{20,28},{24,16},{28,20},{1,9},{5... | collective-permute-start | bytes 786440 | tf_op jit(solution)/shard_map/ppermute | solution.py:846
  512.3 12.4 %collective-permute-start.53 = (f32[2,6144]{1,0:T(2,128)S(1)}, f32[2,6144]{1,0:T(2,128)S(1)}, u32[]{:S(2)}, u32[]{:S(2)}) collective-permute-start(f32[2,6144]{1,0:T(2,128)S(1)} %maximum_select_fusion.7), channel_id=1, source_target_pairs={{0,8},{4,12},{8,0},{12,4},{16,24},{20,28},{24,16},{28,20},{1,9},{5... | collective-permute-start | bytes 147464 | tf_op jit(solution)/shard_map/ppermute | solution.py:846
  521.5 8.2 %collective-permute-start.42 = (bf16[2,64,512]{2,1,0:T(8,128)(2,1)S(1)}, bf16[2,64,512]{2,1,0:T(8,128)(2,1)S(1)}, u32[]{:S(2)}, u32[]{:S(2)}) collective-permute-start(bf16[2,64,512]{2,1,0:T(8,128)(2,1)S(1)} %fusion.21), channel_id=1, source_target_pairs={{0,1},{1,0},{2,3},{3,2},{4,5},{5,4},{6,7},{7,6},{8,9},{9,8},{10,11... | collective-permute-start | bytes 393224 | tf_op jit(solution)/shard_map/ppermute | solution.py:846
  522.6 9.5 %collective-permute-start.46 = (bf16[2,64,512]{2,1,0:T(8,128)(2,1)S(1)}, bf16[2,64,512]{2,1,0:T(8,128)(2,1)S(1)}, u32[]{:S(2)}, u32[]{:S(2)}) collective-permute-start(bf16[2,64,512]{2,1,0:T(8,128)(2,1)S(1)} %fusion.20), channel_id=1, source_target_pairs={{0,1},{1,0},{2,3},{3,2},{4,5},{5,4},{6,7},{7,6},{8,9},{9,8},{10,11... | collective-permute-start | bytes 393224 | tf_op jit(solution)/shard_map/ppermute | solution.py:846
  524.8 11.2 %collective-permute-start.54 = (f32[4,6144]{1,0:T(4,128)S(1)}, f32[4,6144]{1,0:T(4,128)S(1)}, u32[]{:S(2)}, u32[]{:S(2)}) collective-permute-start(f32[4,6144]{1,0:T(4,128)S(1)} %maximum_select_fusion.6), channel_id=1, source_target_pairs={{0,16},{4,20},{8,24},{12,28},{16,0},{20,4},{24,8},{28,12},{1,17},{... | collective-permute-start | bytes 294920 | tf_op jit(solution)/shard_map/ppermute | solution.py:846
  527.5 21.4 %collective-permute-start.48 = (bf16[32,4096]{1,0:T(8,128)(2,1)S(1)}, bf16[32,4096]{1,0:T(8,128)(2,1)S(1)}, u32[]{:S(2)}, u32[]{:S(2)}) collective-permute-start(bf16[32,4096]{1,0:T(8,128)(2,1)S(1)} %get-tuple-element.274), channel_id=1, source_target_pairs={{0,2},{1,3},{2,0},{3,1},{4,6},{5,7},{6,4},{7,5},{8,10},{9,11},{10,... | collective-permute-start | bytes 786440 | tf_op jit(solution)/shard_map/ppermute | solution.py:846
  531.4 14.5 %collective-permute-start.45 = (bf16[64,512]{1,0:T(8,128)(2,1)S(1)}, bf16[64,512]{1,0:T(8,128)(2,1)S(1)}, u32[]{:S(2)}, u32[]{:S(2)}) collective-permute-start(bf16[64,512]{1,0:T(8,128)(2,1)S(1)} %get-tuple-element.271), channel_id=1, source_target_pairs={{0,2},{1,3},{2,0},{3,1},{4,6},{5,7},{6,4},{7,5},{8,10},{9,11},{10,... | collective-permute-start | bytes 196616 | tf_op jit(solution)/shard_map/ppermute | solution.py:846
  533.8 12.1 %collective-permute-start.47 = (bf16[64,512]{1,0:T(8,128)(2,1)S(1)}, bf16[64,512]{1,0:T(8,128)(2,1)S(1)}, u32[]{:S(2)}, u32[]{:S(2)}) collective-permute-start(bf16[64,512]{1,0:T(8,128)(2,1)S(1)} %get-tuple-element.267), channel_id=1, source_target_pairs={{0,2},{1,3},{2,0},{3,1},{4,6},{5,7},{6,4},{7,5},{8,10},{9,11},{10,... | collective-permute-start | bytes 196616 | tf_op jit(solution)/shard_map/ppermute | solution.py:846
  (40 other events, 169.6 us)
Sparse Core Ops, SparseCore 0:
  46.0 66.2 all-gather.2
  134.4 98.1 all-gather.4
  309.7 137.9 reduce-scatter.1

commit v4 on v3

--- a/solution.py
+++ b/solution.py
@@ -285,7 +285,7 @@
         out_shape=[jax.ShapeDtypeStruct((rows, width), BF)] * count
         + [jax.ShapeDtypeStruct((heads, length), F32)],
         scratch_shapes=[pltpu.VMEM((length, 3 * width), BF)],
-        compiler_params=params(60),
+        compiler_params=params(50),
         cost_estimate=cost(16 * length * length * DH * heads, 8 * length * width),
     )(*pieces)
     return outs[:count], outs[count]
@@ -742,7 +742,7 @@
         ),
         out_shape=jax.ShapeDtypeStruct((width, groups * cols) if held is None else held.shape, BF),
         input_output_aliases={2 + groups: 0} if given else {},
-        compiler_params=params(60),
+        compiler_params=params(40),
         cost_estimate=cost(rows * width, 1024),
     )(me, normed, *pieces, *given)
 
@@ -775,7 +775,7 @@
         in_specs=[whole(a.shape) for a in (*given, *states)],
         out_specs=[whole(shape) for shape in shapes],
         out_shape=[jax.ShapeDtypeStruct(shape, F32) for shape in shapes],
-        compiler_params=params(60),
+        compiler_params=params(40),
         cost_estimate=cost(moved, moved),
     )(*given, *states)
 
@@ -1082,7 +1082,7 @@
         axis=1,
     )
     early = (cos_all, sin_all, cos_own, sin_own, cond, grad, down_cot)
-    second_own = gather_pairwise(after(second_own, modulation), seq_bits, early, (normed,))
+    second_own = gather_pairwise(after(second_own, modulation), seq_bits, early, (packed[0][0],))
     second_full = lax.all_gather(second_own, "dp", axis=0, tiled=True)
     qkv_chunks, attended = [], []
     for pieces in arrived:
@@ -1156,22 +1156,23 @@
             ).astype(BF)
         else:
             qkv_part = qkv_grad(normed, pieces, place, None if c else qkv_part)
-        qkv_sums.append(full_sum(qkv_part, planes[::-1]))
-        leave(qkv_sums[-1])
-        if c < count - 1:
-            leave(qkv_sums[-1])
-    ffn_sum = ScatterSum(ffn_part, rising, seq_bits)
-    ffn_sum.step(late=(cot_chunks[-1][-1],))
-    sent.append(ffn_sum.sent)
+        qkv_sums.append(full_sum(qkv_part, planes if c % 2 else planes[::-1]))
+        sent.append(qkv_part)
+    for part in qkv_sums:
+        part.hold(*cot_chunks[-1][1:])
+        leave(part)
     for part in qkv_sums:
         leave(part)
+    ffn_sum = ScatterSum(ffn_part, rising, seq_bits)
+    leave(ffn_sum)
     cot_chunks[-1] = [after(piece, sent[-1]) for piece in cot_chunks[-1]]
     hidden_grad, frames_grad, skip_grad, last_sums = last_back(
         cot_chunks, hidden, middle_grad, first_full, mod, owned, here
     )
-    skip_cot = after(hidden_grad, *[part.terms[-1] for part in qkv_sums])
+    skip_cot = after(hidden_grad, qkv_sums[-1].terms[-1])
+    skip_later = after(skip_cot, qkv_sums[0].terms[-1])
     skip_part = jnp.concatenate(
-        [dot_tn(frames, skip_cot).astype(BF), dot_tn(skips, skip_cot).astype(BF)], axis=0
+        [dot_tn(frames, skip_cot).astype(BF), dot_tn(skips, skip_later).astype(BF)], axis=0
     )
     skip_part = after(skip_part, ffn_sum.terms[-1])
     half = width // 2
@@ -1183,12 +1184,15 @@
         [last_sums[0], last_sums[1], mid_sums[0], mid_sums[1], mid_sums[2], mid_sums[3]]
     ).reshape(1, 6 * width)
     mod_cots = ModulationCots(mod_cot)
+    while mod_cots.order[0][0] == "seq":
+        mod_cots.step(skip_part)
+    mod_cots.settle()
     time_rows = time_own.astype(F32)
     qkv_sum, marks = None, []
     rows_held = owned * seq
     for part in [ffn_sum] + qkv_sums:
         part.hold(hidden_grad)
-    mod_cots.step()
+    ffn_sum.hold(mod_cots.own)
     while skip_sums[0].order or qkv_sum is None or qkv_sum.order:
         for part in skip_sums:
             if part.order:
@@ -1197,7 +1201,7 @@
         if mod_cots.order:
             mod_cots.step(sent[-1])
         later = [part for part in qkv_sums if part.order]
-        for part in later + ([ffn_sum] if ffn_sum.order else []):
+        for part in ([ffn_sum] if ffn_sum.order else []) + later:
             leave(part)
         if qkv_sum is not None and qkv_sum.order and len(marks) > 3:
             leave(qkv_sum)

time: 569 us -> 535 us (0.940)
  Pallas kernels: 205 us -> 188 us
  other arithmetic: 41.1 us -> 31.2 us
    reduce_scatter x1, waiting for transfers between devices: 17.7 us -> 4.78 us  [per_device(): lax.psum_scatter(ffn_whole, 'dp', scatter_dimension=0, tiled=True)]
    ppermute x34, waiting for transfers between devices: 92.7 us -> 103 us  [swap(): lax.ppermute(values, axis, [(i, i ^ 1 << bit) for i in range(lax.axis_siz...]
    pallas_call x4, Pallas kernels: 14.1 us -> 6.93 us  [update(): pl.pallas_call(functools.partial(update_kernel, grads_of, rates), grid=(1...]
    convert_element_type x12, other arithmetic: 16.3 us -> 9.3 us  [step(): total = sum((t.astype(F32) for t in leaving)).astype(total.dtype)]
  transfers between devices with their start and end apart: 58 -> 58, of which waited for: 25 -> 27; matrix products, arithmetic and copies ran while one was open for 10% -> 8% of each run, Pallas kernels for 28% -> 27%
where the time goes in v4:
time: 535 us; the launch traced here: 526 us
  Pallas kernels  188 us (35%)
  waiting for transfers between devices  176 us (33%)
  starting transfers between devices  86.8 us (16%)
  other arithmetic  31.2 us (6%)
  local copies, waits for them, and re-layouts  22.5 us (4%)
  between operations  16.5 us (3%)
  matrix products  5.47 us (1%)
    ppermute x34, waiting for transfers between devices, swap(): lax.ppermute(values, axis, [(i, i ^ 1 << bit) for i in range(lax.axis_siz...  103 us
    ppermute x21, waiting for transfers between devices, exchange(): lax.ppermute(pieces[d], 'seq', [(i, i ^ d) for i in places])  60.8 us
    pallas_call x2, Pallas kernels, attend_back(): pl.pallas_call(functools.partial(attend_back_kernel, heads, block, count)...  55.8 us
    ppermute x21, starting transfers between devices, exchange(): lax.ppermute(pieces[d], 'seq', [(i, i ^ d) for i in places])  46.4 us
    ppermute x34, starting transfers between devices, swap(): lax.ppermute(values, axis, [(i, i ^ 1 << bit) for i in range(lax.axis_siz...  40.3 us
    pallas_call x2, Pallas kernels, attend(): pl.pallas_call(functools.partial(attend_kernel, heads, block, count), gri...  29.7 us
    pallas_call x1, Pallas kernels, ffn(): pl.pallas_call(functools.partial(ffn_kernel, piece), grid=(steps,), in_sp...  24.3 us
    pallas_call x1, Pallas kernels, ffn_grad(): pl.pallas_call(functools.partial(ffn_grad_kernel, owned if owned % 16 ==...  14.5 us
  transfers between devices with their start and end apart: 58, of which 27 were waited for; matrix products, arithmetic and copies ran while one was open for 8% of the time, Pallas kernels for 27%

profile of v4, /device:TPU:0, one launch (start us, length us, event | category | flops | bytes accessed | tf_op | source)
XLA Modules:
  0.0 526.4 jit_solution(6250908583503270494)
XLA Ops:
  9.5 4.1 collective-permute-start
  13.6 14.7 %collective-permute-done = bf16[1,32,5120]{2,1,0:T(8,128)(2,1)S(1)} collective-permute-done((bf16[1,32,5120]{2,1,0:T(8,128)(2,1)S(1)}, bf16[1,32,5120]{2,1,0:T(8,128)(2,1)S(1)}, u32[]{:S(2)}, u32[]{:S(2)}) %collective-permute-start) | collective-permute-done | bytes 327712 | tf_op jit(solution)/shard_map/ppermute | solution.py:846
  29.3 15.1 %collective-permute-done.1 = bf16[2,32,5120]{2,1,0:T(8,128)(2,1)S(1)} collective-permute-done((bf16[2,32,5120]{2,1,0:T(8,128)(2,1)S(1)}, bf16[2,32,5120]{2,1,0:T(8,128)(2,1)S(1)}, u32[]{:S(2)}, u32[]{:S(2)}) %collective-permute-start.1) | collective-permute-done | bytes 655392 | tf_op jit(solution)/shard_map/ppermute | solution.py:846
  47.9 3.7 fusion.17
  52.7 3.0 pad_maximum_fusion.1
  57.3 3.9 collective-permute-done.3
  63.6 2.2 collective-permute-done.4
  66.5 3.1 collective-permute-start.5
  71.4 1.8 collective-permute-start.6
  77.1 3.0 collective-permute-start.8
  82.9 21.0 %collective-permute-done.8 = bf16[1,32,9216]{2,1,0:T(8,128)(2,1)S(1)} collective-permute-done((bf16[1,32,9216]{2,1,0:T(8,128)(2,1)S(1)}, bf16[1,32,9216]{2,1,0:T(8,128)(2,1)S(1)}, u32[]{:S(2)}, u32[]{:S(2)}) %collective-permute-start.8) | collective-permute-done | bytes 589856 | tf_op jit(solution)/shard_map/ppermute | solution.py:846
  104.8 7.5 %all-gather.3.cloned.1.call-done.packed_ref.wq_ref.wk_ref.wv_ref.refs_10_.refs_11_.refs_12_.refs_13_ = bf16[1024,5120]{1,0:T(8,128)(2,1)} async-done(((bf16[128,5120]{1,0:T(8,128)(2,1)}), bf16[1024,5120]{1,0:T(8,128)(2,1)}) %all-gather.3.cloned.1.call-update) | async-done | bytes 10485776 | tf_op jit(solution)/shard_map/all_gather | solution.py:1037
  112.2 7.3 %shard_map.244 = (f32[512,1024]{1,0:T(8,128)}, bf16[512,1024]{1,0:T(8,128)(2,1)}) custom-call(bf16[512,1024]{1,0:T(8,128)(2,1)} %bitcast.318, bf16[512,1024]{1,0:T(8,128)(2,1)} %bitcast.319, bf16[512,1024]{1,0:T(8,128)(2,1)} %bitcast_select_fusion.1.cond_ref, ...), custom_call_target="tpu_custom_call" | custom-call | flops 2147483648 | bytes 10485760 | tf_op jit(solution)/shard_map/pallas_call | solution.py:168
  119.5 9.1 %shard_map.245 = (bf16[512,384]{1,0:T(8,128)(2,1)}, bf16[512,384]{1,0:T(8,128)(2,1)}, bf16[512,384]{1,0:T(8,128)(2,1)}, bf16[512,384]{1,0:T(8,128)(2,1)}, bf16[5...) custom-call(s32[1]{0:T(128)} %bitcast.me_ref, ...), custom_call_target="tpu_custom_call" | custom-call | flops 3221225472 | bytes 10485760 | tf_op jit(solution)/shard_map/pallas_call | solution.py:218
  128.6 3.2 collective-permute-done.9
  133.9 2.4 collective-permute-start.11
  136.3 2.1 collective-permute-start.7
  138.3 2.3 collective-permute-start.15
  140.7 7.2 %collective-permute-done.11.refs_3_ = bf16[512,384]{1,0:T(8,128)(2,1)S(1)} collective-permute-done((bf16[512,384]{1,0:T(8,128)(2,1)S(1)}, bf16[512,384]{1,0:T(8,128)(2,1)S(1)}, u32[]{:S(2)}, u32[]{:S(2)}) %collective-permute-start.11) | collective-permute-done | bytes 393248 | tf_op jit(solution)/shard_map/ppermute | solution.py:916
  147.9 17.3 %collective-permute-start.13 = (bf16[512,384]{1,0:T(8,128)(2,1)S(1)}, bf16[512,384]{1,0:T(8,128)(2,1)S(1)}, u32[]{:S(2)}, u32[]{:S(2)}) collective-permute-start(bf16[512,384]{1,0:T(8,128)(2,1)S(1)} %copy-done.50), channel_id=1, source_target_pairs={{0,1},{1,0},{2,3},{3,2},{4,5},{5,4},{6,7},{7,6},{8,9},{9,8},{10,11... | collective-permute-start | bytes 1179656 | tf_op jit(solution)/shard_map/ppermute | solution.py:916
  165.1 22.7 %collective-permute-done.10.refs_2_ = bf16[512,384]{1,0:T(8,128)(2,1)S(1)} collective-permute-done((bf16[512,384]{1,0:T(8,128)(2,1)S(1)}, bf16[512,384]{1,0:T(8,128)(2,1)S(1)}, u32[]{:S(2)}, u32[]{:S(2)}) %collective-permute-start.10) | collective-permute-done | bytes 393248 | tf_op jit(solution)/shard_map/ppermute | solution.py:916
  187.9 14.9 %shard_map.246 = (bf16[512,128]{1,0:T(8,128)(2,1)S(1)}, bf16[512,128]{1,0:T(8,128)(2,1)S(1)}, bf16[512,128]{1,0:T(8,128)(2,1)S(1)}, bf16[512,128]{1,0:T(8,128)(2,1)S(1)}, f32[2,2048]{1,0:T(2,128)S(1)}) custom-call(bf16[512,384]{1,0:T(8,128)(2,1)S(1)} %copy-done.23, bf16[512,384]{1,0:T(8,128)(2,1)S(1)} %collective-permute-done.7.refs_1_, ...), custom_call_target="tpu_custom_call" | custom-call | flops 8589934592 | bytes 2097152 | tf_op jit(solution)/shard_map/pallas_call | solution.py:279
  204.1 1.9 collective-permute-start.17
  206.0 14.9 %shard_map.247 = (bf16[512,128]{1,0:T(8,128)(2,1)S(1)}, bf16[512,128]{1,0:T(8,128)(2,1)S(1)}, bf16[512,128]{1,0:T(8,128)(2,1)S(1)}, bf16[512,128]{1,0:T(8,128)(2,1)S(1)}, f32[2,2048]{1,0:T(2,128)S(1)}) custom-call(bf16[512,384]{1,0:T(8,128)(2,1)S(1)} %copy-done.22, bf16[512,384]{1,0:T(8,128)(2,1)S(1)} %collective-permute-done.13.refs_1_, ...), custom_call_target="tpu_custom_call" | custom-call | flops 8589934592 | bytes 2097152 | tf_op jit(solution)/shard_map/pallas_call | solution.py:279
  221.6 2.6 collective-permute-start.18
  224.3 2.3 collective-permute-start.19
  226.7 2.0 collective-permute-start.20
  228.6 2.8 collective-permute-done.12.refs_1_
  231.5 2.8 collective-permute-done.20.refs_7_
  235.0 6.0 %shard_map.248 = (bf16[512,1024]{1,0:T(8,128)(2,1)}, f32[512,1024]{1,0:T(8,128)}, f32[512,1024]{1,0:T(8,128)}, bf16[512,1024]{1,0:T(8,128)(2,1)}) custom-call(s32[1]{0:T(128)} %bitcast.me_ref, bf16[512,128]{1,0:T(8,128)(2,1)} %copy-done.21, bf16[512,128]{1,0:T(8,128)(2,1)} %copy-done.45, bf16[512,128]{1,0:T(8,128)(2,1)} %copy-done.43, ...), custom_call_target="tpu_custom_call" | custom-call | flops 1073741824 | bytes 11534336 | tf_op jit(solution)/shard_map/pallas_call | solution.py:412
  241.0 24.3 %shard_map.249 = (f32[512,1024]{1,0:T(8,128)}, f32[512,1024]{1,0:T(8,128)}, bf16[512,4096]{1,0:T(8,128)(2,1)}, bf16[512,4096]{1,0:T(8,128)(2,1)}) custom-call(bf16[512,1024]{1,0:T(8,128)(2,1)} %get-tuple-element.181.x_ref, bf16[512,1024]{1,0:T(8,128)(2,1)} %get-tuple-element.267.dc_ref, ...), custom_call_target="tpu_custom_call" | custom-call | flops 17179869184 | bytes 33554432 | tf_op jit(solution)/shard_map/pallas_call | solution.py:511
  265.2 8.4 %shard_map.250 = (bf16[512,1024]{1,0:T(8,128)(2,1)}, f32[512,1024]{1,0:T(8,128)}, bf16[512,1024]{1,0:T(8,128)(2,1)}, f32[8,1024]{1,0:T(8,128)}, bf16[512,256]{1,...) custom-call(s32[1]{0:T(128)} %bitcast.me_ref, ...), custom_call_target="tpu_custom_call" | custom-call | flops 1073741824 | bytes 16777216 | tf_op jit(solution)/shard_map/pallas_call | solution.py:595
  273.7 4.1 shard_map.251.refs_5_
  282.2 14.5 %shard_map.252 = bf16[1024,8192]{1,0:T(8,128)(2,1)} custom-call(bf16[512,1024]{1,0:T(8,128)(2,1)} %get-tuple-element.181.x_ref, bf16[512,1024]{1,0:T(8,128)(2,1)} %get-tuple-element.267.dc_ref, bf16[512,4096]{1,0:T(8,128)(2,1)} %get-tuple-element.182.activated_ref, bf16[512,4096]{1,0:T(8,128)(2,1)} %get-tuple-element.183.up_cot_ref), custom_call_target="tpu_custom_call" | custom-call | flops 8589934592 | bytes 33554432 | tf_op jit(solution)/shard_map/pallas_call | solution.py:540
  296.7 3.6 collective-permute-done.22.refs_6_
  301.1 27.7 %shard_map.253 = (bf16[512,384]{1,0:T(8,128)(2,1)}, bf16[512,384]{1,0:T(8,128)(2,1)}, bf16[512,384]{1,0:T(8,128)(2,1)}, bf16[512,384]{1,0:T(8,128)(2,1)}) custom-call(bf16[512,384]{1,0:T(8,128)(2,1)} %get-tuple-element.142.refs_0_, bf16[512,384]{1,0:T(8,128)(2,1)} %copy-done.29, bf16[512,384]{1,0:T(8,128)(2,1)} %copy-done.28, bf16[512,384]{1,0:T(8,128)(2,1)} %copy-done.27, ...), custom_call_target="tpu_custom_call" | custom-call | flops 12884901888 | bytes 5242880 | tf_op jit(solution)/shard_map/pallas_call | solution.py:365
  330.4 3.2 collective-permute-start.25
  333.6 28.0 %shard_map.254 = (bf16[512,384]{1,0:T(8,128)(2,1)}, bf16[512,384]{1,0:T(8,128)(2,1)}, bf16[512,384]{1,0:T(8,128)(2,1)}, bf16[512,384]{1,0:T(8,128)(2,1)}) custom-call(bf16[512,384]{1,0:T(8,128)(2,1)} %get-tuple-element.154.refs_0_, bf16[512,384]{1,0:T(8,128)(2,1)} %copy-done.26, bf16[512,384]{1,0:T(8,128)(2,1)} %copy-done.25, bf16[512,384]{1,0:T(8,128)(2,1)} %copy-done.24, ...), custom_call_target="tpu_custom_call" | custom-call | flops 12884901888 | bytes 5242880 | tf_op jit(solution)/shard_map/pallas_call | solution.py:365
  361.7 2.4 collective-permute-start.29
  366.1 2.8 copy-done
  368.9 3.8 shard_map.255
  372.8 2.3 copy-done.1
  375.8 20.9 %collective-permute-done.28.refs_3_.refs_6_ = bf16[512,384]{1,0:T(8,128)(2,1)S(1)} collective-permute-done((bf16[512,384]{1,0:T(8,128)(2,1)}, bf16[512,384]{1,0:T(8,128)(2,1)S(1)}, u32[]{:S(2)}, u32[]{:S(2)}) %collective-permute-start.28) | collective-permute-done | bytes 393248 | tf_op jit(solution)/shard_map/ppermute | solution.py:916
  396.7 3.6 shard_map.256
  404.0 3.5 collective-permute-done.31
  407.4 3.1 fusion
  412.1 2.3 fusion.1
  414.9 4.8 reduce-scatter.2.cloned.1.call-done
  419.7 2.3 dynamic-slice_bitcast_fusion.4
  421.9 3.1 collective-permute-start.34
  425.0 14.4 %shard_map.257 = (bf16[512,1024]{1,0:T(8,128)(2,1)}, bf16[512,1024]{1,0:T(8,128)(2,1)}, bf16[512,1024]{1,0:T(8,128)(2,1)}, f32[8,1024]{1,0:T(8,128)}) custom-call(s32[1]{0:T(128)} %bitcast.me_ref, bf16[512,384]{1,0:T(8,128)(2,1)} %get-tuple-element.191.refs_1_.refs_0_, bf16[512,384]{1,0:T(8,128)(2,1)} %copy-done.14, bf16[512,384]{1,0:T(8,128)(2,1)} %copy-done.13, ...), custom_call_target="tpu_custom_call" | custom-call | flops 1073741824 | bytes 2097152 | tf_op jit(solution)/shard_map/pallas_call | solution.py:660
  439.4 4.7 collective-permute-done.33
  446.6 2.8 convert_bitcast_fusion.1
  451.7 2.5 collective-permute-start.37
  458.4 2.2 collective-permute-start.51
  468.4 11.6 %collective-permute-done.39 = bf16[2,2,32,2560]{3,2,1,0:T(8,128)(2,1)S(1)} collective-permute-done((bf16[2,2,32,2560]{3,2,1,0:T(8,128)(2,1)S(1)}, bf16[2,2,32,2560]{3,2,1,0:T(8,128)(2,1)S(1)}, u32[]{:S(2)}, u32[]{:S(2)}) %collective-permute-start.39) | collective-permute-done | bytes 655392 | tf_op jit(solution)/shard_map/ppermute | solution.py:846
  480.5 1.9 fusion.3
  484.6 3.3 collective-permute-done.38
  488.7 2.5 collective-permute-done.43
  493.6 2.2 shard_map.260
  500.4 3.4 collective-permute-done.44
  504.7 2.0 collective-permute-done.48
  507.6 2.4 shard_map.261
  509.9 7.3 %collective-permute-done.49.refs_3_ = bf16[64,512]{1,0:T(8,128)(2,1)S(1)} collective-permute-done((bf16[64,512]{1,0:T(8,128)(2,1)S(1)}, bf16[64,512]{1,0:T(8,128)(2,1)S(1)}, u32[]{:S(2)}, u32[]{:S(2)}) %collective-permute-start.49) | collective-permute-done | bytes 65568 | tf_op jit(solution)/shard_map/ppermute | solution.py:846
  (284 shorter events, 71.3 us)
Async XLA Ops:
  7.2 105.1 %all-gather.3.cloned.1.call-start = ((), (), s32[]{:S(2)}) async-start(), calls=%async_computation.1 | async-start | bytes 11796480 | tf_op jit(solution)/shard_map/all_gather | solution.py:1037
  9.5 18.8 %collective-permute-start = (bf16[1,32,5120]{2,1,0:T(8,128)(2,1)S(1)}, bf16[1,32,5120]{2,1,0:T(8,128)(2,1)S(1)}, u32[]{:S(2)}, u32[]{:S(2)}) collective-permute-start(bf16[1,32,5120]{2,1,0:T(8,128)(2,1)S(1)} %get-tuple-element.284), channel_id=1, source_target_pairs={{0,2},{1,3},{2,0},{3,1},{4,6},{5,7},{6,4},{7,5},{8,10},{9,11},{10,... | collective-permute-start | bytes 983048 | tf_op jit(solution)/shard_map/ppermute | solution.py:846
  28.5 16.0 %collective-permute-start.1 = (bf16[2,32,5120]{2,1,0:T(8,128)(2,1)S(1)}, bf16[2,32,5120]{2,1,0:T(8,128)(2,1)S(1)}, u32[]{:S(2)}, u32[]{:S(2)}) collective-permute-start(bf16[2,32,5120]{2,1,0:T(8,128)(2,1)S(1)} %maximum_select_fusion.4), channel_id=1, source_target_pairs={{0,1},{1,0},{2,3},{3,2},{4,5},{5,4},{6,7},{7,6},{8,9},{9,8},{10,11... | collective-permute-start | bytes 1966088 | tf_op jit(solution)/shard_map/ppermute | solution.py:846
  45.9 188.4 %all-gather.5.cloned.1.call-start = ((), (), s32[]{:S(2)}) async-start(), calls=%async_computation.2 | async-start | bytes 21233664 | tf_op jit(solution)/shard_map/all_gather | solution.py:1086
  47.6 8.1 %collective-permute-start.2 = (f32[2,2,1,6144]{3,2,1,0:T(1,128)S(1)}, f32[2,2,1,6144]{3,2,1,0:T(1,128)S(1)}, u32[]{:S(2)}, u32[]{:S(2)}) collective-permute-start(f32[2,2,1,6144]{3,2,1,0:T(1,128)S(1)} %constant_dynamic-slice_fusion), channel_id=1, source_target_pairs={{0,4},{4,0},{8,12},{12,8},{16,20},{20,16},{24,28},{28,24},{1,5},{5... | collective-permute-start | bytes 294920 | tf_op jit(solution)/shard_map/ppermute | solution.py:846
  55.9 5.2 collective-permute-start.3
  61.2 4.5 collective-permute-start.4
  66.5 4.9 collective-permute-start.5
  71.4 4.4 collective-permute-start.6
  77.1 26.8 %collective-permute-start.8 = (bf16[1,32,9216]{2,1,0:T(8,128)(2,1)S(1)}, bf16[1,32,9216]{2,1,0:T(8,128)(2,1)S(1)}, u32[]{:S(2)}, u32[]{:S(2)}) collective-permute-start(bf16[1,32,9216]{2,1,0:T(8,128)(2,1)S(1)} %bitcast.320), channel_id=1, source_target_pairs={{0,2},{1,3},{2,0},{3,1},{4,6},{5,7},{6,4},{7,5},{8,10},{9,11},{10,... | collective-permute-start | bytes 1769480 | tf_op jit(solution)/shard_map/ppermute | solution.py:846
  104.0 27.7 %collective-permute-start.9 = (bf16[2,32,9216]{2,1,0:T(8,128)(2,1)S(1)}, bf16[2,32,9216]{2,1,0:T(8,128)(2,1)S(1)}, u32[]{:S(2)}, u32[]{:S(2)}) collective-permute-start(bf16[2,32,9216]{2,1,0:T(8,128)(2,1)S(1)} %maximum_select_fusion.2), channel_id=1, source_target_pairs={{0,1},{1,0},{2,3},{3,2},{4,5},{5,4},{6,7},{7,6},{8,9},{9,8},{10,11... | collective-permute-start | bytes 3538952 | tf_op jit(solution)/shard_map/ppermute | solution.py:846
  133.8 54.1 %copy-start.23 = (bf16[512,384]{1,0:T(8,128)(2,1)S(1)}, bf16[512,384]{1,0:T(8,128)(2,1)}, u32[]{:S(2)}) copy-start(bf16[512,384]{1,0:T(8,128)(2,1)} %get-tuple-element.142.refs_0_) | copy-start | bytes 1179652
  133.8 285.9 %reduce-scatter.2.cloned.1.call-start = ((), (), s32[]{:S(2)}) async-start(), calls=%async_computation.3 | async-start | bytes 18874368 | tf_op jit(solution)/shard_map/reduce_scatter | solution.py:1127
  133.9 14.0 %collective-permute-start.11 = (bf16[512,384]{1,0:T(8,128)(2,1)S(1)}, bf16[512,384]{1,0:T(8,128)(2,1)S(1)}, u32[]{:S(2)}, u32[]{:S(2)}) collective-permute-start(bf16[512,384]{1,0:T(8,128)(2,1)S(1)} %copy-done.55), channel_id=1, source_target_pairs={{0,3},{1,2},{2,1},{3,0},{4,7},{5,6},{6,5},{7,4},{8,11},{9,10},{10,... | collective-permute-start | bytes 1179656 | tf_op jit(solution)/shard_map/ppermute | solution.py:916
  136.3 51.6 %collective-permute-start.10 = (bf16[512,384]{1,0:T(8,128)(2,1)S(1)}, bf16[512,384]{1,0:T(8,128)(2,1)S(1)}, u32[]{:S(2)}, u32[]{:S(2)}) collective-permute-start(bf16[512,384]{1,0:T(8,128)(2,1)S(1)} %copy-done.54), channel_id=1, source_target_pairs={{0,2},{1,3},{2,0},{3,1},{4,6},{5,7},{6,4},{7,5},{8,10},{9,11},{10,... | collective-permute-start | bytes 1179656 | tf_op jit(solution)/shard_map/ppermute | solution.py:916
  136.3 51.6 %collective-permute-start.7 = (bf16[512,384]{1,0:T(8,128)(2,1)S(1)}, bf16[512,384]{1,0:T(8,128)(2,1)S(1)}, u32[]{:S(2)}, u32[]{:S(2)}) collective-permute-start(bf16[512,384]{1,0:T(8,128)(2,1)S(1)} %copy-done.53), channel_id=1, source_target_pairs={{0,1},{1,0},{2,3},{3,2},{4,5},{5,4},{6,7},{7,6},{8,9},{9,8},{10,11... | collective-permute-start | bytes 1179656 | tf_op jit(solution)/shard_map/ppermute | solution.py:916
  138.3 65.7 %collective-permute-start.15 = (bf16[512,384]{1,0:T(8,128)(2,1)S(1)}, bf16[512,384]{1,0:T(8,128)(2,1)S(1)}, u32[]{:S(2)}, u32[]{:S(2)}) collective-permute-start(bf16[512,384]{1,0:T(8,128)(2,1)S(1)} %copy-done.52), channel_id=1, source_target_pairs={{0,3},{1,2},{2,1},{3,0},{4,7},{5,6},{6,5},{7,4},{8,11},{9,10},{10,... | collective-permute-start | bytes 1179656 | tf_op jit(solution)/shard_map/ppermute | solution.py:916
  140.7 63.4 %collective-permute-start.14 = (bf16[512,384]{1,0:T(8,128)(2,1)S(1)}, bf16[512,384]{1,0:T(8,128)(2,1)S(1)}, u32[]{:S(2)}, u32[]{:S(2)}) collective-permute-start(bf16[512,384]{1,0:T(8,128)(2,1)S(1)} %copy-done.51), channel_id=1, source_target_pairs={{0,2},{1,3},{2,0},{3,1},{4,6},{5,7},{6,4},{7,5},{8,10},{9,11},{10,... | collective-permute-start | bytes 1179656 | tf_op jit(solution)/shard_map/ppermute | solution.py:916
  147.9 54.9 %copy-start.27 = (bf16[512,384]{1,0:T(8,128)(2,1)}, bf16[512,384]{1,0:T(8,128)(2,1)S(1)}, u32[]{:S(2)}) copy-start(bf16[512,384]{1,0:T(8,128)(2,1)S(1)} %collective-permute-done.11.refs_3_) | copy-start | bytes 1179652
  147.9 58.1 %copy-start.22 = (bf16[512,384]{1,0:T(8,128)(2,1)S(1)}, bf16[512,384]{1,0:T(8,128)(2,1)}, u32[]{:S(2)}) copy-start(bf16[512,384]{1,0:T(8,128)(2,1)} %get-tuple-element.154.refs_0_) | copy-start | bytes 1179652
  147.9 56.2 %collective-permute-start.13 = (bf16[512,384]{1,0:T(8,128)(2,1)S(1)}, bf16[512,384]{1,0:T(8,128)(2,1)S(1)}, u32[]{:S(2)}, u32[]{:S(2)}) collective-permute-start(bf16[512,384]{1,0:T(8,128)(2,1)S(1)} %copy-done.50), channel_id=1, source_target_pairs={{0,1},{1,0},{2,3},{3,2},{4,5},{5,4},{6,7},{7,6},{8,9},{9,8},{10,11... | collective-permute-start | bytes 1179656 | tf_op jit(solution)/shard_map/ppermute | solution.py:916
  204.1 22.6 %collective-permute-start.17 = (bf16[512,128]{1,0:T(8,128)(2,1)S(1)}, bf16[512,128]{1,0:T(8,128)(2,1)S(1)}, u32[]{:S(2)}, u32[]{:S(2)}) collective-permute-start(bf16[512,128]{1,0:T(8,128)(2,1)S(1)} %get-tuple-element.165.refs_11_), channel_id=1, source_target_pairs={{0,3},{1,2},{2,1},{3,0},{4,7},{5,6},{6,5},{7,4},{8,11},{9,10},{10,... | collective-permute-start | bytes 393224 | tf_op jit(solution)/shard_map/ppermute | solution.py:916
  206.0 22.6 %collective-permute-start.16 = (bf16[512,128]{1,0:T(8,128)(2,1)S(1)}, bf16[512,128]{1,0:T(8,128)(2,1)S(1)}, u32[]{:S(2)}, u32[]{:S(2)}) collective-permute-start(bf16[512,128]{1,0:T(8,128)(2,1)S(1)} %get-tuple-element.163.refs_10_), channel_id=1, source_target_pairs={{0,2},{1,3},{2,0},{3,1},{4,6},{5,7},{6,4},{7,5},{8,10},{9,11},{10,... | collective-permute-start | bytes 393224 | tf_op jit(solution)/shard_map/ppermute | solution.py:916
  221.6 9.8 %collective-permute-start.18 = (bf16[512,128]{1,0:T(8,128)(2,1)S(1)}, bf16[512,128]{1,0:T(8,128)(2,1)S(1)}, u32[]{:S(2)}, u32[]{:S(2)}) collective-permute-start(bf16[512,128]{1,0:T(8,128)(2,1)S(1)} %get-tuple-element.167.refs_9_), channel_id=1, source_target_pairs={{0,1},{1,0},{2,3},{3,2},{4,5},{5,4},{6,7},{7,6},{8,9},{9,8},{10,11... | collective-permute-start | bytes 393224 | tf_op jit(solution)/shard_map/ppermute | solution.py:916
  224.2 7.2 %collective-permute-start.12 = (bf16[512,128]{1,0:T(8,128)(2,1)S(1)}, bf16[512,128]{1,0:T(8,128)(2,1)S(1)}, u32[]{:S(2)}, u32[]{:S(2)}) collective-permute-start(bf16[512,128]{1,0:T(8,128)(2,1)S(1)} %get-tuple-element.153.refs_9_), channel_id=1, source_target_pairs={{0,1},{1,0},{2,3},{3,2},{4,5},{5,4},{6,7},{7,6},{8,9},{9,8},{10,11... | collective-permute-start | bytes 393224 | tf_op jit(solution)/shard_map/ppermute | solution.py:916
  224.3 7.1 %collective-permute-start.19 = (bf16[512,128]{1,0:T(8,128)(2,1)S(1)}, bf16[512,128]{1,0:T(8,128)(2,1)S(1)}, u32[]{:S(2)}, u32[]{:S(2)}) collective-permute-start(bf16[512,128]{1,0:T(8,128)(2,1)S(1)} %get-tuple-element.168.refs_10_), channel_id=1, source_target_pairs={{0,2},{1,3},{2,0},{3,1},{4,6},{5,7},{6,4},{7,5},{8,10},{9,11},{10,... | collective-permute-start | bytes 393224 | tf_op jit(solution)/shard_map/ppermute | solution.py:916
  226.7 7.6 %collective-permute-start.20 = (bf16[512,128]{1,0:T(8,128)(2,1)S(1)}, bf16[512,128]{1,0:T(8,128)(2,1)S(1)}, u32[]{:S(2)}, u32[]{:S(2)}) collective-permute-start(bf16[512,128]{1,0:T(8,128)(2,1)S(1)} %get-tuple-element.169.refs_11_), channel_id=1, source_target_pairs={{0,3},{1,2},{2,1},{3,0},{4,7},{5,6},{6,5},{7,4},{8,11},{9,10},{10,... | collective-permute-start | bytes 393224 | tf_op jit(solution)/shard_map/ppermute | solution.py:916
  277.8 18.9 %collective-permute-start.21 = (bf16[512,256]{1,0:T(8,128)(2,1)S(1)}, bf16[512,256]{1,0:T(8,128)(2,1)S(1)}, u32[]{:S(2)}, u32[]{:S(2)}) collective-permute-start(bf16[512,256]{1,0:T(8,128)(2,1)S(1)} %copy-done.61), channel_id=1, source_target_pairs={{0,1},{1,0},{2,3},{3,2},{4,5},{5,4},{6,7},{7,6},{8,9},{9,8},{10,11... | collective-permute-start | bytes 786440 | tf_op jit(solution)/shard_map/ppermute | solution.py:916
  279.4 21.0 %collective-permute-start.22 = (bf16[512,256]{1,0:T(8,128)(2,1)S(1)}, bf16[512,256]{1,0:T(8,128)(2,1)S(1)}, u32[]{:S(2)}, u32[]{:S(2)}) collective-permute-start(bf16[512,256]{1,0:T(8,128)(2,1)S(1)} %copy-done.60), channel_id=1, source_target_pairs={{0,2},{1,3},{2,0},{3,1},{4,6},{5,7},{6,4},{7,5},{8,10},{9,11},{10,... | collective-permute-start | bytes 786440 | tf_op jit(solution)/shard_map/ppermute | solution.py:916
  280.6 19.8 %collective-permute-start.23 = (bf16[512,256]{1,0:T(8,128)(2,1)S(1)}, bf16[512,256]{1,0:T(8,128)(2,1)S(1)}, u32[]{:S(2)}, u32[]{:S(2)}) collective-permute-start(bf16[512,256]{1,0:T(8,128)(2,1)S(1)} %copy-done.59), channel_id=1, source_target_pairs={{0,3},{1,2},{2,1},{3,0},{4,7},{5,6},{6,5},{7,4},{8,11},{9,10},{10,... | collective-permute-start | bytes 786440 | tf_op jit(solution)/shard_map/ppermute | solution.py:916
  328.9 36.3 %collective-permute-start.26 = (bf16[512,384]{1,0:T(8,128)(2,1)}, bf16[512,384]{1,0:T(8,128)(2,1)S(1)}, u32[]{:S(2)}, u32[]{:S(2)}) collective-permute-start(bf16[512,384]{1,0:T(8,128)(2,1)} %get-tuple-element.198), channel_id=1, source_target_pairs={{0,3},{1,2},{2,1},{3,0},{4,7},{5,6},{6,5},{7,4},{8,11},{9,10},{10,... | collective-permute-start | bytes 1179656 | tf_op jit(solution)/shard_map/ppermute | solution.py:916
  330.4 35.7 %collective-permute-start.25 = (bf16[512,384]{1,0:T(8,128)(2,1)}, bf16[512,384]{1,0:T(8,128)(2,1)S(1)}, u32[]{:S(2)}, u32[]{:S(2)}) collective-permute-start(bf16[512,384]{1,0:T(8,128)(2,1)} %get-tuple-element.196), channel_id=1, source_target_pairs={{0,2},{1,3},{2,0},{3,1},{4,6},{5,7},{6,4},{7,5},{8,10},{9,11},{10,... | collective-permute-start | bytes 1179656 | tf_op jit(solution)/shard_map/ppermute | solution.py:916
  333.6 32.5 %collective-permute-start.24 = (bf16[512,384]{1,0:T(8,128)(2,1)}, bf16[512,384]{1,0:T(8,128)(2,1)S(1)}, u32[]{:S(2)}, u32[]{:S(2)}) collective-permute-start(bf16[512,384]{1,0:T(8,128)(2,1)} %get-tuple-element.192), channel_id=1, source_target_pairs={{0,1},{1,0},{2,3},{3,2},{4,5},{5,4},{6,7},{7,6},{8,9},{9,8},{10,11... | collective-permute-start | bytes 1179656 | tf_op jit(solution)/shard_map/ppermute | solution.py:916
  333.6 32.5 %copy-start.3 = (bf16[512,1024]{1,0:T(8,128)(2,1)S(1)}, bf16[512,1024]{1,0:T(8,128)(2,1)}, u32[]{:S(2)}) copy-start(bf16[512,1024]{1,0:T(8,128)(2,1)} %get-tuple-element.141.x_ref.refs_0_) | copy-start | bytes 3145732
  333.6 32.5 %copy-start.11 = (bf16[512,384]{1,0:T(8,128)(2,1)S(1)}, bf16[512,384]{1,0:T(8,128)(2,1)}, u32[]{:S(2)}) copy-start(bf16[512,384]{1,0:T(8,128)(2,1)} %get-tuple-element.191.refs_1_.refs_0_) | copy-start | bytes 1179652
  361.7 14.1 %collective-permute-start.29 = (bf16[512,384]{1,0:T(8,128)(2,1)}, bf16[512,384]{1,0:T(8,128)(2,1)S(1)}, u32[]{:S(2)}, u32[]{:S(2)}) collective-permute-start(bf16[512,384]{1,0:T(8,128)(2,1)} %get-tuple-element.204), channel_id=1, source_target_pairs={{0,3},{1,2},{2,1},{3,0},{4,7},{5,6},{6,5},{7,4},{8,11},{9,10},{10,... | collective-permute-start | bytes 1179656 | tf_op jit(solution)/shard_map/ppermute | solution.py:916
  364.0 32.7 %collective-permute-start.28 = (bf16[512,384]{1,0:T(8,128)(2,1)}, bf16[512,384]{1,0:T(8,128)(2,1)S(1)}, u32[]{:S(2)}, u32[]{:S(2)}) collective-permute-start(bf16[512,384]{1,0:T(8,128)(2,1)} %get-tuple-element.202), channel_id=1, source_target_pairs={{0,2},{1,3},{2,0},{3,1},{4,6},{5,7},{6,4},{7,5},{8,10},{9,11},{10,... | collective-permute-start | bytes 1179656 | tf_op jit(solution)/shard_map/ppermute | solution.py:916
  365.1 31.6 %collective-permute-start.27 = (bf16[512,384]{1,0:T(8,128)(2,1)}, bf16[512,384]{1,0:T(8,128)(2,1)S(1)}, u32[]{:S(2)}, u32[]{:S(2)}) collective-permute-start(bf16[512,384]{1,0:T(8,128)(2,1)} %get-tuple-element.200), channel_id=1, source_target_pairs={{0,1},{1,0},{2,3},{3,2},{4,5},{5,4},{6,7},{7,6},{8,9},{9,8},{10,11... | collective-permute-start | bytes 1179656 | tf_op jit(solution)/shard_map/ppermute | solution.py:916
  368.9 27.8 %copy-start.15 = (bf16[512,384]{1,0:T(8,128)(2,1)S(1)}, bf16[512,384]{1,0:T(8,128)(2,1)}, u32[]{:S(2)}) copy-start(bf16[512,384]{1,0:T(8,128)(2,1)} %get-tuple-element.213.refs_1_.refs_4_) | copy-start | bytes 1179652
  402.2 5.3 collective-permute-start.31
  403.5 8.6 %collective-permute-start.30 = (bf16[2,2,2,2,32,1536]{5,4,3,2,1,0:T(8,128)(2,1)}, bf16[2,2,2,2,32,1536]{5,4,3,2,1,0:T(8,128)(2,1)}, u32[]{:S(2)}, u32[]{:S(2)}) collective-permute-start(bf16[2,2,2,2,32,1536]{5,4,3,2,1,0:T(8,128)(2,1)} %dynamic-slice_bitcast_fusion.1), channel_id=1, source_target_pairs={{0,4},{4,0},{8,12},{12,8},{16,20},{20,16},{24,28},{28,24},{1,5},{5... | collective-permute-start | bytes 4718600 | tf_op jit(solution)/shard_map/ppermute | solution.py:846
  410.6 33.5 %collective-permute-start.33 = (bf16[2,2,2,32,2560]{4,3,2,1,0:T(8,128)(2,1)}, bf16[2,2,2,32,2560]{4,3,2,1,0:T(8,128)(2,1)}, u32[]{:S(2)}, u32[]{:S(2)}) collective-permute-start(bf16[2,2,2,32,2560]{4,3,2,1,0:T(8,128)(2,1)} %fusion), channel_id=1, source_target_pairs={{0,8},{4,12},{8,0},{12,4},{16,24},{20,28},{24,16},{28,20},{1,9},{5... | collective-permute-start | bytes 3932168 | tf_op jit(solution)/shard_map/ppermute | solution.py:846
  414.3 25.1 %collective-permute-start.32 = (bf16[2,2,2,32,1536]{4,3,2,1,0:T(8,128)(2,1)}, bf16[2,2,2,32,1536]{4,3,2,1,0:T(8,128)(2,1)}, u32[]{:S(2)}, u32[]{:S(2)}) collective-permute-start(bf16[2,2,2,32,1536]{4,3,2,1,0:T(8,128)(2,1)} %fusion.1), channel_id=1, source_target_pairs={{0,16},{4,20},{8,24},{12,28},{16,0},{20,4},{24,8},{28,12},{1,17},{... | collective-permute-start | bytes 2359304 | tf_op jit(solution)/shard_map/ppermute | solution.py:846
  421.9 29.3 %collective-permute-start.34 = (bf16[2,32,8192]{2,1,0:T(8,128)(2,1)}, bf16[2,32,8192]{2,1,0:T(8,128)(2,1)}, u32[]{:S(2)}, u32[]{:S(2)}) collective-permute-start(bf16[2,32,8192]{2,1,0:T(8,128)(2,1)} %dynamic-slice_bitcast_fusion.4), channel_id=1, source_target_pairs={{0,1},{1,0},{2,3},{3,2},{4,5},{5,4},{6,7},{7,6},{8,9},{9,8},{10,11... | collective-permute-start | bytes 3145736 | tf_op jit(solution)/shard_map/ppermute | solution.py:846
  445.0 6.6 %collective-permute-start.36 = (f32[1,6144]{1,0:T(1,128)S(1)}, f32[1,6144]{1,0:T(1,128)S(1)}, u32[]{:S(2)}, u32[]{:S(2)}) collective-permute-start(f32[1,6144]{1,0:T(1,128)S(1)} %bitcast.323), channel_id=1, source_target_pairs={{0,1},{1,0},{2,3},{3,2},{4,5},{5,4},{6,7},{7,6},{8,9},{9,8},{10,11... | collective-permute-start | bytes 73736 | tf_op jit(solution)/shard_map/ppermute | solution.py:846
  451.7 5.1 collective-permute-start.37
  454.4 10.8 %collective-permute-start.35 = (bf16[2,2,2,2,64,512]{5,4,2,3,1,0:T(8,128)(2,1)S(1)}, bf16[2,2,2,2,64,512]{5,4,2,3,1,0:T(8,128)(2,1)S(1)}, u32[]{:S(2)}, u32[]{:S(2)}) collective-permute-start(bf16[2,2,2,2,64,512]{5,4,2,3,1,0:T(8,128)(2,1)S(1)} %copy.55), channel_id=1, source_target_pairs={{0,4},{4,0},{8,12},{12,8},{16,20},{20,16},{24,28},{28,24},{1,5},{5... | collective-permute-start | bytes 3145736 | tf_op jit(solution)/shard_map/ppermute | solution.py:846
  454.4 11.5 %collective-permute-start.40 = (bf16[2,2,2,2,64,512]{5,4,3,2,1,0:T(8,128)(2,1)S(1)}, bf16[2,2,2,2,64,512]{5,4,3,2,1,0:T(8,128)(2,1)S(1)}, u32[]{:S(2)}, u32[]{:S(2)}) collective-permute-start(bf16[2,2,2,2,64,512]{5,4,3,2,1,0:T(8,128)(2,1)S(1)} %dynamic-slice_bitcast_fusion.2), channel_id=1, source_target_pairs={{0,4},{4,0},{8,12},{12,8},{16,20},{20,16},{24,28},{28,24},{1,5},{5... | collective-permute-start | bytes 3145736 | tf_op jit(solution)/shard_map/ppermute | solution.py:846
  456.8 10.9 %collective-permute-start.52 = (f32[1,6144]{1,0:T(1,128)S(1)}, f32[1,6144]{1,0:T(1,128)S(1)}, u32[]{:S(2)}, u32[]{:S(2)}) collective-permute-start(f32[1,6144]{1,0:T(1,128)S(1)} %add.713), channel_id=1, source_target_pairs={{0,4},{4,0},{8,12},{12,8},{16,20},{20,16},{24,28},{28,24},{1,5},{5... | collective-permute-start | bytes 73736 | tf_op jit(solution)/shard_map/ppermute | solution.py:846
  458.4 35.2 %collective-permute-start.51 = (bf16[32,8192]{1,0:T(8,128)(2,1)S(1)}, bf16[32,8192]{1,0:T(8,128)(2,1)S(1)}, u32[]{:S(2)}, u32[]{:S(2)}) collective-permute-start(bf16[32,8192]{1,0:T(8,128)(2,1)S(1)} %get-tuple-element.276), channel_id=1, source_target_pairs={{0,2},{1,3},{2,0},{3,1},{4,6},{5,7},{6,4},{7,5},{8,10},{9,11},{10,... | collective-permute-start | bytes 1572872 | tf_op jit(solution)/shard_map/ppermute | solution.py:846
  462.4 17.6 %collective-permute-start.39 = (bf16[2,2,32,2560]{3,2,1,0:T(8,128)(2,1)S(1)}, bf16[2,2,32,2560]{3,2,1,0:T(8,128)(2,1)S(1)}, u32[]{:S(2)}, u32[]{:S(2)}) collective-permute-start(bf16[2,2,32,2560]{3,2,1,0:T(8,128)(2,1)S(1)} %fusion.4), channel_id=1, source_target_pairs={{0,16},{4,20},{8,24},{12,28},{16,0},{20,4},{24,8},{28,12},{1,17},{... | collective-permute-start | bytes 1966088 | tf_op jit(solution)/shard_map/ppermute | solution.py:846
  465.2 17.2 %collective-permute-start.41 = (bf16[2,2,32,1536]{3,2,1,0:T(8,128)(2,1)S(1)}, bf16[2,2,32,1536]{3,2,1,0:T(8,128)(2,1)S(1)}, u32[]{:S(2)}, u32[]{:S(2)}) collective-permute-start(bf16[2,2,32,1536]{3,2,1,0:T(8,128)(2,1)S(1)} %fusion.10), channel_id=1, source_target_pairs={{0,8},{4,12},{8,0},{12,4},{16,24},{20,28},{24,16},{28,20},{1,9},{5... | collective-permute-start | bytes 1179656 | tf_op jit(solution)/shard_map/ppermute | solution.py:846
  466.0 22.0 %collective-permute-start.38 = (bf16[2,2,2,64,512]{4,3,2,1,0:T(8,128)(2,1)S(1)}, bf16[2,2,2,64,512]{4,3,2,1,0:T(8,128)(2,1)S(1)}, u32[]{:S(2)}, u32[]{:S(2)}) collective-permute-start(bf16[2,2,2,64,512]{4,3,2,1,0:T(8,128)(2,1)S(1)} %fusion.6), channel_id=1, source_target_pairs={{0,8},{4,12},{8,0},{12,4},{16,24},{20,28},{24,16},{28,20},{1,9},{5... | collective-permute-start | bytes 1572872 | tf_op jit(solution)/shard_map/ppermute | solution.py:846
  467.7 23.5 %collective-permute-start.43 = (bf16[2,2,2,64,512]{4,3,2,1,0:T(8,128)(2,1)S(1)}, bf16[2,2,2,64,512]{4,3,2,1,0:T(8,128)(2,1)S(1)}, u32[]{:S(2)}, u32[]{:S(2)}) collective-permute-start(bf16[2,2,2,64,512]{4,3,2,1,0:T(8,128)(2,1)S(1)} %fusion.5), channel_id=1, source_target_pairs={{0,16},{4,20},{8,24},{12,28},{16,0},{20,4},{24,8},{28,12},{1,17},{... | collective-permute-start | bytes 1572872 | tf_op jit(solution)/shard_map/ppermute | solution.py:846
  480.0 12.0 %collective-permute-start.53 = (f32[2,6144]{1,0:T(2,128)S(1)}, f32[2,6144]{1,0:T(2,128)S(1)}, u32[]{:S(2)}, u32[]{:S(2)}) collective-permute-start(f32[2,6144]{1,0:T(2,128)S(1)} %maximum_select_fusion.7), channel_id=1, source_target_pairs={{0,8},{4,12},{8,0},{12,4},{16,24},{20,28},{24,16},{28,20},{1,9},{5... | collective-permute-start | bytes 147464 | tf_op jit(solution)/shard_map/ppermute | solution.py:846
  484.0 15.5 %collective-permute-start.45 = (bf16[2,32,4096]{2,1,0:T(8,128)(2,1)S(1)}, bf16[2,32,4096]{2,1,0:T(8,128)(2,1)S(1)}, u32[]{:S(2)}, u32[]{:S(2)}) collective-permute-start(bf16[2,32,4096]{2,1,0:T(8,128)(2,1)S(1)} %dynamic-slice_bitcast_fusion.5), channel_id=1, source_target_pairs={{0,1},{1,0},{2,3},{3,2},{4,5},{5,4},{6,7},{7,6},{8,9},{9,8},{10,11... | collective-permute-start | bytes 1572872 | tf_op jit(solution)/shard_map/ppermute | solution.py:846
  488.1 9.1 %collective-permute-start.42 = (bf16[2,2,64,512]{3,2,1,0:T(8,128)(2,1)S(1)}, bf16[2,2,64,512]{3,2,1,0:T(8,128)(2,1)S(1)}, u32[]{:S(2)}, u32[]{:S(2)}) collective-permute-start(bf16[2,2,64,512]{3,2,1,0:T(8,128)(2,1)S(1)} %fusion.13), channel_id=1, source_target_pairs={{0,16},{4,20},{8,24},{12,28},{16,0},{20,4},{24,8},{28,12},{1,17},{... | collective-permute-start | bytes 786440 | tf_op jit(solution)/shard_map/ppermute | solution.py:846
  491.3 6.9 %collective-permute-start.46 = (bf16[2,2,64,512]{3,2,1,0:T(8,128)(2,1)S(1)}, bf16[2,2,64,512]{3,2,1,0:T(8,128)(2,1)S(1)}, u32[]{:S(2)}, u32[]{:S(2)}) collective-permute-start(bf16[2,2,64,512]{3,2,1,0:T(8,128)(2,1)S(1)} %fusion.12), channel_id=1, source_target_pairs={{0,8},{4,12},{8,0},{12,4},{16,24},{20,28},{24,16},{28,20},{1,9},{5... | collective-permute-start | bytes 786440 | tf_op jit(solution)/shard_map/ppermute | solution.py:846
  492.0 15.4 %collective-permute-start.54 = (f32[4,6144]{1,0:T(4,128)S(1)}, f32[4,6144]{1,0:T(4,128)S(1)}, u32[]{:S(2)}, u32[]{:S(2)}) collective-permute-start(f32[4,6144]{1,0:T(4,128)S(1)} %maximum_select_fusion.6), channel_id=1, source_target_pairs={{0,16},{4,20},{8,24},{12,28},{16,0},{20,4},{24,8},{28,12},{1,17},{... | collective-permute-start | bytes 294920 | tf_op jit(solution)/shard_map/ppermute | solution.py:846
  497.2 6.7 %collective-permute-start.44 = (bf16[2,64,512]{2,1,0:T(8,128)(2,1)S(1)}, bf16[2,64,512]{2,1,0:T(8,128)(2,1)S(1)}, u32[]{:S(2)}, u32[]{:S(2)}) collective-permute-start(bf16[2,64,512]{2,1,0:T(8,128)(2,1)S(1)} %fusion.21), channel_id=1, source_target_pairs={{0,1},{1,0},{2,3},{3,2},{4,5},{5,4},{6,7},{7,6},{8,9},{9,8},{10,11... | collective-permute-start | bytes 393224 | tf_op jit(solution)/shard_map/ppermute | solution.py:846
  498.3 8.4 %collective-permute-start.48 = (bf16[2,64,512]{2,1,0:T(8,128)(2,1)S(1)}, bf16[2,64,512]{2,1,0:T(8,128)(2,1)S(1)}, u32[]{:S(2)}, u32[]{:S(2)}) collective-permute-start(bf16[2,64,512]{2,1,0:T(8,128)(2,1)S(1)} %fusion.20), channel_id=1, source_target_pairs={{0,1},{1,0},{2,3},{3,2},{4,5},{5,4},{6,7},{7,6},{8,9},{9,8},{10,11... | collective-permute-start | bytes 393224 | tf_op jit(solution)/shard_map/ppermute | solution.py:846
  499.6 18.7 %collective-permute-start.50 = (bf16[32,4096]{1,0:T(8,128)(2,1)S(1)}, bf16[32,4096]{1,0:T(8,128)(2,1)S(1)}, u32[]{:S(2)}, u32[]{:S(2)}) collective-permute-start(bf16[32,4096]{1,0:T(8,128)(2,1)S(1)} %get-tuple-element.280), channel_id=1, source_target_pairs={{0,2},{1,3},{2,0},{3,1},{4,6},{5,7},{6,4},{7,5},{8,10},{9,11},{10,... | collective-permute-start | bytes 786440 | tf_op jit(solution)/shard_map/ppermute | solution.py:846
  504.0 13.2 %collective-permute-start.47 = (bf16[64,512]{1,0:T(8,128)(2,1)S(1)}, bf16[64,512]{1,0:T(8,128)(2,1)S(1)}, u32[]{:S(2)}, u32[]{:S(2)}) collective-permute-start(bf16[64,512]{1,0:T(8,128)(2,1)S(1)} %get-tuple-element.277), channel_id=1, source_target_pairs={{0,2},{1,3},{2,0},{3,1},{4,6},{5,7},{6,4},{7,5},{8,10},{9,11},{10,... | collective-permute-start | bytes 196616 | tf_op jit(solution)/shard_map/ppermute | solution.py:846
  506.9 10.4 %collective-permute-start.49 = (bf16[64,512]{1,0:T(8,128)(2,1)S(1)}, bf16[64,512]{1,0:T(8,128)(2,1)S(1)}, u32[]{:S(2)}, u32[]{:S(2)}) collective-permute-start(bf16[64,512]{1,0:T(8,128)(2,1)S(1)} %get-tuple-element.273), channel_id=1, source_target_pairs={{0,2},{1,3},{2,0},{3,1},{4,6},{5,7},{6,4},{7,5},{8,10},{9,11},{10,... | collective-permute-start | bytes 196616 | tf_op jit(solution)/shard_map/ppermute | solution.py:846
  (57 other events, 513.6 us)
Sparse Core Ops, SparseCore 0:
  46.0 66.2 all-gather.2
  133.9 98.7 all-gather.4
  300.5 119.1 reduce-scatter.1

commit v5 on v4

--- a/solution.py
+++ b/solution.py
@@ -1120,9 +1120,7 @@
     block_out, middle_grad, branch_cot, mid_sums = mid[:4]
     every_bit = dp_bits + seq_bits
     rising = seq_bits[::-1]
-    columns = 3 * width // count + width
-    qkv_part = out_wgrad_part(attended_low, branch_cot, columns) if wide else mid[4]
-    ffn_whole = ffn_grad(after(normed_two, qkv_part), down_cot, *ffn_kept, owned)
+    ffn_whole = ffn_grad(after(normed_two, mid[4]), down_cot, *ffn_kept, owned)
     ffn_whole = after(ffn_whole, *do_pieces[1:])
     ffn_part = lax.psum_scatter(ffn_whole, "dp", scatter_dimension=0, tiled=True)
     do_pieces[1:] = [after(piece, ffn_whole) for piece in do_pieces[1:]]
@@ -1133,6 +1131,11 @@
             attend_back(qkv_chunks[c], do_pieces, c, o, log_total, cos_all, sin_all, heads)
         )
     cot_chunks = [exchange(b) for b in backs]
+    qkv_part = None
+    if wide:
+        qkv_part = out_wgrad_part(
+            after(attended_low, backs[-1][0]), branch_cot, 3 * width // count + width
+        )
 
     sent = [backs[-1][0]]
 
@@ -1170,9 +1173,8 @@
         cot_chunks, hidden, middle_grad, first_full, mod, owned, here
     )
     skip_cot = after(hidden_grad, qkv_sums[-1].terms[-1])
-    skip_later = after(skip_cot, qkv_sums[0].terms[-1])
     skip_part = jnp.concatenate(
-        [dot_tn(frames, skip_cot).astype(BF), dot_tn(skips, skip_later).astype(BF)], axis=0
+        [dot_tn(frames, skip_cot).astype(BF), dot_tn(skips, skip_cot).astype(BF)], axis=0
     )
     skip_part = after(skip_part, ffn_sum.terms[-1])
     half = width // 2

time: 535 us -> 531 us (level)
  waiting for transfers between devices: 176 us -> 169 us
  local copies, waits for them, and re-layouts: 22.5 us -> 28 us
    unnamed x136, local copies, waits for them, and re-layouts: 9.78 us -> 15.3 us
  transfers between devices with their start and end apart: 58 -> 58, of which waited for: 27 -> 25; matrix products, arithmetic and copies ran while one was open for 8% -> 9% of each run, Pallas kernels for 27% -> 28%
where the time goes in v5:
time: 531 us; the launch traced here: 522 us
  Pallas kernels  188 us (35%)
  waiting for transfers between devices  169 us (32%)
  starting transfers between devices  84 us (16%)
  other arithmetic  31.3 us (6%)
  local copies, waits for them, and re-layouts  28 us (5%)
  between operations  16.4 us (3%)
  matrix products  5.47 us (1%)
    ppermute x34, waiting for transfers between devices, swap(): lax.ppermute(values, axis, [(i, i ^ 1 << bit) for i in range(lax.axis_siz...  106 us
    ppermute x21, waiting for transfers between devices, exchange(): lax.ppermute(pieces[d], 'seq', [(i, i ^ d) for i in places])  55.8 us
    pallas_call x2, Pallas kernels, attend_back(): pl.pallas_call(functools.partial(attend_back_kernel, heads, block, count)...  55.7 us
    ppermute x21, starting transfers between devices, exchange(): lax.ppermute(pieces[d], 'seq', [(i, i ^ d) for i in places])  46.5 us
    ppermute x34, starting transfers between devices, swap(): lax.ppermute(values, axis, [(i, i ^ 1 << bit) for i in range(lax.axis_siz...  37.4 us
    pallas_call x2, Pallas kernels, attend(): pl.pallas_call(functools.partial(attend_kernel, heads, block, count), gri...  29.7 us
    pallas_call x1, Pallas kernels, ffn(): pl.pallas_call(functools.partial(ffn_kernel, piece), grid=(steps,), in_sp...  24.4 us
    unnamed x136, local copies, waits for them, and re-layouts  15.3 us
  transfers between devices with their start and end apart: 58, of which 25 were waited for; matrix products, arithmetic and copies ran while one was open for 9% of the time, Pallas kernels for 28%

profile of v5, /device:TPU:0, one launch (start us, length us, event | category | flops | bytes accessed | tf_op | source)
XLA Modules:
  0.0 522.4 jit_solution(882436325267374352)
XLA Ops:
  9.5 4.1 collective-permute-start
  13.6 14.7 %collective-permute-done = bf16[1,32,5120]{2,1,0:T(8,128)(2,1)S(1)} collective-permute-done((bf16[1,32,5120]{2,1,0:T(8,128)(2,1)S(1)}, bf16[1,32,5120]{2,1,0:T(8,128)(2,1)S(1)}, u32[]{:S(2)}, u32[]{:S(2)}) %collective-permute-start) | collective-permute-done | bytes 327712 | tf_op jit(solution)/shard_map/ppermute | solution.py:846
  29.3 15.1 %collective-permute-done.1 = bf16[2,32,5120]{2,1,0:T(8,128)(2,1)S(1)} collective-permute-done((bf16[2,32,5120]{2,1,0:T(8,128)(2,1)S(1)}, bf16[2,32,5120]{2,1,0:T(8,128)(2,1)S(1)}, u32[]{:S(2)}, u32[]{:S(2)}) %collective-permute-start.1) | collective-permute-done | bytes 655392 | tf_op jit(solution)/shard_map/ppermute | solution.py:846
  47.9 3.7 fusion.17
  52.7 3.1 pad_maximum_fusion.1
  57.3 3.9 collective-permute-done.3
  63.6 2.2 collective-permute-done.4
  66.5 3.1 collective-permute-start.5
  71.4 1.9 collective-permute-start.6
  77.1 3.0 collective-permute-start.8
  82.9 20.9 %collective-permute-done.8 = bf16[1,32,9216]{2,1,0:T(8,128)(2,1)S(1)} collective-permute-done((bf16[1,32,9216]{2,1,0:T(8,128)(2,1)S(1)}, bf16[1,32,9216]{2,1,0:T(8,128)(2,1)S(1)}, u32[]{:S(2)}, u32[]{:S(2)}) %collective-permute-start.8) | collective-permute-done | bytes 589856 | tf_op jit(solution)/shard_map/ppermute | solution.py:846
  104.8 7.5 %all-gather.3.cloned.1.call-done.packed_ref.wq_ref.wk_ref.wv_ref.refs_10_.refs_11_.refs_12_.refs_13_ = bf16[1024,5120]{1,0:T(8,128)(2,1)} async-done(((bf16[128,5120]{1,0:T(8,128)(2,1)}), bf16[1024,5120]{1,0:T(8,128)(2,1)}) %all-gather.3.cloned.1.call-update) | async-done | bytes 10485776 | tf_op jit(solution)/shard_map/all_gather | solution.py:1037
  112.2 7.3 %shard_map.244 = (f32[512,1024]{1,0:T(8,128)}, bf16[512,1024]{1,0:T(8,128)(2,1)}) custom-call(bf16[512,1024]{1,0:T(8,128)(2,1)} %bitcast.319, bf16[512,1024]{1,0:T(8,128)(2,1)} %bitcast.318, bf16[512,1024]{1,0:T(8,128)(2,1)} %bitcast_select_fusion.1.cond_ref, ...), custom_call_target="tpu_custom_call" | custom-call | flops 2147483648 | bytes 10485760 | tf_op jit(solution)/shard_map/pallas_call | solution.py:168
  119.5 9.1 %shard_map.245 = (bf16[512,384]{1,0:T(8,128)(2,1)}, bf16[512,384]{1,0:T(8,128)(2,1)}, bf16[512,384]{1,0:T(8,128)(2,1)}, bf16[512,384]{1,0:T(8,128)(2,1)}, bf16[5...) custom-call(s32[1]{0:T(128)} %bitcast.me_ref, ...), custom_call_target="tpu_custom_call" | custom-call | flops 3221225472 | bytes 10485760 | tf_op jit(solution)/shard_map/pallas_call | solution.py:218
  128.6 3.2 collective-permute-done.9
  133.9 2.4 collective-permute-start.11
  136.3 2.1 collective-permute-start.7
  138.3 2.3 collective-permute-start.15
  140.6 7.2 %collective-permute-done.11.refs_3_ = bf16[512,384]{1,0:T(8,128)(2,1)S(1)} collective-permute-done((bf16[512,384]{1,0:T(8,128)(2,1)S(1)}, bf16[512,384]{1,0:T(8,128)(2,1)S(1)}, u32[]{:S(2)}, u32[]{:S(2)}) %collective-permute-start.11) | collective-permute-done | bytes 393248 | tf_op jit(solution)/shard_map/ppermute | solution.py:916
  147.9 17.3 %collective-permute-start.13 = (bf16[512,384]{1,0:T(8,128)(2,1)S(1)}, bf16[512,384]{1,0:T(8,128)(2,1)S(1)}, u32[]{:S(2)}, u32[]{:S(2)}) collective-permute-start(bf16[512,384]{1,0:T(8,128)(2,1)S(1)} %copy-done.53), channel_id=1, source_target_pairs={{0,1},{1,0},{2,3},{3,2},{4,5},{5,4},{6,7},{7,6},{8,9},{9,8},{10,11... | collective-permute-start | bytes 1179656 | tf_op jit(solution)/shard_map/ppermute | solution.py:916
  165.1 22.7 %collective-permute-done.10.refs_2_ = bf16[512,384]{1,0:T(8,128)(2,1)S(1)} collective-permute-done((bf16[512,384]{1,0:T(8,128)(2,1)S(1)}, bf16[512,384]{1,0:T(8,128)(2,1)S(1)}, u32[]{:S(2)}, u32[]{:S(2)}) %collective-permute-start.10) | collective-permute-done | bytes 393248 | tf_op jit(solution)/shard_map/ppermute | solution.py:916
  187.8 14.9 %shard_map.246 = (bf16[512,128]{1,0:T(8,128)(2,1)S(1)}, bf16[512,128]{1,0:T(8,128)(2,1)S(1)}, bf16[512,128]{1,0:T(8,128)(2,1)S(1)}, bf16[512,128]{1,0:T(8,128)(2,1)S(1)}, f32[2,2048]{1,0:T(2,128)S(1)}) custom-call(bf16[512,384]{1,0:T(8,128)(2,1)S(1)} %copy-done.26, bf16[512,384]{1,0:T(8,128)(2,1)S(1)} %collective-permute-done.7.refs_1_, ...), custom_call_target="tpu_custom_call" | custom-call | flops 8589934592 | bytes 2097152 | tf_op jit(solution)/shard_map/pallas_call | solution.py:279
  204.1 1.9 collective-permute-start.17
  206.0 14.9 %shard_map.247 = (bf16[512,128]{1,0:T(8,128)(2,1)S(1)}, bf16[512,128]{1,0:T(8,128)(2,1)S(1)}, bf16[512,128]{1,0:T(8,128)(2,1)S(1)}, bf16[512,128]{1,0:T(8,128)(2,1)S(1)}, f32[2,2048]{1,0:T(2,128)S(1)}) custom-call(bf16[512,384]{1,0:T(8,128)(2,1)S(1)} %copy-done.25, bf16[512,384]{1,0:T(8,128)(2,1)S(1)} %collective-permute-done.13.refs_1_, ...), custom_call_target="tpu_custom_call" | custom-call | flops 8589934592 | bytes 2097152 | tf_op jit(solution)/shard_map/pallas_call | solution.py:279
  221.6 2.6 collective-permute-start.18
  224.3 2.3 collective-permute-start.19
  226.6 2.0 collective-permute-start.20
  228.6 2.8 collective-permute-done.12.refs_1_
  231.5 2.8 collective-permute-done.20.refs_7_
  235.0 6.0 %shard_map.248 = (bf16[512,1024]{1,0:T(8,128)(2,1)}, f32[512,1024]{1,0:T(8,128)}, f32[512,1024]{1,0:T(8,128)}, bf16[512,1024]{1,0:T(8,128)(2,1)}) custom-call(s32[1]{0:T(128)} %bitcast.me_ref, bf16[512,128]{1,0:T(8,128)(2,1)} %copy-done.24, bf16[512,128]{1,0:T(8,128)(2,1)} %copy-done.48, bf16[512,128]{1,0:T(8,128)(2,1)} %copy-done.46, ...), custom_call_target="tpu_custom_call" | custom-call | flops 1073741824 | bytes 11534336 | tf_op jit(solution)/shard_map/pallas_call | solution.py:412
  241.0 24.4 %shard_map.249 = (f32[512,1024]{1,0:T(8,128)}, f32[512,1024]{1,0:T(8,128)}, bf16[512,4096]{1,0:T(8,128)(2,1)}, bf16[512,4096]{1,0:T(8,128)(2,1)}) custom-call(bf16[512,1024]{1,0:T(8,128)(2,1)} %get-tuple-element.179.x_ref, bf16[512,1024]{1,0:T(8,128)(2,1)} %get-tuple-element.267.dc_ref, ...), custom_call_target="tpu_custom_call" | custom-call | flops 17179869184 | bytes 33554432 | tf_op jit(solution)/shard_map/pallas_call | solution.py:511
  265.4 8.4 %shard_map.250 = (bf16[512,1024]{1,0:T(8,128)(2,1)}, f32[512,1024]{1,0:T(8,128)}, bf16[512,1024]{1,0:T(8,128)(2,1)}, f32[8,1024]{1,0:T(8,128)}, bf16[512,256]{1,...) custom-call(s32[1]{0:T(128)} %bitcast.me_ref, ...), custom_call_target="tpu_custom_call" | custom-call | flops 1073741824 | bytes 16777216 | tf_op jit(solution)/shard_map/pallas_call | solution.py:595
  278.3 14.5 %shard_map.251 = bf16[1024,8192]{1,0:T(8,128)(2,1)} custom-call(bf16[512,1024]{1,0:T(8,128)(2,1)} %get-tuple-element.179.x_ref, bf16[512,1024]{1,0:T(8,128)(2,1)} %get-tuple-element.267.dc_ref, bf16[512,4096]{1,0:T(8,128)(2,1)} %get-tuple-element.180.activated_ref, bf16[512,4096]{1,0:T(8,128)(2,1)} %get-tuple-element.181.up_cot_ref), custom_call_target="tpu_custom_call" | custom-call | flops 8589934592 | bytes 33554432 | tf_op jit(solution)/shard_map/pallas_call | solution.py:540
  292.8 3.8 collective-permute-done.22.refs_6_
  297.4 27.8 %shard_map.252 = (bf16[512,384]{1,0:T(8,128)(2,1)}, bf16[512,384]{1,0:T(8,128)(2,1)}, bf16[512,384]{1,0:T(8,128)(2,1)}, bf16[512,384]{1,0:T(8,128)(2,1)}) custom-call(bf16[512,384]{1,0:T(8,128)(2,1)} %get-tuple-element.142.refs_0_, bf16[512,384]{1,0:T(8,128)(2,1)} %copy-done.32, bf16[512,384]{1,0:T(8,128)(2,1)} %copy-done.31, bf16[512,384]{1,0:T(8,128)(2,1)} %copy-done.30, ...), custom_call_target="tpu_custom_call" | custom-call | flops 12884901888 | bytes 5242880 | tf_op jit(solution)/shard_map/pallas_call | solution.py:365
  326.8 3.2 collective-permute-start.25
  330.0 28.0 %shard_map.253 = (bf16[512,384]{1,0:T(8,128)(2,1)}, bf16[512,384]{1,0:T(8,128)(2,1)}, bf16[512,384]{1,0:T(8,128)(2,1)}, bf16[512,384]{1,0:T(8,128)(2,1)}) custom-call(bf16[512,384]{1,0:T(8,128)(2,1)} %get-tuple-element.154.refs_0_, bf16[512,384]{1,0:T(8,128)(2,1)} %copy-done.29, bf16[512,384]{1,0:T(8,128)(2,1)} %copy-done.28, bf16[512,384]{1,0:T(8,128)(2,1)} %copy-done.27, ...), custom_call_target="tpu_custom_call" | custom-call | flops 12884901888 | bytes 5242880 | tf_op jit(solution)/shard_map/pallas_call | solution.py:365
  357.9 2.4 collective-permute-start.29
  362.3 4.3 shard_map.254.refs_5_
  366.7 3.0 copy-done
  369.7 3.8 shard_map.255
  373.6 2.3 copy-done.1
  376.6 16.4 %collective-permute-done.28.refs_3_.refs_6_ = bf16[512,384]{1,0:T(8,128)(2,1)S(1)} collective-permute-done((bf16[512,384]{1,0:T(8,128)(2,1)}, bf16[512,384]{1,0:T(8,128)(2,1)S(1)}, u32[]{:S(2)}, u32[]{:S(2)}) %collective-permute-start.28) | collective-permute-done | bytes 393248 | tf_op jit(solution)/shard_map/ppermute | solution.py:916
  397.6 3.6 shard_map.256
  401.3 1.8 dynamic-slice_bitcast_fusion
  404.8 3.5 collective-permute-done.31
  408.3 3.2 fusion
  412.9 2.3 fusion.1
  415.7 2.3 dynamic-slice_bitcast_fusion.4
  418.0 14.4 %shard_map.257 = (bf16[512,1024]{1,0:T(8,128)(2,1)}, bf16[512,1024]{1,0:T(8,128)(2,1)}, bf16[512,1024]{1,0:T(8,128)(2,1)}, f32[8,1024]{1,0:T(8,128)}) custom-call(s32[1]{0:T(128)} %bitcast.me_ref, bf16[512,384]{1,0:T(8,128)(2,1)} %get-tuple-element.189.refs_1_.refs_0_, bf16[512,384]{1,0:T(8,128)(2,1)} %copy-done.14, bf16[512,384]{1,0:T(8,128)(2,1)} %copy-done.13, ...), custom_call_target="tpu_custom_call" | custom-call | flops 1073741824 | bytes 2097152 | tf_op jit(solution)/shard_map/pallas_call | solution.py:660
  432.4 2.4 collective-permute-done.32
  435.8 6.8 %collective-permute-done.35 = bf16[2,2,2,32,2560]{4,3,2,1,0:T(8,128)(2,1)} collective-permute-done((bf16[2,2,2,32,2560]{4,3,2,1,0:T(8,128)(2,1)}, bf16[2,2,2,32,2560]{4,3,2,1,0:T(8,128)(2,1)}, u32[]{:S(2)}, u32[]{:S(2)}) %collective-permute-start.35) | collective-permute-done | bytes 1310752 | tf_op jit(solution)/shard_map/ppermute | solution.py:846
  442.6 2.8 convert_bitcast_fusion
  448.8 3.7 collective-permute-done.37
  454.5 1.7 fusion.4
  462.2 11.6 %collective-permute-done.39 = bf16[2,2,32,2560]{3,2,1,0:T(8,128)(2,1)S(1)} collective-permute-done((bf16[2,2,32,2560]{3,2,1,0:T(8,128)(2,1)S(1)}, bf16[2,2,32,2560]{3,2,1,0:T(8,128)(2,1)S(1)}, u32[]{:S(2)}, u32[]{:S(2)}) %collective-permute-start.39) | collective-permute-done | bytes 655392 | tf_op jit(solution)/shard_map/ppermute | solution.py:846
  475.1 1.9 fusion.3
  478.6 3.1 collective-permute-start.45
  482.6 2.5 collective-permute-done.43
  487.4 2.2 shard_map.260
  491.2 2.6 collective-permute-start.44
  496.0 4.1 collective-permute-done.44
  503.8 2.4 shard_map.261
  506.2 7.0 %collective-permute-done.49.refs_3_ = bf16[64,512]{1,0:T(8,128)(2,1)S(1)} collective-permute-done((bf16[64,512]{1,0:T(8,128)(2,1)S(1)}, bf16[64,512]{1,0:T(8,128)(2,1)S(1)}, u32[]{:S(2)}, u32[]{:S(2)}) %collective-permute-start.49) | collective-permute-done | bytes 65568 | tf_op jit(solution)/shard_map/ppermute | solution.py:846
  (284 shorter events, 71.2 us)
Async XLA Ops:
  7.2 105.1 %all-gather.3.cloned.1.call-start = ((), (), s32[]{:S(2)}) async-start(), calls=%async_computation.1 | async-start | bytes 11796480 | tf_op jit(solution)/shard_map/all_gather | solution.py:1037
  9.5 18.8 %collective-permute-start = (bf16[1,32,5120]{2,1,0:T(8,128)(2,1)S(1)}, bf16[1,32,5120]{2,1,0:T(8,128)(2,1)S(1)}, u32[]{:S(2)}, u32[]{:S(2)}) collective-permute-start(bf16[1,32,5120]{2,1,0:T(8,128)(2,1)S(1)} %get-tuple-element.284), channel_id=1, source_target_pairs={{0,2},{1,3},{2,0},{3,1},{4,6},{5,7},{6,4},{7,5},{8,10},{9,11},{10,... | collective-permute-start | bytes 983048 | tf_op jit(solution)/shard_map/ppermute | solution.py:846
  28.5 16.0 %collective-permute-start.1 = (bf16[2,32,5120]{2,1,0:T(8,128)(2,1)S(1)}, bf16[2,32,5120]{2,1,0:T(8,128)(2,1)S(1)}, u32[]{:S(2)}, u32[]{:S(2)}) collective-permute-start(bf16[2,32,5120]{2,1,0:T(8,128)(2,1)S(1)} %maximum_select_fusion.4), channel_id=1, source_target_pairs={{0,1},{1,0},{2,3},{3,2},{4,5},{5,4},{6,7},{7,6},{8,9},{9,8},{10,11... | collective-permute-start | bytes 1966088 | tf_op jit(solution)/shard_map/ppermute | solution.py:846
  45.9 188.4 %all-gather.5.cloned.1.call-start = ((), (), s32[]{:S(2)}) async-start(), calls=%async_computation.2 | async-start | bytes 21233664 | tf_op jit(solution)/shard_map/all_gather | solution.py:1086
  47.6 8.2 %collective-permute-start.2 = (f32[2,2,1,6144]{3,2,1,0:T(1,128)S(1)}, f32[2,2,1,6144]{3,2,1,0:T(1,128)S(1)}, u32[]{:S(2)}, u32[]{:S(2)}) collective-permute-start(f32[2,2,1,6144]{3,2,1,0:T(1,128)S(1)} %constant_dynamic-slice_fusion), channel_id=1, source_target_pairs={{0,4},{4,0},{8,12},{12,8},{16,20},{20,16},{24,28},{28,24},{1,5},{5... | collective-permute-start | bytes 294920 | tf_op jit(solution)/shard_map/ppermute | solution.py:846
  55.8 24.3 %copy-start.42 = (bf16[1,512,1024]{2,1,0:T(8,128)(2,1)S(1)}, bf16[1,512,1024]{2,1,0:T(8,128)(2,1)}, u32[]{:S(2)}) copy-start(bf16[1,512,1024]{2,1,0:T(8,128)(2,1)} %param.15) | copy-start | bytes 3145732
  55.9 5.2 %collective-permute-start.3 = (f32[2,1,6144]{2,1,0:T(1,128)S(1)}, f32[2,1,6144]{2,1,0:T(1,128)S(1)}, u32[]{:S(2)}, u32[]{:S(2)}) collective-permute-start(f32[2,1,6144]{2,1,0:T(1,128)S(1)} %dynamic-slice_bitcast_fusion.6), channel_id=1, source_target_pairs={{0,16},{4,20},{8,24},{12,28},{16,0},{20,4},{24,8},{28,12},{1,17},{... | collective-permute-start | bytes 147464 | tf_op jit(solution)/shard_map/ppermute | solution.py:846
  61.3 4.5 collective-permute-start.4
  66.5 4.9 collective-permute-start.5
  71.4 4.4 collective-permute-start.6
  77.1 26.7 %collective-permute-start.8 = (bf16[1,32,9216]{2,1,0:T(8,128)(2,1)S(1)}, bf16[1,32,9216]{2,1,0:T(8,128)(2,1)S(1)}, u32[]{:S(2)}, u32[]{:S(2)}) collective-permute-start(bf16[1,32,9216]{2,1,0:T(8,128)(2,1)S(1)} %bitcast.320), channel_id=1, source_target_pairs={{0,2},{1,3},{2,0},{3,1},{4,6},{5,7},{6,4},{7,5},{8,10},{9,11},{10,... | collective-permute-start | bytes 1769480 | tf_op jit(solution)/shard_map/ppermute | solution.py:846
  104.0 27.7 %collective-permute-start.9 = (bf16[2,32,9216]{2,1,0:T(8,128)(2,1)S(1)}, bf16[2,32,9216]{2,1,0:T(8,128)(2,1)S(1)}, u32[]{:S(2)}, u32[]{:S(2)}) collective-permute-start(bf16[2,32,9216]{2,1,0:T(8,128)(2,1)S(1)} %maximum_select_fusion.2), channel_id=1, source_target_pairs={{0,1},{1,0},{2,3},{3,2},{4,5},{5,4},{6,7},{7,6},{8,9},{9,8},{10,11... | collective-permute-start | bytes 3538952 | tf_op jit(solution)/shard_map/ppermute | solution.py:846
  133.8 54.1 %copy-start.26 = (bf16[512,384]{1,0:T(8,128)(2,1)S(1)}, bf16[512,384]{1,0:T(8,128)(2,1)}, u32[]{:S(2)}) copy-start(bf16[512,384]{1,0:T(8,128)(2,1)} %get-tuple-element.142.refs_0_) | copy-start | bytes 1179652
  133.8 281.9 %reduce-scatter.2.cloned.1.call-start = ((), (), s32[]{:S(2)}) async-start(), calls=%async_computation.3 | async-start | bytes 18874368 | tf_op jit(solution)/shard_map/reduce_scatter | solution.py:1125
  133.9 14.0 %collective-permute-start.11 = (bf16[512,384]{1,0:T(8,128)(2,1)S(1)}, bf16[512,384]{1,0:T(8,128)(2,1)S(1)}, u32[]{:S(2)}, u32[]{:S(2)}) collective-permute-start(bf16[512,384]{1,0:T(8,128)(2,1)S(1)} %copy-done.58), channel_id=1, source_target_pairs={{0,3},{1,2},{2,1},{3,0},{4,7},{5,6},{6,5},{7,4},{8,11},{9,10},{10,... | collective-permute-start | bytes 1179656 | tf_op jit(solution)/shard_map/ppermute | solution.py:916
  136.2 51.6 %collective-permute-start.10 = (bf16[512,384]{1,0:T(8,128)(2,1)S(1)}, bf16[512,384]{1,0:T(8,128)(2,1)S(1)}, u32[]{:S(2)}, u32[]{:S(2)}) collective-permute-start(bf16[512,384]{1,0:T(8,128)(2,1)S(1)} %copy-done.57), channel_id=1, source_target_pairs={{0,2},{1,3},{2,0},{3,1},{4,6},{5,7},{6,4},{7,5},{8,10},{9,11},{10,... | collective-permute-start | bytes 1179656 | tf_op jit(solution)/shard_map/ppermute | solution.py:916
  136.3 51.6 %collective-permute-start.7 = (bf16[512,384]{1,0:T(8,128)(2,1)S(1)}, bf16[512,384]{1,0:T(8,128)(2,1)S(1)}, u32[]{:S(2)}, u32[]{:S(2)}) collective-permute-start(bf16[512,384]{1,0:T(8,128)(2,1)S(1)} %copy-done.56), channel_id=1, source_target_pairs={{0,1},{1,0},{2,3},{3,2},{4,5},{5,4},{6,7},{7,6},{8,9},{9,8},{10,11... | collective-permute-start | bytes 1179656 | tf_op jit(solution)/shard_map/ppermute | solution.py:916
  138.3 65.7 %collective-permute-start.15 = (bf16[512,384]{1,0:T(8,128)(2,1)S(1)}, bf16[512,384]{1,0:T(8,128)(2,1)S(1)}, u32[]{:S(2)}, u32[]{:S(2)}) collective-permute-start(bf16[512,384]{1,0:T(8,128)(2,1)S(1)} %copy-done.55), channel_id=1, source_target_pairs={{0,3},{1,2},{2,1},{3,0},{4,7},{5,6},{6,5},{7,4},{8,11},{9,10},{10,... | collective-permute-start | bytes 1179656 | tf_op jit(solution)/shard_map/ppermute | solution.py:916
  140.6 63.4 %collective-permute-start.14 = (bf16[512,384]{1,0:T(8,128)(2,1)S(1)}, bf16[512,384]{1,0:T(8,128)(2,1)S(1)}, u32[]{:S(2)}, u32[]{:S(2)}) collective-permute-start(bf16[512,384]{1,0:T(8,128)(2,1)S(1)} %copy-done.54), channel_id=1, source_target_pairs={{0,2},{1,3},{2,0},{3,1},{4,6},{5,7},{6,4},{7,5},{8,10},{9,11},{10,... | collective-permute-start | bytes 1179656 | tf_op jit(solution)/shard_map/ppermute | solution.py:916
  147.9 54.9 %copy-start.30 = (bf16[512,384]{1,0:T(8,128)(2,1)}, bf16[512,384]{1,0:T(8,128)(2,1)S(1)}, u32[]{:S(2)}) copy-start(bf16[512,384]{1,0:T(8,128)(2,1)S(1)} %collective-permute-done.11.refs_3_) | copy-start | bytes 1179652
  147.9 58.1 %copy-start.25 = (bf16[512,384]{1,0:T(8,128)(2,1)S(1)}, bf16[512,384]{1,0:T(8,128)(2,1)}, u32[]{:S(2)}) copy-start(bf16[512,384]{1,0:T(8,128)(2,1)} %get-tuple-element.154.refs_0_) | copy-start | bytes 1179652
  147.9 56.2 %collective-permute-start.13 = (bf16[512,384]{1,0:T(8,128)(2,1)S(1)}, bf16[512,384]{1,0:T(8,128)(2,1)S(1)}, u32[]{:S(2)}, u32[]{:S(2)}) collective-permute-start(bf16[512,384]{1,0:T(8,128)(2,1)S(1)} %copy-done.53), channel_id=1, source_target_pairs={{0,1},{1,0},{2,3},{3,2},{4,5},{5,4},{6,7},{7,6},{8,9},{9,8},{10,11... | collective-permute-start | bytes 1179656 | tf_op jit(solution)/shard_map/ppermute | solution.py:916
  204.1 22.6 %collective-permute-start.17 = (bf16[512,128]{1,0:T(8,128)(2,1)S(1)}, bf16[512,128]{1,0:T(8,128)(2,1)S(1)}, u32[]{:S(2)}, u32[]{:S(2)}) collective-permute-start(bf16[512,128]{1,0:T(8,128)(2,1)S(1)} %get-tuple-element.165.refs_11_), channel_id=1, source_target_pairs={{0,3},{1,2},{2,1},{3,0},{4,7},{5,6},{6,5},{7,4},{8,11},{9,10},{10,... | collective-permute-start | bytes 393224 | tf_op jit(solution)/shard_map/ppermute | solution.py:916
  206.0 22.6 %collective-permute-start.16 = (bf16[512,128]{1,0:T(8,128)(2,1)S(1)}, bf16[512,128]{1,0:T(8,128)(2,1)S(1)}, u32[]{:S(2)}, u32[]{:S(2)}) collective-permute-start(bf16[512,128]{1,0:T(8,128)(2,1)S(1)} %get-tuple-element.163.refs_10_), channel_id=1, source_target_pairs={{0,2},{1,3},{2,0},{3,1},{4,6},{5,7},{6,4},{7,5},{8,10},{9,11},{10,... | collective-permute-start | bytes 393224 | tf_op jit(solution)/shard_map/ppermute | solution.py:916
  221.6 9.8 %collective-permute-start.18 = (bf16[512,128]{1,0:T(8,128)(2,1)S(1)}, bf16[512,128]{1,0:T(8,128)(2,1)S(1)}, u32[]{:S(2)}, u32[]{:S(2)}) collective-permute-start(bf16[512,128]{1,0:T(8,128)(2,1)S(1)} %get-tuple-element.167.refs_9_), channel_id=1, source_target_pairs={{0,1},{1,0},{2,3},{3,2},{4,5},{5,4},{6,7},{7,6},{8,9},{9,8},{10,11... | collective-permute-start | bytes 393224 | tf_op jit(solution)/shard_map/ppermute | solution.py:916
  224.2 7.2 %collective-permute-start.12 = (bf16[512,128]{1,0:T(8,128)(2,1)S(1)}, bf16[512,128]{1,0:T(8,128)(2,1)S(1)}, u32[]{:S(2)}, u32[]{:S(2)}) collective-permute-start(bf16[512,128]{1,0:T(8,128)(2,1)S(1)} %get-tuple-element.153.refs_9_), channel_id=1, source_target_pairs={{0,1},{1,0},{2,3},{3,2},{4,5},{5,4},{6,7},{7,6},{8,9},{9,8},{10,11... | collective-permute-start | bytes 393224 | tf_op jit(solution)/shard_map/ppermute | solution.py:916
  224.3 7.2 %collective-permute-start.19 = (bf16[512,128]{1,0:T(8,128)(2,1)S(1)}, bf16[512,128]{1,0:T(8,128)(2,1)S(1)}, u32[]{:S(2)}, u32[]{:S(2)}) collective-permute-start(bf16[512,128]{1,0:T(8,128)(2,1)S(1)} %get-tuple-element.168.refs_10_), channel_id=1, source_target_pairs={{0,2},{1,3},{2,0},{3,1},{4,6},{5,7},{6,4},{7,5},{8,10},{9,11},{10,... | collective-permute-start | bytes 393224 | tf_op jit(solution)/shard_map/ppermute | solution.py:916
  226.6 7.6 %collective-permute-start.20 = (bf16[512,128]{1,0:T(8,128)(2,1)S(1)}, bf16[512,128]{1,0:T(8,128)(2,1)S(1)}, u32[]{:S(2)}, u32[]{:S(2)}) collective-permute-start(bf16[512,128]{1,0:T(8,128)(2,1)S(1)} %get-tuple-element.169.refs_11_), channel_id=1, source_target_pairs={{0,3},{1,2},{2,1},{3,0},{4,7},{5,6},{6,5},{7,4},{8,11},{9,10},{10,... | collective-permute-start | bytes 393224 | tf_op jit(solution)/shard_map/ppermute | solution.py:916
  273.8 19.0 %collective-permute-start.21 = (bf16[512,256]{1,0:T(8,128)(2,1)}, bf16[512,256]{1,0:T(8,128)(2,1)S(1)}, u32[]{:S(2)}, u32[]{:S(2)}) collective-permute-start(bf16[512,256]{1,0:T(8,128)(2,1)} %get-tuple-element.178), channel_id=1, source_target_pairs={{0,1},{1,0},{2,3},{3,2},{4,5},{5,4},{6,7},{7,6},{8,9},{9,8},{10,11... | collective-permute-start | bytes 786440 | tf_op jit(solution)/shard_map/ppermute | solution.py:916
  275.4 21.2 %collective-permute-start.22 = (bf16[512,256]{1,0:T(8,128)(2,1)}, bf16[512,256]{1,0:T(8,128)(2,1)S(1)}, u32[]{:S(2)}, u32[]{:S(2)}) collective-permute-start(bf16[512,256]{1,0:T(8,128)(2,1)} %get-tuple-element.182), channel_id=1, source_target_pairs={{0,2},{1,3},{2,0},{3,1},{4,6},{5,7},{6,4},{7,5},{8,10},{9,11},{10,... | collective-permute-start | bytes 786440 | tf_op jit(solution)/shard_map/ppermute | solution.py:916
  276.6 20.0 %collective-permute-start.23 = (bf16[512,256]{1,0:T(8,128)(2,1)}, bf16[512,256]{1,0:T(8,128)(2,1)S(1)}, u32[]{:S(2)}, u32[]{:S(2)}) collective-permute-start(bf16[512,256]{1,0:T(8,128)(2,1)} %get-tuple-element.183), channel_id=1, source_target_pairs={{0,3},{1,2},{2,1},{3,0},{4,7},{5,6},{6,5},{7,4},{8,11},{9,10},{10,... | collective-permute-start | bytes 786440 | tf_op jit(solution)/shard_map/ppermute | solution.py:916
  325.2 36.2 %collective-permute-start.26 = (bf16[512,384]{1,0:T(8,128)(2,1)}, bf16[512,384]{1,0:T(8,128)(2,1)S(1)}, u32[]{:S(2)}, u32[]{:S(2)}) collective-permute-start(bf16[512,384]{1,0:T(8,128)(2,1)} %get-tuple-element.196), channel_id=1, source_target_pairs={{0,3},{1,2},{2,1},{3,0},{4,7},{5,6},{6,5},{7,4},{8,11},{9,10},{10,... | collective-permute-start | bytes 1179656 | tf_op jit(solution)/shard_map/ppermute | solution.py:916
  326.8 39.9 %collective-permute-start.25 = (bf16[512,384]{1,0:T(8,128)(2,1)}, bf16[512,384]{1,0:T(8,128)(2,1)S(1)}, u32[]{:S(2)}, u32[]{:S(2)}) collective-permute-start(bf16[512,384]{1,0:T(8,128)(2,1)} %get-tuple-element.194), channel_id=1, source_target_pairs={{0,2},{1,3},{2,0},{3,1},{4,6},{5,7},{6,4},{7,5},{8,10},{9,11},{10,... | collective-permute-start | bytes 1179656 | tf_op jit(solution)/shard_map/ppermute | solution.py:916
  330.0 36.7 %collective-permute-start.24 = (bf16[512,384]{1,0:T(8,128)(2,1)}, bf16[512,384]{1,0:T(8,128)(2,1)S(1)}, u32[]{:S(2)}, u32[]{:S(2)}) collective-permute-start(bf16[512,384]{1,0:T(8,128)(2,1)} %get-tuple-element.190), channel_id=1, source_target_pairs={{0,1},{1,0},{2,3},{3,2},{4,5},{5,4},{6,7},{7,6},{8,9},{9,8},{10,11... | collective-permute-start | bytes 1179656 | tf_op jit(solution)/shard_map/ppermute | solution.py:916
  357.9 17.9 %collective-permute-start.29 = (bf16[512,384]{1,0:T(8,128)(2,1)}, bf16[512,384]{1,0:T(8,128)(2,1)S(1)}, u32[]{:S(2)}, u32[]{:S(2)}) collective-permute-start(bf16[512,384]{1,0:T(8,128)(2,1)} %get-tuple-element.205), channel_id=1, source_target_pairs={{0,3},{1,2},{2,1},{3,0},{4,7},{5,6},{6,5},{7,4},{8,11},{9,10},{10,... | collective-permute-start | bytes 1179656 | tf_op jit(solution)/shard_map/ppermute | solution.py:916
  360.3 32.7 %collective-permute-start.28 = (bf16[512,384]{1,0:T(8,128)(2,1)}, bf16[512,384]{1,0:T(8,128)(2,1)S(1)}, u32[]{:S(2)}, u32[]{:S(2)}) collective-permute-start(bf16[512,384]{1,0:T(8,128)(2,1)} %get-tuple-element.203), channel_id=1, source_target_pairs={{0,2},{1,3},{2,0},{3,1},{4,6},{5,7},{6,4},{7,5},{8,10},{9,11},{10,... | collective-permute-start | bytes 1179656 | tf_op jit(solution)/shard_map/ppermute | solution.py:916
  361.4 32.4 %collective-permute-start.27 = (bf16[512,384]{1,0:T(8,128)(2,1)}, bf16[512,384]{1,0:T(8,128)(2,1)S(1)}, u32[]{:S(2)}, u32[]{:S(2)}) collective-permute-start(bf16[512,384]{1,0:T(8,128)(2,1)} %get-tuple-element.198), channel_id=1, source_target_pairs={{0,1},{1,0},{2,3},{3,2},{4,5},{5,4},{6,7},{7,6},{8,9},{9,8},{10,11... | collective-permute-start | bytes 1179656 | tf_op jit(solution)/shard_map/ppermute | solution.py:916
  369.7 24.9 %copy-start.4 = (bf16[512,1024]{1,0:T(8,128)(2,1)S(1)}, bf16[512,1024]{1,0:T(8,128)(2,1)}, u32[]{:S(2)}) copy-start(bf16[512,1024]{1,0:T(8,128)(2,1)} %get-tuple-element.141.x_ref.refs_0_) | copy-start | bytes 3145732
  369.7 24.9 %copy-start.15 = (bf16[512,384]{1,0:T(8,128)(2,1)S(1)}, bf16[512,384]{1,0:T(8,128)(2,1)}, u32[]{:S(2)}) copy-start(bf16[512,384]{1,0:T(8,128)(2,1)} %get-tuple-element.214.refs_1_.refs_4_) | copy-start | bytes 1179652
  403.0 5.3 %collective-permute-start.31 = (bf16[2,2,2,2,32,2560]{5,4,3,2,1,0:T(8,128)(2,1)}, bf16[2,2,2,2,32,2560]{5,4,3,2,1,0:T(8,128)(2,1)}, u32[]{:S(2)}, u32[]{:S(2)}) collective-permute-start(bf16[2,2,2,2,32,2560]{5,4,3,2,1,0:T(8,128)(2,1)} %dynamic-slice_bitcast_fusion), channel_id=1, source_target_pairs={{0,4},{4,0},{8,12},{12,8},{16,20},{20,16},{24,28},{28,24},{1,5},{5... | collective-permute-start | bytes 7864328 | tf_op jit(solution)/shard_map/ppermute | solution.py:846
  404.3 8.6 %collective-permute-start.30 = (bf16[2,2,2,2,32,1536]{5,4,3,2,1,0:T(8,128)(2,1)}, bf16[2,2,2,2,32,1536]{5,4,3,2,1,0:T(8,128)(2,1)}, u32[]{:S(2)}, u32[]{:S(2)}) collective-permute-start(bf16[2,2,2,2,32,1536]{5,4,3,2,1,0:T(8,128)(2,1)} %dynamic-slice_bitcast_fusion.1), channel_id=1, source_target_pairs={{0,4},{4,0},{8,12},{12,8},{16,20},{20,16},{24,28},{28,24},{1,5},{5... | collective-permute-start | bytes 4718600 | tf_op jit(solution)/shard_map/ppermute | solution.py:846
  411.4 31.1 %collective-permute-start.35 = (bf16[2,2,2,32,2560]{4,3,2,1,0:T(8,128)(2,1)}, bf16[2,2,2,32,2560]{4,3,2,1,0:T(8,128)(2,1)}, u32[]{:S(2)}, u32[]{:S(2)}) collective-permute-start(bf16[2,2,2,32,2560]{4,3,2,1,0:T(8,128)(2,1)} %fusion), channel_id=1, source_target_pairs={{0,8},{4,12},{8,0},{12,4},{16,24},{20,28},{24,16},{28,20},{1,9},{5... | collective-permute-start | bytes 3932168 | tf_op jit(solution)/shard_map/ppermute | solution.py:846
  415.2 19.6 %collective-permute-start.32 = (bf16[2,2,2,32,1536]{4,3,2,1,0:T(8,128)(2,1)}, bf16[2,2,2,32,1536]{4,3,2,1,0:T(8,128)(2,1)}, u32[]{:S(2)}, u32[]{:S(2)}) collective-permute-start(bf16[2,2,2,32,1536]{4,3,2,1,0:T(8,128)(2,1)} %fusion.1), channel_id=1, source_target_pairs={{0,16},{4,20},{8,24},{12,28},{16,0},{20,4},{24,8},{28,12},{1,17},{... | collective-permute-start | bytes 2359304 | tf_op jit(solution)/shard_map/ppermute | solution.py:846
  418.0 29.3 %collective-permute-start.33 = (bf16[2,32,8192]{2,1,0:T(8,128)(2,1)}, bf16[2,32,8192]{2,1,0:T(8,128)(2,1)}, u32[]{:S(2)}, u32[]{:S(2)}) collective-permute-start(bf16[2,32,8192]{2,1,0:T(8,128)(2,1)} %dynamic-slice_bitcast_fusion.4), channel_id=1, source_target_pairs={{0,1},{1,0},{2,3},{3,2},{4,5},{5,4},{6,7},{7,6},{8,9},{9,8},{10,11... | collective-permute-start | bytes 3145736 | tf_op jit(solution)/shard_map/ppermute | solution.py:846
  435.7 11.9 %collective-permute-start.36 = (f32[1,6144]{1,0:T(1,128)S(1)}, f32[1,6144]{1,0:T(1,128)S(1)}, u32[]{:S(2)}, u32[]{:S(2)}) collective-permute-start(f32[1,6144]{1,0:T(1,128)S(1)} %bitcast.323), channel_id=1, source_target_pairs={{0,1},{1,0},{2,3},{3,2},{4,5},{5,4},{6,7},{7,6},{8,9},{9,8},{10,11... | collective-permute-start | bytes 73736 | tf_op jit(solution)/shard_map/ppermute | solution.py:846
  447.7 4.8 collective-permute-start.37
  448.2 10.8 %collective-permute-start.34 = (bf16[2,2,2,2,64,512]{5,4,2,3,1,0:T(8,128)(2,1)S(1)}, bf16[2,2,2,2,64,512]{5,4,2,3,1,0:T(8,128)(2,1)S(1)}, u32[]{:S(2)}, u32[]{:S(2)}) collective-permute-start(bf16[2,2,2,2,64,512]{5,4,2,3,1,0:T(8,128)(2,1)S(1)} %copy.55), channel_id=1, source_target_pairs={{0,4},{4,0},{8,12},{12,8},{16,20},{20,16},{24,28},{28,24},{1,5},{5... | collective-permute-start | bytes 3145736 | tf_op jit(solution)/shard_map/ppermute | solution.py:846
  448.3 11.5 %collective-permute-start.40 = (bf16[2,2,2,2,64,512]{5,4,3,2,1,0:T(8,128)(2,1)S(1)}, bf16[2,2,2,2,64,512]{5,4,3,2,1,0:T(8,128)(2,1)S(1)}, u32[]{:S(2)}, u32[]{:S(2)}) collective-permute-start(bf16[2,2,2,2,64,512]{5,4,3,2,1,0:T(8,128)(2,1)S(1)} %dynamic-slice_bitcast_fusion.2), channel_id=1, source_target_pairs={{0,4},{4,0},{8,12},{12,8},{16,20},{20,16},{24,28},{28,24},{1,5},{5... | collective-permute-start | bytes 3145736 | tf_op jit(solution)/shard_map/ppermute | solution.py:846
  452.5 9.0 %collective-permute-start.52 = (f32[1,6144]{1,0:T(1,128)S(1)}, f32[1,6144]{1,0:T(1,128)S(1)}, u32[]{:S(2)}, u32[]{:S(2)}) collective-permute-start(f32[1,6144]{1,0:T(1,128)S(1)} %add.713), channel_id=1, source_target_pairs={{0,4},{4,0},{8,12},{12,8},{16,20},{20,16},{24,28},{28,24},{1,5},{5... | collective-permute-start | bytes 73736 | tf_op jit(solution)/shard_map/ppermute | solution.py:846
  454.2 33.3 %collective-permute-start.51 = (bf16[32,8192]{1,0:T(8,128)(2,1)S(1)}, bf16[32,8192]{1,0:T(8,128)(2,1)S(1)}, u32[]{:S(2)}, u32[]{:S(2)}) collective-permute-start(bf16[32,8192]{1,0:T(8,128)(2,1)S(1)} %get-tuple-element.276), channel_id=1, source_target_pairs={{0,2},{1,3},{2,0},{3,1},{4,6},{5,7},{6,4},{7,5},{8,10},{9,11},{10,... | collective-permute-start | bytes 1572872 | tf_op jit(solution)/shard_map/ppermute | solution.py:846
  456.2 17.6 %collective-permute-start.39 = (bf16[2,2,32,2560]{3,2,1,0:T(8,128)(2,1)S(1)}, bf16[2,2,32,2560]{3,2,1,0:T(8,128)(2,1)S(1)}, u32[]{:S(2)}, u32[]{:S(2)}) collective-permute-start(bf16[2,2,32,2560]{3,2,1,0:T(8,128)(2,1)S(1)} %fusion.4), channel_id=1, source_target_pairs={{0,16},{4,20},{8,24},{12,28},{16,0},{20,4},{24,8},{28,12},{1,17},{... | collective-permute-start | bytes 1966088 | tf_op jit(solution)/shard_map/ppermute | solution.py:846
  459.1 18.0 %collective-permute-start.41 = (bf16[2,2,32,1536]{3,2,1,0:T(8,128)(2,1)S(1)}, bf16[2,2,32,1536]{3,2,1,0:T(8,128)(2,1)S(1)}, u32[]{:S(2)}, u32[]{:S(2)}) collective-permute-start(bf16[2,2,32,1536]{3,2,1,0:T(8,128)(2,1)S(1)} %fusion.10), channel_id=1, source_target_pairs={{0,8},{4,12},{8,0},{12,4},{16,24},{20,28},{24,16},{28,20},{1,9},{5... | collective-permute-start | bytes 1179656 | tf_op jit(solution)/shard_map/ppermute | solution.py:846
  459.8 22.0 %collective-permute-start.38 = (bf16[2,2,2,64,512]{4,3,2,1,0:T(8,128)(2,1)S(1)}, bf16[2,2,2,64,512]{4,3,2,1,0:T(8,128)(2,1)S(1)}, u32[]{:S(2)}, u32[]{:S(2)}) collective-permute-start(bf16[2,2,2,64,512]{4,3,2,1,0:T(8,128)(2,1)S(1)} %fusion.6), channel_id=1, source_target_pairs={{0,8},{4,12},{8,0},{12,4},{16,24},{20,28},{24,16},{28,20},{1,9},{5... | collective-permute-start | bytes 1572872 | tf_op jit(solution)/shard_map/ppermute | solution.py:846
  461.5 23.5 %collective-permute-start.43 = (bf16[2,2,2,64,512]{4,3,2,1,0:T(8,128)(2,1)S(1)}, bf16[2,2,2,64,512]{4,3,2,1,0:T(8,128)(2,1)S(1)}, u32[]{:S(2)}, u32[]{:S(2)}) collective-permute-start(bf16[2,2,2,64,512]{4,3,2,1,0:T(8,128)(2,1)S(1)} %fusion.5), channel_id=1, source_target_pairs={{0,16},{4,20},{8,24},{12,28},{16,0},{20,4},{24,8},{28,12},{1,17},{... | collective-permute-start | bytes 1572872 | tf_op jit(solution)/shard_map/ppermute | solution.py:846
  473.8 12.7 %collective-permute-start.53 = (f32[2,6144]{1,0:T(2,128)S(1)}, f32[2,6144]{1,0:T(2,128)S(1)}, u32[]{:S(2)}, u32[]{:S(2)}) collective-permute-start(f32[2,6144]{1,0:T(2,128)S(1)} %maximum_select_fusion.7), channel_id=1, source_target_pairs={{0,8},{4,12},{8,0},{12,4},{16,24},{20,28},{24,16},{28,20},{1,9},{5... | collective-permute-start | bytes 147464 | tf_op jit(solution)/shard_map/ppermute | solution.py:846
  478.6 16.6 %collective-permute-start.45 = (bf16[2,32,4096]{2,1,0:T(8,128)(2,1)S(1)}, bf16[2,32,4096]{2,1,0:T(8,128)(2,1)S(1)}, u32[]{:S(2)}, u32[]{:S(2)}) collective-permute-start(bf16[2,32,4096]{2,1,0:T(8,128)(2,1)S(1)} %dynamic-slice_bitcast_fusion.5), channel_id=1, source_target_pairs={{0,1},{1,0},{2,3},{3,2},{4,5},{5,4},{6,7},{7,6},{8,9},{9,8},{10,11... | collective-permute-start | bytes 1572872 | tf_op jit(solution)/shard_map/ppermute | solution.py:846
  481.9 9.1 %collective-permute-start.42 = (bf16[2,2,64,512]{3,2,1,0:T(8,128)(2,1)S(1)}, bf16[2,2,64,512]{3,2,1,0:T(8,128)(2,1)S(1)}, u32[]{:S(2)}, u32[]{:S(2)}) collective-permute-start(bf16[2,2,64,512]{3,2,1,0:T(8,128)(2,1)S(1)} %fusion.13), channel_id=1, source_target_pairs={{0,16},{4,20},{8,24},{12,28},{16,0},{20,4},{24,8},{28,12},{1,17},{... | collective-permute-start | bytes 786440 | tf_op jit(solution)/shard_map/ppermute | solution.py:846
  485.2 8.6 %collective-permute-start.46 = (bf16[2,2,64,512]{3,2,1,0:T(8,128)(2,1)S(1)}, bf16[2,2,64,512]{3,2,1,0:T(8,128)(2,1)S(1)}, u32[]{:S(2)}, u32[]{:S(2)}) collective-permute-start(bf16[2,2,64,512]{3,2,1,0:T(8,128)(2,1)S(1)} %fusion.12), channel_id=1, source_target_pairs={{0,8},{4,12},{8,0},{12,4},{16,24},{20,28},{24,16},{28,20},{1,9},{5... | collective-permute-start | bytes 786440 | tf_op jit(solution)/shard_map/ppermute | solution.py:846
  486.6 17.1 %collective-permute-start.54 = (f32[4,6144]{1,0:T(4,128)S(1)}, f32[4,6144]{1,0:T(4,128)S(1)}, u32[]{:S(2)}, u32[]{:S(2)}) collective-permute-start(f32[4,6144]{1,0:T(4,128)S(1)} %maximum_select_fusion.6), channel_id=1, source_target_pairs={{0,16},{4,20},{8,24},{12,28},{16,0},{20,4},{24,8},{28,12},{1,17},{... | collective-permute-start | bytes 294920 | tf_op jit(solution)/shard_map/ppermute | solution.py:846
  491.2 8.9 %collective-permute-start.44 = (bf16[2,64,512]{2,1,0:T(8,128)(2,1)S(1)}, bf16[2,64,512]{2,1,0:T(8,128)(2,1)S(1)}, u32[]{:S(2)}, u32[]{:S(2)}) collective-permute-start(bf16[2,64,512]{2,1,0:T(8,128)(2,1)S(1)} %fusion.21), channel_id=1, source_target_pairs={{0,1},{1,0},{2,3},{3,2},{4,5},{5,4},{6,7},{7,6},{8,9},{9,8},{10,11... | collective-permute-start | bytes 393224 | tf_op jit(solution)/shard_map/ppermute | solution.py:846
  493.8 8.8 %collective-permute-start.48 = (bf16[2,64,512]{2,1,0:T(8,128)(2,1)S(1)}, bf16[2,64,512]{2,1,0:T(8,128)(2,1)S(1)}, u32[]{:S(2)}, u32[]{:S(2)}) collective-permute-start(bf16[2,64,512]{2,1,0:T(8,128)(2,1)S(1)} %fusion.20), channel_id=1, source_target_pairs={{0,1},{1,0},{2,3},{3,2},{4,5},{5,4},{6,7},{7,6},{8,9},{9,8},{10,11... | collective-permute-start | bytes 393224 | tf_op jit(solution)/shard_map/ppermute | solution.py:846
  495.3 19.0 %collective-permute-start.50 = (bf16[32,4096]{1,0:T(8,128)(2,1)S(1)}, bf16[32,4096]{1,0:T(8,128)(2,1)S(1)}, u32[]{:S(2)}, u32[]{:S(2)}) collective-permute-start(bf16[32,4096]{1,0:T(8,128)(2,1)S(1)} %get-tuple-element.280), channel_id=1, source_target_pairs={{0,2},{1,3},{2,0},{3,1},{4,6},{5,7},{6,4},{7,5},{8,10},{9,11},{10,... | collective-permute-start | bytes 786440 | tf_op jit(solution)/shard_map/ppermute | solution.py:846
  500.2 13.0 %collective-permute-start.47 = (bf16[64,512]{1,0:T(8,128)(2,1)S(1)}, bf16[64,512]{1,0:T(8,128)(2,1)S(1)}, u32[]{:S(2)}, u32[]{:S(2)}) collective-permute-start(bf16[64,512]{1,0:T(8,128)(2,1)S(1)} %get-tuple-element.277), channel_id=1, source_target_pairs={{0,2},{1,3},{2,0},{3,1},{4,6},{5,7},{6,4},{7,5},{8,10},{9,11},{10,... | collective-permute-start | bytes 196616 | tf_op jit(solution)/shard_map/ppermute | solution.py:846
  502.8 10.4 %collective-permute-start.49 = (bf16[64,512]{1,0:T(8,128)(2,1)S(1)}, bf16[64,512]{1,0:T(8,128)(2,1)S(1)}, u32[]{:S(2)}, u32[]{:S(2)}) collective-permute-start(bf16[64,512]{1,0:T(8,128)(2,1)S(1)} %get-tuple-element.273), channel_id=1, source_target_pairs={{0,2},{1,3},{2,0},{3,1},{4,6},{5,7},{6,4},{7,5},{8,10},{9,11},{10,... | collective-permute-start | bytes 196616 | tf_op jit(solution)/shard_map/ppermute | solution.py:846
  (57 other events, 427.8 us)
Sparse Core Ops, SparseCore 0:
  46.0 66.2 all-gather.2
  133.9 98.8 all-gather.4
  296.8 116.9 reduce-scatter.1
